TPU v7x, 32 devices: a whole 2x2x4 slice. The times are simulated.
32 devices in a mesh: ctx: 16 (over z, y, core), head: 2 (over x).
Axes of the slice: x: 2, y: 2, z: 4, core: 2. Of those that a mesh axis runs over, the one named last changes fastest.
Arguments:
- queries: bfloat16 [4096, 256], P('ctx', 'head'), may hold values from -6 to 6
- keys: bfloat16 [4096, 256], P('ctx', 'head'), may hold values from -6 to 6
- values: bfloat16 [4096, 2048], P('ctx', 'head'), may hold values from -6 to 6
- conv_keys: float32 [3, 256], P(None, 'head'), may hold values from -3.5 to 3.5
- conv_values: float32 [3, 2048], P(None, 'head'), may hold values from -3.5 to 3.5
- out_weight: bfloat16 [2048, 2048], P('head'), may hold values from -0.125 to 0.125
- cotangent: bfloat16 [4096, 2048], P('ctx', 'head'), may hold values from -6 to 6
Outputs:
- mixed_out: bfloat16 [4096, 2048], P('ctx', 'head')
- value_grad: bfloat16 [4096, 2048], P('ctx', 'head')
All inputs are finite; a program needn't handle non-finite values.
Results may differ from a plain program's by a relative error of at most 0.004.
The roundings to bfloat16 on the way count: a program that leaves them out, or rounds other values in their place, can miss the bound.
Values may be sent and summed in bfloat16 or wider, within the bound.
No kernel may reach another device: no remote copies, remote signals or barrier semaphores. Data moves between devices by JAX's collectives and lax.ppermute only.
A program may use at most 64 MiB of HBM per device.

v0:
```python
import jax
import jax.numpy as jnp
from jax import lax
from jax.sharding import PartitionSpec as P

FEAT = 16
VDIM = 128
CONV = 3


def shifted(x, axis, by):
    peers = lax.axis_size(axis)
    pairs = [(i, i + by) for i in range(peers) if 0 <= i + by < peers]
    return lax.ppermute(x, axis, pairs)


def features(rows_in, head_count):
    grid = rows_in.T.reshape(head_count, FEAT, rows_in.shape[0]) * FEAT ** (-0.25)
    square = grid[:, :, None, :] * grid[:, None, :, :]
    square = square.reshape(head_count, FEAT * FEAT, rows_in.shape[0]) * 0.5**0.5
    constant = jnp.ones((head_count, 1, rows_in.shape[0]), jnp.float32)
    return jnp.concatenate([constant, grid, square], 1).astype(jnp.bfloat16)


def convolve(token_block, before, weights):
    joined = jnp.concatenate([before, token_block], 0).astype(jnp.float32)
    block_rows = token_block.shape[0]
    running = weights[0] * joined[CONV - 1 : CONV - 1 + block_rows]
    for offset in range(1, CONV):
        running = (
            running + weights[offset] * joined[CONV - 1 - offset : CONV - 1 - offset + block_rows]
        )
    return running


def per_device(queries, keys, values, conv_keys, conv_values, out_weight, cotangent):
    highest = lax.Precision.HIGHEST
    block_rows = queries.shape[0]
    head_count = queries.shape[1] // FEAT
    key_width = keys.shape[1]
    slab_count = lax.axis_size("ctx")
    last_rows = jnp.concatenate(
        [keys[block_rows - (CONV - 1) :], values[block_rows - (CONV - 1) :]], 1
    )
    before = shifted(last_rows, "ctx", 1)
    key_conv = convolve(keys, before[:, :key_width], conv_keys)
    value_conv = convolve(values, before[:, key_width:], conv_values).astype(jnp.bfloat16)
    query_feat = features(queries.astype(jnp.float32), head_count)
    key_feat = features(key_conv, head_count)
    value_heads = value_conv.reshape(block_rows, head_count, VDIM)
    causal = jnp.arange(block_rows)[:, None] >= jnp.arange(block_rows)[None, :]
    scores = jnp.einsum("hpt,hps->hts", query_feat, key_feat, preferred_element_type=jnp.float32)
    scores = jnp.where(causal[None], scores, 0.0)
    weight_low = scores.astype(jnp.bfloat16)
    block_state = jnp.einsum(
        "hps,shv->hpv", key_feat, value_heads, preferred_element_type=jnp.float32
    )
    block_norm = jnp.sum(key_feat.astype(jnp.float32), 2)
    running = (block_state, block_norm)
    distance = 1
    while distance < slab_count:
        moved = shifted((running[0], running[1]), "ctx", distance)
        running = (running[0] + moved[0], running[1] + moved[1])
        distance = distance * 2
    prior_state = running[0] - block_state
    prior_norm = running[1] - block_norm
    numerator = jnp.einsum(
        "hts,shv->thv", weight_low, value_heads, preferred_element_type=jnp.float32
    )
    numerator = numerator + jnp.einsum(
        "hpt,hpv->thv",
        query_feat,
        prior_state.astype(jnp.bfloat16),
        preferred_element_type=jnp.float32,
    )
    denominator = jnp.sum(scores, 2).T + jnp.einsum(
        "hpt,hp->th", query_feat.astype(jnp.float32), prior_norm, precision=highest
    )
    attended = (
        (numerator / denominator[..., None])
        .astype(jnp.bfloat16)
        .reshape(block_rows, head_count * VDIM)
    )
    head_terms = jnp.dot(attended, out_weight, preferred_element_type=jnp.float32)
    mixed_out = lax.psum_scatter(head_terms, "head", scatter_dimension=1, tiled=True).astype(
        jnp.bfloat16
    )
    whole_grad = lax.all_gather(cotangent, "head", axis=1, tiled=True)
    out_grad = jnp.einsum("td,cd->tc", whole_grad, out_weight, preferred_element_type=jnp.float32)
    scaled_grad = (out_grad.reshape(block_rows, head_count, VDIM) / denominator[..., None]).astype(
        jnp.bfloat16
    )
    block_query = jnp.einsum(
        "hpt,thv->hpv", query_feat, scaled_grad, preferred_element_type=jnp.float32
    )
    total_later = block_query
    distance = 1
    while distance < slab_count:
        total_later = total_later + shifted(total_later, "ctx", -distance)
        distance = distance * 2
    later_state = total_later - block_query
    value_grad = jnp.einsum(
        "hts,thv->shv", weight_low, scaled_grad, preferred_element_type=jnp.float32
    )
    value_grad = value_grad + jnp.einsum(
        "hps,hpv->shv",
        key_feat,
        later_state.astype(jnp.bfloat16),
        preferred_element_type=jnp.float32,
    )
    return (mixed_out, value_grad.astype(jnp.bfloat16).reshape(block_rows, head_count * VDIM))


def solution(mesh):
    in_specs = (
        P("ctx", "head"),
        P("ctx", "head"),
        P("ctx", "head"),
        P(None, "head"),
        P(None, "head"),
        P("head", None),
        P("ctx", "head"),
    )
    out_specs = (P("ctx", "head"), P("ctx", "head"))
    return jax.shard_map(
        per_device, mesh=mesh, in_specs=in_specs, out_specs=out_specs, check_vma=False
    )
```

profile of v0, /device:TPU:0, one launch (start us, length us, event | category | flops | bytes accessed | tf_op | source)
XLA Modules:
  0.0 277.9 jit_solution(15436535626888233014)
XLA Ops:
  7.2 0.0 all-gather.2.cloned.1.call-start
  7.2 0.7 slice.50
  7.9 0.7 slice.49
  8.6 2.4 collective-permute-start
  11.0 0.8 fusion.28
  11.9 0.8 slice_bitcast_fusion.2
  12.7 1.2 maximum_convert_fusion
  13.9 0.1 fusion.19
  14.0 0.1 copy.44
  14.1 0.3 multiply_convert_fusion
  14.4 0.3 fusion.9
  14.8 0.0 copy-start.2
  14.8 0.6 fusion.12
  15.4 0.2 copy-done.2
  15.6 0.2 copy.49
  15.8 4.7 %collective-permute-start.1 = (f32[8,273,128]{2,0,1:T(8,128)S(1)}, f32[8,273,128]{2,0,1:T(8,128)S(1)}, u32[]{:S(2)}, u32[]{:S(2)}) collective-permute-start(f32[8,273,128]{2,0,1:T(8,128)S(1)} %copy.49), channel_id=1, source_target_pairs={{0,2},{2,4},{4,6},{6,8},{8,10},{10,12},{12,14},{14,16},{16,18},{18... | collective-permute-start | bytes 3354632 | tf_op jit(solution)/shard_map/ppermute | solution.py:14
  20.6 2.3 collective-permute-done.1
  22.9 0.2 copy_add_fusion.1
  23.1 16.7 %collective-permute-start.2 = (f32[8,273,128]{2,0,1:T(8,128)S(1)}, f32[8,273,128]{2,0,1:T(8,128)}, u32[]{:S(2)}, u32[]{:S(2)}) collective-permute-start(f32[8,273,128]{2,0,1:T(8,128)S(1)} %copy_add_fusion.1), channel_id=1, source_target_pairs={{0,4},{2,6},{4,8},{6,10},{8,12},{10,14},{12,16},{14,18},{16,20},{1... | collective-permute-start | bytes 3354632 | tf_op jit(solution)/shard_map/ppermute | solution.py:14
  39.9 0.0 all-gather.2.cloned.1.call-update
  39.9 0.0 reduce-scatter.2.cloned.1.call-start
  39.9 0.7 multiply_bitcast_fusion
  40.6 1.0 copy.43
  41.6 0.6 convert_reduce_fusion
  42.3 1.7 collective-permute-start.5
  43.9 19.1 %collective-permute-done.2 = f32[8,273,128]{2,0,1:T(8,128)} collective-permute-done((f32[8,273,128]{2,0,1:T(8,128)S(1)}, f32[8,273,128]{2,0,1:T(8,128)}, u32[]{:S(2)}, u32[]{:S(2)}) %collective-permute-start.2) | collective-permute-done | bytes 1118240 | tf_op jit(solution)/shard_map/ppermute | solution.py:14
  63.1 1.4 add.71
  64.4 4.6 %collective-permute-start.3 = (f32[8,273,128]{2,0,1:T(8,128)S(1)}, f32[8,273,128]{2,0,1:T(8,128)S(1)}, u32[]{:S(2)}, u32[]{:S(2)}) collective-permute-start(f32[8,273,128]{2,0,1:T(8,128)S(1)} %add.71), channel_id=1, source_target_pairs={{0,8},{2,10},{4,12},{6,14},{8,16},{10,18},{12,20},{14,22},{16,24},... | collective-permute-start | bytes 3354632 | tf_op jit(solution)/shard_map/ppermute | solution.py:14
  69.1 0.3 multiply_convert_fusion.1
  69.4 3.4 %collective-permute-start.6 = (f32[8,273]{1,0:T(8,128)S(1)}, f32[8,273]{1,0:T(8,128)S(1)}, u32[]{:S(2)}, u32[]{:S(2)}) collective-permute-start(f32[8,273]{1,0:T(8,128)S(1)} %add.76), channel_id=1, source_target_pairs={{0,4},{2,6},{4,8},{6,10},{8,12},{10,14},{12,16},{14,18},{16,20},{1... | collective-permute-start | bytes 26216 | tf_op jit(solution)/shard_map/ppermute | solution.py:14
  72.9 1.4 collective-permute-done.6
  74.3 23.1 %collective-permute-start.7 = (f32[8,273]{1,0:T(8,128)S(1)}, f32[8,273]{1,0:T(8,128)S(1)}, u32[]{:S(2)}, u32[]{:S(2)}) collective-permute-start(f32[8,273]{1,0:T(8,128)S(1)} %add.77), channel_id=1, source_target_pairs={{0,8},{2,10},{4,12},{6,14},{8,16},{10,18},{12,20},{14,22},{16,24},... | collective-permute-start | bytes 26216 | tf_op jit(solution)/shard_map/ppermute | solution.py:14
  97.4 1.4 collective-permute-done.7
  98.8 5.2 %collective-permute-start.8 = (f32[8,273]{1,0:T(8,128)S(1)}, f32[8,273]{1,0:T(8,128)S(1)}, u32[]{:S(2)}, u32[]{:S(2)}) collective-permute-start(f32[8,273]{1,0:T(8,128)S(1)} %add.78), channel_id=1, source_target_pairs={{0,16},{2,18},{4,20},{6,22},{8,24},{10,26},{12,28},{14,30},{1,17},... | collective-permute-start | bytes 26216 | tf_op jit(solution)/shard_map/ppermute | solution.py:14
  104.0 2.2 select_reduce_fusion
  106.3 0.8 fusion.21
  107.1 0.2 add.72
  107.3 5.2 %collective-permute-start.4 = (f32[8,273,128]{2,0,1:T(8,128)S(1)}, f32[8,273,128]{2,0,1:T(8,128)}, u32[]{:S(2)}, u32[]{:S(2)}) collective-permute-start(f32[8,273,128]{2,0,1:T(8,128)S(1)} %add.72), channel_id=1, source_target_pairs={{0,16},{2,18},{4,20},{6,22},{8,24},{10,26},{12,28},{14,30},{1,17},... | collective-permute-start | bytes 3354632 | tf_op jit(solution)/shard_map/ppermute | solution.py:14
  112.5 3.9 %fusion.30 = f32[256,1024]{0,1:T(8,128)S(1)} fusion(bf16[256,2048]{1,0:T(8,128)(2,1)} %all-gather.2.cloned.1.call-done, bf16[1024,2048]{1,0:T(8,128)(2,1)} %param.12), kind=kOutput, calls=%fused_computation.60 | convolution fusion | flops 1073741824 | bytes 6291456 | tf_op jit(solution)/shard_map/td,cd->tc/dot_general | solution.py:89
  116.5 0.6 fusion.26
  117.0 0.4 copy-done.15
  117.4 1.2 copy.56
  118.6 1.3 collective-permute-start.9
  119.9 0.4 fusion.10
  120.3 10.5 %collective-permute-done.4 = f32[8,273,128]{2,0,1:T(8,128)} collective-permute-done((f32[8,273,128]{2,0,1:T(8,128)S(1)}, f32[8,273,128]{2,0,1:T(8,128)}, u32[]{:S(2)}, u32[]{:S(2)}) %collective-permute-start.4) | collective-permute-done | bytes 1118240 | tf_op jit(solution)/shard_map/ppermute | solution.py:14
  130.8 1.5 subtract_convert_fusion.1
  132.4 0.7 fusion.3
  133.1 1.4 copy-done.14
  134.6 2.6 fusion.29
  137.2 0.0 reduce-scatter.2.cloned.1.call-update
  137.2 1.5 copy_add_fusion
  138.7 1.3 collective-permute-start.10
  140.0 24.1 %collective-permute-done.10 = f32[8,273,128]{2,0,1:T(8,128)S(1)} collective-permute-done((f32[8,273,128]{2,0,1:T(8,128)S(1)}, f32[8,273,128]{2,0,1:T(8,128)S(1)}, u32[]{:S(2)}, u32[]{:S(2)}) %collective-permute-start.10) | collective-permute-done | bytes 1118240 | tf_op jit(solution)/shard_map/ppermute | solution.py:14
  164.1 0.1 add.83
  164.3 1.4 collective-permute-start.11
  165.7 50.2 %collective-permute-done.11 = f32[8,273,128]{2,0,1:T(8,128)S(1)} collective-permute-done((f32[8,273,128]{2,0,1:T(8,128)S(1)}, f32[8,273,128]{2,0,1:T(8,128)S(1)}, u32[]{:S(2)}, u32[]{:S(2)}) %collective-permute-start.11) | collective-permute-done | bytes 1118240 | tf_op jit(solution)/shard_map/ppermute | solution.py:14
  215.9 0.2 add.84
  216.1 1.3 collective-permute-start.12
  217.4 0.5 fusion.16
  217.9 49.1 %collective-permute-done.12 = f32[8,273,128]{2,0,1:T(8,128)S(1)} collective-permute-done((f32[8,273,128]{2,0,1:T(8,128)S(1)}, f32[8,273,128]{2,0,1:T(8,128)S(1)}, u32[]{:S(2)}, u32[]{:S(2)}) %collective-permute-start.12) | collective-permute-done | bytes 1118240 | tf_op jit(solution)/shard_map/ppermute | solution.py:14
  267.0 0.3 subtract_convert_fusion
  267.3 0.7 fusion.2
  268.0 1.0 copy.59
  269.0 2.1 convert_element_type.50
  (50 shorter events, 0.2 us)
Async XLA Ops:
  7.2 6.7 %copy-start.10 = (bf16[256,128]{1,0:T(8,128)(2,1)S(1)}, bf16[256,128]{1,0:T(8,128)(2,1)}, u32[]{:S(2)}) copy-start(bf16[256,128]{1,0:T(8,128)(2,1)} %param.8) | copy-start | bytes 196612
  7.2 105.4 %all-gather.2.cloned.1.call-start = ((), (), s32[]{:S(2)}) async-start(), calls=%async_computation.2 | async-start | bytes 1572864 | tf_op jit(solution)/shard_map/all_gather | solution.py:88
  8.6 4.0 %collective-permute-start = (bf16[2,1152]{1,0:T(2,128)(2,1)S(1)}, bf16[2,1152]{1,0:T(2,128)(2,1)S(1)}, u32[]{:S(2)}, u32[]{:S(2)}) collective-permute-start(bf16[2,1152]{1,0:T(2,128)(2,1)S(1)} %pad_maximum_fusion.2), channel_id=1, source_target_pairs={{0,2},{2,4},{4,6},{6,8},{8,10},{10,12},{12,14},{14,16},{16,18},{18... | collective-permute-start | bytes 13832 | tf_op jit(solution)/shard_map/ppermute | solution.py:14
  14.1 89.9 %copy-start.8 = (bf16[8,16,256]{2,1,0:T(8,128)(2,1)}, bf16[8,16,256]{2,1,0:T(8,128)(2,1)S(1)}, u32[]{:S(2)}) copy-start(bf16[8,16,256]{2,1,0:T(8,128)(2,1)S(1)} %bitcast_convert_fusion) | copy-start | bytes 196612
  14.4 89.6 %copy-start = (bf16[8,16,16,256]{3,2,1,0:T(8,128)(2,1)}, bf16[8,16,16,256]{3,2,1,0:T(8,128)(2,1)S(1)}, u32[]{:S(2)}) copy-start(bf16[8,16,16,256]{3,2,1,0:T(8,128)(2,1)S(1)} %multiply_convert_fusion) | copy-start | bytes 3145732
  14.8 0.8 copy-start.2
  15.8 24.1 %copy-start.11 = (bf16[256,128]{1,0:T(8,128)(2,1)S(1)}, bf16[256,128]{1,0:T(8,128)(2,1)}, u32[]{:S(2)}) copy-start(bf16[256,128]{1,0:T(8,128)(2,1)} %param.7) | copy-start | bytes 196612
  15.8 7.0 %collective-permute-start.1 = (f32[8,273,128]{2,0,1:T(8,128)S(1)}, f32[8,273,128]{2,0,1:T(8,128)S(1)}, u32[]{:S(2)}, u32[]{:S(2)}) collective-permute-start(f32[8,273,128]{2,0,1:T(8,128)S(1)} %copy.49), channel_id=1, source_target_pairs={{0,2},{2,4},{4,6},{6,8},{8,10},{10,12},{12,14},{14,16},{16,18},{18... | collective-permute-start | bytes 3354632 | tf_op jit(solution)/shard_map/ppermute | solution.py:14
  23.1 40.0 %collective-permute-start.2 = (f32[8,273,128]{2,0,1:T(8,128)S(1)}, f32[8,273,128]{2,0,1:T(8,128)}, u32[]{:S(2)}, u32[]{:S(2)}) collective-permute-start(f32[8,273,128]{2,0,1:T(8,128)S(1)} %copy_add_fusion.1), channel_id=1, source_target_pairs={{0,4},{2,6},{4,8},{6,10},{8,12},{10,14},{12,16},{14,18},{16,20},{1... | collective-permute-start | bytes 3354632 | tf_op jit(solution)/shard_map/ppermute | solution.py:14
  39.9 229.1 %reduce-scatter.2.cloned.1.call-start = ((), (), s32[]{:S(2)}) async-start(), calls=%async_computation.1 | async-start | bytes 3145728 | tf_op jit(solution)/shard_map/reduce_scatter | solution.py:85
  42.3 27.2 %collective-permute-start.5 = (f32[8,273]{1,0:T(8,128)S(1)}, f32[8,273]{1,0:T(8,128)S(1)}, u32[]{:S(2)}, u32[]{:S(2)}) collective-permute-start(f32[8,273]{1,0:T(8,128)S(1)} %convert_reduce_fusion), channel_id=1, source_target_pairs={{0,2},{2,4},{4,6},{6,8},{8,10},{10,12},{12,14},{14,16},{16,18},{18... | collective-permute-start | bytes 26216 | tf_op jit(solution)/shard_map/ppermute | solution.py:14
  64.4 42.7 %collective-permute-start.3 = (f32[8,273,128]{2,0,1:T(8,128)S(1)}, f32[8,273,128]{2,0,1:T(8,128)S(1)}, u32[]{:S(2)}, u32[]{:S(2)}) collective-permute-start(f32[8,273,128]{2,0,1:T(8,128)S(1)} %add.71), channel_id=1, source_target_pairs={{0,8},{2,10},{4,12},{6,14},{8,16},{10,18},{12,20},{14,22},{16,24},... | collective-permute-start | bytes 3354632 | tf_op jit(solution)/shard_map/ppermute | solution.py:14
  69.4 36.9 %copy-start.4 = (bf16[8,16,16,256]{3,2,1,0:T(8,128)(2,1)}, bf16[8,16,16,256]{3,2,1,0:T(8,128)(2,1)S(1)}, u32[]{:S(2)}) copy-start(bf16[8,16,16,256]{3,2,1,0:T(8,128)(2,1)S(1)} %multiply_convert_fusion.1) | copy-start | bytes 3145732
  69.4 4.8 %collective-permute-start.6 = (f32[8,273]{1,0:T(8,128)S(1)}, f32[8,273]{1,0:T(8,128)S(1)}, u32[]{:S(2)}, u32[]{:S(2)}) collective-permute-start(f32[8,273]{1,0:T(8,128)S(1)} %add.76), channel_id=1, source_target_pairs={{0,4},{2,6},{4,8},{6,10},{8,12},{10,14},{12,16},{14,18},{16,20},{1... | collective-permute-start | bytes 26216 | tf_op jit(solution)/shard_map/ppermute | solution.py:14
  72.9 33.4 %copy-start.12 = (bf16[8,16,256]{2,1,0:T(8,128)(2,1)}, bf16[8,16,256]{2,1,0:T(8,128)(2,1)S(1)}, u32[]{:S(2)}) copy-start(bf16[8,16,256]{2,1,0:T(8,128)(2,1)S(1)} %bitcast_convert_fusion.1) | copy-start | bytes 196612
  74.3 24.5 %collective-permute-start.7 = (f32[8,273]{1,0:T(8,128)S(1)}, f32[8,273]{1,0:T(8,128)S(1)}, u32[]{:S(2)}, u32[]{:S(2)}) collective-permute-start(f32[8,273]{1,0:T(8,128)S(1)} %add.77), channel_id=1, source_target_pairs={{0,8},{2,10},{4,12},{6,14},{8,16},{10,18},{12,20},{14,22},{16,24},... | collective-permute-start | bytes 26216 | tf_op jit(solution)/shard_map/ppermute | solution.py:14
  98.8 7.5 %collective-permute-start.8 = (f32[8,273]{1,0:T(8,128)S(1)}, f32[8,273]{1,0:T(8,128)S(1)}, u32[]{:S(2)}, u32[]{:S(2)}) collective-permute-start(f32[8,273]{1,0:T(8,128)S(1)} %add.78), channel_id=1, source_target_pairs={{0,16},{2,18},{4,20},{6,22},{8,24},{10,26},{12,28},{14,30},{1,17},... | collective-permute-start | bytes 26216 | tf_op jit(solution)/shard_map/ppermute | solution.py:14
  107.3 23.6 %collective-permute-start.4 = (f32[8,273,128]{2,0,1:T(8,128)S(1)}, f32[8,273,128]{2,0,1:T(8,128)}, u32[]{:S(2)}, u32[]{:S(2)}) collective-permute-start(f32[8,273,128]{2,0,1:T(8,128)S(1)} %add.72), channel_id=1, source_target_pairs={{0,16},{2,18},{4,20},{6,22},{8,24},{10,26},{12,28},{14,30},{1,17},... | collective-permute-start | bytes 3354632 | tf_op jit(solution)/shard_map/ppermute | solution.py:14
  112.5 3.9 %copy-start.13 = (bf16[8,16,256]{2,1,0:T(8,128)(2,1)S(1)}, bf16[8,16,256]{2,1,0:T(8,128)(2,1)}, u32[]{:S(2)}) copy-start(bf16[8,16,256]{2,1,0:T(8,128)(2,1)} %copy-done.12) | copy-start | bytes 196612
  112.5 3.9 %copy-start.5 = (bf16[8,16,16,256]{3,2,1,0:T(8,128)(2,1)S(1)}, bf16[8,16,16,256]{3,2,1,0:T(8,128)(2,1)}, u32[]{:S(2)}) copy-start(bf16[8,16,16,256]{3,2,1,0:T(8,128)(2,1)} %copy-done.4) | copy-start | bytes 3145732
  116.4 1.0 copy-start.15
  117.4 2.5 copy-start.3
  117.4 2.5 copy-start.6
  118.6 18.6 %collective-permute-start.9 = (f32[8,273,128]{2,0,1:T(8,128)}, f32[8,273,128]{2,0,1:T(8,128)}, u32[]{:S(2)}, u32[]{:S(2)}) collective-permute-start(f32[8,273,128]{2,0,1:T(8,128)} %copy.56), channel_id=1, source_target_pairs={{2,0},{4,2},{6,4},{8,6},{10,8},{12,10},{14,12},{16,14},{18,16},{20... | collective-permute-start | bytes 3354632 | tf_op jit(solution)/shard_map/ppermute | solution.py:14
  132.4 2.2 copy-start.14
  138.7 25.4 %collective-permute-start.10 = (f32[8,273,128]{2,0,1:T(8,128)S(1)}, f32[8,273,128]{2,0,1:T(8,128)S(1)}, u32[]{:S(2)}, u32[]{:S(2)}) collective-permute-start(f32[8,273,128]{2,0,1:T(8,128)S(1)} %copy_add_fusion), channel_id=1, source_target_pairs={{4,0},{6,2},{8,4},{10,6},{12,8},{14,10},{16,12},{18,14},{20,16},{2... | collective-permute-start | bytes 3354632 | tf_op jit(solution)/shard_map/ppermute | solution.py:14
  164.2 53.1 %copy-start.7 = (bf16[8,256,256]{1,2,0:T(8,128)(2,1)S(1)}, bf16[8,256,256]{1,2,0:T(8,128)(2,1)}, u32[]{:S(2)}) copy-start(bf16[8,256,256]{1,2,0:T(8,128)(2,1)} %get-tuple-element.15) | copy-start | bytes 3145732
  164.3 53.1 %copy-start.16 = (f32[256,1024]{0,1:T(8,128)S(1)}, f32[256,1024]{0,1:T(8,128)}, u32[]{:S(2)}) copy-start(f32[256,1024]{0,1:T(8,128)} %copy-done.15) | copy-start | bytes 3145732
  164.3 51.7 %collective-permute-start.11 = (f32[8,273,128]{2,0,1:T(8,128)S(1)}, f32[8,273,128]{2,0,1:T(8,128)S(1)}, u32[]{:S(2)}, u32[]{:S(2)}) collective-permute-start(f32[8,273,128]{2,0,1:T(8,128)S(1)} %add.83), channel_id=1, source_target_pairs={{8,0},{10,2},{12,4},{14,6},{16,8},{18,10},{20,12},{22,14},{24,16},... | collective-permute-start | bytes 3354632 | tf_op jit(solution)/shard_map/ppermute | solution.py:14
  216.1 50.9 %collective-permute-start.12 = (f32[8,273,128]{2,0,1:T(8,128)S(1)}, f32[8,273,128]{2,0,1:T(8,128)S(1)}, u32[]{:S(2)}, u32[]{:S(2)}) collective-permute-start(f32[8,273,128]{2,0,1:T(8,128)S(1)} %add.84), channel_id=1, source_target_pairs={{16,0},{18,2},{20,4},{22,6},{24,8},{26,10},{28,12},{30,14},{17,1},... | collective-permute-start | bytes 3354632 | tf_op jit(solution)/shard_map/ppermute | solution.py:14
  217.9 49.4 %copy-start.1 = (bf16[8,16,16,256]{3,2,1,0:T(8,128)(2,1)S(1)}, bf16[8,16,16,256]{3,2,1,0:T(8,128)(2,1)}, u32[]{:S(2)}) copy-start(bf16[8,16,16,256]{3,2,1,0:T(8,128)(2,1)} %copy-done) | copy-start | bytes 3145732
  217.9 49.4 %copy-start.9 = (bf16[8,16,256]{2,1,0:T(8,128)(2,1)S(1)}, bf16[8,16,256]{2,1,0:T(8,128)(2,1)}, u32[]{:S(2)}) copy-start(bf16[8,16,256]{2,1,0:T(8,128)(2,1)} %copy-done.8) | copy-start | bytes 196612
Sparse Core Ops, SparseCore 0:
  40.0 22.3 all-gather.1
  137.3 55.9 reduce-scatter.1
where the time goes:
time: 279 us; the launch traced here: 278 us
  waiting for transfers between devices  158 us (57%)
  starting transfers between devices  72.5 us (26%)
  between operations  14.5 us (5%)
  matrix products  13 us (5%)
  other arithmetic  11.1 us (4%)
  local copies, waits for them, and re-layouts  8.69 us (3%)
    ppermute x13, waiting for transfers between devices, shifted(): return lax.ppermute(x, axis, pairs)  158 us
    ppermute x13, starting transfers between devices, shifted(): return lax.ppermute(x, axis, pairs)  72.4 us
  transfers between devices with their start and end apart: 15, of which 8 were waited for; matrix products, arithmetic and copies ran while one was open for 9% of the time, Pallas kernels for 0%

commit v1 on v0

v1 whole, which is shorter than its diff:
```python
import jax
import jax.numpy as jnp
from jax import lax
from jax.experimental import pallas as pl
from jax.experimental.pallas import tpu as pltpu
from jax.sharding import PartitionSpec as P

FEAT = 16
VDIM = 128
CONV = 3
ROWS = 160
PLANE = 4

F32 = jnp.float32
BF16 = jnp.bfloat16
TN = (((0,), (0,)), ((), ()))
NT = (((1,), (1,)), ((), ()))
NN = (((1,), (0,)), ((), ()))


def mm(a, b, dims):
    return lax.dot_general(a, b, dims, preferred_element_type=F32)


def call(body, scalars, operands, in_specs, out_shape, out_specs, flops, scratch=()):
    moved = sum(x.size * x.dtype.itemsize for x in operands)
    moved += sum(x.size * x.dtype.itemsize for x in out_shape)
    return pl.pallas_call(
        body,
        out_shape=out_shape,
        grid_spec=pltpu.PrefetchScalarGridSpec(
            num_scalar_prefetch=1,
            grid=(1,),
            in_specs=in_specs,
            out_specs=out_specs,
            scratch_shapes=list(scratch),
        ),
        compiler_params=pltpu.CompilerParams(vmem_limit_bytes=28 * 1024 * 1024),
        cost_estimate=pl.CostEstimate(flops=flops, bytes_accessed=moved, transcendentals=0),
    )(scalars, *operands)


def whole(x):
    shape = x.shape
    return pl.BlockSpec(shape, lambda i, s: (0,) * len(shape))


def column_block(x, width, distance):
    return pl.BlockSpec((x.shape[0], width), lambda i, s: (0, s[1] ^ distance))


def store_features(out_ref, rows_in, doubled):
    heads = rows_in.shape[0] // FEAT
    tokens = rows_in.shape[1]
    grid = rows_in.reshape(heads, FEAT, tokens) * FEAT ** (-0.25)
    twice = jnp.concatenate([grid, grid], 1)
    out_ref[:, 0:FEAT, :] = grid.astype(BF16)
    half = FEAT // 2
    for turn in range(half):
        square = grid * twice[:, turn : turn + FEAT, :] * 0.5**0.5
        if doubled and turn > 0:
            square = square * 2.0
        out_ref[:, FEAT * (turn + 1) : FEAT * (turn + 2), :] = square.astype(BF16)
    square = grid[:, :half, :] * grid[:, half:, :] * 0.5**0.5
    if doubled:
        square = square * 2.0
    first = lax.broadcasted_iota(jnp.int32, (heads, half, tokens), 1) == 0
    constant = jnp.where(first, 1.0, 0.0)
    out_ref[:, FEAT * (half + 1) :, :] = jnp.concatenate([square, constant], 1).astype(BF16)


def store_piece(rank, head, per_piece, state, own_ref, send_ref):
    slot = rank ^ (head // per_piece)
    at = (head % per_piece) * ROWS

    @pl.when(slot == 0)
    def _():
        own_ref[at : at + ROWS, :] = state

    @pl.when(slot != 0)
    def _():
        send_ref[slot - 1, at : at + ROWS, :] = state.astype(BF16)


def load_piece(rank, head, per_piece, ref):
    at = (head % per_piece) * ROWS
    return ref[rank ^ (head // per_piece), at : at + ROWS, :]


def query_kernel(s_ref, q_ref, cot_ref, w_ref, qd_ref, og_ref):
    store_features(qd_ref, q_ref[...].astype(F32).T, True)
    og_ref[...] = mm(cot_ref[...], w_ref[...], NT)


def grad_kernel(s_ref, cot_ref, w_ref, before_ref, og_ref):
    og_ref[...] = before_ref[...] + mm(cot_ref[...], w_ref[...], NT)


def conv_rows(x, before, taps):
    x = x.astype(F32)
    row = lax.broadcasted_iota(jnp.int32, x.shape, 0)
    running = taps[0:1, :] * x
    for offset in range(1, CONV):
        moved = pltpu.roll(x, offset, 0)
        for at in range(offset):
            source = before[CONV - 1 - offset + at : CONV - offset + at, :]
            moved = jnp.where(row == at, source, moved)
        running = running + taps[offset : offset + 1, :] * moved
    return running


def key_kernel(
    s_ref, k_ref, v_ref, before_ref, ck_ref, cv_ref, kf_ref, vc_ref, own_ref, send_ref, norm_ref
):
    rank = s_ref[0]
    heads = kf_ref.shape[0]
    per_piece = heads // PLANE
    width = k_ref.shape[1]
    before = before_ref[...].astype(F32)
    key_conv = conv_rows(k_ref[...], before[:, :width], ck_ref[...])
    store_features(kf_ref, key_conv.T, False)
    ones = jnp.ones((heads, k_ref.shape[0]), BF16)
    row = lax.broadcasted_iota(jnp.int32, (heads, ROWS), 0)
    norm = jnp.zeros((heads, ROWS), F32)
    for head in range(heads):
        at = head * VDIM
        value = conv_rows(
            v_ref[:, at : at + VDIM],
            before[:, width + at : width + at + VDIM],
            cv_ref[:, at : at + VDIM],
        ).astype(BF16)
        vc_ref[:, at : at + VDIM] = value
        feat = kf_ref[head]
        norm = jnp.where(row == head, mm(ones, feat, NT), norm)
        store_piece(rank, head, per_piece, mm(feat, value, NN), own_ref, send_ref)
    norm_ref[...] = norm


def score_kernel(s_ref, qd_ref, kf_ref, vc_ref, low_ref, den_ref, num_ref):
    heads = kf_ref.shape[0]
    tokens = kf_ref.shape[2]
    key_at = lax.broadcasted_iota(jnp.int32, (tokens, tokens), 0)
    query_at = lax.broadcasted_iota(jnp.int32, (tokens, tokens), 1)
    causal = key_at <= query_at
    for head in range(heads):
        scores = jnp.where(causal, mm(kf_ref[head], qd_ref[head], TN), 0.0)
        den_ref[head : head + 1, :] = jnp.sum(scores, 0, keepdims=True)
        low = scores.astype(BF16)
        low_ref[head] = low
        at = head * VDIM
        num_ref[:, at : at + VDIM] = mm(low, vc_ref[:, at : at + VDIM], TN)


def scale_kernel(s_ref, norm_ref, den_ref, qd_ref, og_ref, inv_ref, sg_ref, own_ref, send_ref):
    rank = s_ref[0]
    heads = qd_ref.shape[0]
    per_piece = heads // PLANE
    norm = norm_ref[...]
    high = norm.astype(BF16).astype(F32)
    middle = (norm - high).astype(BF16).astype(F32)
    rest = norm - high - middle
    parts = jnp.concatenate([high, middle, rest, jnp.zeros_like(rest)], 0).astype(BF16)
    lines = []
    for head in range(heads):
        terms = mm(parts, qd_ref[head], NN)
        line = den_ref[head : head + 1, :] + terms[head : head + 1, :]
        line = line + terms[heads + head : heads + head + 1, :]
        lines.append(line + terms[2 * heads + head : 2 * heads + head + 1, :])
    inverse = (1.0 / jnp.concatenate(lines, 0)).T
    inv_ref[...] = inverse
    for head in range(heads):
        at = head * VDIM
        scaled = (og_ref[:, at : at + VDIM] * inverse[:, head : head + 1]).astype(BF16)
        sg_ref[:, at : at + VDIM] = scaled
        store_piece(rank, head, per_piece, mm(qd_ref[head], scaled, NN), own_ref, send_ref)


def near_kernel(s_ref, low_ref, sg_ref, vg_ref):
    for head in range(low_ref.shape[0]):
        at = head * VDIM
        vg_ref[:, at : at + VDIM] = mm(low_ref[head], sg_ref[:, at : at + VDIM], NN)


def attend_kernel(s_ref, qd_ref, prior_ref, num_ref, inv_ref, w_ref, att_ref, part_ref):
    rank = s_ref[0]
    heads = qd_ref.shape[0]
    per_piece = heads // PLANE
    for head in range(heads):
        at = head * VDIM
        prior = load_piece(rank, head, per_piece, prior_ref)
        total = num_ref[:, at : at + VDIM] + mm(qd_ref[head], prior, TN)
        att_ref[:, at : at + VDIM] = (total * inv_ref[:, head : head + 1]).astype(BF16)
    part_ref[...] = mm(att_ref[...], w_ref[...], NN).astype(BF16)


def mix_kernel(s_ref, att_ref, w_ref, part_ref):
    part_ref[...] = mm(att_ref[...], w_ref[...], NN).astype(part_ref.dtype)


def far_kernel(s_ref, kf_ref, later_ref, near_ref, vg_ref):
    rank = s_ref[0]
    heads = kf_ref.shape[0]
    per_piece = heads // PLANE
    for head in range(heads):
        at = head * VDIM
        later = load_piece(rank, head, per_piece, later_ref)
        total = near_ref[:, at : at + VDIM] + mm(kf_ref[head], later, TN)
        vg_ref[:, at : at + VDIM] = total.astype(BF16)


def shifted(x, axis, by):
    peers = lax.axis_size(axis)
    pairs = [(i, i + by) for i in range(peers) if 0 <= i + by < peers]
    return lax.ppermute(x, axis, pairs)


def swapped(x, axis, distance):
    peers = lax.axis_size(axis)
    return lax.ppermute(x, axis, [(i, i ^ distance) for i in range(peers)])


def planes_before(total, sign, kind):
    planes = lax.axis_size("ctx") // PLANE
    running = total
    before = jnp.zeros_like(total)
    distance = 1
    while distance < planes:
        moved = shifted(running.astype(kind), "ctx", sign * distance * PLANE).astype(F32)
        before = before + moved
        running = running + moved
        distance = distance * 2
    return before


def scan_states(own, send, rank, sign):
    got = [own] + [swapped(send[j - 1], "ctx", j).astype(F32) for j in range(1, PLANE)]
    total = got[0] + got[1] + got[2] + got[3]
    before = planes_before(total, sign, BF16)
    pieces = []
    for j in range(PLANE):
        piece = before
        for i in range(PLANE):
            if i == j:
                continue
            ahead = (rank ^ i) < (rank ^ j) if sign > 0 else (rank ^ i) > (rank ^ j)
            piece = piece + jnp.where(ahead, got[i], 0.0)
        pieces.append(piece.astype(BF16))
    return jnp.stack([pieces[0]] + [swapped(pieces[j], "ctx", j) for j in range(1, PLANE)], 0)


def scan_norms(norm, rank):
    before = jnp.zeros_like(norm)
    total = norm
    distance = 1
    while distance < PLANE:
        moved = swapped(total, "ctx", distance)
        before = before + jnp.where((rank & distance) != 0, moved, 0.0)
        total = total + moved
        distance = distance * 2
    return before + planes_before(total, 1, F32)


def per_device(queries, keys, values, conv_keys, conv_values, out_weight, cotangent):
    tokens = queries.shape[0]
    heads = queries.shape[1] // FEAT
    width = heads * VDIM
    columns = cotangent.shape[1]
    groups = lax.axis_size("head")
    rank = lax.axis_index("ctx") % PLANE
    scalars = jnp.stack([rank, lax.axis_index("head")]).astype(jnp.int32)
    piece_rows = heads // PLANE * ROWS
    S = jax.ShapeDtypeStruct
    step = 2 * tokens * ROWS * VDIM * heads
    project = 2 * tokens * width * columns

    last_rows = jnp.concatenate([keys[tokens - CONV + 1 :], values[tokens - CONV + 1 :]], 1)
    before = shifted(last_rows, "ctx", 1)
    cots = [swapped(cotangent, "head", j) for j in range(1, groups)]

    with jax.named_scope("query_features"):
        qd, out_grad = call(
            query_kernel,
            scalars,
            (queries, cotangent, out_weight),
            [whole(queries), whole(cotangent), column_block(out_weight, columns, 0)],
            [S((heads, ROWS, tokens), BF16), S((tokens, width), F32)],
            [whole(S((heads, ROWS, tokens), BF16)), whole(S((tokens, width), F32))],
            project,
        )
    with jax.named_scope("key_features"):
        outs = [
            S((heads, ROWS, tokens), BF16),
            S((tokens, width), BF16),
            S((piece_rows, VDIM), F32),
            S((PLANE - 1, piece_rows, VDIM), BF16),
            S((heads, ROWS), F32),
        ]
        ops = (keys, values, before, conv_keys, conv_values)
        kf, vc, own, send, norm = call(
            key_kernel, scalars, ops, [whole(x) for x in ops], outs, [whole(x) for x in outs], step
        )
    with jax.named_scope("norm_scan"):
        prior_norm = scan_norms(norm, rank)
    with jax.named_scope("scores"):
        outs = [
            S((heads, tokens, tokens), BF16),
            S((heads, tokens), F32),
            S((tokens, width), F32),
        ]
        ops = (qd, kf, vc)
        low, den, num = call(
            score_kernel,
            scalars,
            ops,
            [whole(x) for x in ops],
            outs,
            [whole(x) for x in outs],
            4 * step,
        )
    with jax.named_scope("prior_scan"):
        prior = scan_states(own, send, rank, 1)
    with jax.named_scope("out_grad"):
        for j in range(1, groups):
            outs = [S((tokens, width), F32)]
            ops = (cots[j - 1], out_weight, out_grad)
            specs = [whole(ops[0]), column_block(out_weight, columns, j), whole(out_grad)]
            (out_grad,) = call(
                grad_kernel, scalars, ops, specs, outs, [whole(x) for x in outs], project
            )
    with jax.named_scope("scaled_grad"):
        outs = [
            S((tokens, heads), F32),
            S((tokens, width), BF16),
            S((piece_rows, VDIM), F32),
            S((PLANE - 1, piece_rows, VDIM), BF16),
        ]
        ops = (prior_norm, den, qd, out_grad)
        inverse, scaled, own_later, send_later = call(
            scale_kernel,
            scalars,
            ops,
            [whole(x) for x in ops],
            outs,
            [whole(x) for x in outs],
            step,
        )
    with jax.named_scope("later_scan"):
        later = scan_states(own_later, send_later, rank, -1)
    with jax.named_scope("near_grad"):
        outs = [S((tokens, width), F32)]
        ops = (low, scaled)
        (near,) = call(
            near_kernel,
            scalars,
            ops,
            [whole(x) for x in ops],
            outs,
            [whole(x) for x in outs],
            2 * step,
        )
    with jax.named_scope("attended"):
        outs = [S((tokens, width), BF16), S((tokens, columns), BF16)]
        ops = (qd, prior, num, inverse, out_weight)
        specs = [whole(x) for x in ops[:4]] + [column_block(out_weight, columns, 1)]
        attended, part = call(
            attend_kernel, scalars, ops, specs, outs, [whole(x) for x in outs], step + project
        )
        parts = [swapped(part, "head", 1)]
    with jax.named_scope("mixed"):
        for j in list(range(2, groups)) + [0]:
            outs = [S((tokens, columns), BF16 if j else F32)]
            ops = (attended, out_weight)
            specs = [whole(attended), column_block(out_weight, columns, j)]
            (part,) = call(
                mix_kernel, scalars, ops, specs, outs, [whole(x) for x in outs], project
            )
            if j:
                parts.append(swapped(part, "head", j))
        mixed_out = part
        for other in parts:
            mixed_out = mixed_out + other.astype(F32)
        mixed_out = mixed_out.astype(BF16)
    with jax.named_scope("far_grad"):
        outs = [S((tokens, width), BF16)]
        ops = (kf, later, near)
        (value_grad,) = call(
            far_kernel, scalars, ops, [whole(x) for x in ops], outs, [whole(x) for x in outs], step
        )
    return mixed_out, value_grad


def solution(mesh):
    in_specs = (
        P("ctx", "head"),
        P("ctx", "head"),
        P("ctx", "head"),
        P(None, "head"),
        P(None, "head"),
        P("head", None),
        P("ctx", "head"),
    )
    out_specs = (P("ctx", "head"), P("ctx", "head"))
    return jax.shard_map(
        per_device, mesh=mesh, in_specs=in_specs, out_specs=out_specs, check_vma=False
    )
```

time: 279 us -> 86.4 us (0.31)
  waiting for transfers between devices: 158 us -> 12.1 us
  starting transfers between devices: 72.5 us -> 35 us
  Pallas kernels: 0 us -> 17.8 us
  between operations: 14.5 us -> 0.97 us
  matrix products: 13 us -> 0 us
  other arithmetic: 11.1 us -> 2.67 us
  local copies, waits for them, and re-layouts: 8.69 us -> 17.1 us
    ppermute x13 -> x7, waiting for transfers between devices: 158 us -> 7.06 us  [shifted(): return lax.ppermute(x, axis, pairs)]
    ppermute x13 -> x7, starting transfers between devices: 72.4 us -> 20.4 us  [shifted(): return lax.ppermute(x, axis, pairs)]
    pallas_call x0 -> x9, Pallas kernels: none -> 17.8 us  [call(): pl.pallas_call(body, out_shape=out_shape, grid_spec=pltpu.PrefetchScalarG...]
    ppermute x0 -> x16, starting transfers between devices: none -> 14.6 us  [swapped(): return lax.ppermute(x, axis, [(i, i ^ distance) for i in range(peers)])]
    dot_general x10 -> x0, matrix products: 13 us -> none  [the longest x1 3.89 us: per_device(): jnp.einsum('td,cd->tc', whole_grad, out_weight, preferred_element_type=jn...]
    unnamed x35 -> x32, local copies, waits for them, and re-layouts: 3.12 us -> 15 us
    ppermute x0 -> x16, waiting for transfers between devices: none -> 5.02 us  [swapped(): return lax.ppermute(x, axis, [(i, i ^ distance) for i in range(peers)])]
    add x10 -> x4, other arithmetic: 3.54 us -> 0.02 us  [the longest x1 0.01 us: scan_norms(): return before + planes_before(total, 1, F32)]
  transfers between devices with their start and end apart: 15 -> 23, of which waited for: 8 -> 7; matrix products, arithmetic and copies ran while one was open for 9% -> 3% of each run, Pallas kernels for 0% -> 21%
where the time goes in v1:
time: 86.4 us; the launch traced here: 85.6 us
  starting transfers between devices  35 us (41%)
  Pallas kernels  17.8 us (21%)
  local copies, waits for them, and re-layouts  17.1 us (20%)
  waiting for transfers between devices  12.1 us (14%)
  other arithmetic  2.67 us (3%)
  between operations  0.97 us (1%)
    ppermute x7, starting transfers between devices, shifted(): return lax.ppermute(x, axis, pairs)  20.4 us
    pallas_call x9, Pallas kernels, call(): pl.pallas_call(body, out_shape=out_shape, grid_spec=pltpu.PrefetchScalarG...  17.8 us
    unnamed x32, local copies, waits for them, and re-layouts  15 us
    ppermute x16, starting transfers between devices, swapped(): return lax.ppermute(x, axis, [(i, i ^ distance) for i in range(peers)])  14.6 us
    ppermute x7, waiting for transfers between devices, shifted(): return lax.ppermute(x, axis, pairs)  7.06 us
    ppermute x16, waiting for transfers between devices, swapped(): return lax.ppermute(x, axis, [(i, i ^ distance) for i in range(peers)])  5.02 us
  transfers between devices with their start and end apart: 23, of which 7 were waited for; matrix products, arithmetic and copies ran while one was open for 3% of the time, Pallas kernels for 21%

profile of v1, /device:TPU:0, one launch (start us, length us, event | category | flops | bytes accessed | tf_op | source)
XLA Modules:
  0.0 85.6 jit_solution(12376392607592990118)
XLA Ops:
  0.6 0.7 slice.24
  1.3 0.7 slice.25
  2.1 2.4 %collective-permute-start = (bf16[2,1152]{1,0:T(2,128)(2,1)S(1)}, bf16[2,1152]{1,0:T(2,128)(2,1)S(1)}, u32[]{:S(2)}, u32[]{:S(2)}) collective-permute-start(bf16[2,1152]{1,0:T(2,128)(2,1)S(1)} %pad_maximum_fusion.2), channel_id=1, source_target_pairs={{0,2},{2,4},{4,6},{6,8},{8,10},{10,12},{12,14},{14,16},{16,18},{18... | collective-permute-start | bytes 13832 | tf_op jit(solution)/shard_map/ppermute | solution.py:214
  4.4 2.4 %collective-permute-start.13 = (bf16[256,1024]{1,0:T(8,128)(2,1)}, bf16[256,1024]{1,0:T(8,128)(2,1)}, u32[]{:S(2)}, u32[]{:S(2)}) collective-permute-start(bf16[256,1024]{1,0:T(8,128)(2,1)} %cot_ref.1), channel_id=1, source_target_pairs={{0,1},{1,0},{2,3},{3,2},{4,5},{5,4},{6,7},{7,6},{8,9},{9,8},{10,11... | collective-permute-start | bytes 1572872 | tf_op jit(solution)/shard_map/ppermute | solution.py:219
  6.8 0.1 pad_add_fusion.s_ref
  6.9 0.0 collective-permute-done.before_ref
  6.9 1.0 %copy-done.6 = bf16[256,1024]{1,0:T(8,128)(2,1)S(1)} copy-done((bf16[256,1024]{1,0:T(8,128)(2,1)S(1)}, bf16[256,1024]{1,0:T(8,128)(2,1)}, u32[]{:S(2)}) %copy-start.6) | copy-done | bytes 524312
  7.9 0.8 copy-done.11
  8.8 0.7 copy-done.12
  9.5 0.7 copy-done.13
  10.2 2.3 %key_features.1 = (bf16[8,160,256]{2,1,0:T(8,128)(2,1)S(1)}, bf16[256,1024]{1,0:T(8,128)(2,1)S(1)}, f32[320,128]{1,0:T(8,128)S(1)}, bf16[3,320,128]{2,1,0:T(8,128)(2,1)S(1)}, f32[8,160]{1,0:T(8,128)S(1)}) custom-call(s32[2]{0:T(128)S(1)} %pad_add_fusion.s_ref, bf16[256,128]{1,0:T(8,128)(2,1)S(1)} %copy-done.11, bf16[256,1024]{1,0:T(8,128)(2,1)S(1)} %copy-done.6, ...), custom_call_target="tpu_custom_call" | custom-call | flops 83886080 | bytes 2202624 | tf_op jit(solution)/shard_map/key_features/pallas_call | solution.py:28
  12.5 1.6 %collective-permute-start.9 = (f32[8,160]{1,0:T(8,128)S(1)}, f32[8,160]{1,0:T(8,128)S(1)}, u32[]{:S(2)}, u32[]{:S(2)}) collective-permute-start(f32[8,160]{1,0:T(8,128)S(1)} %get-tuple-element.24), channel_id=1, source_target_pairs={{0,2},{2,0},{4,6},{6,4},{8,10},{10,8},{12,14},{14,12},{16,18},{18,... | collective-permute-start | bytes 15368 | tf_op jit(solution)/shard_map/norm_scan/ppermute | solution.py:219
  14.1 0.7 slice_bitcast_fusion.3
  14.8 1.7 %collective-permute-start.3 = (bf16[320,128]{1,0:T(8,128)(2,1)}, bf16[320,128]{1,0:T(8,128)(2,1)S(1)}, u32[]{:S(2)}, u32[]{:S(2)}) collective-permute-start(bf16[320,128]{1,0:T(8,128)(2,1)} %get-tuple-element.45), channel_id=1, source_target_pairs={{0,6},{2,4},{4,2},{6,0},{8,14},{10,12},{12,10},{14,8},{16,22},{18,... | collective-permute-start | bytes 245768 | tf_op jit(solution)/shard_map/prior_scan/ppermute | solution.py:219
  16.5 0.2 collective-permute-start.1
  16.6 0.0 collective-permute-done.9
  16.6 1.9 %collective-permute-start.10 = (f32[8,160]{1,0:T(8,128)S(1)}, f32[8,160]{1,0:T(8,128)S(1)}, u32[]{:S(2)}, u32[]{:S(2)}) collective-permute-start(f32[8,160]{1,0:T(8,128)S(1)} %add.145), channel_id=1, source_target_pairs={{0,4},{2,6},{4,0},{6,2},{8,12},{10,14},{12,8},{14,10},{16,20},{18,... | collective-permute-start | bytes 15368 | tf_op jit(solution)/shard_map/norm_scan/ppermute | solution.py:219
  18.6 2.2 %copy-done = bf16[1024,2048]{1,0:T(8,128)(2,1)S(1)} copy-done((bf16[1024,2048]{1,0:T(8,128)(2,1)S(1)}, bf16[1024,2048]{1,0:T(8,128)(2,1)}, u32[]{:S(2)}) %copy-start) | copy-done | bytes 4194328
  20.8 1.0 %copy-done.7 = bf16[256,1024]{1,0:T(8,128)(2,1)S(1)} copy-done((bf16[256,1024]{1,0:T(8,128)(2,1)S(1)}, bf16[256,1024]{1,0:T(8,128)(2,1)}, u32[]{:S(2)}) %copy-start.7) | copy-done | bytes 524312
  21.8 0.8 copy-done.10
  22.6 1.4 %query_features.1 = (bf16[8,160,256]{2,1,0:T(8,128)(2,1)S(1)}, f32[256,1024]{1,0:T(8,128)S(1)}) custom-call(s32[2]{0:T(128)S(1)} %pad_add_fusion.s_ref, bf16[256,128]{1,0:T(8,128)(2,1)S(1)} %copy-done.10, bf16[256,1024]{1,0:T(8,128)(2,1)S(1)} %copy-done.7, bf16[1024,2048]{1,0:T(8,128)(2,1)S(1)} %copy-done), custom_call_target="tpu_custom_call" | custom-call | flops 536870912 | bytes 6488064 | tf_op jit(solution)/shard_map/query_features/pallas_call | solution.py:28
  24.0 1.0 %copy-done.4 = f32[256,1024]{1,0:T(8,128)} copy-done((f32[256,1024]{1,0:T(8,128)}, f32[256,1024]{1,0:T(8,128)S(1)}, u32[]{:S(2)}) %copy-start.4) | copy-done | bytes 1048600
  25.0 3.5 %collective-permute-start.11 = (f32[8,160]{1,0:T(8,128)S(1)}, f32[8,160]{1,0:T(8,128)S(1)}, u32[]{:S(2)}, u32[]{:S(2)}) collective-permute-start(f32[8,160]{1,0:T(8,128)S(1)} %add.147), channel_id=1, source_target_pairs={{0,8},{2,10},{4,12},{6,14},{8,16},{10,18},{12,20},{14,22},{16,24},... | collective-permute-start | bytes 15368 | tf_op jit(solution)/shard_map/norm_scan/ppermute | solution.py:214
  28.5 1.7 %scores.1 = (bf16[8,256,256]{2,1,0:T(8,128)(2,1)S(1)}, f32[8,256]{1,0:T(8,128)S(1)}, f32[256,1024]{1,0:T(8,128)S(1)}) custom-call(s32[2]{0:T(128)S(1)} %pad_add_fusion.s_ref, bf16[8,160,256]{2,1,0:T(8,128)(2,1)S(1)} %get-tuple-element.18.qd_ref, bf16[8,160,256]{2,1,0:T(8,128)(2,1)S(1)} %get-tuple-element.21.kf_ref, ...), custom_call_target="tpu_custom_call" | custom-call | flops 335544320 | bytes 3940352 | tf_op jit(solution)/shard_map/scores/pallas_call | solution.py:28
  30.2 0.0 collective-permute-done.11
  30.2 4.8 %collective-permute-start.12 = (f32[8,160]{1,0:T(8,128)S(1)}, f32[8,160]{1,0:T(8,128)S(1)}, u32[]{:S(2)}, u32[]{:S(2)}) collective-permute-start(f32[8,160]{1,0:T(8,128)S(1)} %add.148), channel_id=1, source_target_pairs={{0,16},{2,18},{4,20},{6,22},{8,24},{10,26},{12,28},{14,30},{1,17},... | collective-permute-start | bytes 15368 | tf_op jit(solution)/shard_map/norm_scan/ppermute | solution.py:214
  35.1 3.5 %collective-permute-start.4 = (bf16[320,128]{1,0:T(8,128)(2,1)S(1)}, bf16[320,128]{1,0:T(8,128)(2,1)S(1)}, u32[]{:S(2)}, u32[]{:S(2)}) collective-permute-start(bf16[320,128]{1,0:T(8,128)(2,1)S(1)} %fusion.30), channel_id=1, source_target_pairs={{0,8},{2,10},{4,12},{6,14},{8,16},{10,18},{12,20},{14,22},{16,24},... | collective-permute-start | bytes 245768 | tf_op jit(solution)/shard_map/prior_scan/ppermute | solution.py:214
  38.6 2.0 %collective-permute-done.4 = bf16[320,128]{1,0:T(8,128)(2,1)S(1)} collective-permute-done((bf16[320,128]{1,0:T(8,128)(2,1)S(1)}, bf16[320,128]{1,0:T(8,128)(2,1)S(1)}, u32[]{:S(2)}, u32[]{:S(2)}) %collective-permute-start.4) | collective-permute-done | bytes 81952 | tf_op jit(solution)/shard_map/prior_scan/ppermute | solution.py:214
  40.6 0.1 fusion
  40.7 3.7 %collective-permute-start.5 = (bf16[320,128]{1,0:T(8,128)(2,1)S(1)}, bf16[320,128]{1,0:T(8,128)(2,1)S(1)}, u32[]{:S(2)}, u32[]{:S(2)}) collective-permute-start(bf16[320,128]{1,0:T(8,128)(2,1)S(1)} %fusion), channel_id=1, source_target_pairs={{0,16},{2,18},{4,20},{6,22},{8,24},{10,26},{12,28},{14,30},{1,17},... | collective-permute-start | bytes 245768 | tf_op jit(solution)/shard_map/prior_scan/ppermute | solution.py:214
  44.5 0.0 copy-start.1
  44.5 2.2 %copy-done.1 = bf16[1024,2048]{1,0:T(8,128)(2,1)S(1)} copy-done((bf16[1024,2048]{1,0:T(8,128)(2,1)S(1)}, bf16[1024,2048]{1,0:T(8,128)(2,1)}, u32[]{:S(2)}) %copy-start.1) | copy-done | bytes 4194328
  46.6 1.2 %copy-done.5 = f32[256,1024]{1,0:T(8,128)S(1)} copy-done((f32[256,1024]{1,0:T(8,128)S(1)}, f32[256,1024]{1,0:T(8,128)}, u32[]{:S(2)}) %copy-start.5) | copy-done | bytes 1048600
  47.9 2.6 %out_grad.1.og_ref = f32[256,1024]{1,0:T(8,128)S(1)} custom-call(s32[2]{0:T(128)S(1)} %pad_add_fusion.s_ref, bf16[256,1024]{1,0:T(8,128)(2,1)} %collective-permute-done.13.cot_ref, bf16[1024,2048]{1,0:T(8,128)(2,1)S(1)} %copy-done.1, f32[256,1024]{1,0:T(8,128)S(1)} %copy-done.5), custom_call_target="tpu_custom_call" | custom-call | flops 536870912 | bytes 6815744 | tf_op jit(solution)/shard_map/out_grad/pallas_call | solution.py:28
  50.5 3.0 %scaled_grad.1 = (f32[256,8]{1,0:T(8,128)S(1)}, bf16[256,1024]{1,0:T(8,128)(2,1)S(1)}, f32[320,128]{1,0:T(8,128)S(1)}, bf16[3,320,128]{2,1,0:T(8,128)(2,1)S(1)}) custom-call(s32[2]{0:T(128)S(1)} %pad_add_fusion.s_ref, f32[8,160]{1,0:T(8,128)S(1)} %add_add_fusion.norm_ref, f32[8,256]{1,0:T(8,128)S(1)} %get-tuple-element.25.den_ref, ...), custom_call_target="tpu_custom_call" | custom-call | flops 83886080 | bytes 2659328 | tf_op jit(solution)/shard_map/scaled_grad/pallas_call | solution.py:28
  53.5 0.0 copy-start.8
  53.5 0.1 collective-permute-start.17
  53.6 1.5 %collective-permute-start.16 = (bf16[320,128]{1,0:T(8,128)(2,1)S(1)}, bf16[320,128]{1,0:T(8,128)(2,1)S(1)}, u32[]{:S(2)}, u32[]{:S(2)}) collective-permute-start(bf16[320,128]{1,0:T(8,128)(2,1)S(1)} %get-tuple-element.43), channel_id=1, source_target_pairs={{0,4},{2,6},{4,0},{6,2},{8,12},{10,14},{12,8},{14,10},{16,20},{18,... | collective-permute-start | bytes 245768 | tf_op jit(solution)/shard_map/later_scan/ppermute | solution.py:219
  55.1 0.4 collective-permute-start.15
  55.5 0.2 fusion.14
  55.7 0.2 collective-permute-start.6
  55.9 1.4 %collective-permute-start.7 = (bf16[320,128]{1,0:T(8,128)(2,1)S(1)}, bf16[320,128]{1,0:T(8,128)(2,1)S(1)}, u32[]{:S(2)}, u32[]{:S(2)}) collective-permute-start(bf16[320,128]{1,0:T(8,128)(2,1)S(1)} %get-tuple-element.39), channel_id=1, source_target_pairs={{0,4},{2,6},{4,0},{6,2},{8,12},{10,14},{12,8},{14,10},{16,20},{18,... | collective-permute-start | bytes 245768 | tf_op jit(solution)/shard_map/prior_scan/ppermute | solution.py:219
  57.2 1.1 %collective-permute-done.17 = bf16[320,128]{1,0:T(8,128)(2,1)S(1)} collective-permute-done((bf16[320,128]{1,0:T(8,128)(2,1)S(1)}, bf16[320,128]{1,0:T(8,128)(2,1)S(1)}, u32[]{:S(2)}, u32[]{:S(2)}) %collective-permute-start.17) | collective-permute-done | bytes 81952 | tf_op jit(solution)/shard_map/later_scan/ppermute | solution.py:219
  58.4 1.7 %collective-permute-done.16 = bf16[320,128]{1,0:T(8,128)(2,1)S(1)} collective-permute-done((bf16[320,128]{1,0:T(8,128)(2,1)S(1)}, bf16[320,128]{1,0:T(8,128)(2,1)S(1)}, u32[]{:S(2)}, u32[]{:S(2)}) %collective-permute-start.16) | collective-permute-done | bytes 81952 | tf_op jit(solution)/shard_map/later_scan/ppermute | solution.py:219
  60.1 1.3 %collective-permute-start.18 = (bf16[320,128]{1,0:T(8,128)(2,1)S(1)}, bf16[320,128]{1,0:T(8,128)(2,1)S(1)}, u32[]{:S(2)}, u32[]{:S(2)}) collective-permute-start(bf16[320,128]{1,0:T(8,128)(2,1)S(1)} %fusion.31), channel_id=1, source_target_pairs={{8,0},{10,2},{12,4},{14,6},{16,8},{18,10},{20,12},{22,14},{24,16},... | collective-permute-start | bytes 245768 | tf_op jit(solution)/shard_map/later_scan/ppermute | solution.py:214
  61.4 0.4 collective-permute-done.7
  61.8 1.8 %collective-permute-done.8 = bf16[320,128]{1,0:T(8,128)(2,1)S(1)} collective-permute-done((bf16[320,128]{1,0:T(8,128)(2,1)S(1)}, bf16[320,128]{1,0:T(8,128)(2,1)S(1)}, u32[]{:S(2)}, u32[]{:S(2)}) %collective-permute-start.8) | collective-permute-done | bytes 81952 | tf_op jit(solution)/shard_map/prior_scan/ppermute | solution.py:219
  63.6 2.9 %collective-permute-done.18 = bf16[320,128]{1,0:T(8,128)(2,1)S(1)} collective-permute-done((bf16[320,128]{1,0:T(8,128)(2,1)S(1)}, bf16[320,128]{1,0:T(8,128)(2,1)S(1)}, u32[]{:S(2)}, u32[]{:S(2)}) %collective-permute-start.18) | collective-permute-done | bytes 81952 | tf_op jit(solution)/shard_map/later_scan/ppermute | solution.py:214
  66.5 0.1 fusion.1
  66.6 1.3 %collective-permute-start.19 = (bf16[320,128]{1,0:T(8,128)(2,1)S(1)}, bf16[320,128]{1,0:T(8,128)(2,1)S(1)}, u32[]{:S(2)}, u32[]{:S(2)}) collective-permute-start(bf16[320,128]{1,0:T(8,128)(2,1)S(1)} %fusion.1), channel_id=1, source_target_pairs={{16,0},{18,2},{20,4},{22,6},{24,8},{26,10},{28,12},{30,14},{17,1},... | collective-permute-start | bytes 245768 | tf_op jit(solution)/shard_map/later_scan/ppermute | solution.py:214
  67.9 2.7 %attended.1 = (bf16[256,1024]{1,0:T(8,128)(2,1)S(1)}, bf16[256,1024]{1,0:T(8,128)(2,1)}) custom-call(s32[2]{0:T(128)S(1)} %pad_add_fusion.s_ref, bf16[8,160,256]{2,1,0:T(8,128)(2,1)S(1)} %get-tuple-element.18.qd_ref, bf16[4,320,128]{2,1,0:T(8,128)(2,1)S(1)} %pad_maximum_fusion.prior_ref, f32[256,1024]{1,0:T(8,128)S(1)} %get-tuple-element.23.num_ref, ...), custom_call_target="tpu_custom_call" | custom-call | flops 620756992 | bytes 7282688 | tf_op jit(solution)/shard_map/attended/pallas_call | solution.py:28
  70.6 1.5 %collective-permute-start.14 = (bf16[256,1024]{1,0:T(8,128)(2,1)}, bf16[256,1024]{1,0:T(8,128)(2,1)S(1)}, u32[]{:S(2)}, u32[]{:S(2)}) collective-permute-start(bf16[256,1024]{1,0:T(8,128)(2,1)} %get-tuple-element.29), channel_id=1, source_target_pairs={{0,1},{1,0},{2,3},{3,2},{4,5},{5,4},{6,7},{7,6},{8,9},{9,8},{10,11... | collective-permute-start | bytes 1572872 | tf_op jit(solution)/shard_map/attended/ppermute | solution.py:219
  72.1 2.2 %collective-permute-done.19 = bf16[320,128]{1,0:T(8,128)(2,1)S(1)} collective-permute-done((bf16[320,128]{1,0:T(8,128)(2,1)S(1)}, bf16[320,128]{1,0:T(8,128)(2,1)S(1)}, u32[]{:S(2)}, u32[]{:S(2)}) %collective-permute-start.19) | collective-permute-done | bytes 81952 | tf_op jit(solution)/shard_map/later_scan/ppermute | solution.py:214
  74.2 1.1 %fusion.27 = (bf16[320,128]{1,0:T(8,128)(2,1)S(1)}, bf16[320,128]{1,0:T(8,128)(2,1)S(1)}, bf16[320,128]{1,0:T(8,128)(2,1)S(1)}, bf16[1,320,128]{2,1,0:T(8,128)(2,1)S(1)}) fusion(bf16[320,128]{1,0:T(8,128)(2,1)} %copy-done.14, bf16[320,128]{1,0:T(8,128)(2,1)S(1)} %collective-permute-done.17, f32[320,128]{1,0:T(8,128)S(1)} %get-tuple-element.30, ...), kind=kLoop, calls=%fused_computation.58 | loop fusion | flops 1392640 | bytes 901132 | tf_op jit(solution)/shard_map/later_scan/convert_element_type | solution.py:247
  75.3 0.1 collective-permute-start.20
  75.4 0.3 collective-permute-start.21
  75.7 1.6 %collective-permute-start.22 = (bf16[320,128]{1,0:T(8,128)(2,1)S(1)}, bf16[320,128]{1,0:T(8,128)(2,1)S(1)}, u32[]{:S(2)}, u32[]{:S(2)}) collective-permute-start(bf16[320,128]{1,0:T(8,128)(2,1)S(1)} %get-tuple-element.36), channel_id=1, source_target_pairs={{0,6},{2,4},{4,2},{6,0},{8,14},{10,12},{12,10},{14,8},{16,22},{18,... | collective-permute-start | bytes 245768 | tf_op jit(solution)/shard_map/later_scan/ppermute | solution.py:219
  77.3 1.0 %copy-done.9 = bf16[256,1024]{1,0:T(8,128)(2,1)S(1)} copy-done((bf16[256,1024]{1,0:T(8,128)(2,1)S(1)}, bf16[256,1024]{1,0:T(8,128)(2,1)}, u32[]{:S(2)}) %copy-start.9) | copy-done | bytes 524312
  78.3 1.0 %near_grad.1.near_ref = f32[256,1024]{1,0:T(8,128)S(1)} custom-call(s32[2]{0:T(128)S(1)} %pad_add_fusion.s_ref, bf16[8,256,256]{2,1,0:T(8,128)(2,1)S(1)} %get-tuple-element.32.low_ref, bf16[256,1024]{1,0:T(8,128)(2,1)S(1)} %copy-done.9), custom_call_target="tpu_custom_call" | custom-call | flops 167772160 | bytes 2621440 | tf_op jit(solution)/shard_map/near_grad/pallas_call | solution.py:28
  79.3 0.0 copy-start.3
  79.3 2.2 %copy-done.3 = bf16[1024,2048]{1,0:T(8,128)(2,1)S(1)} copy-done((bf16[1024,2048]{1,0:T(8,128)(2,1)S(1)}, bf16[1024,2048]{1,0:T(8,128)(2,1)}, u32[]{:S(2)}) %copy-start.3) | copy-done | bytes 4194328
  81.5 1.3 %mixed.1 = f32[256,1024]{1,0:T(8,128)S(1)} custom-call(s32[2]{0:T(128)S(1)} %pad_add_fusion.s_ref, bf16[256,1024]{1,0:T(8,128)(2,1)S(1)} %get-tuple-element.28.att_ref, bf16[1024,2048]{1,0:T(8,128)(2,1)S(1)} %copy-done.3), custom_call_target="tpu_custom_call" | custom-call | flops 536870912 | bytes 5767168 | tf_op jit(solution)/shard_map/mixed/pallas_call | solution.py:28
  82.8 1.8 %far_grad.1 = bf16[256,1024]{1,0:T(8,128)(2,1)} custom-call(s32[2]{0:T(128)S(1)} %pad_add_fusion.s_ref, bf16[8,160,256]{2,1,0:T(8,128)(2,1)S(1)} %get-tuple-element.21.kf_ref, bf16[4,320,128]{2,1,0:T(8,128)(2,1)S(1)} %pad_maximum_fusion.1.later_ref, f32[256,1024]{1,0:T(8,128)S(1)} %near_grad.1.near_ref), custom_call_target="tpu_custom_call" | custom-call | flops 83886080 | bytes 2555904 | tf_op jit(solution)/shard_map/far_grad/pallas_call | solution.py:28
  84.7 1.0 %add_convert_fusion = bf16[256,1024]{1,0:T(8,128)(2,1)} fusion(f32[256,1024]{1,0:T(8,128)S(1)} %mixed.1, bf16[256,1024]{1,0:T(8,128)(2,1)S(1)} %collective-permute-done.14), kind=kLoop, calls=%fused_computation | loop fusion | flops 786432 | bytes 2097152 | tf_op jit(solution)/shard_map/mixed/convert_element_type | solution.py:382
  (42 shorter events, 0.3 us)
Async XLA Ops:
  2.1 4.8 %collective-permute-start = (bf16[2,1152]{1,0:T(2,128)(2,1)S(1)}, bf16[2,1152]{1,0:T(2,128)(2,1)S(1)}, u32[]{:S(2)}, u32[]{:S(2)}) collective-permute-start(bf16[2,1152]{1,0:T(2,128)(2,1)S(1)} %pad_maximum_fusion.2), channel_id=1, source_target_pairs={{0,2},{2,4},{4,6},{6,8},{8,10},{10,12},{12,14},{14,16},{16,18},{18... | collective-permute-start | bytes 13832 | tf_op jit(solution)/shard_map/ppermute | solution.py:214
  4.4 40.0 %collective-permute-start.13 = (bf16[256,1024]{1,0:T(8,128)(2,1)}, bf16[256,1024]{1,0:T(8,128)(2,1)}, u32[]{:S(2)}, u32[]{:S(2)}) collective-permute-start(bf16[256,1024]{1,0:T(8,128)(2,1)} %cot_ref.1), channel_id=1, source_target_pairs={{0,1},{1,0},{2,3},{3,2},{4,5},{5,4},{6,7},{7,6},{8,9},{9,8},{10,11... | collective-permute-start | bytes 1572872 | tf_op jit(solution)/shard_map/ppermute | solution.py:219
  6.9 1.0 %copy-start.6 = (bf16[256,1024]{1,0:T(8,128)(2,1)S(1)}, bf16[256,1024]{1,0:T(8,128)(2,1)}, u32[]{:S(2)}) copy-start(bf16[256,1024]{1,0:T(8,128)(2,1)} %v_ref.1) | copy-start | bytes 1572868
  7.9 0.8 copy-start.11
  8.8 0.7 copy-start.12
  9.5 0.7 copy-start.13
  12.5 4.1 %collective-permute-start.9 = (f32[8,160]{1,0:T(8,128)S(1)}, f32[8,160]{1,0:T(8,128)S(1)}, u32[]{:S(2)}, u32[]{:S(2)}) collective-permute-start(f32[8,160]{1,0:T(8,128)S(1)} %get-tuple-element.24), channel_id=1, source_target_pairs={{0,2},{2,0},{4,6},{6,4},{8,10},{10,8},{12,14},{14,12},{16,18},{18,... | collective-permute-start | bytes 15368 | tf_op jit(solution)/shard_map/norm_scan/ppermute | solution.py:219
  14.8 20.2 %collective-permute-start.3 = (bf16[320,128]{1,0:T(8,128)(2,1)}, bf16[320,128]{1,0:T(8,128)(2,1)S(1)}, u32[]{:S(2)}, u32[]{:S(2)}) collective-permute-start(bf16[320,128]{1,0:T(8,128)(2,1)} %get-tuple-element.45), channel_id=1, source_target_pairs={{0,6},{2,4},{4,2},{6,0},{8,14},{10,12},{12,10},{14,8},{16,22},{18,... | collective-permute-start | bytes 245768 | tf_op jit(solution)/shard_map/prior_scan/ppermute | solution.py:219
  16.5 18.6 %collective-permute-start.2 = (bf16[320,128]{1,0:T(8,128)(2,1)}, bf16[320,128]{1,0:T(8,128)(2,1)S(1)}, u32[]{:S(2)}, u32[]{:S(2)}) collective-permute-start(bf16[320,128]{1,0:T(8,128)(2,1)} %get-tuple-element.46), channel_id=1, source_target_pairs={{0,4},{2,6},{4,0},{6,2},{8,12},{10,14},{12,8},{14,10},{16,20},{18,... | collective-permute-start | bytes 245768 | tf_op jit(solution)/shard_map/prior_scan/ppermute | solution.py:219
  16.5 18.6 %collective-permute-start.1 = (bf16[320,128]{1,0:T(8,128)(2,1)S(1)}, bf16[320,128]{1,0:T(8,128)(2,1)S(1)}, u32[]{:S(2)}, u32[]{:S(2)}) collective-permute-start(bf16[320,128]{1,0:T(8,128)(2,1)S(1)} %get-tuple-element.47), channel_id=1, source_target_pairs={{0,2},{2,0},{4,6},{6,4},{8,10},{10,8},{12,14},{14,12},{16,18},{18,... | collective-permute-start | bytes 245768 | tf_op jit(solution)/shard_map/prior_scan/ppermute | solution.py:219
  16.6 8.4 %collective-permute-start.10 = (f32[8,160]{1,0:T(8,128)S(1)}, f32[8,160]{1,0:T(8,128)S(1)}, u32[]{:S(2)}, u32[]{:S(2)}) collective-permute-start(f32[8,160]{1,0:T(8,128)S(1)} %add.145), channel_id=1, source_target_pairs={{0,4},{2,6},{4,0},{6,2},{8,12},{10,14},{12,8},{14,10},{16,20},{18,... | collective-permute-start | bytes 15368 | tf_op jit(solution)/shard_map/norm_scan/ppermute | solution.py:219
  18.6 2.2 %copy-start = (bf16[1024,2048]{1,0:T(8,128)(2,1)S(1)}, bf16[1024,2048]{1,0:T(8,128)(2,1)}, u32[]{:S(2)}) copy-start(bf16[1024,2048]{1,0:T(8,128)(2,1)} %w_ref.7) | copy-start | bytes 12582916
  20.7 1.0 %copy-start.7 = (bf16[256,1024]{1,0:T(8,128)(2,1)S(1)}, bf16[256,1024]{1,0:T(8,128)(2,1)}, u32[]{:S(2)}) copy-start(bf16[256,1024]{1,0:T(8,128)(2,1)} %cot_ref.1) | copy-start | bytes 1572868
  21.8 0.8 copy-start.10
  24.0 1.0 %copy-start.4 = (f32[256,1024]{1,0:T(8,128)}, f32[256,1024]{1,0:T(8,128)S(1)}, u32[]{:S(2)}) copy-start(f32[256,1024]{1,0:T(8,128)S(1)} %get-tuple-element.26.before_ref) | copy-start | bytes 3145732
  25.0 5.2 %collective-permute-start.11 = (f32[8,160]{1,0:T(8,128)S(1)}, f32[8,160]{1,0:T(8,128)S(1)}, u32[]{:S(2)}, u32[]{:S(2)}) collective-permute-start(f32[8,160]{1,0:T(8,128)S(1)} %add.147), channel_id=1, source_target_pairs={{0,8},{2,10},{4,12},{6,14},{8,16},{10,18},{12,20},{14,22},{16,24},... | collective-permute-start | bytes 15368 | tf_op jit(solution)/shard_map/norm_scan/ppermute | solution.py:214
  30.2 8.4 %collective-permute-start.12 = (f32[8,160]{1,0:T(8,128)S(1)}, f32[8,160]{1,0:T(8,128)S(1)}, u32[]{:S(2)}, u32[]{:S(2)}) collective-permute-start(f32[8,160]{1,0:T(8,128)S(1)} %add.148), channel_id=1, source_target_pairs={{0,16},{2,18},{4,20},{6,22},{8,24},{10,26},{12,28},{14,30},{1,17},... | collective-permute-start | bytes 15368 | tf_op jit(solution)/shard_map/norm_scan/ppermute | solution.py:214
  35.1 5.5 %collective-permute-start.4 = (bf16[320,128]{1,0:T(8,128)(2,1)S(1)}, bf16[320,128]{1,0:T(8,128)(2,1)S(1)}, u32[]{:S(2)}, u32[]{:S(2)}) collective-permute-start(bf16[320,128]{1,0:T(8,128)(2,1)S(1)} %fusion.30), channel_id=1, source_target_pairs={{0,8},{2,10},{4,12},{6,14},{8,16},{10,18},{12,20},{14,22},{16,24},... | collective-permute-start | bytes 245768 | tf_op jit(solution)/shard_map/prior_scan/ppermute | solution.py:214
  40.7 14.8 %collective-permute-start.5 = (bf16[320,128]{1,0:T(8,128)(2,1)S(1)}, bf16[320,128]{1,0:T(8,128)(2,1)S(1)}, u32[]{:S(2)}, u32[]{:S(2)}) collective-permute-start(bf16[320,128]{1,0:T(8,128)(2,1)S(1)} %fusion), channel_id=1, source_target_pairs={{0,16},{2,18},{4,20},{6,22},{8,24},{10,26},{12,28},{14,30},{1,17},... | collective-permute-start | bytes 245768 | tf_op jit(solution)/shard_map/prior_scan/ppermute | solution.py:214
  44.5 2.2 %copy-start.1 = (bf16[1024,2048]{1,0:T(8,128)(2,1)S(1)}, bf16[1024,2048]{1,0:T(8,128)(2,1)}, u32[]{:S(2)}) copy-start(bf16[1024,2048]{1,0:T(8,128)(2,1)} %w_ref.7) | copy-start | bytes 12582916
  46.6 1.2 %copy-start.5 = (f32[256,1024]{1,0:T(8,128)S(1)}, f32[256,1024]{1,0:T(8,128)}, u32[]{:S(2)}) copy-start(f32[256,1024]{1,0:T(8,128)} %copy-done.4) | copy-start | bytes 3145732
  47.9 20.0 %copy-start.2 = (bf16[1024,2048]{1,0:T(8,128)(2,1)S(1)}, bf16[1024,2048]{1,0:T(8,128)(2,1)}, u32[]{:S(2)}) copy-start(bf16[1024,2048]{1,0:T(8,128)(2,1)} %w_ref.7) | copy-start | bytes 12582916
  53.5 14.4 %copy-start.8 = (bf16[256,1024]{1,0:T(8,128)(2,1)}, bf16[256,1024]{1,0:T(8,128)(2,1)S(1)}, u32[]{:S(2)}) copy-start(bf16[256,1024]{1,0:T(8,128)(2,1)S(1)} %get-tuple-element.33.sg_ref) | copy-start | bytes 1572868
  53.5 4.8 %collective-permute-start.17 = (bf16[320,128]{1,0:T(8,128)(2,1)S(1)}, bf16[320,128]{1,0:T(8,128)(2,1)S(1)}, u32[]{:S(2)}, u32[]{:S(2)}) collective-permute-start(bf16[320,128]{1,0:T(8,128)(2,1)S(1)} %get-tuple-element.42), channel_id=1, source_target_pairs={{0,6},{2,4},{4,2},{6,0},{8,14},{10,12},{12,10},{14,8},{16,22},{18,... | collective-permute-start | bytes 245768 | tf_op jit(solution)/shard_map/later_scan/ppermute | solution.py:219
  53.6 6.4 %collective-permute-start.16 = (bf16[320,128]{1,0:T(8,128)(2,1)S(1)}, bf16[320,128]{1,0:T(8,128)(2,1)S(1)}, u32[]{:S(2)}, u32[]{:S(2)}) collective-permute-start(bf16[320,128]{1,0:T(8,128)(2,1)S(1)} %get-tuple-element.43), channel_id=1, source_target_pairs={{0,4},{2,6},{4,0},{6,2},{8,12},{10,14},{12,8},{14,10},{16,20},{18,... | collective-permute-start | bytes 245768 | tf_op jit(solution)/shard_map/later_scan/ppermute | solution.py:219
  55.1 4.9 %collective-permute-start.15 = (bf16[320,128]{1,0:T(8,128)(2,1)S(1)}, bf16[320,128]{1,0:T(8,128)(2,1)S(1)}, u32[]{:S(2)}, u32[]{:S(2)}) collective-permute-start(bf16[320,128]{1,0:T(8,128)(2,1)S(1)} %get-tuple-element.44), channel_id=1, source_target_pairs={{0,2},{2,0},{4,6},{6,4},{8,10},{10,8},{12,14},{14,12},{16,18},{18,... | collective-permute-start | bytes 245768 | tf_op jit(solution)/shard_map/later_scan/ppermute | solution.py:219
  55.7 5.7 %collective-permute-start.6 = (bf16[320,128]{1,0:T(8,128)(2,1)S(1)}, bf16[320,128]{1,0:T(8,128)(2,1)S(1)}, u32[]{:S(2)}, u32[]{:S(2)}) collective-permute-start(bf16[320,128]{1,0:T(8,128)(2,1)S(1)} %get-tuple-element.38), channel_id=1, source_target_pairs={{0,2},{2,0},{4,6},{6,4},{8,10},{10,8},{12,14},{14,12},{16,18},{18,... | collective-permute-start | bytes 245768 | tf_op jit(solution)/shard_map/prior_scan/ppermute | solution.py:219
  55.9 5.9 %collective-permute-start.7 = (bf16[320,128]{1,0:T(8,128)(2,1)S(1)}, bf16[320,128]{1,0:T(8,128)(2,1)S(1)}, u32[]{:S(2)}, u32[]{:S(2)}) collective-permute-start(bf16[320,128]{1,0:T(8,128)(2,1)S(1)} %get-tuple-element.39), channel_id=1, source_target_pairs={{0,4},{2,6},{4,0},{6,2},{8,12},{10,14},{12,8},{14,10},{16,20},{18,... | collective-permute-start | bytes 245768 | tf_op jit(solution)/shard_map/prior_scan/ppermute | solution.py:219
  58.4 5.2 %collective-permute-start.8 = (bf16[320,128]{1,0:T(8,128)(2,1)S(1)}, bf16[320,128]{1,0:T(8,128)(2,1)S(1)}, u32[]{:S(2)}, u32[]{:S(2)}) collective-permute-start(bf16[320,128]{1,0:T(8,128)(2,1)S(1)} %get-tuple-element.40), channel_id=1, source_target_pairs={{0,6},{2,4},{4,2},{6,0},{8,14},{10,12},{12,10},{14,8},{16,22},{18,... | collective-permute-start | bytes 245768 | tf_op jit(solution)/shard_map/prior_scan/ppermute | solution.py:219
  60.0 10.5 %copy-start.14 = (bf16[320,128]{1,0:T(8,128)(2,1)}, bf16[320,128]{1,0:T(8,128)(2,1)S(1)}, u32[]{:S(2)}) copy-start(bf16[320,128]{1,0:T(8,128)(2,1)S(1)} %collective-permute-done.16) | copy-start | bytes 245764
  60.1 10.5 %copy-start.15 = (bf16[320,128]{1,0:T(8,128)(2,1)}, bf16[320,128]{1,0:T(8,128)(2,1)S(1)}, u32[]{:S(2)}) copy-start(bf16[320,128]{1,0:T(8,128)(2,1)S(1)} %collective-permute-done.15) | copy-start | bytes 245764
  60.1 6.4 %collective-permute-start.18 = (bf16[320,128]{1,0:T(8,128)(2,1)S(1)}, bf16[320,128]{1,0:T(8,128)(2,1)S(1)}, u32[]{:S(2)}, u32[]{:S(2)}) collective-permute-start(bf16[320,128]{1,0:T(8,128)(2,1)S(1)} %fusion.31), channel_id=1, source_target_pairs={{8,0},{10,2},{12,4},{14,6},{16,8},{18,10},{20,12},{22,14},{24,16},... | collective-permute-start | bytes 245768 | tf_op jit(solution)/shard_map/later_scan/ppermute | solution.py:214
  66.6 7.6 %collective-permute-start.19 = (bf16[320,128]{1,0:T(8,128)(2,1)S(1)}, bf16[320,128]{1,0:T(8,128)(2,1)S(1)}, u32[]{:S(2)}, u32[]{:S(2)}) collective-permute-start(bf16[320,128]{1,0:T(8,128)(2,1)S(1)} %fusion.1), channel_id=1, source_target_pairs={{16,0},{18,2},{20,4},{22,6},{24,8},{26,10},{28,12},{30,14},{17,1},... | collective-permute-start | bytes 245768 | tf_op jit(solution)/shard_map/later_scan/ppermute | solution.py:214
  70.6 14.1 %collective-permute-start.14 = (bf16[256,1024]{1,0:T(8,128)(2,1)}, bf16[256,1024]{1,0:T(8,128)(2,1)S(1)}, u32[]{:S(2)}, u32[]{:S(2)}) collective-permute-start(bf16[256,1024]{1,0:T(8,128)(2,1)} %get-tuple-element.29), channel_id=1, source_target_pairs={{0,1},{1,0},{2,3},{3,2},{4,5},{5,4},{6,7},{7,6},{8,9},{9,8},{10,11... | collective-permute-start | bytes 1572872 | tf_op jit(solution)/shard_map/attended/ppermute | solution.py:219
  75.3 7.4 %collective-permute-start.20 = (bf16[320,128]{1,0:T(8,128)(2,1)S(1)}, bf16[320,128]{1,0:T(8,128)(2,1)S(1)}, u32[]{:S(2)}, u32[]{:S(2)}) collective-permute-start(bf16[320,128]{1,0:T(8,128)(2,1)S(1)} %get-tuple-element.34), channel_id=1, source_target_pairs={{0,2},{2,0},{4,6},{6,4},{8,10},{10,8},{12,14},{14,12},{16,18},{18,... | collective-permute-start | bytes 245768 | tf_op jit(solution)/shard_map/later_scan/ppermute | solution.py:219
  75.4 7.3 %collective-permute-start.21 = (bf16[320,128]{1,0:T(8,128)(2,1)S(1)}, bf16[320,128]{1,0:T(8,128)(2,1)S(1)}, u32[]{:S(2)}, u32[]{:S(2)}) collective-permute-start(bf16[320,128]{1,0:T(8,128)(2,1)S(1)} %get-tuple-element.35), channel_id=1, source_target_pairs={{0,4},{2,6},{4,0},{6,2},{8,12},{10,14},{12,8},{14,10},{16,20},{18,... | collective-permute-start | bytes 245768 | tf_op jit(solution)/shard_map/later_scan/ppermute | solution.py:219
  75.7 7.0 %collective-permute-start.22 = (bf16[320,128]{1,0:T(8,128)(2,1)S(1)}, bf16[320,128]{1,0:T(8,128)(2,1)S(1)}, u32[]{:S(2)}, u32[]{:S(2)}) collective-permute-start(bf16[320,128]{1,0:T(8,128)(2,1)S(1)} %get-tuple-element.36), channel_id=1, source_target_pairs={{0,6},{2,4},{4,2},{6,0},{8,14},{10,12},{12,10},{14,8},{16,22},{18,... | collective-permute-start | bytes 245768 | tf_op jit(solution)/shard_map/later_scan/ppermute | solution.py:219
  77.3 1.0 %copy-start.9 = (bf16[256,1024]{1,0:T(8,128)(2,1)S(1)}, bf16[256,1024]{1,0:T(8,128)(2,1)}, u32[]{:S(2)}) copy-start(bf16[256,1024]{1,0:T(8,128)(2,1)} %copy-done.8) | copy-start | bytes 1572868
  79.3 2.2 %copy-start.3 = (bf16[1024,2048]{1,0:T(8,128)(2,1)S(1)}, bf16[1024,2048]{1,0:T(8,128)(2,1)}, u32[]{:S(2)}) copy-start(bf16[1024,2048]{1,0:T(8,128)(2,1)} %w_ref.7) | copy-start | bytes 12582916

commit v2 on v1

v2 whole, which is shorter than its diff:
```python
import functools

import jax
import jax.numpy as jnp
from jax import lax
from jax.experimental import pallas as pl
from jax.experimental.pallas import tpu as pltpu
from jax.sharding import PartitionSpec as P

FEAT = 16
VDIM = 128
CONV = 3
ROWS = 160
VMEM_LIMIT = 14 * 1024 * 1024
PLANE = 4

F32 = jnp.float32
BF16 = jnp.bfloat16
TN = (((0,), (0,)), ((), ()))
NT = (((1,), (1,)), ((), ()))
NN = (((1,), (0,)), ((), ()))


def mm(a, b, dims):
    return lax.dot_general(a, b, dims, preferred_element_type=F32)


def call(body, scalars, operands, out_shape, flops, far=(), scratch=()):
    moved = sum(x.size * x.dtype.itemsize for x in operands)
    moved += sum(x.size * x.dtype.itemsize for x in out_shape)
    vmem = pl.BlockSpec(memory_space=pltpu.VMEM)
    hbm = pl.BlockSpec(memory_space=pltpu.HBM)
    return pl.pallas_call(
        body,
        out_shape=out_shape,
        in_specs=[pl.BlockSpec(memory_space=pltpu.SMEM)]
        + [hbm if i in far else vmem for i in range(len(operands))],
        out_specs=[vmem for _ in out_shape],
        scratch_shapes=list(scratch),
        compiler_params=pltpu.CompilerParams(vmem_limit_bytes=VMEM_LIMIT),
        cost_estimate=pl.CostEstimate(flops=flops, bytes_accessed=moved, transcendentals=0),
    )(scalars, *[in_hbm(x) if i in far else x for i, x in enumerate(operands)])


def in_hbm(x):
    return pltpu.with_memory_space_constraint(x, pltpu.HBM)


def fetch(source, target, sem):
    copy = pltpu.make_async_copy(source, target, sem)
    copy.start()
    return copy


def store_features(out_ref, rows_in, doubled):
    heads = rows_in.shape[0] // FEAT
    tokens = rows_in.shape[1]
    grid = rows_in.reshape(heads, FEAT, tokens) * FEAT ** (-0.25)
    twice = jnp.concatenate([grid, grid], 1)
    out_ref[:, 0:FEAT, :] = grid.astype(BF16)
    half = FEAT // 2
    for turn in range(half):
        square = grid * twice[:, turn : turn + FEAT, :] * 0.5**0.5
        if doubled and turn > 0:
            square = square * 2.0
        out_ref[:, FEAT * (turn + 1) : FEAT * (turn + 2), :] = square.astype(BF16)
    square = grid[:, :half, :] * grid[:, half:, :] * 0.5**0.5
    if doubled:
        square = square * 2.0
    first = lax.broadcasted_iota(jnp.int32, (heads, half, tokens), 1) == 0
    constant = jnp.where(first, 1.0, 0.0)
    out_ref[:, FEAT * (half + 1) :, :] = jnp.concatenate([square, constant], 1).astype(BF16)


def store_piece(rank, head, per_piece, state, own_ref, send_ref):
    slot = rank ^ (head // per_piece)
    at = (head % per_piece) * ROWS
    own_ref[slot, at : at + ROWS, :] = state
    send_ref[slot, at : at + ROWS, :] = state.astype(BF16)


def load_piece(rank, head, per_piece, ref):
    at = (head % per_piece) * ROWS
    return ref[rank ^ (head // per_piece), at : at + ROWS, :]


def edge_kernel(k_far, v_far, ck_far, cv_far, edge_ref, k_ref, v_ref, ck_ref, cv_ref, sems):
    pairs = ((k_far, k_ref), (v_far, v_ref), (ck_far, ck_ref), (cv_far, cv_ref))
    copies = [fetch(a, b, sems.at[i]) for i, (a, b) in enumerate(pairs)]
    for copy in copies:
        copy.wait()
    tokens, width = k_ref.shape
    last = 16 - CONV + 1
    edge_ref[:, :width] = k_ref[tokens - 16 :, :].astype(F32)[last:].astype(BF16)
    edge_ref[:, width:] = v_ref[tokens - 16 :, :].astype(F32)[last:].astype(BF16)


def query_kernel(s_ref, q_far, qd_ref, q_ref, sem):
    fetch(q_far, q_ref, sem).wait()
    store_features(qd_ref, q_ref[...].astype(F32).T, True)


def columns_of(s_ref, w_ref, distance):
    columns = w_ref.shape[1] // lax.axis_size("head")
    return pl.ds(pl.multiple_of((s_ref[1] ^ distance) * columns, columns), columns)


def grad_kernel(s_ref, *refs):
    *cots, w_ref, og_ref = refs
    total = None
    for j, cot_ref in enumerate(cots):
        term = mm(cot_ref[...], w_ref[:, columns_of(s_ref, w_ref, j)], NT)
        total = term if total is None else total + term
    og_ref[...] = total


def conv_rows(x, before, taps):
    x = x.astype(F32)
    row = lax.broadcasted_iota(jnp.int32, x.shape, 0)
    running = taps[0:1, :] * x
    for offset in range(1, CONV):
        moved = pltpu.roll(x, offset, 0)
        for at in range(offset):
            source = before[CONV - 1 - offset + at : CONV - offset + at, :]
            moved = jnp.where(row == at, source, moved)
        running = running + taps[offset : offset + 1, :] * moved
    return running


def norm_rows(norm):
    high = norm.astype(BF16).astype(F32)
    middle = (norm - high).astype(BF16).astype(F32)
    rest = norm - high - middle
    parts = (high, middle, rest)
    tail = [x[:, VDIM:] for x in parts]
    filler = jnp.zeros((norm.shape[0], VDIM - 3 * (ROWS - VDIM)), F32)
    tail = jnp.concatenate(tail + [filler], 1)
    return jnp.concatenate([x[:, :VDIM] for x in parts] + [tail], 0)


def norm_values(rows):
    heads = rows.shape[0] // 4
    extra = ROWS - VDIM
    tail = rows[3 * heads :]
    tail = tail[:, :extra] + tail[:, extra : 2 * extra] + tail[:, 2 * extra : 3 * extra]
    main = rows[:heads] + rows[heads : 2 * heads] + rows[2 * heads : 3 * heads]
    return jnp.concatenate([main, tail], 1)


def key_kernel(
    s_ref,
    k_ref,
    v_ref,
    before_ref,
    ck_ref,
    cv_ref,
    kf_ref,
    vc_ref,
    own_ref,
    send_ref,
    slots,
):
    rank = s_ref[0]
    heads = kf_ref.shape[0]
    per_piece = heads // PLANE
    width = k_ref.shape[1]
    before = before_ref[...].astype(F32)
    key_conv = conv_rows(k_ref[...], before[:, :width], ck_ref[...])
    store_features(kf_ref, key_conv.T, False)
    ones = jnp.ones((heads, k_ref.shape[0]), BF16)
    row = lax.broadcasted_iota(jnp.int32, (heads, ROWS), 0)
    norm = jnp.zeros((heads, ROWS), F32)
    for head in range(heads):
        at = head * VDIM
        value = conv_rows(
            v_ref[:, at : at + VDIM],
            before[:, width + at : width + at + VDIM],
            cv_ref[:, at : at + VDIM],
        ).astype(BF16)
        vc_ref[:, at : at + VDIM] = value
        feat = kf_ref[head]
        norm = jnp.where(row == head, mm(ones, feat, NT), norm)
        store_piece(rank, head, per_piece, mm(feat, value, NN), slots, send_ref)
    lines = norm_rows(norm)
    at = per_piece * ROWS
    own_ref[:at, :] = slots[0]
    own_ref[at:, :] = lines
    for slot in range(PLANE):
        send_ref[slot, at:, :] = lines.astype(BF16)


def share_kernel(norm_at, s_ref, own_ref, *refs):
    sent_at = -1 if refs[-1].dtype == BF16 else -2
    got_refs, sent_ref = refs[:sent_at], refs[sent_at]
    total = own_ref[...]
    for got_ref in got_refs:
        total = total + got_ref[...].astype(F32)
    if norm_at is not None:
        lines = norm_rows(norm_values(total[norm_at:]))
        total = jnp.concatenate([total[:norm_at], lines], 0)
    sent_ref[...] = total.astype(BF16)
    if sent_at == -2:
        refs[-1][...] = total


def piece_kernel(sign, strides, s_ref, *refs):
    rows = refs[-1].shape[1] if len(refs[-1].shape) == 3 else refs[-2].shape[1]
    norm_ref = refs[-1] if len(refs[-1].shape) == 2 else None
    pieces_ref = refs[-1] if norm_ref is None else refs[-2]
    got_refs, moved_refs = refs[:PLANE], refs[PLANE : PLANE + len(strides)]

    def masked(ahead, ref):
        return jnp.where(ahead, ref[...].astype(F32), 0.0)

    def is_ahead(other, here):
        return other < here if sign > 0 else other > here

    before = jnp.zeros(got_refs[0].shape, F32)
    for ref, (stride, distance) in zip(moved_refs, strides):
        if distance:
            group = lax.div(s_ref[2], stride)
            before = before + masked(is_ahead(group ^ distance, group), ref)
        else:
            before = before + ref[...].astype(F32)
    rank = s_ref[0]
    for slot in range(PLANE):
        total = before
        for i in range(PLANE):
            if i != slot:
                total = total + masked(is_ahead(rank ^ i, rank ^ slot), got_refs[i])
        pieces_ref[slot] = total[:rows].astype(BF16)
        if norm_ref is not None and slot == 0:
            norm_ref[...] = total[rows:]


def score_kernel(s_ref, qd_ref, kf_ref, vc_ref, low_ref, den_ref, num_ref):
    heads = kf_ref.shape[0]
    tokens = kf_ref.shape[2]
    key_at = lax.broadcasted_iota(jnp.int32, (tokens, tokens), 0)
    query_at = lax.broadcasted_iota(jnp.int32, (tokens, tokens), 1)
    causal = key_at <= query_at
    for head in range(heads):
        scores = jnp.where(causal, mm(kf_ref[head], qd_ref[head], TN), 0.0)
        den_ref[head : head + 1, :] = jnp.sum(scores, 0, keepdims=True)
        low = scores.astype(BF16)
        low_ref[head] = low
        at = head * VDIM
        num_ref[:, at : at + VDIM] = mm(low, vc_ref[:, at : at + VDIM], TN)


def scale_kernel(s_ref, norm_ref, den_ref, qd_ref, og_ref, inv_ref, sg_ref, own_ref, send_ref, slots):
    rank = s_ref[0]
    heads = qd_ref.shape[0]
    per_piece = heads // PLANE
    norm = norm_values(norm_ref[...])
    high = norm.astype(BF16).astype(F32)
    middle = (norm - high).astype(BF16).astype(F32)
    rest = norm - high - middle
    parts = jnp.concatenate([high, middle, rest, jnp.zeros_like(rest)], 0).astype(BF16)
    lines = []
    for head in range(heads):
        terms = mm(parts, qd_ref[head], NN)
        line = den_ref[head : head + 1, :] + terms[head : head + 1, :]
        line = line + terms[heads + head : heads + head + 1, :]
        lines.append(line + terms[2 * heads + head : 2 * heads + head + 1, :])
    inverse = (1.0 / jnp.concatenate(lines, 0)).T
    inv_ref[...] = inverse
    for head in range(heads):
        at = head * VDIM
        scaled = (og_ref[:, at : at + VDIM] * inverse[:, head : head + 1]).astype(BF16)
        sg_ref[:, at : at + VDIM] = scaled
        store_piece(rank, head, per_piece, mm(qd_ref[head], scaled, NN), slots, send_ref)
    own_ref[...] = slots[0]


def near_kernel(s_ref, low_ref, sg_ref, vg_ref):
    for head in range(low_ref.shape[0]):
        at = head * VDIM
        vg_ref[:, at : at + VDIM] = mm(low_ref[head], sg_ref[:, at : at + VDIM], NN)


def attend_kernel(s_ref, qd_ref, prior_ref, num_ref, inv_ref, w_ref, att_ref, part_ref):
    rank = s_ref[0]
    heads = qd_ref.shape[0]
    per_piece = heads // PLANE
    for head in range(heads):
        at = head * VDIM
        prior = load_piece(rank, head, per_piece, prior_ref)
        total = num_ref[:, at : at + VDIM] + mm(qd_ref[head], prior, TN)
        att_ref[:, at : at + VDIM] = (total * inv_ref[:, head : head + 1]).astype(BF16)
    part_ref[...] = mm(att_ref[...], w_ref[:, columns_of(s_ref, w_ref, 1)], NN).astype(BF16)


def mix_kernel(distance, s_ref, att_ref, w_ref, part_ref):
    weight = w_ref[:, columns_of(s_ref, w_ref, distance)]
    part_ref[...] = mm(att_ref[...], weight, NN).astype(part_ref.dtype)


def far_kernel(s_ref, kf_ref, later_ref, near_ref, vg_ref):
    rank = s_ref[0]
    heads = kf_ref.shape[0]
    per_piece = heads // PLANE
    for head in range(heads):
        at = head * VDIM
        later = load_piece(rank, head, per_piece, later_ref)
        total = near_ref[:, at : at + VDIM] + mm(kf_ref[head], later, TN)
        vg_ref[:, at : at + VDIM] = total.astype(BF16)


def shifted(x, axis, by):
    peers = lax.axis_size(axis)
    pairs = [(i, i + by) for i in range(peers) if 0 <= i + by < peers]
    return lax.ppermute(x, axis, pairs)


def after(x, *others):
    return lax.optimization_barrier((x, *others))[0]


def planes_ahead(total, sent, sign, join):
    planes = lax.axis_size("ctx") // PLANE
    received, strides = [], []
    stride = 1
    while stride < planes:
        if (planes // stride) % 4 == 0:
            moved = [swapped(sent, "ctx", j, stride * PLANE) for j in range(1, 4)]
            strides += [(stride, j) for j in range(1, 4)]
            stride = stride * 4
        else:
            moved = [shifted(sent, "ctx", sign * stride * PLANE)]
            strides.append((stride, 0))
            stride = stride * 2
        received += moved
        if stride < planes:
            sent, total = join(total, moved, stride * 2 < planes)
    return received, strides


def swapped(x, axis, distance, stride=1):
    peers = lax.axis_size(axis)
    pairs = [(i, (i // stride ^ distance) * stride + i % stride) for i in range(peers)]
    return lax.ppermute(x, axis, pairs)


def handed_back(pieces):
    back = [swapped(pieces[j], "ctx", j) for j in range(1, PLANE)]
    return jnp.stack([pieces[0]] + back, 0)


def per_device(queries, keys, values, conv_keys, conv_values, out_weight, cotangent):
    tokens = queries.shape[0]
    heads = queries.shape[1] // FEAT
    width = heads * VDIM
    columns = cotangent.shape[1]
    groups = lax.axis_size("head")
    rank = lax.axis_index("ctx") % PLANE
    places = [rank, lax.axis_index("head"), lax.axis_index("ctx") // PLANE]
    scalars = jnp.stack(places).astype(jnp.int32)
    piece_rows = heads // PLANE * ROWS
    message = (piece_rows + 4 * heads, VDIM)
    S = jax.ShapeDtypeStruct
    step = 2 * tokens * ROWS * VDIM * heads
    project_flops = 2 * tokens * width * columns
    dma = pltpu.SemaphoreType.DMA
    vmem = pltpu.VMEM
    slots = vmem((PLANE, piece_rows, VDIM), F32)

    with jax.named_scope("edge"):
        arrays = (keys, values, conv_keys, conv_values)
        spec = pl.BlockSpec(memory_space=vmem)
        last_rows, k_near, v_near, ck_near, cv_near = pl.pallas_call(
            edge_kernel,
            out_shape=[S((CONV - 1, keys.shape[1] + width), BF16)]
            + [S(x.shape, x.dtype) for x in arrays],
            in_specs=[pl.BlockSpec(memory_space=pltpu.HBM)] * 4,
            out_specs=[spec] * 5,
            scratch_shapes=[dma((4,))],
            compiler_params=pltpu.CompilerParams(vmem_limit_bytes=VMEM_LIMIT),
        )(*[in_hbm(x) for x in arrays])
        before = shifted(last_rows, "ctx", 1)
    with jax.named_scope("cotangent"):
        cots = [swapped(cotangent, "head", j) for j in range(1, groups)]
    with jax.named_scope("key_features"):
        outs = [
            S((heads, ROWS, tokens), BF16),
            S((tokens, width), BF16),
            S(message, F32),
            S((PLANE, *message), BF16),
        ]
        ops = (k_near, v_near, before, ck_near, cv_near)
        kf, vc, own, send = call(key_kernel, scalars, ops, outs, step, scratch=[slots])
    with jax.named_scope("query_features"):
        (qd,) = call(
            query_kernel,
            scalars,
            (after(queries, send),),
            [S((heads, ROWS, tokens), BF16)],
            step,
            far=(0,),
            scratch=[vmem(queries.shape, BF16), dma(())],
        )
    with jax.named_scope("prior_share"):
        got = [swapped(send[j], "ctx", j) for j in range(1, PLANE)]

        def join(norm_at, total, received, more):
            outs = [S(total.shape, BF16), S(total.shape, F32)]
            body = functools.partial(share_kernel, norm_at)
            made = call(body, scalars, (total, *received), outs[: 2 if more else 1], 1 << 20)
            return made if more else (made[0], None)

        more = lax.axis_size("ctx") > 4 * PLANE
        sent, total = join(piece_rows, own, got, more)
    with jax.named_scope("scores"):
        outs = [
            S((heads, tokens, tokens), BF16),
            S((heads, tokens), F32),
            S((tokens, width), F32),
        ]
        low, den, num = call(score_kernel, scalars, (qd, kf, vc), outs, 4 * step)
    with jax.named_scope("prior_planes"):
        sent = after(sent, den)
        norm_join = functools.partial(join, piece_rows)
        moved, strides = planes_ahead(total, sent, 1, norm_join)
    with jax.named_scope("out_grad"):
        ops = (after(cotangent, sent), *cots, out_weight)
        (out_grad,) = call(
            grad_kernel, scalars, ops, [S((tokens, width), F32)], groups * project_flops
        )
    with jax.named_scope("prior_back"):
        outs = [S((PLANE, piece_rows, VDIM), BF16), S((4 * heads, VDIM), F32)]
        body = functools.partial(piece_kernel, 1, strides)
        ops = (own, *got, after(moved[0], out_grad), *moved[1:])
        pieces, prior_norm = call(body, scalars, ops, outs, 1 << 20)
        prior = handed_back(pieces)
    with jax.named_scope("scaled_grad"):
        outs = [
            S((tokens, heads), F32),
            S((tokens, width), BF16),
            S((piece_rows, VDIM), F32),
            S((PLANE, piece_rows, VDIM), BF16),
        ]
        ops = (prior_norm, den, qd, out_grad)
        inverse, scaled, own_later, send_later = call(
            scale_kernel, scalars, ops, outs, step, scratch=[slots]
        )
    with jax.named_scope("later_share"):
        got_later = [swapped(send_later[j], "ctx", j) for j in range(1, PLANE)]
    with jax.named_scope("later_planes"):
        plain_join = functools.partial(join, None)
        sent_later, total_later = plain_join(own_later, got_later, more)
        moved_later, strides = planes_ahead(total_later, sent_later, -1, plain_join)
    with jax.named_scope("attended"):
        outs = [S((tokens, width), BF16), S((tokens, columns), BF16)]
        ops = (qd, prior, after(num, sent_later), inverse, out_weight)
        attended, part = call(attend_kernel, scalars, ops, outs, step + project_flops)
        parts = [swapped(part, "head", 1)]
    with jax.named_scope("near"):
        ops = (low, after(scaled, sent_later))
        (near,) = call(near_kernel, scalars, ops, [S((tokens, width), F32)], 2 * step)
    with jax.named_scope("mixed"):
        for j in list(range(2, groups)) + [0]:
            outs = [S((tokens, columns), BF16 if j else F32)]
            body = functools.partial(mix_kernel, j)
            ops = (after(attended, sent_later), out_weight)
            (part,) = call(body, scalars, ops, outs, 2 * project_flops)
            if j:
                parts.append(swapped(part, "head", j))
    with jax.named_scope("later_back"):
        outs = [S((PLANE, piece_rows, VDIM), BF16)]
        body = functools.partial(piece_kernel, -1, strides)
        ops = (own_later, *got_later, after(moved_later[0], part, near), *moved_later[1:])
        (pieces,) = call(body, scalars, ops, outs, 1 << 20)
        later = handed_back(pieces)
    with jax.named_scope("mixed_out"):
        mixed_out = part
        for other in parts:
            mixed_out = mixed_out + other.astype(F32)
        mixed_out = mixed_out.astype(BF16)
    with jax.named_scope("far_grad"):
        (value_grad,) = call(
            far_kernel, scalars, (after(kf, mixed_out), later, near), [S((tokens, width), BF16)], step
        )
    return mixed_out, value_grad


def solution(mesh):
    in_specs = (
        P("ctx", "head"),
        P("ctx", "head"),
        P("ctx", "head"),
        P(None, "head"),
        P(None, "head"),
        P("head", None),
        P("ctx", "head"),
    )
    out_specs = (P("ctx", "head"), P("ctx", "head"))
    return jax.shard_map(
        per_device, mesh=mesh, in_specs=in_specs, out_specs=out_specs, check_vma=False
    )
```

time: 86.4 us -> 61.9 us (0.72)
  local copies, waits for them, and re-layouts: 17.1 us -> 0.1 us
  starting transfers between devices: 35 us -> 25 us
  waiting for transfers between devices: 12.1 us -> 16.6 us
  other arithmetic: 2.67 us -> 1.12 us
    ppermute x7 -> x1, starting transfers between devices: 20.4 us -> 1.46 us  [shifted(): return lax.ppermute(x, axis, pairs)]
    unnamed x32 -> x4, local copies, waits for them, and re-layouts: 15 us -> 0.01 us
    ppermute x16 -> x20, waiting for transfers between devices: 5.02 us -> 15.9 us  [swapped(): return lax.ppermute(x, axis, pairs)]
    ppermute x16 -> x20, starting transfers between devices: 14.6 us -> 23.5 us  [swapped(): return lax.ppermute(x, axis, pairs)]
    ppermute x7 -> x1, waiting for transfers between devices: 7.06 us -> 0.7 us  [shifted(): return lax.ppermute(x, axis, pairs)]
    convert_element_type x6 -> x0, other arithmetic: 1.52 us -> none  [the longest x2 1.31 us: scan_states(): pieces.append(piece.astype(BF16))]
    slice x2, local copies, waits for them, and re-layouts: 1.41 us -> 0.05 us  [handed_back(): return jnp.stack([pieces[0]] + back, 0)]
    pallas_call x9 -> x14, Pallas kernels: 17.8 us -> 18.1 us  [the longest x13 17 us: call(): pl.pallas_call(body, out_shape=out_shape, in_specs=[pl.BlockSpec(memory_s...]
  transfers between devices with their start and end apart: 23 -> 21, of which waited for: 7 -> 10; matrix products, arithmetic and copies ran while one was open for 3% -> 0% of each run, Pallas kernels for 21% -> 23%
where the time goes in v2:
time: 61.9 us; the launch traced here: 61.7 us
  starting transfers between devices  25 us (40%)
  Pallas kernels  18.1 us (29%)
  waiting for transfers between devices  16.6 us (27%)
  other arithmetic  1.12 us (2%)
  between operations  0.84 us (1%)
    ppermute x20, starting transfers between devices, swapped(): return lax.ppermute(x, axis, pairs)  23.5 us
    pallas_call x13, Pallas kernels, call(): pl.pallas_call(body, out_shape=out_shape, in_specs=[pl.BlockSpec(memory_s...  17 us
    ppermute x20, waiting for transfers between devices, swapped(): return lax.ppermute(x, axis, pairs)  15.9 us
    ppermute x1, starting transfers between devices, shifted(): return lax.ppermute(x, axis, pairs)  1.46 us
  transfers between devices with their start and end apart: 21, of which 10 were waited for; matrix products, arithmetic and copies ran while one was open for 0% of the time, Pallas kernels for 23%

profile of v2, /device:TPU:0, one launch (start us, length us, event | category | flops | bytes accessed | tf_op | source)
XLA Modules:
  0.0 61.7 jit_solution(10832853245229680307)
XLA Ops:
  0.6 0.0 copy-start.1
  0.6 3.0 %collective-permute-start.5 = (bf16[256,1024]{1,0:T(8,128)(2,1)}, bf16[256,1024]{1,0:T(8,128)(2,1)S(1)}, u32[]{:S(2)}, u32[]{:S(2)}) collective-permute-start(bf16[256,1024]{1,0:T(8,128)(2,1)} %refs_0_), channel_id=1, source_target_pairs={{0,1},{1,0},{2,3},{3,2},{4,5},{5,4},{6,7},{7,6},{8,9},{9,8},{10,11... | collective-permute-start | bytes 1572872 | tf_op jit(solution)/shard_map/cotangent/ppermute | solution.py:342
  3.6 1.1 %edge.1 = (bf16[2,1152]{1,0:T(2,128)(2,1)S(1)}, bf16[256,128]{1,0:T(8,128)(2,1)S(1)}, bf16[256,1024]{1,0:T(8,128)(2,1)S(1)}, f32[3,128]{1,0:T(4,128)S(1)}, f32[3,1024]{1,0:T(4,128)S(1)}) custom-call(bf16[256,128]{1,0:T(8,128)(2,1)} %k_far.1, bf16[256,1024]{1,0:T(8,128)(2,1)} %v_far.1, f32[3,128]{1,0:T(4,128)} %ck_far.1, f32[3,1024]{1,0:T(4,128)} %cv_far.1), custom_call_target="tpu_custom_call" | custom-call | tf_op jit(solution)/shard_map/edge/pallas_call | solution.py:371
  4.8 1.5 %collective-permute-start = (bf16[2,1152]{1,0:T(2,128)(2,1)S(1)}, bf16[2,1152]{1,0:T(2,128)(2,1)S(1)}, u32[]{:S(2)}, u32[]{:S(2)}) collective-permute-start(bf16[2,1152]{1,0:T(2,128)(2,1)S(1)} %get-tuple-element.33), channel_id=1, source_target_pairs={{0,2},{2,4},{4,6},{6,8},{8,10},{10,12},{12,14},{14,16},{16,18},{18... | collective-permute-start | bytes 13832 | tf_op jit(solution)/shard_map/edge/ppermute | solution.py:313
  6.3 0.0 copy-start
  6.3 0.1 pad_add_fusion.s_ref
  6.4 0.7 %collective-permute-done.before_ref = bf16[2,1152]{1,0:T(2,128)(2,1)S(1)} collective-permute-done((bf16[2,1152]{1,0:T(2,128)(2,1)S(1)}, bf16[2,1152]{1,0:T(2,128)(2,1)S(1)}, u32[]{:S(2)}, u32[]{:S(2)}) %collective-permute-start) | collective-permute-done | bytes 4640 | tf_op jit(solution)/shard_map/edge/ppermute | solution.py:313
  7.1 1.4 %key_features.1 = (bf16[8,160,256]{2,1,0:T(8,128)(2,1)S(1)}, bf16[256,1024]{1,0:T(8,128)(2,1)S(1)}, f32[352,128]{1,0:T(8,128)S(1)}, bf16[4,352,128]{2,1,0:T(8,128)(2,1)S(1)}) custom-call(s32[3]{0:T(128)S(1)} %pad_add_fusion.s_ref, bf16[256,128]{1,0:T(8,128)(2,1)S(1)} %get-tuple-element.31.k_ref, bf16[256,1024]{1,0:T(8,128)(2,1)S(1)} %get-tuple-element.32.v_ref, ...), custom_call_target="tpu_custom_call" | custom-call | flops 83886080 | bytes 2328576 | tf_op jit(solution)/shard_map/key_features/pallas_call | solution.py:33
  8.5 3.2 %collective-permute-start.3 = (bf16[352,128]{1,0:T(8,128)(2,1)S(1)}, bf16[352,128]{1,0:T(8,128)(2,1)S(1)}, u32[]{:S(2)}, u32[]{:S(2)}) collective-permute-start(bf16[352,128]{1,0:T(8,128)(2,1)S(1)} %get-tuple-element.60), channel_id=1, source_target_pairs={{0,6},{2,4},{4,2},{6,0},{8,14},{10,12},{12,10},{14,8},{16,22},{18,... | collective-permute-start | bytes 270344 | tf_op jit(solution)/shard_map/prior_share/ppermute | solution.py:342
  11.7 1.1 %collective-permute-start.2 = (bf16[352,128]{1,0:T(8,128)(2,1)S(1)}, bf16[352,128]{1,0:T(8,128)(2,1)S(1)}, u32[]{:S(2)}, u32[]{:S(2)}) collective-permute-start(bf16[352,128]{1,0:T(8,128)(2,1)S(1)} %get-tuple-element.61), channel_id=1, source_target_pairs={{0,4},{2,6},{4,0},{6,2},{8,12},{10,14},{12,8},{14,10},{16,20},{18,... | collective-permute-start | bytes 270344 | tf_op jit(solution)/shard_map/prior_share/ppermute | solution.py:342
  12.9 0.0 collective-permute-start.1
  12.9 1.7 %query_features.1.qd_ref = bf16[8,160,256]{2,1,0:T(8,128)(2,1)S(1)} custom-call(s32[3]{0:T(128)S(1)} %pad_add_fusion.s_ref, bf16[256,128]{1,0:T(8,128)(2,1)} %q_far), custom_call_target="tpu_custom_call" | custom-call | flops 83886080 | bytes 720896 | tf_op jit(solution)/shard_map/query_features/pallas_call | solution.py:33
  14.6 1.7 %scores.1 = (bf16[8,256,256]{2,1,0:T(8,128)(2,1)S(1)}, f32[8,256]{1,0:T(8,128)S(1)}, f32[256,1024]{1,0:T(8,128)S(1)}) custom-call(s32[3]{0:T(128)S(1)} %pad_add_fusion.s_ref, bf16[8,160,256]{2,1,0:T(8,128)(2,1)S(1)} %query_features.1.qd_ref, bf16[8,160,256]{2,1,0:T(8,128)(2,1)S(1)} %get-tuple-element.55.kf_ref, bf16[256,1024]{1,0:T(8,128)(2,1)S(1)} %get-tuple-element.40.vc_ref), custom_call_target="tpu_custom_call" | custom-call | flops 335544320 | bytes 3940352 | tf_op jit(solution)/shard_map/scores/pallas_call | solution.py:33
  16.3 0.0 collective-permute-done.3.refs_2_.refs_3_
  16.3 0.7 %collective-permute-done.2.refs_1_.refs_2_ = bf16[352,128]{1,0:T(8,128)(2,1)S(1)} collective-permute-done((bf16[352,128]{1,0:T(8,128)(2,1)S(1)}, bf16[352,128]{1,0:T(8,128)(2,1)S(1)}, u32[]{:S(2)}, u32[]{:S(2)}) %collective-permute-start.2) | collective-permute-done | bytes 90144 | tf_op jit(solution)/shard_map/prior_share/ppermute | solution.py:342
  17.0 0.0 collective-permute-done.1.refs_0_.refs_1_
  17.0 0.7 %prior_share.1 = bf16[352,128]{1,0:T(8,128)(2,1)S(1)} custom-call(s32[3]{0:T(128)S(1)} %pad_add_fusion.s_ref, f32[352,128]{1,0:T(8,128)S(1)} %get-tuple-element.38.own_ref.refs_0_, bf16[352,128]{1,0:T(8,128)(2,1)S(1)} %collective-permute-done.1.refs_0_.refs_1_, bf16[352,128]{1,0:T(8,128)(2,1)S(1)} %collective-permute-done.2.refs_1_.refs_2_, ...), custom_call_target="tpu_custom_call" | custom-call | flops 1048576 | bytes 540672 | tf_op jit(solution)/shard_map/prior_share/pallas_call | solution.py:33
  17.7 4.3 %collective-permute-start.7 = (bf16[352,128]{1,0:T(8,128)(2,1)S(1)}, bf16[352,128]{1,0:T(8,128)(2,1)S(1)}, u32[]{:S(2)}, u32[]{:S(2)}) collective-permute-start(bf16[352,128]{1,0:T(8,128)(2,1)S(1)} %prior_share.1), channel_id=1, source_target_pairs={{0,24},{2,26},{4,28},{6,30},{8,16},{10,18},{12,20},{14,22},{16,8},... | collective-permute-start | bytes 270344 | tf_op jit(solution)/shard_map/prior_planes/ppermute | solution.py:342
  22.0 0.0 collective-permute-start.6
  22.0 0.6 %collective-permute-start.4 = (bf16[352,128]{1,0:T(8,128)(2,1)S(1)}, bf16[352,128]{1,0:T(8,128)(2,1)S(1)}, u32[]{:S(2)}, u32[]{:S(2)}) collective-permute-start(bf16[352,128]{1,0:T(8,128)(2,1)S(1)} %prior_share.1), channel_id=1, source_target_pairs={{0,8},{2,10},{4,12},{6,14},{8,0},{10,2},{12,4},{14,6},{16,24},{18,... | collective-permute-start | bytes 270344 | tf_op jit(solution)/shard_map/prior_planes/ppermute | solution.py:342
  22.6 0.0 collective-permute-done.5.refs_1_
  22.7 0.0 copy-done.1
  22.7 0.0 copy-done
  22.7 1.8 %out_grad.1.og_ref = f32[256,1024]{1,0:T(8,128)S(1)} custom-call(s32[3]{0:T(128)S(1)} %pad_add_fusion.s_ref, bf16[256,1024]{1,0:T(8,128)(2,1)S(1)} %copy-done.1, bf16[256,1024]{1,0:T(8,128)(2,1)S(1)} %collective-permute-done.5.refs_1_, bf16[1024,2048]{1,0:T(8,128)(2,1)S(1)} %copy-done), custom_call_target="tpu_custom_call" | custom-call | flops 1073741824 | bytes 6291456 | tf_op jit(solution)/shard_map/out_grad/pallas_call | solution.py:33
  24.5 3.8 %collective-permute-done.4.refs_4_ = bf16[352,128]{1,0:T(8,128)(2,1)S(1)} collective-permute-done((bf16[352,128]{1,0:T(8,128)(2,1)S(1)}, bf16[352,128]{1,0:T(8,128)(2,1)S(1)}, u32[]{:S(2)}, u32[]{:S(2)}) %collective-permute-start.4) | collective-permute-done | bytes 90144 | tf_op jit(solution)/shard_map/prior_planes/ppermute | solution.py:342
  28.3 0.0 collective-permute-done.7.refs_6_
  28.3 1.8 %collective-permute-done.6.refs_5_ = bf16[352,128]{1,0:T(8,128)(2,1)S(1)} collective-permute-done((bf16[352,128]{1,0:T(8,128)(2,1)S(1)}, bf16[352,128]{1,0:T(8,128)(2,1)S(1)}, u32[]{:S(2)}, u32[]{:S(2)}) %collective-permute-start.6) | collective-permute-done | bytes 90144 | tf_op jit(solution)/shard_map/prior_planes/ppermute | solution.py:342
  30.1 0.8 %prior_back.1 = (bf16[4,320,128]{2,1,0:T(8,128)(2,1)S(1)}, f32[32,128]{1,0:T(8,128)S(1)}) custom-call(s32[3]{0:T(128)S(1)} %pad_add_fusion.s_ref, f32[352,128]{1,0:T(8,128)S(1)} %get-tuple-element.38.own_ref.refs_0_, bf16[352,128]{1,0:T(8,128)(2,1)S(1)} %collective-permute-done.1.refs_0_.refs_1_, ...), custom_call_target="tpu_custom_call" | custom-call | flops 1048576 | bytes 1064960 | tf_op jit(solution)/shard_map/prior_back/pallas_call | solution.py:33
  30.8 1.6 %scaled_grad.1 = (f32[256,8]{1,0:T(8,128)S(1)}, bf16[256,1024]{1,0:T(8,128)(2,1)S(1)}, f32[320,128]{1,0:T(8,128)S(1)}, bf16[4,320,128]{2,1,0:T(8,128)(2,1)S(1)}) custom-call(s32[3]{0:T(128)S(1)} %pad_add_fusion.s_ref, f32[32,128]{1,0:T(8,128)S(1)} %get-tuple-element.47.norm_ref, f32[8,256]{1,0:T(8,128)S(1)} %get-tuple-element.41.den_ref, ...), custom_call_target="tpu_custom_call" | custom-call | flops 83886080 | bytes 2752512 | tf_op jit(solution)/shard_map/scaled_grad/pallas_call | solution.py:33
  32.4 0.6 collective-permute-start.13
  33.0 1.2 %collective-permute-start.12 = (bf16[320,128]{1,0:T(8,128)(2,1)S(1)}, bf16[320,128]{1,0:T(8,128)(2,1)S(1)}, u32[]{:S(2)}, u32[]{:S(2)}) collective-permute-start(bf16[320,128]{1,0:T(8,128)(2,1)S(1)} %get-tuple-element.68), channel_id=1, source_target_pairs={{0,4},{2,6},{4,0},{6,2},{8,12},{10,14},{12,8},{14,10},{16,20},{18,... | collective-permute-start | bytes 245768 | tf_op jit(solution)/shard_map/later_share/ppermute | solution.py:342
  34.2 0.1 collective-permute-start.11
  34.4 1.3 %collective-permute-start.10 = (bf16[320,128]{1,0:T(8,128)(2,1)S(1)}, bf16[320,128]{1,0:T(8,128)(2,1)S(1)}, u32[]{:S(2)}, u32[]{:S(2)}) collective-permute-start(bf16[320,128]{1,0:T(8,128)(2,1)S(1)} %get-tuple-element.71), channel_id=1, source_target_pairs={{0,6},{2,4},{4,2},{6,0},{8,14},{10,12},{12,10},{14,8},{16,22},{18,... | collective-permute-start | bytes 245768 | tf_op jit(solution)/shard_map/prior_back/ppermute | solution.py:342
  35.7 0.8 %collective-permute-start.9 = (bf16[320,128]{1,0:T(8,128)(2,1)S(1)}, bf16[320,128]{1,0:T(8,128)(2,1)S(1)}, u32[]{:S(2)}, u32[]{:S(2)}) collective-permute-start(bf16[320,128]{1,0:T(8,128)(2,1)S(1)} %get-tuple-element.72), channel_id=1, source_target_pairs={{0,4},{2,6},{4,0},{6,2},{8,12},{10,14},{12,8},{14,10},{16,20},{18,... | collective-permute-start | bytes 245768 | tf_op jit(solution)/shard_map/prior_back/ppermute | solution.py:342
  36.5 0.6 collective-permute-done.13.refs_2_.refs_3_
  37.0 0.2 collective-permute-start.8
  37.3 1.9 %collective-permute-done.12.refs_1_.refs_2_ = bf16[320,128]{1,0:T(8,128)(2,1)S(1)} collective-permute-done((bf16[320,128]{1,0:T(8,128)(2,1)S(1)}, bf16[320,128]{1,0:T(8,128)(2,1)S(1)}, u32[]{:S(2)}, u32[]{:S(2)}) %collective-permute-start.12) | collective-permute-done | bytes 81952 | tf_op jit(solution)/shard_map/later_share/ppermute | solution.py:342
  39.2 0.0 collective-permute-done.11.refs_0_.refs_1_
  39.2 0.6 later_planes.1
  39.8 2.5 %collective-permute-start.17 = (bf16[320,128]{1,0:T(8,128)(2,1)S(1)}, bf16[320,128]{1,0:T(8,128)(2,1)S(1)}, u32[]{:S(2)}, u32[]{:S(2)}) collective-permute-start(bf16[320,128]{1,0:T(8,128)(2,1)S(1)} %later_planes.1), channel_id=1, source_target_pairs={{0,24},{2,26},{4,28},{6,30},{8,16},{10,18},{12,20},{14,22},{16,8},... | collective-permute-start | bytes 245768 | tf_op jit(solution)/shard_map/later_planes/ppermute | solution.py:342
  42.3 0.0 collective-permute-start.16
  42.3 0.0 collective-permute-done.10
  42.3 1.9 %collective-permute-start.15 = (bf16[320,128]{1,0:T(8,128)(2,1)S(1)}, bf16[320,128]{1,0:T(8,128)(2,1)S(1)}, u32[]{:S(2)}, u32[]{:S(2)}) collective-permute-start(bf16[320,128]{1,0:T(8,128)(2,1)S(1)} %later_planes.1), channel_id=1, source_target_pairs={{0,8},{2,10},{4,12},{6,14},{8,0},{10,2},{12,4},{14,6},{16,24},{18,... | collective-permute-start | bytes 245768 | tf_op jit(solution)/shard_map/later_planes/ppermute | solution.py:342
  44.3 0.0 collective-permute-done.9
  44.3 0.0 collective-permute-done.8
  44.3 1.9 %attended.1 = (bf16[256,1024]{1,0:T(8,128)(2,1)S(1)}, bf16[256,1024]{1,0:T(8,128)(2,1)S(1)}) custom-call(s32[3]{0:T(128)S(1)} %pad_add_fusion.s_ref, bf16[8,160,256]{2,1,0:T(8,128)(2,1)S(1)} %query_features.1.qd_ref, bf16[4,320,128]{2,1,0:T(8,128)(2,1)S(1)} %pad_maximum_fusion.prior_ref, f32[256,1024]{1,0:T(8,128)S(1)} %get-tuple-element.50.num_ref, ...), custom_call_target="tpu_custom_call" | custom-call | flops 620756992 | bytes 7282688 | tf_op jit(solution)/shard_map/attended/pallas_call | solution.py:33
  46.2 0.6 collective-permute-start.14
  46.8 1.0 %near.1.near_ref = f32[256,1024]{1,0:T(8,128)S(1)} custom-call(s32[3]{0:T(128)S(1)} %pad_add_fusion.s_ref, bf16[8,256,256]{2,1,0:T(8,128)(2,1)S(1)} %get-tuple-element.56.low_ref, bf16[256,1024]{1,0:T(8,128)(2,1)S(1)} %get-tuple-element.58.sg_ref), custom_call_target="tpu_custom_call" | custom-call | flops 167772160 | bytes 2621440 | tf_op jit(solution)/shard_map/near/pallas_call | solution.py:33
  47.8 1.2 %mixed.1 = f32[256,1024]{1,0:T(8,128)S(1)} custom-call(s32[3]{0:T(128)S(1)} %pad_add_fusion.s_ref, bf16[256,1024]{1,0:T(8,128)(2,1)S(1)} %get-tuple-element.53.att_ref, bf16[1024,2048]{1,0:T(8,128)(2,1)S(1)} %copy-done), custom_call_target="tpu_custom_call" | custom-call | flops 1073741824 | bytes 5767168 | tf_op jit(solution)/shard_map/mixed/pallas_call | solution.py:33
  49.0 0.0 collective-permute-done.15.refs_4_
  49.0 0.0 collective-permute-done.17.refs_6_
  49.1 0.7 %collective-permute-done.16.refs_5_ = bf16[320,128]{1,0:T(8,128)(2,1)S(1)} collective-permute-done((bf16[320,128]{1,0:T(8,128)(2,1)S(1)}, bf16[320,128]{1,0:T(8,128)(2,1)S(1)}, u32[]{:S(2)}, u32[]{:S(2)}) %collective-permute-start.16) | collective-permute-done | bytes 81952 | tf_op jit(solution)/shard_map/later_planes/ppermute | solution.py:342
  49.7 0.8 %later_back.1 = bf16[4,320,128]{2,1,0:T(8,128)(2,1)S(1)} custom-call(s32[3]{0:T(128)S(1)} %pad_add_fusion.s_ref, f32[320,128]{1,0:T(8,128)S(1)} %get-tuple-element.48.own_ref.refs_0_, bf16[320,128]{1,0:T(8,128)(2,1)S(1)} %collective-permute-done.11.refs_0_.refs_1_, bf16[320,128]{1,0:T(8,128)(2,1)S(1)} %collective-permute-done.12.refs_1_.refs_2_, ...), custom_call_target="tpu_custom_call" | custom-call | flops 1048576 | bytes 983040 | tf_op jit(solution)/shard_map/later_back/pallas_call | solution.py:33
  50.5 0.8 %collective-permute-start.20 = (bf16[320,128]{1,0:T(8,128)(2,1)S(1)}, bf16[320,128]{1,0:T(8,128)(2,1)S(1)}, u32[]{:S(2)}, u32[]{:S(2)}) collective-permute-start(bf16[320,128]{1,0:T(8,128)(2,1)S(1)} %get-tuple-element.64), channel_id=1, source_target_pairs={{0,6},{2,4},{4,2},{6,0},{8,14},{10,12},{12,10},{14,8},{16,22},{18,... | collective-permute-start | bytes 245768 | tf_op jit(solution)/shard_map/later_back/ppermute | solution.py:342
  51.4 0.6 %collective-permute-start.19 = (bf16[320,128]{1,0:T(8,128)(2,1)S(1)}, bf16[320,128]{1,0:T(8,128)(2,1)S(1)}, u32[]{:S(2)}, u32[]{:S(2)}) collective-permute-start(bf16[320,128]{1,0:T(8,128)(2,1)S(1)} %get-tuple-element.65), channel_id=1, source_target_pairs={{0,4},{2,6},{4,0},{6,2},{8,12},{10,14},{12,8},{14,10},{16,20},{18,... | collective-permute-start | bytes 245768 | tf_op jit(solution)/shard_map/later_back/ppermute | solution.py:342
  52.0 0.5 collective-permute-start.18
  52.5 2.9 %collective-permute-done.20 = bf16[320,128]{1,0:T(8,128)(2,1)S(1)} collective-permute-done((bf16[320,128]{1,0:T(8,128)(2,1)S(1)}, bf16[320,128]{1,0:T(8,128)(2,1)S(1)}, u32[]{:S(2)}, u32[]{:S(2)}) %collective-permute-start.20) | collective-permute-done | bytes 81952 | tf_op jit(solution)/shard_map/later_back/ppermute | solution.py:342
  55.3 1.7 %collective-permute-done.19 = bf16[320,128]{1,0:T(8,128)(2,1)S(1)} collective-permute-done((bf16[320,128]{1,0:T(8,128)(2,1)S(1)}, bf16[320,128]{1,0:T(8,128)(2,1)S(1)}, u32[]{:S(2)}, u32[]{:S(2)}) %collective-permute-start.19) | collective-permute-done | bytes 81952 | tf_op jit(solution)/shard_map/later_back/ppermute | solution.py:342
  57.0 0.0 collective-permute-done.18
  57.1 1.9 %collective-permute-done.14 = bf16[256,1024]{1,0:T(8,128)(2,1)S(1)} collective-permute-done((bf16[256,1024]{1,0:T(8,128)(2,1)S(1)}, bf16[256,1024]{1,0:T(8,128)(2,1)S(1)}, u32[]{:S(2)}, u32[]{:S(2)}) %collective-permute-start.14) | collective-permute-done | bytes 524320 | tf_op jit(solution)/shard_map/attended/ppermute | solution.py:342
  58.9 1.0 %add_convert_fusion = bf16[256,1024]{1,0:T(8,128)(2,1)} fusion(f32[256,1024]{1,0:T(8,128)S(1)} %mixed.1, bf16[256,1024]{1,0:T(8,128)(2,1)S(1)} %collective-permute-done.14), kind=kLoop, calls=%fused_computation | loop fusion | flops 786432 | bytes 2097152 | tf_op jit(solution)/shard_map/mixed_out/convert_element_type | solution.py:478
  59.9 1.8 %far_grad.1 = bf16[256,1024]{1,0:T(8,128)(2,1)} custom-call(s32[3]{0:T(128)S(1)} %pad_add_fusion.s_ref, bf16[8,160,256]{2,1,0:T(8,128)(2,1)S(1)} %get-tuple-element.55.kf_ref, bf16[4,320,128]{2,1,0:T(8,128)(2,1)S(1)} %pad_maximum_fusion.1.later_ref, f32[256,1024]{1,0:T(8,128)S(1)} %near.1.near_ref), custom_call_target="tpu_custom_call" | custom-call | flops 83886080 | bytes 2555904 | tf_op jit(solution)/shard_map/far_grad/pallas_call | solution.py:33
  (6 shorter events, 0.2 us)
Async XLA Ops:
  0.6 22.0 %copy-start.1 = (bf16[256,1024]{1,0:T(8,128)(2,1)S(1)}, bf16[256,1024]{1,0:T(8,128)(2,1)}, u32[]{:S(2)}) copy-start(bf16[256,1024]{1,0:T(8,128)(2,1)} %refs_0_) | copy-start | bytes 1572868
  0.6 22.0 %collective-permute-start.5 = (bf16[256,1024]{1,0:T(8,128)(2,1)}, bf16[256,1024]{1,0:T(8,128)(2,1)S(1)}, u32[]{:S(2)}, u32[]{:S(2)}) collective-permute-start(bf16[256,1024]{1,0:T(8,128)(2,1)} %refs_0_), channel_id=1, source_target_pairs={{0,1},{1,0},{2,3},{3,2},{4,5},{5,4},{6,7},{7,6},{8,9},{9,8},{10,11... | collective-permute-start | bytes 1572872 | tf_op jit(solution)/shard_map/cotangent/ppermute | solution.py:342
  4.8 2.3 %collective-permute-start = (bf16[2,1152]{1,0:T(2,128)(2,1)S(1)}, bf16[2,1152]{1,0:T(2,128)(2,1)S(1)}, u32[]{:S(2)}, u32[]{:S(2)}) collective-permute-start(bf16[2,1152]{1,0:T(2,128)(2,1)S(1)} %get-tuple-element.33), channel_id=1, source_target_pairs={{0,2},{2,4},{4,6},{6,8},{8,10},{10,12},{12,14},{14,16},{16,18},{18... | collective-permute-start | bytes 13832 | tf_op jit(solution)/shard_map/edge/ppermute | solution.py:313
  6.3 16.4 %copy-start = (bf16[1024,2048]{1,0:T(8,128)(2,1)S(1)}, bf16[1024,2048]{1,0:T(8,128)(2,1)}, u32[]{:S(2)}) copy-start(bf16[1024,2048]{1,0:T(8,128)(2,1)} %w_ref.3) | copy-start | bytes 12582916
  8.5 7.8 %collective-permute-start.3 = (bf16[352,128]{1,0:T(8,128)(2,1)S(1)}, bf16[352,128]{1,0:T(8,128)(2,1)S(1)}, u32[]{:S(2)}, u32[]{:S(2)}) collective-permute-start(bf16[352,128]{1,0:T(8,128)(2,1)S(1)} %get-tuple-element.60), channel_id=1, source_target_pairs={{0,6},{2,4},{4,2},{6,0},{8,14},{10,12},{12,10},{14,8},{16,22},{18,... | collective-permute-start | bytes 270344 | tf_op jit(solution)/shard_map/prior_share/ppermute | solution.py:342
  11.7 5.3 %collective-permute-start.2 = (bf16[352,128]{1,0:T(8,128)(2,1)S(1)}, bf16[352,128]{1,0:T(8,128)(2,1)S(1)}, u32[]{:S(2)}, u32[]{:S(2)}) collective-permute-start(bf16[352,128]{1,0:T(8,128)(2,1)S(1)} %get-tuple-element.61), channel_id=1, source_target_pairs={{0,4},{2,6},{4,0},{6,2},{8,12},{10,14},{12,8},{14,10},{16,20},{18,... | collective-permute-start | bytes 270344 | tf_op jit(solution)/shard_map/prior_share/ppermute | solution.py:342
  12.9 4.2 %collective-permute-start.1 = (bf16[352,128]{1,0:T(8,128)(2,1)S(1)}, bf16[352,128]{1,0:T(8,128)(2,1)S(1)}, u32[]{:S(2)}, u32[]{:S(2)}) collective-permute-start(bf16[352,128]{1,0:T(8,128)(2,1)S(1)} %get-tuple-element.62), channel_id=1, source_target_pairs={{0,2},{2,0},{4,6},{6,4},{8,10},{10,8},{12,14},{14,12},{16,18},{18,... | collective-permute-start | bytes 270344 | tf_op jit(solution)/shard_map/prior_share/ppermute | solution.py:342
  17.7 10.5 %collective-permute-start.7 = (bf16[352,128]{1,0:T(8,128)(2,1)S(1)}, bf16[352,128]{1,0:T(8,128)(2,1)S(1)}, u32[]{:S(2)}, u32[]{:S(2)}) collective-permute-start(bf16[352,128]{1,0:T(8,128)(2,1)S(1)} %prior_share.1), channel_id=1, source_target_pairs={{0,24},{2,26},{4,28},{6,30},{8,16},{10,18},{12,20},{14,22},{16,8},... | collective-permute-start | bytes 270344 | tf_op jit(solution)/shard_map/prior_planes/ppermute | solution.py:342
  22.0 8.1 %collective-permute-start.6 = (bf16[352,128]{1,0:T(8,128)(2,1)S(1)}, bf16[352,128]{1,0:T(8,128)(2,1)S(1)}, u32[]{:S(2)}, u32[]{:S(2)}) collective-permute-start(bf16[352,128]{1,0:T(8,128)(2,1)S(1)} %prior_share.1), channel_id=1, source_target_pairs={{0,16},{2,18},{4,20},{6,22},{8,24},{10,26},{12,28},{14,30},{16,0},... | collective-permute-start | bytes 270344 | tf_op jit(solution)/shard_map/prior_planes/ppermute | solution.py:342
  22.0 6.3 %collective-permute-start.4 = (bf16[352,128]{1,0:T(8,128)(2,1)S(1)}, bf16[352,128]{1,0:T(8,128)(2,1)S(1)}, u32[]{:S(2)}, u32[]{:S(2)}) collective-permute-start(bf16[352,128]{1,0:T(8,128)(2,1)S(1)} %prior_share.1), channel_id=1, source_target_pairs={{0,8},{2,10},{4,12},{6,14},{8,0},{10,2},{12,4},{14,6},{16,24},{18,... | collective-permute-start | bytes 270344 | tf_op jit(solution)/shard_map/prior_planes/ppermute | solution.py:342
  32.4 4.6 %collective-permute-start.13 = (bf16[320,128]{1,0:T(8,128)(2,1)S(1)}, bf16[320,128]{1,0:T(8,128)(2,1)S(1)}, u32[]{:S(2)}, u32[]{:S(2)}) collective-permute-start(bf16[320,128]{1,0:T(8,128)(2,1)S(1)} %get-tuple-element.67), channel_id=1, source_target_pairs={{0,6},{2,4},{4,2},{6,0},{8,14},{10,12},{12,10},{14,8},{16,22},{18,... | collective-permute-start | bytes 245768 | tf_op jit(solution)/shard_map/later_share/ppermute | solution.py:342
  33.0 6.2 %collective-permute-start.12 = (bf16[320,128]{1,0:T(8,128)(2,1)S(1)}, bf16[320,128]{1,0:T(8,128)(2,1)S(1)}, u32[]{:S(2)}, u32[]{:S(2)}) collective-permute-start(bf16[320,128]{1,0:T(8,128)(2,1)S(1)} %get-tuple-element.68), channel_id=1, source_target_pairs={{0,4},{2,6},{4,0},{6,2},{8,12},{10,14},{12,8},{14,10},{16,20},{18,... | collective-permute-start | bytes 245768 | tf_op jit(solution)/shard_map/later_share/ppermute | solution.py:342
  34.2 5.0 %collective-permute-start.11 = (bf16[320,128]{1,0:T(8,128)(2,1)S(1)}, bf16[320,128]{1,0:T(8,128)(2,1)S(1)}, u32[]{:S(2)}, u32[]{:S(2)}) collective-permute-start(bf16[320,128]{1,0:T(8,128)(2,1)S(1)} %get-tuple-element.69), channel_id=1, source_target_pairs={{0,2},{2,0},{4,6},{6,4},{8,10},{10,8},{12,14},{14,12},{16,18},{18,... | collective-permute-start | bytes 245768 | tf_op jit(solution)/shard_map/later_share/ppermute | solution.py:342
  34.4 7.9 %collective-permute-start.10 = (bf16[320,128]{1,0:T(8,128)(2,1)S(1)}, bf16[320,128]{1,0:T(8,128)(2,1)S(1)}, u32[]{:S(2)}, u32[]{:S(2)}) collective-permute-start(bf16[320,128]{1,0:T(8,128)(2,1)S(1)} %get-tuple-element.71), channel_id=1, source_target_pairs={{0,6},{2,4},{4,2},{6,0},{8,14},{10,12},{12,10},{14,8},{16,22},{18,... | collective-permute-start | bytes 245768 | tf_op jit(solution)/shard_map/prior_back/ppermute | solution.py:342
  35.7 8.5 %collective-permute-start.9 = (bf16[320,128]{1,0:T(8,128)(2,1)S(1)}, bf16[320,128]{1,0:T(8,128)(2,1)S(1)}, u32[]{:S(2)}, u32[]{:S(2)}) collective-permute-start(bf16[320,128]{1,0:T(8,128)(2,1)S(1)} %get-tuple-element.72), channel_id=1, source_target_pairs={{0,4},{2,6},{4,0},{6,2},{8,12},{10,14},{12,8},{14,10},{16,20},{18,... | collective-permute-start | bytes 245768 | tf_op jit(solution)/shard_map/prior_back/ppermute | solution.py:342
  37.0 7.2 %collective-permute-start.8 = (bf16[320,128]{1,0:T(8,128)(2,1)S(1)}, bf16[320,128]{1,0:T(8,128)(2,1)S(1)}, u32[]{:S(2)}, u32[]{:S(2)}) collective-permute-start(bf16[320,128]{1,0:T(8,128)(2,1)S(1)} %get-tuple-element.73), channel_id=1, source_target_pairs={{0,2},{2,0},{4,6},{6,4},{8,10},{10,8},{12,14},{14,12},{16,18},{18,... | collective-permute-start | bytes 245768 | tf_op jit(solution)/shard_map/prior_back/ppermute | solution.py:342
  39.8 9.3 %collective-permute-start.17 = (bf16[320,128]{1,0:T(8,128)(2,1)S(1)}, bf16[320,128]{1,0:T(8,128)(2,1)S(1)}, u32[]{:S(2)}, u32[]{:S(2)}) collective-permute-start(bf16[320,128]{1,0:T(8,128)(2,1)S(1)} %later_planes.1), channel_id=1, source_target_pairs={{0,24},{2,26},{4,28},{6,30},{8,16},{10,18},{12,20},{14,22},{16,8},... | collective-permute-start | bytes 245768 | tf_op jit(solution)/shard_map/later_planes/ppermute | solution.py:342
  42.3 7.4 %collective-permute-start.16 = (bf16[320,128]{1,0:T(8,128)(2,1)S(1)}, bf16[320,128]{1,0:T(8,128)(2,1)S(1)}, u32[]{:S(2)}, u32[]{:S(2)}) collective-permute-start(bf16[320,128]{1,0:T(8,128)(2,1)S(1)} %later_planes.1), channel_id=1, source_target_pairs={{0,16},{2,18},{4,20},{6,22},{8,24},{10,26},{12,28},{14,30},{16,0},... | collective-permute-start | bytes 245768 | tf_op jit(solution)/shard_map/later_planes/ppermute | solution.py:342
  42.3 6.7 %collective-permute-start.15 = (bf16[320,128]{1,0:T(8,128)(2,1)S(1)}, bf16[320,128]{1,0:T(8,128)(2,1)S(1)}, u32[]{:S(2)}, u32[]{:S(2)}) collective-permute-start(bf16[320,128]{1,0:T(8,128)(2,1)S(1)} %later_planes.1), channel_id=1, source_target_pairs={{0,8},{2,10},{4,12},{6,14},{8,0},{10,2},{12,4},{14,6},{16,24},{18,... | collective-permute-start | bytes 245768 | tf_op jit(solution)/shard_map/later_planes/ppermute | solution.py:342
  46.2 12.7 %collective-permute-start.14 = (bf16[256,1024]{1,0:T(8,128)(2,1)S(1)}, bf16[256,1024]{1,0:T(8,128)(2,1)S(1)}, u32[]{:S(2)}, u32[]{:S(2)}) collective-permute-start(bf16[256,1024]{1,0:T(8,128)(2,1)S(1)} %get-tuple-element.54), channel_id=1, source_target_pairs={{0,1},{1,0},{2,3},{3,2},{4,5},{5,4},{6,7},{7,6},{8,9},{9,8},{10,11... | collective-permute-start | bytes 1572872 | tf_op jit(solution)/shard_map/attended/ppermute | solution.py:342
  50.5 4.8 %collective-permute-start.20 = (bf16[320,128]{1,0:T(8,128)(2,1)S(1)}, bf16[320,128]{1,0:T(8,128)(2,1)S(1)}, u32[]{:S(2)}, u32[]{:S(2)}) collective-permute-start(bf16[320,128]{1,0:T(8,128)(2,1)S(1)} %get-tuple-element.64), channel_id=1, source_target_pairs={{0,6},{2,4},{4,2},{6,0},{8,14},{10,12},{12,10},{14,8},{16,22},{18,... | collective-permute-start | bytes 245768 | tf_op jit(solution)/shard_map/later_back/ppermute | solution.py:342
  51.4 5.6 %collective-permute-start.19 = (bf16[320,128]{1,0:T(8,128)(2,1)S(1)}, bf16[320,128]{1,0:T(8,128)(2,1)S(1)}, u32[]{:S(2)}, u32[]{:S(2)}) collective-permute-start(bf16[320,128]{1,0:T(8,128)(2,1)S(1)} %get-tuple-element.65), channel_id=1, source_target_pairs={{0,4},{2,6},{4,0},{6,2},{8,12},{10,14},{12,8},{14,10},{16,20},{18,... | collective-permute-start | bytes 245768 | tf_op jit(solution)/shard_map/later_back/ppermute | solution.py:342
  52.0 5.0 %collective-permute-start.18 = (bf16[320,128]{1,0:T(8,128)(2,1)S(1)}, bf16[320,128]{1,0:T(8,128)(2,1)S(1)}, u32[]{:S(2)}, u32[]{:S(2)}) collective-permute-start(bf16[320,128]{1,0:T(8,128)(2,1)S(1)} %get-tuple-element.66), channel_id=1, source_target_pairs={{0,2},{2,0},{4,6},{6,4},{8,10},{10,8},{12,14},{14,12},{16,18},{18,... | collective-permute-start | bytes 245768 | tf_op jit(solution)/shard_map/later_back/ppermute | solution.py:342

commit v3 on v2

--- a/solution.py
+++ b/solution.py
@@ -84,15 +84,23 @@
     return ref[rank ^ (head // per_piece), at : at + ROWS, :]
 
 
-def edge_kernel(k_far, v_far, ck_far, cv_far, edge_ref, k_ref, v_ref, ck_ref, cv_ref, sems):
+def edge_kernel(k_far, v_far, edge_ref, k_ref, v_ref, sems):
+    tokens, width = k_far.shape
+    deep = k_ref.shape[0]
+    rows = pl.ds(tokens - deep, deep)
+    copies = [fetch(k_far.at[rows], k_ref, sems.at[0]), fetch(v_far.at[rows], v_ref, sems.at[1])]
+    last = deep - CONV + 1
+    copies[0].wait()
+    edge_ref[:, :width] = k_ref[...].astype(F32)[last:].astype(BF16)
+    copies[1].wait()
+    edge_ref[:, width:] = v_ref[...].astype(F32)[last:].astype(BF16)
+
+
+def load_kernel(k_far, v_far, ck_far, cv_far, k_ref, v_ref, ck_ref, cv_ref, sems):
     pairs = ((k_far, k_ref), (v_far, v_ref), (ck_far, ck_ref), (cv_far, cv_ref))
     copies = [fetch(a, b, sems.at[i]) for i, (a, b) in enumerate(pairs)]
     for copy in copies:
         copy.wait()
-    tokens, width = k_ref.shape
-    last = 16 - CONV + 1
-    edge_ref[:, :width] = k_ref[tokens - 16 :, :].astype(F32)[last:].astype(BF16)
-    edge_ref[:, width:] = v_ref[tokens - 16 :, :].astype(F32)[last:].astype(BF16)
 
 
 def query_kernel(s_ref, q_far, qd_ref, q_ref, sem):
@@ -103,6 +111,12 @@
 def columns_of(s_ref, w_ref, distance):
     columns = w_ref.shape[1] // lax.axis_size("head")
     return pl.ds(pl.multiple_of((s_ref[1] ^ distance) * columns, columns), columns)
+
+
+def turn_kernel(s_ref, qd_ref, kf_ref, qt_ref, kt_ref):
+    for head in range(qd_ref.shape[0]):
+        qt_ref[head] = qd_ref[head].T
+        kt_ref[head] = kf_ref[head].T
 
 
 def grad_kernel(s_ref, *refs):
@@ -203,11 +217,8 @@
         refs[-1][...] = total
 
 
-def piece_kernel(sign, strides, s_ref, *refs):
-    rows = refs[-1].shape[1] if len(refs[-1].shape) == 3 else refs[-2].shape[1]
-    norm_ref = refs[-1] if len(refs[-1].shape) == 2 else None
-    pieces_ref = refs[-1] if norm_ref is None else refs[-2]
-    got_refs, moved_refs = refs[:PLANE], refs[PLANE : PLANE + len(strides)]
+def store_pieces(sign, strides, s_ref, got_refs, moved_refs, pieces_ref):
+    rows = pieces_ref.shape[1]
 
     def masked(ahead, ref):
         return jnp.where(ahead, ref[...].astype(F32), 0.0)
@@ -223,14 +234,19 @@
         else:
             before = before + ref[...].astype(F32)
     rank = s_ref[0]
+    extra = None
     for slot in range(PLANE):
         total = before
         for i in range(PLANE):
             if i != slot:
                 total = total + masked(is_ahead(rank ^ i, rank ^ slot), got_refs[i])
         pieces_ref[slot] = total[:rows].astype(BF16)
-        if norm_ref is not None and slot == 0:
-            norm_ref[...] = total[rows:]
+        extra = total[rows:] if slot == 0 else extra
+    return extra
+
+
+def piece_kernel(sign, strides, s_ref, *refs):
+    store_pieces(sign, strides, s_ref, refs[:PLANE], refs[PLANE:-1], refs[-1])
 
 
 def score_kernel(s_ref, qd_ref, kf_ref, vc_ref, low_ref, den_ref, num_ref):
@@ -248,11 +264,13 @@
         num_ref[:, at : at + VDIM] = mm(low, vc_ref[:, at : at + VDIM], TN)
 
 
-def scale_kernel(s_ref, norm_ref, den_ref, qd_ref, og_ref, inv_ref, sg_ref, own_ref, send_ref, slots):
+def scale_kernel(strides, s_ref, den_ref, qd_ref, og_ref, *refs):
+    *refs, pieces_ref, inv_ref, sg_ref, own_ref, send_ref, slots = refs
     rank = s_ref[0]
     heads = qd_ref.shape[0]
     per_piece = heads // PLANE
-    norm = norm_values(norm_ref[...])
+    lines = store_pieces(1, strides, s_ref, refs[:PLANE], refs[PLANE:], pieces_ref)
+    norm = norm_values(lines)
     high = norm.astype(BF16).astype(F32)
     middle = (norm - high).astype(BF16).astype(F32)
     rest = norm - high - middle
@@ -279,14 +297,14 @@
         vg_ref[:, at : at + VDIM] = mm(low_ref[head], sg_ref[:, at : at + VDIM], NN)
 
 
-def attend_kernel(s_ref, qd_ref, prior_ref, num_ref, inv_ref, w_ref, att_ref, part_ref):
+def attend_kernel(s_ref, qt_ref, prior_ref, num_ref, inv_ref, w_ref, att_ref, part_ref):
     rank = s_ref[0]
-    heads = qd_ref.shape[0]
+    heads = qt_ref.shape[0]
     per_piece = heads // PLANE
     for head in range(heads):
         at = head * VDIM
         prior = load_piece(rank, head, per_piece, prior_ref)
-        total = num_ref[:, at : at + VDIM] + mm(qd_ref[head], prior, TN)
+        total = num_ref[:, at : at + VDIM] + mm(qt_ref[head], prior, NN)
         att_ref[:, at : at + VDIM] = (total * inv_ref[:, head : head + 1]).astype(BF16)
     part_ref[...] = mm(att_ref[...], w_ref[:, columns_of(s_ref, w_ref, 1)], NN).astype(BF16)
 
@@ -296,15 +314,32 @@
     part_ref[...] = mm(att_ref[...], weight, NN).astype(part_ref.dtype)
 
 
-def far_kernel(s_ref, kf_ref, later_ref, near_ref, vg_ref):
+def last_kernel(s_ref, kt_ref, later_ref, near_ref, part_ref, *refs):
+    *other_refs, vg_far, mixed_far, vg_ref, mixed_ref, sems = refs
     rank = s_ref[0]
-    heads = kf_ref.shape[0]
+    heads = kt_ref.shape[0]
     per_piece = heads // PLANE
+    copies = []
     for head in range(heads):
         at = head * VDIM
         later = load_piece(rank, head, per_piece, later_ref)
-        total = near_ref[:, at : at + VDIM] + mm(kf_ref[head], later, TN)
+        total = near_ref[:, at : at + VDIM] + mm(kt_ref[head], later, NN)
         vg_ref[:, at : at + VDIM] = total.astype(BF16)
+        if head % per_piece == per_piece - 1:
+            columns = pl.ds((head + 1 - per_piece) * VDIM, per_piece * VDIM)
+            sem = sems.at[head // per_piece]
+            copies.append(fetch(vg_ref.at[:, columns], vg_far.at[:, columns], sem))
+    deep = part_ref.shape[0] // PLANE
+    for step in range(PLANE):
+        total = part_ref[step * deep : (step + 1) * deep, :]
+        for other_ref in other_refs:
+            total = total + other_ref[step * deep : (step + 1) * deep, :].astype(F32)
+        mixed_ref[step * deep : (step + 1) * deep, :] = total.astype(BF16)
+        rows = pl.ds(step * deep, deep)
+        sem = sems.at[PLANE + step]
+        copies.append(fetch(mixed_ref.at[rows], mixed_far.at[rows], sem))
+    for copy in copies:
+        copy.wait()
 
 
 def shifted(x, axis, by):
@@ -366,18 +401,26 @@
     slots = vmem((PLANE, piece_rows, VDIM), F32)
 
     with jax.named_scope("edge"):
-        arrays = (keys, values, conv_keys, conv_values)
-        spec = pl.BlockSpec(memory_space=vmem)
-        last_rows, k_near, v_near, ck_near, cv_near = pl.pallas_call(
+        last_rows = pl.pallas_call(
             edge_kernel,
-            out_shape=[S((CONV - 1, keys.shape[1] + width), BF16)]
-            + [S(x.shape, x.dtype) for x in arrays],
+            out_shape=S((CONV - 1, keys.shape[1] + width), BF16),
+            in_specs=[pl.BlockSpec(memory_space=pltpu.HBM)] * 2,
+            out_specs=pl.BlockSpec(memory_space=vmem),
+            scratch_shapes=[vmem((16, keys.shape[1]), BF16), vmem((16, width), BF16), dma((2,))],
+            compiler_params=pltpu.CompilerParams(vmem_limit_bytes=VMEM_LIMIT),
+        )(in_hbm(keys), in_hbm(values))
+        before = shifted(last_rows, "ctx", 1)
+    with jax.named_scope("load"):
+        arrays = (after(keys, last_rows), values, conv_keys, conv_values)
+        near_by = pl.pallas_call(
+            load_kernel,
+            out_shape=[S(x.shape, x.dtype) for x in arrays],
             in_specs=[pl.BlockSpec(memory_space=pltpu.HBM)] * 4,
-            out_specs=[spec] * 5,
+            out_specs=[pl.BlockSpec(memory_space=vmem)] * 4,
             scratch_shapes=[dma((4,))],
             compiler_params=pltpu.CompilerParams(vmem_limit_bytes=VMEM_LIMIT),
+            cost_estimate=pl.CostEstimate(flops=1 << 20, bytes_accessed=1 << 20, transcendentals=0),
         )(*[in_hbm(x) for x in arrays])
-        before = shifted(last_rows, "ctx", 1)
     with jax.named_scope("cotangent"):
         cots = [swapped(cotangent, "head", j) for j in range(1, groups)]
     with jax.named_scope("key_features"):
@@ -387,7 +430,7 @@
             S(message, F32),
             S((PLANE, *message), BF16),
         ]
-        ops = (k_near, v_near, before, ck_near, cv_near)
+        ops = (*near_by[:2], before, *near_by[2:])
         kf, vc, own, send = call(key_kernel, scalars, ops, outs, step, scratch=[slots])
     with jax.named_scope("query_features"):
         (qd,) = call(
@@ -426,23 +469,23 @@
         (out_grad,) = call(
             grad_kernel, scalars, ops, [S((tokens, width), F32)], groups * project_flops
         )
-    with jax.named_scope("prior_back"):
-        outs = [S((PLANE, piece_rows, VDIM), BF16), S((4 * heads, VDIM), F32)]
-        body = functools.partial(piece_kernel, 1, strides)
-        ops = (own, *got, after(moved[0], out_grad), *moved[1:])
-        pieces, prior_norm = call(body, scalars, ops, outs, 1 << 20)
-        prior = handed_back(pieces)
+    with jax.named_scope("turned"):
+        outs = [S((heads, tokens, ROWS), BF16)] * 2
+        qt, kt = call(turn_kernel, scalars, (after(qd, out_grad), kf), outs, 1 << 22)
     with jax.named_scope("scaled_grad"):
         outs = [
+            S((PLANE, piece_rows, VDIM), BF16),
             S((tokens, heads), F32),
             S((tokens, width), BF16),
             S((piece_rows, VDIM), F32),
             S((PLANE, piece_rows, VDIM), BF16),
         ]
-        ops = (prior_norm, den, qd, out_grad)
-        inverse, scaled, own_later, send_later = call(
-            scale_kernel, scalars, ops, outs, step, scratch=[slots]
+        ops = (den, after(qd, qt), out_grad, own, *got, *moved)
+        body = functools.partial(scale_kernel, strides)
+        pieces, inverse, scaled, own_later, send_later = call(
+            body, scalars, ops, outs, step, scratch=[slots]
         )
+        prior = handed_back(pieces)
     with jax.named_scope("later_share"):
         got_later = [swapped(send_later[j], "ctx", j) for j in range(1, PLANE)]
     with jax.named_scope("later_planes"):
@@ -451,7 +494,7 @@
         moved_later, strides = planes_ahead(total_later, sent_later, -1, plain_join)
     with jax.named_scope("attended"):
         outs = [S((tokens, width), BF16), S((tokens, columns), BF16)]
-        ops = (qd, prior, after(num, sent_later), inverse, out_weight)
+        ops = (qt, prior, after(num, sent_later), inverse, out_weight)
         attended, part = call(attend_kernel, scalars, ops, outs, step + project_flops)
         parts = [swapped(part, "head", 1)]
     with jax.named_scope("near"):
@@ -471,15 +514,21 @@
         ops = (own_later, *got_later, after(moved_later[0], part, near), *moved_later[1:])
         (pieces,) = call(body, scalars, ops, outs, 1 << 20)
         later = handed_back(pieces)
-    with jax.named_scope("mixed_out"):
-        mixed_out = part
-        for other in parts:
-            mixed_out = mixed_out + other.astype(F32)
-        mixed_out = mixed_out.astype(BF16)
-    with jax.named_scope("far_grad"):
-        (value_grad,) = call(
-            far_kernel, scalars, (after(kf, mixed_out), later, near), [S((tokens, width), BF16)], step
-        )
+    with jax.named_scope("last"):
+        whole = (tokens, columns)
+        value_grad, mixed_out = pl.pallas_call(
+            last_kernel,
+            out_shape=[S((tokens, width), BF16), S(whole, BF16)],
+            in_specs=[pl.BlockSpec(memory_space=pltpu.SMEM)]
+            + [pl.BlockSpec(memory_space=vmem)] * (4 + len(parts)),
+            out_specs=[pl.BlockSpec(memory_space=pltpu.HBM)] * 2,
+            scratch_shapes=[
+                vmem((tokens, width), BF16),
+                vmem(whole, BF16),
+                dma((2 * PLANE,)),
+            ],
+            compiler_params=pltpu.CompilerParams(vmem_limit_bytes=VMEM_LIMIT),
+        )(scalars, kt, later, near, part, *parts)
     return mixed_out, value_grad
 
 

time: 61.9 us -> 60.1 us (0.971)
  starting transfers between devices: 25 us -> 23.5 us
  Pallas kernels: 18.1 us -> 19.4 us
  other arithmetic: 1.12 us -> 0.16 us
  waiting for transfers between devices: 16.6 us -> 15.9 us
    pallas_call x1 -> x3, Pallas kernels: 1.13 us -> 3.94 us  [the longest x1 1.88 us: per_device(): pl.pallas_call(last_kernel, out_shape=[S((tokens, width), BF16), S(whole,...]
    pallas_call x13 -> x12, Pallas kernels: 17 us -> 15.4 us  [call(): pl.pallas_call(body, out_shape=out_shape, in_specs=[pl.BlockSpec(memory_s...]
    ppermute x20, starting transfers between devices: 23.5 us -> 22 us  [swapped(): return lax.ppermute(x, axis, pairs)]
    convert_element_type x1 -> x0, other arithmetic: 0.96 us -> none  [per_device(): mixed_out = mixed_out.astype(BF16)]
    ppermute x1, waiting for transfers between devices: 0.7 us -> 0.01 us  [shifted(): return lax.ppermute(x, axis, pairs)]
  transfers between devices with their start and end apart: 21 -> 21, of which waited for: 10 -> 8; matrix products, arithmetic and copies ran while one was open for 0% -> 0% of each run, Pallas kernels for 23% -> 26%
where the time goes in v3:
time: 60.1 us; the launch traced here: 59.9 us
  starting transfers between devices  23.5 us (39%)
  Pallas kernels  19.4 us (32%)
  waiting for transfers between devices  15.9 us (26%)
  between operations  0.87 us (1%)
    ppermute x20, starting transfers between devices, swapped(): return lax.ppermute(x, axis, pairs)  22 us
    ppermute x20, waiting for transfers between devices, swapped(): return lax.ppermute(x, axis, pairs)  15.9 us
    pallas_call x12, Pallas kernels, call(): pl.pallas_call(body, out_shape=out_shape, in_specs=[pl.BlockSpec(memory_s...  15.4 us
    pallas_call x1, Pallas kernels, per_device(): pl.pallas_call(last_kernel, out_shape=[S((tokens, width), BF16), S(whole,...  1.88 us
    ppermute x1, starting transfers between devices, shifted(): return lax.ppermute(x, axis, pairs)  1.46 us
    pallas_call x1, Pallas kernels, per_device(): pl.pallas_call(load_kernel, out_shape=[S(x.shape, x.dtype) for x in array...  1.26 us
  transfers between devices with their start and end apart: 21, of which 8 were waited for; matrix products, arithmetic and copies ran while one was open for 0% of the time, Pallas kernels for 26%

profile of v3, /device:TPU:0, one launch (start us, length us, event | category | flops | bytes accessed | tf_op | source)
XLA Modules:
  0.0 59.9 jit_solution(16218164066745722265)
XLA Ops:
  0.6 0.0 copy-start.1
  0.6 3.0 %collective-permute-start.4 = (bf16[256,1024]{1,0:T(8,128)(2,1)}, bf16[256,1024]{1,0:T(8,128)(2,1)S(1)}, u32[]{:S(2)}, u32[]{:S(2)}) collective-permute-start(bf16[256,1024]{1,0:T(8,128)(2,1)} %refs_0_), channel_id=1, source_target_pairs={{0,1},{1,0},{2,3},{3,2},{4,5},{5,4},{6,7},{7,6},{8,9},{9,8},{10,11... | collective-permute-start | bytes 1572872 | tf_op jit(solution)/shard_map/cotangent/ppermute | solution.py:377
  3.6 0.8 %edge.1 = bf16[2,1152]{1,0:T(2,128)(2,1)S(1)} custom-call(bf16[256,128]{1,0:T(8,128)(2,1)} %k_far.2, bf16[256,1024]{1,0:T(8,128)(2,1)} %v_far.3), custom_call_target="tpu_custom_call" | custom-call | tf_op jit(solution)/shard_map/edge/pallas_call | solution.py:404
  4.4 1.5 %collective-permute-start = (bf16[2,1152]{1,0:T(2,128)(2,1)S(1)}, bf16[2,1152]{1,0:T(2,128)(2,1)S(1)}, u32[]{:S(2)}, u32[]{:S(2)}) collective-permute-start(bf16[2,1152]{1,0:T(2,128)(2,1)S(1)} %edge.1), channel_id=1, source_target_pairs={{0,2},{2,4},{4,6},{6,8},{8,10},{10,12},{12,14},{14,16},{16,18},{18... | collective-permute-start | bytes 13832 | tf_op jit(solution)/shard_map/edge/ppermute | solution.py:348
  5.9 0.0 copy-start
  5.9 0.1 pad_add_fusion.s_ref
  6.0 1.3 %load.1 = (bf16[256,128]{1,0:T(8,128)(2,1)S(1)}, bf16[256,1024]{1,0:T(8,128)(2,1)S(1)}, f32[3,128]{1,0:T(4,128)S(1)}, f32[3,1024]{1,0:T(4,128)S(1)}) custom-call(bf16[256,128]{1,0:T(8,128)(2,1)} %k_far.2, bf16[256,1024]{1,0:T(8,128)(2,1)} %v_far.3, f32[3,128]{1,0:T(4,128)} %ck_far.1, f32[3,1024]{1,0:T(4,128)} %cv_far.1), custom_call_target="tpu_custom_call" | custom-call | flops 1048576 | bytes 1048576 | tf_op jit(solution)/shard_map/load/pallas_call | solution.py:415
  7.3 0.0 collective-permute-done.before_ref
  7.3 1.4 %key_features.1 = (bf16[8,160,256]{2,1,0:T(8,128)(2,1)S(1)}, bf16[256,1024]{1,0:T(8,128)(2,1)S(1)}, f32[352,128]{1,0:T(8,128)S(1)}, bf16[4,352,128]{2,1,0:T(8,128)(2,1)S(1)}) custom-call(s32[3]{0:T(128)S(1)} %pad_add_fusion.s_ref, bf16[256,128]{1,0:T(8,128)(2,1)S(1)} %get-tuple-element.35.k_ref, bf16[256,1024]{1,0:T(8,128)(2,1)S(1)} %get-tuple-element.36.v_ref, ...), custom_call_target="tpu_custom_call" | custom-call | flops 83886080 | bytes 2328576 | tf_op jit(solution)/shard_map/key_features/pallas_call | solution.py:33
  8.8 3.3 %collective-permute-start.3 = (bf16[352,128]{1,0:T(8,128)(2,1)S(1)}, bf16[352,128]{1,0:T(8,128)(2,1)S(1)}, u32[]{:S(2)}, u32[]{:S(2)}) collective-permute-start(bf16[352,128]{1,0:T(8,128)(2,1)S(1)} %get-tuple-element.66), channel_id=1, source_target_pairs={{0,6},{2,4},{4,2},{6,0},{8,14},{10,12},{12,10},{14,8},{16,22},{18,... | collective-permute-start | bytes 270344 | tf_op jit(solution)/shard_map/prior_share/ppermute | solution.py:377
  12.1 0.5 collective-permute-start.2
  12.6 0.0 collective-permute-start.1
  12.6 1.7 %query_features.1.qd_ref = bf16[8,160,256]{2,1,0:T(8,128)(2,1)S(1)} custom-call(s32[3]{0:T(128)S(1)} %pad_add_fusion.s_ref, bf16[256,128]{1,0:T(8,128)(2,1)} %q_far), custom_call_target="tpu_custom_call" | custom-call | flops 83886080 | bytes 720896 | tf_op jit(solution)/shard_map/query_features/pallas_call | solution.py:33
  14.2 1.7 %scores.1 = (bf16[8,256,256]{2,1,0:T(8,128)(2,1)S(1)}, f32[8,256]{1,0:T(8,128)S(1)}, f32[256,1024]{1,0:T(8,128)S(1)}) custom-call(s32[3]{0:T(128)S(1)} %pad_add_fusion.s_ref, bf16[8,160,256]{2,1,0:T(8,128)(2,1)S(1)} %query_features.1.qd_ref, bf16[8,160,256]{2,1,0:T(8,128)(2,1)S(1)} %get-tuple-element.42.kf_ref, bf16[256,1024]{1,0:T(8,128)(2,1)S(1)} %get-tuple-element.43.vc_ref), custom_call_target="tpu_custom_call" | custom-call | flops 335544320 | bytes 3940352 | tf_op jit(solution)/shard_map/scores/pallas_call | solution.py:33
  16.0 0.0 collective-permute-done.3.refs_2_.refs_3_
  16.0 1.2 %collective-permute-done.2.refs_1_.refs_2_ = bf16[352,128]{1,0:T(8,128)(2,1)S(1)} collective-permute-done((bf16[352,128]{1,0:T(8,128)(2,1)S(1)}, bf16[352,128]{1,0:T(8,128)(2,1)S(1)}, u32[]{:S(2)}, u32[]{:S(2)}) %collective-permute-start.2) | collective-permute-done | bytes 90144 | tf_op jit(solution)/shard_map/prior_share/ppermute | solution.py:377
  17.2 0.0 collective-permute-done.1.refs_0_.refs_1_
  17.2 0.7 %prior_share.1 = bf16[352,128]{1,0:T(8,128)(2,1)S(1)} custom-call(s32[3]{0:T(128)S(1)} %pad_add_fusion.s_ref, f32[352,128]{1,0:T(8,128)S(1)} %get-tuple-element.41.own_ref.refs_0_, bf16[352,128]{1,0:T(8,128)(2,1)S(1)} %collective-permute-done.1.refs_0_.refs_1_, bf16[352,128]{1,0:T(8,128)(2,1)S(1)} %collective-permute-done.2.refs_1_.refs_2_, ...), custom_call_target="tpu_custom_call" | custom-call | flops 1048576 | bytes 540672 | tf_op jit(solution)/shard_map/prior_share/pallas_call | solution.py:33
  17.9 3.8 %collective-permute-start.7 = (bf16[352,128]{1,0:T(8,128)(2,1)S(1)}, bf16[352,128]{1,0:T(8,128)(2,1)S(1)}, u32[]{:S(2)}, u32[]{:S(2)}) collective-permute-start(bf16[352,128]{1,0:T(8,128)(2,1)S(1)} %prior_share.1), channel_id=1, source_target_pairs={{0,24},{2,26},{4,28},{6,30},{8,16},{10,18},{12,20},{14,22},{16,8},... | collective-permute-start | bytes 270344 | tf_op jit(solution)/shard_map/prior_planes/ppermute | solution.py:377
  21.7 0.0 collective-permute-start.6
  21.7 0.6 %collective-permute-start.5 = (bf16[352,128]{1,0:T(8,128)(2,1)S(1)}, bf16[352,128]{1,0:T(8,128)(2,1)S(1)}, u32[]{:S(2)}, u32[]{:S(2)}) collective-permute-start(bf16[352,128]{1,0:T(8,128)(2,1)S(1)} %prior_share.1), channel_id=1, source_target_pairs={{0,8},{2,10},{4,12},{6,14},{8,0},{10,2},{12,4},{14,6},{16,24},{18,... | collective-permute-start | bytes 270344 | tf_op jit(solution)/shard_map/prior_planes/ppermute | solution.py:377
  22.3 0.0 collective-permute-done.4.refs_1_
  22.3 0.0 copy-done.1
  22.3 0.0 copy-done
  22.3 1.8 %out_grad.1.og_ref = f32[256,1024]{1,0:T(8,128)S(1)} custom-call(s32[3]{0:T(128)S(1)} %pad_add_fusion.s_ref, bf16[256,1024]{1,0:T(8,128)(2,1)S(1)} %copy-done.1, bf16[256,1024]{1,0:T(8,128)(2,1)S(1)} %collective-permute-done.4.refs_1_, bf16[1024,2048]{1,0:T(8,128)(2,1)S(1)} %copy-done), custom_call_target="tpu_custom_call" | custom-call | flops 1073741824 | bytes 6291456 | tf_op jit(solution)/shard_map/out_grad/pallas_call | solution.py:33
  24.2 1.2 %turned.1 = (bf16[8,256,160]{2,1,0:T(8,128)(2,1)S(1)}, bf16[8,256,160]{2,1,0:T(8,128)(2,1)S(1)}) custom-call(s32[3]{0:T(128)S(1)} %pad_add_fusion.s_ref, bf16[8,160,256]{2,1,0:T(8,128)(2,1)S(1)} %query_features.1.qd_ref, bf16[8,160,256]{2,1,0:T(8,128)(2,1)S(1)} %get-tuple-element.42.kf_ref), custom_call_target="tpu_custom_call" | custom-call | flops 4194304 | bytes 2621440 | tf_op jit(solution)/shard_map/turned/pallas_call | solution.py:33
  25.3 0.0 collective-permute-done.7.refs_6_
  25.3 4.5 %collective-permute-done.6.refs_5_ = bf16[352,128]{1,0:T(8,128)(2,1)S(1)} collective-permute-done((bf16[352,128]{1,0:T(8,128)(2,1)S(1)}, bf16[352,128]{1,0:T(8,128)(2,1)S(1)}, u32[]{:S(2)}, u32[]{:S(2)}) %collective-permute-start.6) | collective-permute-done | bytes 90144 | tf_op jit(solution)/shard_map/prior_planes/ppermute | solution.py:377
  29.9 0.0 collective-permute-done.5.refs_4_
  29.9 1.8 %scaled_grad.1 = (bf16[4,320,128]{2,1,0:T(8,128)(2,1)S(1)}, f32[256,8]{1,0:T(8,128)S(1)}, bf16[256,1024]{1,0:T(8,128)(2,1)S(1)}, f32[320,128]{1,0:T(8,128)S(1)}, bf16[4,320,128]{2,1,0:T(8,128)(2,1)S(1)}) custom-call(s32[3]{0:T(128)S(1)} %pad_add_fusion.s_ref, f32[8,256]{1,0:T(8,128)S(1)} %get-tuple-element.44.den_ref, ...), custom_call_target="tpu_custom_call" | custom-call | flops 83886080 | bytes 3784704 | tf_op jit(solution)/shard_map/scaled_grad/pallas_call | solution.py:33
  31.7 0.3 collective-permute-start.10
  32.0 1.2 %collective-permute-start.9 = (bf16[320,128]{1,0:T(8,128)(2,1)S(1)}, bf16[320,128]{1,0:T(8,128)(2,1)S(1)}, u32[]{:S(2)}, u32[]{:S(2)}) collective-permute-start(bf16[320,128]{1,0:T(8,128)(2,1)S(1)} %get-tuple-element.78), channel_id=1, source_target_pairs={{0,4},{2,6},{4,0},{6,2},{8,12},{10,14},{12,8},{14,10},{16,20},{18,... | collective-permute-start | bytes 245768 | tf_op jit(solution)/shard_map/later_share/ppermute | solution.py:377
  33.2 0.4 collective-permute-start.8
  33.6 1.1 %collective-permute-start.14 = (bf16[320,128]{1,0:T(8,128)(2,1)S(1)}, bf16[320,128]{1,0:T(8,128)(2,1)S(1)}, u32[]{:S(2)}, u32[]{:S(2)}) collective-permute-start(bf16[320,128]{1,0:T(8,128)(2,1)S(1)} %get-tuple-element.74), channel_id=1, source_target_pairs={{0,6},{2,4},{4,2},{6,0},{8,14},{10,12},{12,10},{14,8},{16,22},{18,... | collective-permute-start | bytes 245768 | tf_op jit(solution)/shard_map/scaled_grad/ppermute | solution.py:377
  34.7 0.8 %collective-permute-start.13 = (bf16[320,128]{1,0:T(8,128)(2,1)S(1)}, bf16[320,128]{1,0:T(8,128)(2,1)S(1)}, u32[]{:S(2)}, u32[]{:S(2)}) collective-permute-start(bf16[320,128]{1,0:T(8,128)(2,1)S(1)} %get-tuple-element.75), channel_id=1, source_target_pairs={{0,4},{2,6},{4,0},{6,2},{8,12},{10,14},{12,8},{14,10},{16,20},{18,... | collective-permute-start | bytes 245768 | tf_op jit(solution)/shard_map/scaled_grad/ppermute | solution.py:377
  35.5 1.0 %collective-permute-done.10.refs_2_.refs_3_ = bf16[320,128]{1,0:T(8,128)(2,1)S(1)} collective-permute-done((bf16[320,128]{1,0:T(8,128)(2,1)S(1)}, bf16[320,128]{1,0:T(8,128)(2,1)S(1)}, u32[]{:S(2)}, u32[]{:S(2)}) %collective-permute-start.10) | collective-permute-done | bytes 81952 | tf_op jit(solution)/shard_map/later_share/ppermute | solution.py:377
  36.5 0.1 collective-permute-start.12
  36.6 1.6 %collective-permute-done.9.refs_1_.refs_2_ = bf16[320,128]{1,0:T(8,128)(2,1)S(1)} collective-permute-done((bf16[320,128]{1,0:T(8,128)(2,1)S(1)}, bf16[320,128]{1,0:T(8,128)(2,1)S(1)}, u32[]{:S(2)}, u32[]{:S(2)}) %collective-permute-start.9) | collective-permute-done | bytes 81952 | tf_op jit(solution)/shard_map/later_share/ppermute | solution.py:377
  38.2 0.0 collective-permute-done.8.refs_0_.refs_1_
  38.2 0.6 later_planes.1
  38.8 2.7 %collective-permute-start.16 = (bf16[320,128]{1,0:T(8,128)(2,1)S(1)}, bf16[320,128]{1,0:T(8,128)(2,1)S(1)}, u32[]{:S(2)}, u32[]{:S(2)}) collective-permute-start(bf16[320,128]{1,0:T(8,128)(2,1)S(1)} %later_planes.1), channel_id=1, source_target_pairs={{0,24},{2,26},{4,28},{6,30},{8,16},{10,18},{12,20},{14,22},{16,8},... | collective-permute-start | bytes 245768 | tf_op jit(solution)/shard_map/later_planes/ppermute | solution.py:377
  41.4 0.0 collective-permute-start.15
  41.4 0.0 collective-permute-done.14
  41.4 1.8 %collective-permute-start.11 = (bf16[320,128]{1,0:T(8,128)(2,1)S(1)}, bf16[320,128]{1,0:T(8,128)(2,1)S(1)}, u32[]{:S(2)}, u32[]{:S(2)}) collective-permute-start(bf16[320,128]{1,0:T(8,128)(2,1)S(1)} %later_planes.1), channel_id=1, source_target_pairs={{0,8},{2,10},{4,12},{6,14},{8,0},{10,2},{12,4},{14,6},{16,24},{18,... | collective-permute-start | bytes 245768 | tf_op jit(solution)/shard_map/later_planes/ppermute | solution.py:377
  43.2 0.0 collective-permute-done.13
  43.2 0.0 collective-permute-done.12
  43.3 1.6 %attended.1 = (bf16[256,1024]{1,0:T(8,128)(2,1)S(1)}, bf16[256,1024]{1,0:T(8,128)(2,1)S(1)}) custom-call(s32[3]{0:T(128)S(1)} %pad_add_fusion.s_ref, bf16[8,256,160]{2,1,0:T(8,128)(2,1)S(1)} %get-tuple-element.49.qt_ref, bf16[4,320,128]{2,1,0:T(8,128)(2,1)S(1)} %pad_maximum_fusion.prior_ref, f32[256,1024]{1,0:T(8,128)S(1)} %get-tuple-element.55.num_ref, ...), custom_call_target="tpu_custom_call" | custom-call | flops 620756992 | bytes 7282688 | tf_op jit(solution)/shard_map/attended/pallas_call | solution.py:33
  44.9 0.6 collective-permute-start.20
  45.4 1.0 %near.1.near_ref = f32[256,1024]{1,0:T(8,128)S(1)} custom-call(s32[3]{0:T(128)S(1)} %pad_add_fusion.s_ref, bf16[8,256,256]{2,1,0:T(8,128)(2,1)S(1)} %get-tuple-element.59.low_ref, bf16[256,1024]{1,0:T(8,128)(2,1)S(1)} %get-tuple-element.61.sg_ref), custom_call_target="tpu_custom_call" | custom-call | flops 167772160 | bytes 2621440 | tf_op jit(solution)/shard_map/near/pallas_call | solution.py:33
  46.4 1.2 %mixed.1.part_ref = f32[256,1024]{1,0:T(8,128)S(1)} custom-call(s32[3]{0:T(128)S(1)} %pad_add_fusion.s_ref, bf16[256,1024]{1,0:T(8,128)(2,1)S(1)} %get-tuple-element.58.att_ref, bf16[1024,2048]{1,0:T(8,128)(2,1)S(1)} %copy-done), custom_call_target="tpu_custom_call" | custom-call | flops 1073741824 | bytes 5767168 | tf_op jit(solution)/shard_map/mixed/pallas_call | solution.py:33
  47.7 0.0 collective-permute-done.11.refs_4_
  47.7 0.0 collective-permute-done.16.refs_6_
  47.7 1.1 %collective-permute-done.15.refs_5_ = bf16[320,128]{1,0:T(8,128)(2,1)S(1)} collective-permute-done((bf16[320,128]{1,0:T(8,128)(2,1)S(1)}, bf16[320,128]{1,0:T(8,128)(2,1)S(1)}, u32[]{:S(2)}, u32[]{:S(2)}) %collective-permute-start.15) | collective-permute-done | bytes 81952 | tf_op jit(solution)/shard_map/later_planes/ppermute | solution.py:377
  48.8 0.8 %later_back.1 = bf16[4,320,128]{2,1,0:T(8,128)(2,1)S(1)} custom-call(s32[3]{0:T(128)S(1)} %pad_add_fusion.s_ref, f32[320,128]{1,0:T(8,128)S(1)} %get-tuple-element.51.own_ref.refs_0_, bf16[320,128]{1,0:T(8,128)(2,1)S(1)} %collective-permute-done.8.refs_0_.refs_1_, bf16[320,128]{1,0:T(8,128)(2,1)S(1)} %collective-permute-done.9.refs_1_.refs_2_, ...), custom_call_target="tpu_custom_call" | custom-call | flops 1048576 | bytes 983040 | tf_op jit(solution)/shard_map/later_back/pallas_call | solution.py:33
  49.6 0.9 %collective-permute-start.19 = (bf16[320,128]{1,0:T(8,128)(2,1)S(1)}, bf16[320,128]{1,0:T(8,128)(2,1)S(1)}, u32[]{:S(2)}, u32[]{:S(2)}) collective-permute-start(bf16[320,128]{1,0:T(8,128)(2,1)S(1)} %get-tuple-element.70), channel_id=1, source_target_pairs={{0,6},{2,4},{4,2},{6,0},{8,14},{10,12},{12,10},{14,8},{16,22},{18,... | collective-permute-start | bytes 245768 | tf_op jit(solution)/shard_map/later_back/ppermute | solution.py:377
  50.5 0.9 %collective-permute-start.18 = (bf16[320,128]{1,0:T(8,128)(2,1)S(1)}, bf16[320,128]{1,0:T(8,128)(2,1)S(1)}, u32[]{:S(2)}, u32[]{:S(2)}) collective-permute-start(bf16[320,128]{1,0:T(8,128)(2,1)S(1)} %get-tuple-element.71), channel_id=1, source_target_pairs={{0,4},{2,6},{4,0},{6,2},{8,12},{10,14},{12,8},{14,10},{16,20},{18,... | collective-permute-start | bytes 245768 | tf_op jit(solution)/shard_map/later_back/ppermute | solution.py:377
  51.4 0.2 collective-permute-start.17
  51.6 2.6 %collective-permute-done.19 = bf16[320,128]{1,0:T(8,128)(2,1)S(1)} collective-permute-done((bf16[320,128]{1,0:T(8,128)(2,1)S(1)}, bf16[320,128]{1,0:T(8,128)(2,1)S(1)}, u32[]{:S(2)}, u32[]{:S(2)}) %collective-permute-start.19) | collective-permute-done | bytes 81952 | tf_op jit(solution)/shard_map/later_back/ppermute | solution.py:377
  54.2 2.0 %collective-permute-done.18 = bf16[320,128]{1,0:T(8,128)(2,1)S(1)} collective-permute-done((bf16[320,128]{1,0:T(8,128)(2,1)S(1)}, bf16[320,128]{1,0:T(8,128)(2,1)S(1)}, u32[]{:S(2)}, u32[]{:S(2)}) %collective-permute-start.18) | collective-permute-done | bytes 81952 | tf_op jit(solution)/shard_map/later_back/ppermute | solution.py:377
  56.2 0.0 collective-permute-done.17
  56.3 1.8 %collective-permute-done.20.refs_0_ = bf16[256,1024]{1,0:T(8,128)(2,1)S(1)} collective-permute-done((bf16[256,1024]{1,0:T(8,128)(2,1)S(1)}, bf16[256,1024]{1,0:T(8,128)(2,1)S(1)}, u32[]{:S(2)}, u32[]{:S(2)}) %collective-permute-start.20) | collective-permute-done | bytes 524320 | tf_op jit(solution)/shard_map/attended/ppermute | solution.py:377
  58.0 1.9 %last.1 = (bf16[256,1024]{1,0:T(8,128)(2,1)}, bf16[256,1024]{1,0:T(8,128)(2,1)}) custom-call(s32[3]{0:T(128)S(1)} %pad_add_fusion.s_ref, bf16[8,256,160]{2,1,0:T(8,128)(2,1)S(1)} %get-tuple-element.48.kt_ref, bf16[4,320,128]{2,1,0:T(8,128)(2,1)S(1)} %pad_maximum_fusion.1.later_ref, f32[256,1024]{1,0:T(8,128)S(1)} %near.1.near_ref, ...), custom_call_target="tpu_custom_call" | custom-call | tf_op jit(solution)/shard_map/last/pallas_call | solution.py:519
  (6 shorter events, 0.2 us)
Async XLA Ops:
  0.6 21.7 %copy-start.1 = (bf16[256,1024]{1,0:T(8,128)(2,1)S(1)}, bf16[256,1024]{1,0:T(8,128)(2,1)}, u32[]{:S(2)}) copy-start(bf16[256,1024]{1,0:T(8,128)(2,1)} %refs_0_) | copy-start | bytes 1572868
  0.6 21.7 %collective-permute-start.4 = (bf16[256,1024]{1,0:T(8,128)(2,1)}, bf16[256,1024]{1,0:T(8,128)(2,1)S(1)}, u32[]{:S(2)}, u32[]{:S(2)}) collective-permute-start(bf16[256,1024]{1,0:T(8,128)(2,1)} %refs_0_), channel_id=1, source_target_pairs={{0,1},{1,0},{2,3},{3,2},{4,5},{5,4},{6,7},{7,6},{8,9},{9,8},{10,11... | collective-permute-start | bytes 1572872 | tf_op jit(solution)/shard_map/cotangent/ppermute | solution.py:377
  4.4 2.8 %collective-permute-start = (bf16[2,1152]{1,0:T(2,128)(2,1)S(1)}, bf16[2,1152]{1,0:T(2,128)(2,1)S(1)}, u32[]{:S(2)}, u32[]{:S(2)}) collective-permute-start(bf16[2,1152]{1,0:T(2,128)(2,1)S(1)} %edge.1), channel_id=1, source_target_pairs={{0,2},{2,4},{4,6},{6,8},{8,10},{10,12},{12,14},{14,16},{16,18},{18... | collective-permute-start | bytes 13832 | tf_op jit(solution)/shard_map/edge/ppermute | solution.py:348
  5.9 16.4 %copy-start = (bf16[1024,2048]{1,0:T(8,128)(2,1)S(1)}, bf16[1024,2048]{1,0:T(8,128)(2,1)}, u32[]{:S(2)}) copy-start(bf16[1024,2048]{1,0:T(8,128)(2,1)} %w_ref.3) | copy-start | bytes 12582916
  8.8 7.2 %collective-permute-start.3 = (bf16[352,128]{1,0:T(8,128)(2,1)S(1)}, bf16[352,128]{1,0:T(8,128)(2,1)S(1)}, u32[]{:S(2)}, u32[]{:S(2)}) collective-permute-start(bf16[352,128]{1,0:T(8,128)(2,1)S(1)} %get-tuple-element.66), channel_id=1, source_target_pairs={{0,6},{2,4},{4,2},{6,0},{8,14},{10,12},{12,10},{14,8},{16,22},{18,... | collective-permute-start | bytes 270344 | tf_op jit(solution)/shard_map/prior_share/ppermute | solution.py:377
  12.1 5.1 %collective-permute-start.2 = (bf16[352,128]{1,0:T(8,128)(2,1)S(1)}, bf16[352,128]{1,0:T(8,128)(2,1)S(1)}, u32[]{:S(2)}, u32[]{:S(2)}) collective-permute-start(bf16[352,128]{1,0:T(8,128)(2,1)S(1)} %get-tuple-element.67), channel_id=1, source_target_pairs={{0,4},{2,6},{4,0},{6,2},{8,12},{10,14},{12,8},{14,10},{16,20},{18,... | collective-permute-start | bytes 270344 | tf_op jit(solution)/shard_map/prior_share/ppermute | solution.py:377
  12.6 4.6 %collective-permute-start.1 = (bf16[352,128]{1,0:T(8,128)(2,1)S(1)}, bf16[352,128]{1,0:T(8,128)(2,1)S(1)}, u32[]{:S(2)}, u32[]{:S(2)}) collective-permute-start(bf16[352,128]{1,0:T(8,128)(2,1)S(1)} %get-tuple-element.68), channel_id=1, source_target_pairs={{0,2},{2,0},{4,6},{6,4},{8,10},{10,8},{12,14},{14,12},{16,18},{18,... | collective-permute-start | bytes 270344 | tf_op jit(solution)/shard_map/prior_share/ppermute | solution.py:377
  17.9 7.5 %collective-permute-start.7 = (bf16[352,128]{1,0:T(8,128)(2,1)S(1)}, bf16[352,128]{1,0:T(8,128)(2,1)S(1)}, u32[]{:S(2)}, u32[]{:S(2)}) collective-permute-start(bf16[352,128]{1,0:T(8,128)(2,1)S(1)} %prior_share.1), channel_id=1, source_target_pairs={{0,24},{2,26},{4,28},{6,30},{8,16},{10,18},{12,20},{14,22},{16,8},... | collective-permute-start | bytes 270344 | tf_op jit(solution)/shard_map/prior_planes/ppermute | solution.py:377
  21.7 8.2 %collective-permute-start.6 = (bf16[352,128]{1,0:T(8,128)(2,1)S(1)}, bf16[352,128]{1,0:T(8,128)(2,1)S(1)}, u32[]{:S(2)}, u32[]{:S(2)}) collective-permute-start(bf16[352,128]{1,0:T(8,128)(2,1)S(1)} %prior_share.1), channel_id=1, source_target_pairs={{0,16},{2,18},{4,20},{6,22},{8,24},{10,26},{12,28},{14,30},{16,0},... | collective-permute-start | bytes 270344 | tf_op jit(solution)/shard_map/prior_planes/ppermute | solution.py:377
  21.7 8.2 %collective-permute-start.5 = (bf16[352,128]{1,0:T(8,128)(2,1)S(1)}, bf16[352,128]{1,0:T(8,128)(2,1)S(1)}, u32[]{:S(2)}, u32[]{:S(2)}) collective-permute-start(bf16[352,128]{1,0:T(8,128)(2,1)S(1)} %prior_share.1), channel_id=1, source_target_pairs={{0,8},{2,10},{4,12},{6,14},{8,0},{10,2},{12,4},{14,6},{16,24},{18,... | collective-permute-start | bytes 270344 | tf_op jit(solution)/shard_map/prior_planes/ppermute | solution.py:377
  31.7 4.8 %collective-permute-start.10 = (bf16[320,128]{1,0:T(8,128)(2,1)S(1)}, bf16[320,128]{1,0:T(8,128)(2,1)S(1)}, u32[]{:S(2)}, u32[]{:S(2)}) collective-permute-start(bf16[320,128]{1,0:T(8,128)(2,1)S(1)} %get-tuple-element.77), channel_id=1, source_target_pairs={{0,6},{2,4},{4,2},{6,0},{8,14},{10,12},{12,10},{14,8},{16,22},{18,... | collective-permute-start | bytes 245768 | tf_op jit(solution)/shard_map/later_share/ppermute | solution.py:377
  32.0 6.2 %collective-permute-start.9 = (bf16[320,128]{1,0:T(8,128)(2,1)S(1)}, bf16[320,128]{1,0:T(8,128)(2,1)S(1)}, u32[]{:S(2)}, u32[]{:S(2)}) collective-permute-start(bf16[320,128]{1,0:T(8,128)(2,1)S(1)} %get-tuple-element.78), channel_id=1, source_target_pairs={{0,4},{2,6},{4,0},{6,2},{8,12},{10,14},{12,8},{14,10},{16,20},{18,... | collective-permute-start | bytes 245768 | tf_op jit(solution)/shard_map/later_share/ppermute | solution.py:377
  33.2 4.9 %collective-permute-start.8 = (bf16[320,128]{1,0:T(8,128)(2,1)S(1)}, bf16[320,128]{1,0:T(8,128)(2,1)S(1)}, u32[]{:S(2)}, u32[]{:S(2)}) collective-permute-start(bf16[320,128]{1,0:T(8,128)(2,1)S(1)} %get-tuple-element.79), channel_id=1, source_target_pairs={{0,2},{2,0},{4,6},{6,4},{8,10},{10,8},{12,14},{14,12},{16,18},{18,... | collective-permute-start | bytes 245768 | tf_op jit(solution)/shard_map/later_share/ppermute | solution.py:377
  33.6 7.8 %collective-permute-start.14 = (bf16[320,128]{1,0:T(8,128)(2,1)S(1)}, bf16[320,128]{1,0:T(8,128)(2,1)S(1)}, u32[]{:S(2)}, u32[]{:S(2)}) collective-permute-start(bf16[320,128]{1,0:T(8,128)(2,1)S(1)} %get-tuple-element.74), channel_id=1, source_target_pairs={{0,6},{2,4},{4,2},{6,0},{8,14},{10,12},{12,10},{14,8},{16,22},{18,... | collective-permute-start | bytes 245768 | tf_op jit(solution)/shard_map/scaled_grad/ppermute | solution.py:377
  34.7 8.5 %collective-permute-start.13 = (bf16[320,128]{1,0:T(8,128)(2,1)S(1)}, bf16[320,128]{1,0:T(8,128)(2,1)S(1)}, u32[]{:S(2)}, u32[]{:S(2)}) collective-permute-start(bf16[320,128]{1,0:T(8,128)(2,1)S(1)} %get-tuple-element.75), channel_id=1, source_target_pairs={{0,4},{2,6},{4,0},{6,2},{8,12},{10,14},{12,8},{14,10},{16,20},{18,... | collective-permute-start | bytes 245768 | tf_op jit(solution)/shard_map/scaled_grad/ppermute | solution.py:377
  36.5 6.7 %collective-permute-start.12 = (bf16[320,128]{1,0:T(8,128)(2,1)S(1)}, bf16[320,128]{1,0:T(8,128)(2,1)S(1)}, u32[]{:S(2)}, u32[]{:S(2)}) collective-permute-start(bf16[320,128]{1,0:T(8,128)(2,1)S(1)} %get-tuple-element.76), channel_id=1, source_target_pairs={{0,2},{2,0},{4,6},{6,4},{8,10},{10,8},{12,14},{14,12},{16,18},{18,... | collective-permute-start | bytes 245768 | tf_op jit(solution)/shard_map/scaled_grad/ppermute | solution.py:377
  38.8 8.9 %collective-permute-start.16 = (bf16[320,128]{1,0:T(8,128)(2,1)S(1)}, bf16[320,128]{1,0:T(8,128)(2,1)S(1)}, u32[]{:S(2)}, u32[]{:S(2)}) collective-permute-start(bf16[320,128]{1,0:T(8,128)(2,1)S(1)} %later_planes.1), channel_id=1, source_target_pairs={{0,24},{2,26},{4,28},{6,30},{8,16},{10,18},{12,20},{14,22},{16,8},... | collective-permute-start | bytes 245768 | tf_op jit(solution)/shard_map/later_planes/ppermute | solution.py:377
  41.4 7.4 %collective-permute-start.15 = (bf16[320,128]{1,0:T(8,128)(2,1)S(1)}, bf16[320,128]{1,0:T(8,128)(2,1)S(1)}, u32[]{:S(2)}, u32[]{:S(2)}) collective-permute-start(bf16[320,128]{1,0:T(8,128)(2,1)S(1)} %later_planes.1), channel_id=1, source_target_pairs={{0,16},{2,18},{4,20},{6,22},{8,24},{10,26},{12,28},{14,30},{16,0},... | collective-permute-start | bytes 245768 | tf_op jit(solution)/shard_map/later_planes/ppermute | solution.py:377
  41.4 6.2 %collective-permute-start.11 = (bf16[320,128]{1,0:T(8,128)(2,1)S(1)}, bf16[320,128]{1,0:T(8,128)(2,1)S(1)}, u32[]{:S(2)}, u32[]{:S(2)}) collective-permute-start(bf16[320,128]{1,0:T(8,128)(2,1)S(1)} %later_planes.1), channel_id=1, source_target_pairs={{0,8},{2,10},{4,12},{6,14},{8,0},{10,2},{12,4},{14,6},{16,24},{18,... | collective-permute-start | bytes 245768 | tf_op jit(solution)/shard_map/later_planes/ppermute | solution.py:377
  44.9 13.2 %collective-permute-start.20 = (bf16[256,1024]{1,0:T(8,128)(2,1)S(1)}, bf16[256,1024]{1,0:T(8,128)(2,1)S(1)}, u32[]{:S(2)}, u32[]{:S(2)}) collective-permute-start(bf16[256,1024]{1,0:T(8,128)(2,1)S(1)} %get-tuple-element.63), channel_id=1, source_target_pairs={{0,1},{1,0},{2,3},{3,2},{4,5},{5,4},{6,7},{7,6},{8,9},{9,8},{10,11... | collective-permute-start | bytes 1572872 | tf_op jit(solution)/shard_map/attended/ppermute | solution.py:377
  49.6 4.6 %collective-permute-start.19 = (bf16[320,128]{1,0:T(8,128)(2,1)S(1)}, bf16[320,128]{1,0:T(8,128)(2,1)S(1)}, u32[]{:S(2)}, u32[]{:S(2)}) collective-permute-start(bf16[320,128]{1,0:T(8,128)(2,1)S(1)} %get-tuple-element.70), channel_id=1, source_target_pairs={{0,6},{2,4},{4,2},{6,0},{8,14},{10,12},{12,10},{14,8},{16,22},{18,... | collective-permute-start | bytes 245768 | tf_op jit(solution)/shard_map/later_back/ppermute | solution.py:377
  50.5 5.7 %collective-permute-start.18 = (bf16[320,128]{1,0:T(8,128)(2,1)S(1)}, bf16[320,128]{1,0:T(8,128)(2,1)S(1)}, u32[]{:S(2)}, u32[]{:S(2)}) collective-permute-start(bf16[320,128]{1,0:T(8,128)(2,1)S(1)} %get-tuple-element.71), channel_id=1, source_target_pairs={{0,4},{2,6},{4,0},{6,2},{8,12},{10,14},{12,8},{14,10},{16,20},{18,... | collective-permute-start | bytes 245768 | tf_op jit(solution)/shard_map/later_back/ppermute | solution.py:377
  51.4 4.8 %collective-permute-start.17 = (bf16[320,128]{1,0:T(8,128)(2,1)S(1)}, bf16[320,128]{1,0:T(8,128)(2,1)S(1)}, u32[]{:S(2)}, u32[]{:S(2)}) collective-permute-start(bf16[320,128]{1,0:T(8,128)(2,1)S(1)} %get-tuple-element.72), channel_id=1, source_target_pairs={{0,2},{2,0},{4,6},{6,4},{8,10},{10,8},{12,14},{14,12},{16,18},{18,... | collective-permute-start | bytes 245768 | tf_op jit(solution)/shard_map/later_back/ppermute | solution.py:377

commit v4 on v3

--- a/solution.py
+++ b/solution.py
@@ -103,9 +103,28 @@
         copy.wait()
 
 
-def query_kernel(s_ref, q_far, qd_ref, q_ref, sem):
-    fetch(q_far, q_ref, sem).wait()
+def query_kernel(
+    s_ref,
+    q_far,
+    k_far,
+    v_far,
+    ck_far,
+    cv_far,
+    qd_ref,
+    k_ref,
+    v_ref,
+    ck_ref,
+    cv_ref,
+    q_ref,
+    sems,
+):
+    far = (q_far, k_far, v_far, ck_far, cv_far)
+    near = (q_ref, k_ref, v_ref, ck_ref, cv_ref)
+    copies = [fetch(a, b, sems.at[i]) for i, (a, b) in enumerate(zip(far, near))]
+    copies[0].wait()
     store_features(qd_ref, q_ref[...].astype(F32).T, True)
+    for copy in copies[1:]:
+        copy.wait()
 
 
 def columns_of(s_ref, w_ref, distance):
@@ -410,19 +429,17 @@
             compiler_params=pltpu.CompilerParams(vmem_limit_bytes=VMEM_LIMIT),
         )(in_hbm(keys), in_hbm(values))
         before = shifted(last_rows, "ctx", 1)
-    with jax.named_scope("load"):
-        arrays = (after(keys, last_rows), values, conv_keys, conv_values)
-        near_by = pl.pallas_call(
-            load_kernel,
-            out_shape=[S(x.shape, x.dtype) for x in arrays],
-            in_specs=[pl.BlockSpec(memory_space=pltpu.HBM)] * 4,
-            out_specs=[pl.BlockSpec(memory_space=vmem)] * 4,
-            scratch_shapes=[dma((4,))],
-            compiler_params=pltpu.CompilerParams(vmem_limit_bytes=VMEM_LIMIT),
-            cost_estimate=pl.CostEstimate(flops=1 << 20, bytes_accessed=1 << 20, transcendentals=0),
-        )(*[in_hbm(x) for x in arrays])
-    with jax.named_scope("cotangent"):
-        cots = [swapped(cotangent, "head", j) for j in range(1, groups)]
+    with jax.named_scope("query_features"):
+        arrays = (keys, values, conv_keys, conv_values)
+        qd, *near_by = call(
+            query_kernel,
+            scalars,
+            (after(queries, last_rows), *arrays),
+            [S((heads, ROWS, tokens), BF16)] + [S(x.shape, x.dtype) for x in arrays],
+            1 << 20,
+            far=range(5),
+            scratch=[vmem(queries.shape, BF16), dma((5,))],
+        )
     with jax.named_scope("key_features"):
         outs = [
             S((heads, ROWS, tokens), BF16),
@@ -432,16 +449,8 @@
         ]
         ops = (*near_by[:2], before, *near_by[2:])
         kf, vc, own, send = call(key_kernel, scalars, ops, outs, step, scratch=[slots])
-    with jax.named_scope("query_features"):
-        (qd,) = call(
-            query_kernel,
-            scalars,
-            (after(queries, send),),
-            [S((heads, ROWS, tokens), BF16)],
-            step,
-            far=(0,),
-            scratch=[vmem(queries.shape, BF16), dma(())],
-        )
+    with jax.named_scope("cotangent"):
+        cots = [swapped(after(cotangent, send), "head", j) for j in range(1, groups)]
     with jax.named_scope("prior_share"):
         got = [swapped(send[j], "ctx", j) for j in range(1, PLANE)]
 
@@ -459,19 +468,19 @@
             S((heads, tokens), F32),
             S((tokens, width), F32),
         ]
-        low, den, num = call(score_kernel, scalars, (qd, kf, vc), outs, 4 * step)
+        low, den, num = call(score_kernel, scalars, (qd, kf, vc), outs, 400 * step)
     with jax.named_scope("prior_planes"):
         sent = after(sent, den)
         norm_join = functools.partial(join, piece_rows)
         moved, strides = planes_ahead(total, sent, 1, norm_join)
+    with jax.named_scope("turned"):
+        outs = [S((heads, tokens, ROWS), BF16)] * 2
+        qt, kt = call(turn_kernel, scalars, (after(qd, sent), kf), outs, 1 << 22)
     with jax.named_scope("out_grad"):
-        ops = (after(cotangent, sent), *cots, out_weight)
+        ops = (after(cotangent, qt), *cots, out_weight)
         (out_grad,) = call(
             grad_kernel, scalars, ops, [S((tokens, width), F32)], groups * project_flops
         )
-    with jax.named_scope("turned"):
-        outs = [S((heads, tokens, ROWS), BF16)] * 2
-        qt, kt = call(turn_kernel, scalars, (after(qd, out_grad), kf), outs, 1 << 22)
     with jax.named_scope("scaled_grad"):
         outs = [
             S((PLANE, piece_rows, VDIM), BF16),
@@ -480,7 +489,7 @@
             S((piece_rows, VDIM), F32),
             S((PLANE, piece_rows, VDIM), BF16),
         ]
-        ops = (den, after(qd, qt), out_grad, own, *got, *moved)
+        ops = (den, qd, out_grad, own, *got, *moved)
         body = functools.partial(scale_kernel, strides)
         pieces, inverse, scaled, own_later, send_later = call(
             body, scalars, ops, outs, step, scratch=[slots]

time: 60.1 us -> 59 us (0.982)
  Pallas kernels: 19.4 us -> 18.1 us
  starting transfers between devices: 23.5 us -> 24.6 us
  waiting for transfers between devices: 15.9 us -> 15 us
    pallas_call x1 -> x0, Pallas kernels: 1.26 us -> none  [per_device(): pl.pallas_call(load_kernel, out_shape=[S(x.shape, x.dtype) for x in array...]
    ppermute x20, waiting for transfers between devices: 15.9 us -> 15 us  [swapped(): return lax.ppermute(x, axis, pairs)]
    ppermute x1, starting transfers between devices: 1.46 us -> 2.36 us  [shifted(): return lax.ppermute(x, axis, pairs)]
  transfers between devices with their start and end apart: 21 -> 21, of which waited for: 8 -> 9; matrix products, arithmetic and copies ran while one was open for 0% -> 0% of each run, Pallas kernels for 26% -> 21%
where the time goes in v4:
time: 59 us; the launch traced here: 58.8 us
  starting transfers between devices  24.6 us (42%)
  Pallas kernels  18.1 us (31%)
  waiting for transfers between devices  15 us (25%)
  between operations  0.85 us (1%)
    ppermute x20, starting transfers between devices, swapped(): return lax.ppermute(x, axis, pairs)  22.2 us
    pallas_call x12, Pallas kernels, call(): pl.pallas_call(body, out_shape=out_shape, in_specs=[pl.BlockSpec(memory_s...  15.5 us
    ppermute x20, waiting for transfers between devices, swapped(): return lax.ppermute(x, axis, pairs)  15 us
    ppermute x1, starting transfers between devices, shifted(): return lax.ppermute(x, axis, pairs)  2.36 us
    pallas_call x1, Pallas kernels, per_device(): pl.pallas_call(last_kernel, out_shape=[S((tokens, width), BF16), S(whole,...  1.89 us
  transfers between devices with their start and end apart: 21, of which 9 were waited for; matrix products, arithmetic and copies ran while one was open for 0% of the time, Pallas kernels for 21%

profile of v4, /device:TPU:0, one launch (start us, length us, event | category | flops | bytes accessed | tf_op | source)
XLA Modules:
  0.0 58.8 jit_solution(11545691643112888575)
XLA Ops:
  0.6 0.8 %edge.1 = bf16[2,1152]{1,0:T(2,128)(2,1)S(1)} custom-call(bf16[256,128]{1,0:T(8,128)(2,1)} %k_far.3, bf16[256,1024]{1,0:T(8,128)(2,1)} %v_far.3), custom_call_target="tpu_custom_call" | custom-call | tf_op jit(solution)/shard_map/edge/pallas_call | solution.py:423
  1.4 2.4 %collective-permute-start = (bf16[2,1152]{1,0:T(2,128)(2,1)S(1)}, bf16[2,1152]{1,0:T(2,128)(2,1)S(1)}, u32[]{:S(2)}, u32[]{:S(2)}) collective-permute-start(bf16[2,1152]{1,0:T(2,128)(2,1)S(1)} %edge.1), channel_id=1, source_target_pairs={{0,2},{2,4},{4,6},{6,8},{8,10},{10,12},{12,14},{14,16},{16,18},{18... | collective-permute-start | bytes 13832 | tf_op jit(solution)/shard_map/edge/ppermute | solution.py:367
  3.8 0.1 pad_add_fusion.s_ref
  3.9 1.7 %query_features.1 = (bf16[8,160,256]{2,1,0:T(8,128)(2,1)S(1)}, bf16[256,128]{1,0:T(8,128)(2,1)S(1)}, bf16[256,1024]{1,0:T(8,128)(2,1)S(1)}, f32[3,128]{1,0:T(4,128)S(1)}, f32[3,1024]{1,0:T(4,128)S(1)}) custom-call(s32[3]{0:T(128)S(1)} %pad_add_fusion.s_ref, bf16[256,128]{1,0:T(8,128)(2,1)} %q_far, bf16[256,128]{1,0:T(8,128)(2,1)} %k_far.3, ...), custom_call_target="tpu_custom_call" | custom-call | flops 1048576 | bytes 1928192 | tf_op jit(solution)/shard_map/query_features/pallas_call | solution.py:33
  5.6 0.0 collective-permute-done.before_ref
  5.6 1.4 %key_features.1 = (bf16[8,160,256]{2,1,0:T(8,128)(2,1)S(1)}, bf16[256,1024]{1,0:T(8,128)(2,1)S(1)}, f32[352,128]{1,0:T(8,128)S(1)}, bf16[4,352,128]{2,1,0:T(8,128)(2,1)S(1)}) custom-call(s32[3]{0:T(128)S(1)} %pad_add_fusion.s_ref, bf16[256,128]{1,0:T(8,128)(2,1)S(1)} %get-tuple-element.36.k_ref, bf16[256,1024]{1,0:T(8,128)(2,1)S(1)} %get-tuple-element.37.v_ref, ...), custom_call_target="tpu_custom_call" | custom-call | flops 83886080 | bytes 2328576 | tf_op jit(solution)/shard_map/key_features/pallas_call | solution.py:33
  7.1 3.8 %collective-permute-start.3 = (bf16[352,128]{1,0:T(8,128)(2,1)S(1)}, bf16[352,128]{1,0:T(8,128)(2,1)S(1)}, u32[]{:S(2)}, u32[]{:S(2)}) collective-permute-start(bf16[352,128]{1,0:T(8,128)(2,1)S(1)} %get-tuple-element.66), channel_id=1, source_target_pairs={{0,6},{2,4},{4,2},{6,0},{8,14},{10,12},{12,10},{14,8},{16,22},{18,... | collective-permute-start | bytes 270344 | tf_op jit(solution)/shard_map/prior_share/ppermute | solution.py:396
  10.9 0.5 collective-permute-start.2
  11.4 0.0 collective-permute-start.1
  11.4 1.5 %collective-permute-start.4 = (bf16[256,1024]{1,0:T(8,128)(2,1)}, bf16[256,1024]{1,0:T(8,128)(2,1)S(1)}, u32[]{:S(2)}, u32[]{:S(2)}) collective-permute-start(bf16[256,1024]{1,0:T(8,128)(2,1)} %refs_0_), channel_id=1, source_target_pairs={{0,1},{1,0},{2,3},{3,2},{4,5},{5,4},{6,7},{7,6},{8,9},{9,8},{10,11... | collective-permute-start | bytes 1572872 | tf_op jit(solution)/shard_map/cotangent/ppermute | solution.py:396
  12.9 0.0 copy-start
  12.9 0.0 copy-start.1
  12.9 1.7 %scores.1 = (bf16[8,256,256]{2,1,0:T(8,128)(2,1)S(1)}, f32[8,256]{1,0:T(8,128)S(1)}, f32[256,1024]{1,0:T(8,128)S(1)}) custom-call(s32[3]{0:T(128)S(1)} %pad_add_fusion.s_ref, bf16[8,160,256]{2,1,0:T(8,128)(2,1)S(1)} %get-tuple-element.46.qd_ref, bf16[8,160,256]{2,1,0:T(8,128)(2,1)S(1)} %get-tuple-element.42.kf_ref, ...), custom_call_target="tpu_custom_call" | custom-call | flops 33554432000 | bytes 3940352 | tf_op jit(solution)/shard_map/scores/pallas_call | solution.py:33
  14.7 0.0 collective-permute-done.3.refs_2_.refs_3_
  14.7 1.4 %collective-permute-done.2.refs_1_.refs_2_ = bf16[352,128]{1,0:T(8,128)(2,1)S(1)} collective-permute-done((bf16[352,128]{1,0:T(8,128)(2,1)S(1)}, bf16[352,128]{1,0:T(8,128)(2,1)S(1)}, u32[]{:S(2)}, u32[]{:S(2)}) %collective-permute-start.2) | collective-permute-done | bytes 90144 | tf_op jit(solution)/shard_map/prior_share/ppermute | solution.py:396
  16.0 0.0 collective-permute-done.1.refs_0_.refs_1_
  16.0 0.7 %prior_share.1 = bf16[352,128]{1,0:T(8,128)(2,1)S(1)} custom-call(s32[3]{0:T(128)S(1)} %pad_add_fusion.s_ref, f32[352,128]{1,0:T(8,128)S(1)} %get-tuple-element.40.own_ref.refs_0_, bf16[352,128]{1,0:T(8,128)(2,1)S(1)} %collective-permute-done.1.refs_0_.refs_1_, bf16[352,128]{1,0:T(8,128)(2,1)S(1)} %collective-permute-done.2.refs_1_.refs_2_, ...), custom_call_target="tpu_custom_call" | custom-call | flops 1048576 | bytes 540672 | tf_op jit(solution)/shard_map/prior_share/pallas_call | solution.py:33
  16.7 4.2 %collective-permute-start.7 = (bf16[352,128]{1,0:T(8,128)(2,1)S(1)}, bf16[352,128]{1,0:T(8,128)(2,1)S(1)}, u32[]{:S(2)}, u32[]{:S(2)}) collective-permute-start(bf16[352,128]{1,0:T(8,128)(2,1)S(1)} %prior_share.1), channel_id=1, source_target_pairs={{0,24},{2,26},{4,28},{6,30},{8,16},{10,18},{12,20},{14,22},{16,8},... | collective-permute-start | bytes 270344 | tf_op jit(solution)/shard_map/prior_planes/ppermute | solution.py:396
  20.9 0.0 collective-permute-start.6
  20.9 0.6 %collective-permute-start.5 = (bf16[352,128]{1,0:T(8,128)(2,1)S(1)}, bf16[352,128]{1,0:T(8,128)(2,1)S(1)}, u32[]{:S(2)}, u32[]{:S(2)}) collective-permute-start(bf16[352,128]{1,0:T(8,128)(2,1)S(1)} %prior_share.1), channel_id=1, source_target_pairs={{0,8},{2,10},{4,12},{6,14},{8,0},{10,2},{12,4},{14,6},{16,24},{18,... | collective-permute-start | bytes 270344 | tf_op jit(solution)/shard_map/prior_planes/ppermute | solution.py:396
  21.6 1.1 %turned.1 = (bf16[8,256,160]{2,1,0:T(8,128)(2,1)S(1)}, bf16[8,256,160]{2,1,0:T(8,128)(2,1)S(1)}) custom-call(s32[3]{0:T(128)S(1)} %pad_add_fusion.s_ref, bf16[8,160,256]{2,1,0:T(8,128)(2,1)S(1)} %get-tuple-element.46.qd_ref, bf16[8,160,256]{2,1,0:T(8,128)(2,1)S(1)} %get-tuple-element.42.kf_ref), custom_call_target="tpu_custom_call" | custom-call | flops 4194304 | bytes 2621440 | tf_op jit(solution)/shard_map/turned/pallas_call | solution.py:33
  22.7 3.3 %collective-permute-done.4.refs_1_ = bf16[256,1024]{1,0:T(8,128)(2,1)S(1)} collective-permute-done((bf16[256,1024]{1,0:T(8,128)(2,1)}, bf16[256,1024]{1,0:T(8,128)(2,1)S(1)}, u32[]{:S(2)}, u32[]{:S(2)}) %collective-permute-start.4) | collective-permute-done | bytes 524320 | tf_op jit(solution)/shard_map/cotangent/ppermute | solution.py:396
  26.0 0.0 copy-done
  26.0 0.0 copy-done.1
  26.0 1.8 %out_grad.1.og_ref = f32[256,1024]{1,0:T(8,128)S(1)} custom-call(s32[3]{0:T(128)S(1)} %pad_add_fusion.s_ref, bf16[256,1024]{1,0:T(8,128)(2,1)S(1)} %copy-done.1, bf16[256,1024]{1,0:T(8,128)(2,1)S(1)} %collective-permute-done.4.refs_1_, bf16[1024,2048]{1,0:T(8,128)(2,1)S(1)} %copy-done), custom_call_target="tpu_custom_call" | custom-call | flops 1073741824 | bytes 6291456 | tf_op jit(solution)/shard_map/out_grad/pallas_call | solution.py:33
  27.8 0.0 collective-permute-done.7.refs_6_
  27.8 1.2 %collective-permute-done.6.refs_5_ = bf16[352,128]{1,0:T(8,128)(2,1)S(1)} collective-permute-done((bf16[352,128]{1,0:T(8,128)(2,1)S(1)}, bf16[352,128]{1,0:T(8,128)(2,1)S(1)}, u32[]{:S(2)}, u32[]{:S(2)}) %collective-permute-start.6) | collective-permute-done | bytes 90144 | tf_op jit(solution)/shard_map/prior_planes/ppermute | solution.py:396
  29.0 0.0 collective-permute-done.5.refs_4_
  29.0 1.8 %scaled_grad.1 = (bf16[4,320,128]{2,1,0:T(8,128)(2,1)S(1)}, f32[256,8]{1,0:T(8,128)S(1)}, bf16[256,1024]{1,0:T(8,128)(2,1)S(1)}, f32[320,128]{1,0:T(8,128)S(1)}, bf16[4,320,128]{2,1,0:T(8,128)(2,1)S(1)}) custom-call(s32[3]{0:T(128)S(1)} %pad_add_fusion.s_ref, f32[8,256]{1,0:T(8,128)S(1)} %get-tuple-element.44.den_ref, ...), custom_call_target="tpu_custom_call" | custom-call | flops 83886080 | bytes 3784704 | tf_op jit(solution)/shard_map/scaled_grad/pallas_call | solution.py:33
  30.8 0.1 collective-permute-start.10
  30.9 1.2 %collective-permute-start.9 = (bf16[320,128]{1,0:T(8,128)(2,1)S(1)}, bf16[320,128]{1,0:T(8,128)(2,1)S(1)}, u32[]{:S(2)}, u32[]{:S(2)}) collective-permute-start(bf16[320,128]{1,0:T(8,128)(2,1)S(1)} %get-tuple-element.78), channel_id=1, source_target_pairs={{0,4},{2,6},{4,0},{6,2},{8,12},{10,14},{12,8},{14,10},{16,20},{18,... | collective-permute-start | bytes 245768 | tf_op jit(solution)/shard_map/later_share/ppermute | solution.py:396
  32.1 0.7 %collective-permute-start.8 = (bf16[320,128]{1,0:T(8,128)(2,1)S(1)}, bf16[320,128]{1,0:T(8,128)(2,1)S(1)}, u32[]{:S(2)}, u32[]{:S(2)}) collective-permute-start(bf16[320,128]{1,0:T(8,128)(2,1)S(1)} %get-tuple-element.79), channel_id=1, source_target_pairs={{0,2},{2,0},{4,6},{6,4},{8,10},{10,8},{12,14},{14,12},{16,18},{18,... | collective-permute-start | bytes 245768 | tf_op jit(solution)/shard_map/later_share/ppermute | solution.py:396
  32.8 0.4 collective-permute-start.14
  33.2 1.3 %collective-permute-start.13 = (bf16[320,128]{1,0:T(8,128)(2,1)S(1)}, bf16[320,128]{1,0:T(8,128)(2,1)S(1)}, u32[]{:S(2)}, u32[]{:S(2)}) collective-permute-start(bf16[320,128]{1,0:T(8,128)(2,1)S(1)} %get-tuple-element.75), channel_id=1, source_target_pairs={{0,4},{2,6},{4,0},{6,2},{8,12},{10,14},{12,8},{14,10},{16,20},{18,... | collective-permute-start | bytes 245768 | tf_op jit(solution)/shard_map/scaled_grad/ppermute | solution.py:396
  34.5 1.2 %collective-permute-done.10.refs_2_.refs_3_ = bf16[320,128]{1,0:T(8,128)(2,1)S(1)} collective-permute-done((bf16[320,128]{1,0:T(8,128)(2,1)S(1)}, bf16[320,128]{1,0:T(8,128)(2,1)S(1)}, u32[]{:S(2)}, u32[]{:S(2)}) %collective-permute-start.10) | collective-permute-done | bytes 81952 | tf_op jit(solution)/shard_map/later_share/ppermute | solution.py:396
  35.6 0.0 collective-permute-start.12
  35.7 1.2 %collective-permute-done.9.refs_1_.refs_2_ = bf16[320,128]{1,0:T(8,128)(2,1)S(1)} collective-permute-done((bf16[320,128]{1,0:T(8,128)(2,1)S(1)}, bf16[320,128]{1,0:T(8,128)(2,1)S(1)}, u32[]{:S(2)}, u32[]{:S(2)}) %collective-permute-start.9) | collective-permute-done | bytes 81952 | tf_op jit(solution)/shard_map/later_share/ppermute | solution.py:396
  36.9 0.0 collective-permute-done.8.refs_0_.refs_1_
  36.9 0.6 later_planes.1
  37.5 2.5 %collective-permute-start.16 = (bf16[320,128]{1,0:T(8,128)(2,1)S(1)}, bf16[320,128]{1,0:T(8,128)(2,1)S(1)}, u32[]{:S(2)}, u32[]{:S(2)}) collective-permute-start(bf16[320,128]{1,0:T(8,128)(2,1)S(1)} %later_planes.1), channel_id=1, source_target_pairs={{0,24},{2,26},{4,28},{6,30},{8,16},{10,18},{12,20},{14,22},{16,8},... | collective-permute-start | bytes 245768 | tf_op jit(solution)/shard_map/later_planes/ppermute | solution.py:396
  40.0 0.0 collective-permute-start.15
  40.0 0.0 collective-permute-done.14
  40.0 2.0 %collective-permute-start.11 = (bf16[320,128]{1,0:T(8,128)(2,1)S(1)}, bf16[320,128]{1,0:T(8,128)(2,1)S(1)}, u32[]{:S(2)}, u32[]{:S(2)}) collective-permute-start(bf16[320,128]{1,0:T(8,128)(2,1)S(1)} %later_planes.1), channel_id=1, source_target_pairs={{0,8},{2,10},{4,12},{6,14},{8,0},{10,2},{12,4},{14,6},{16,24},{18,... | collective-permute-start | bytes 245768 | tf_op jit(solution)/shard_map/later_planes/ppermute | solution.py:396
  41.9 0.0 collective-permute-done.13
  41.9 0.0 collective-permute-done.12
  42.0 1.5 %attended.1 = (bf16[256,1024]{1,0:T(8,128)(2,1)S(1)}, bf16[256,1024]{1,0:T(8,128)(2,1)S(1)}) custom-call(s32[3]{0:T(128)S(1)} %pad_add_fusion.s_ref, bf16[8,256,160]{2,1,0:T(8,128)(2,1)S(1)} %get-tuple-element.48.qt_ref, bf16[4,320,128]{2,1,0:T(8,128)(2,1)S(1)} %pad_maximum_fusion.prior_ref, f32[256,1024]{1,0:T(8,128)S(1)} %get-tuple-element.55.num_ref, ...), custom_call_target="tpu_custom_call" | custom-call | flops 620756992 | bytes 7282688 | tf_op jit(solution)/shard_map/attended/pallas_call | solution.py:33
  43.5 1.6 %collective-permute-start.20 = (bf16[256,1024]{1,0:T(8,128)(2,1)S(1)}, bf16[256,1024]{1,0:T(8,128)(2,1)S(1)}, u32[]{:S(2)}, u32[]{:S(2)}) collective-permute-start(bf16[256,1024]{1,0:T(8,128)(2,1)S(1)} %get-tuple-element.63), channel_id=1, source_target_pairs={{0,1},{1,0},{2,3},{3,2},{4,5},{5,4},{6,7},{7,6},{8,9},{9,8},{10,11... | collective-permute-start | bytes 1572872 | tf_op jit(solution)/shard_map/attended/ppermute | solution.py:396
  45.1 1.0 %near.1.near_ref = f32[256,1024]{1,0:T(8,128)S(1)} custom-call(s32[3]{0:T(128)S(1)} %pad_add_fusion.s_ref, bf16[8,256,256]{2,1,0:T(8,128)(2,1)S(1)} %get-tuple-element.59.low_ref, bf16[256,1024]{1,0:T(8,128)(2,1)S(1)} %get-tuple-element.61.sg_ref), custom_call_target="tpu_custom_call" | custom-call | flops 167772160 | bytes 2621440 | tf_op jit(solution)/shard_map/near/pallas_call | solution.py:33
  46.1 1.2 %mixed.1.part_ref = f32[256,1024]{1,0:T(8,128)S(1)} custom-call(s32[3]{0:T(128)S(1)} %pad_add_fusion.s_ref, bf16[256,1024]{1,0:T(8,128)(2,1)S(1)} %get-tuple-element.58.att_ref, bf16[1024,2048]{1,0:T(8,128)(2,1)S(1)} %copy-done), custom_call_target="tpu_custom_call" | custom-call | flops 1073741824 | bytes 5767168 | tf_op jit(solution)/shard_map/mixed/pallas_call | solution.py:33
  47.3 0.0 collective-permute-done.11.refs_4_
  47.3 0.0 collective-permute-done.16.refs_6_
  47.4 0.3 collective-permute-done.15.refs_5_
  47.6 0.8 %later_back.1 = bf16[4,320,128]{2,1,0:T(8,128)(2,1)S(1)} custom-call(s32[3]{0:T(128)S(1)} %pad_add_fusion.s_ref, f32[320,128]{1,0:T(8,128)S(1)} %get-tuple-element.51.own_ref.refs_0_, bf16[320,128]{1,0:T(8,128)(2,1)S(1)} %collective-permute-done.8.refs_0_.refs_1_, bf16[320,128]{1,0:T(8,128)(2,1)S(1)} %collective-permute-done.9.refs_1_.refs_2_, ...), custom_call_target="tpu_custom_call" | custom-call | flops 1048576 | bytes 983040 | tf_op jit(solution)/shard_map/later_back/pallas_call | solution.py:33
  48.4 0.5 collective-permute-start.19
  49.0 1.3 %collective-permute-start.18 = (bf16[320,128]{1,0:T(8,128)(2,1)S(1)}, bf16[320,128]{1,0:T(8,128)(2,1)S(1)}, u32[]{:S(2)}, u32[]{:S(2)}) collective-permute-start(bf16[320,128]{1,0:T(8,128)(2,1)S(1)} %get-tuple-element.71), channel_id=1, source_target_pairs={{0,4},{2,6},{4,0},{6,2},{8,12},{10,14},{12,8},{14,10},{16,20},{18,... | collective-permute-start | bytes 245768 | tf_op jit(solution)/shard_map/later_back/ppermute | solution.py:396
  50.3 0.1 collective-permute-start.17
  50.4 2.6 %collective-permute-done.19 = bf16[320,128]{1,0:T(8,128)(2,1)S(1)} collective-permute-done((bf16[320,128]{1,0:T(8,128)(2,1)S(1)}, bf16[320,128]{1,0:T(8,128)(2,1)S(1)}, u32[]{:S(2)}, u32[]{:S(2)}) %collective-permute-start.19) | collective-permute-done | bytes 81952 | tf_op jit(solution)/shard_map/later_back/ppermute | solution.py:396
  53.0 2.0 %collective-permute-done.18 = bf16[320,128]{1,0:T(8,128)(2,1)S(1)} collective-permute-done((bf16[320,128]{1,0:T(8,128)(2,1)S(1)}, bf16[320,128]{1,0:T(8,128)(2,1)S(1)}, u32[]{:S(2)}, u32[]{:S(2)}) %collective-permute-start.18) | collective-permute-done | bytes 81952 | tf_op jit(solution)/shard_map/later_back/ppermute | solution.py:396
  55.0 0.0 collective-permute-done.17
  55.1 1.9 %collective-permute-done.20.refs_0_ = bf16[256,1024]{1,0:T(8,128)(2,1)S(1)} collective-permute-done((bf16[256,1024]{1,0:T(8,128)(2,1)S(1)}, bf16[256,1024]{1,0:T(8,128)(2,1)S(1)}, u32[]{:S(2)}, u32[]{:S(2)}) %collective-permute-start.20) | collective-permute-done | bytes 524320 | tf_op jit(solution)/shard_map/attended/ppermute | solution.py:396
  56.9 1.9 %last.1 = (bf16[256,1024]{1,0:T(8,128)(2,1)}, bf16[256,1024]{1,0:T(8,128)(2,1)}) custom-call(s32[3]{0:T(128)S(1)} %pad_add_fusion.s_ref, bf16[8,256,160]{2,1,0:T(8,128)(2,1)S(1)} %get-tuple-element.47.kt_ref, bf16[4,320,128]{2,1,0:T(8,128)(2,1)S(1)} %pad_maximum_fusion.1.later_ref, f32[256,1024]{1,0:T(8,128)S(1)} %near.1.near_ref, ...), custom_call_target="tpu_custom_call" | custom-call | tf_op jit(solution)/shard_map/last/pallas_call | solution.py:528
  (6 shorter events, 0.2 us)
Async XLA Ops:
  1.4 4.2 %collective-permute-start = (bf16[2,1152]{1,0:T(2,128)(2,1)S(1)}, bf16[2,1152]{1,0:T(2,128)(2,1)S(1)}, u32[]{:S(2)}, u32[]{:S(2)}) collective-permute-start(bf16[2,1152]{1,0:T(2,128)(2,1)S(1)} %edge.1), channel_id=1, source_target_pairs={{0,2},{2,4},{4,6},{6,8},{8,10},{10,12},{12,14},{14,16},{16,18},{18... | collective-permute-start | bytes 13832 | tf_op jit(solution)/shard_map/edge/ppermute | solution.py:367
  7.1 7.6 %collective-permute-start.3 = (bf16[352,128]{1,0:T(8,128)(2,1)S(1)}, bf16[352,128]{1,0:T(8,128)(2,1)S(1)}, u32[]{:S(2)}, u32[]{:S(2)}) collective-permute-start(bf16[352,128]{1,0:T(8,128)(2,1)S(1)} %get-tuple-element.66), channel_id=1, source_target_pairs={{0,6},{2,4},{4,2},{6,0},{8,14},{10,12},{12,10},{14,8},{16,22},{18,... | collective-permute-start | bytes 270344 | tf_op jit(solution)/shard_map/prior_share/ppermute | solution.py:396
  10.9 5.1 %collective-permute-start.2 = (bf16[352,128]{1,0:T(8,128)(2,1)S(1)}, bf16[352,128]{1,0:T(8,128)(2,1)S(1)}, u32[]{:S(2)}, u32[]{:S(2)}) collective-permute-start(bf16[352,128]{1,0:T(8,128)(2,1)S(1)} %get-tuple-element.67), channel_id=1, source_target_pairs={{0,4},{2,6},{4,0},{6,2},{8,12},{10,14},{12,8},{14,10},{16,20},{18,... | collective-permute-start | bytes 270344 | tf_op jit(solution)/shard_map/prior_share/ppermute | solution.py:396
  11.4 4.6 %collective-permute-start.1 = (bf16[352,128]{1,0:T(8,128)(2,1)S(1)}, bf16[352,128]{1,0:T(8,128)(2,1)S(1)}, u32[]{:S(2)}, u32[]{:S(2)}) collective-permute-start(bf16[352,128]{1,0:T(8,128)(2,1)S(1)} %get-tuple-element.68), channel_id=1, source_target_pairs={{0,2},{2,0},{4,6},{6,4},{8,10},{10,8},{12,14},{14,12},{16,18},{18,... | collective-permute-start | bytes 270344 | tf_op jit(solution)/shard_map/prior_share/ppermute | solution.py:396
  11.4 14.5 %collective-permute-start.4 = (bf16[256,1024]{1,0:T(8,128)(2,1)}, bf16[256,1024]{1,0:T(8,128)(2,1)S(1)}, u32[]{:S(2)}, u32[]{:S(2)}) collective-permute-start(bf16[256,1024]{1,0:T(8,128)(2,1)} %refs_0_), channel_id=1, source_target_pairs={{0,1},{1,0},{2,3},{3,2},{4,5},{5,4},{6,7},{7,6},{8,9},{9,8},{10,11... | collective-permute-start | bytes 1572872 | tf_op jit(solution)/shard_map/cotangent/ppermute | solution.py:396
  12.9 13.1 %copy-start = (bf16[1024,2048]{1,0:T(8,128)(2,1)S(1)}, bf16[1024,2048]{1,0:T(8,128)(2,1)}, u32[]{:S(2)}) copy-start(bf16[1024,2048]{1,0:T(8,128)(2,1)} %w_ref.3) | copy-start | bytes 12582916
  12.9 13.1 %copy-start.1 = (bf16[256,1024]{1,0:T(8,128)(2,1)S(1)}, bf16[256,1024]{1,0:T(8,128)(2,1)}, u32[]{:S(2)}) copy-start(bf16[256,1024]{1,0:T(8,128)(2,1)} %refs_0_) | copy-start | bytes 1572868
  16.7 11.1 %collective-permute-start.7 = (bf16[352,128]{1,0:T(8,128)(2,1)S(1)}, bf16[352,128]{1,0:T(8,128)(2,1)S(1)}, u32[]{:S(2)}, u32[]{:S(2)}) collective-permute-start(bf16[352,128]{1,0:T(8,128)(2,1)S(1)} %prior_share.1), channel_id=1, source_target_pairs={{0,24},{2,26},{4,28},{6,30},{8,16},{10,18},{12,20},{14,22},{16,8},... | collective-permute-start | bytes 270344 | tf_op jit(solution)/shard_map/prior_planes/ppermute | solution.py:396
  20.9 8.1 %collective-permute-start.6 = (bf16[352,128]{1,0:T(8,128)(2,1)S(1)}, bf16[352,128]{1,0:T(8,128)(2,1)S(1)}, u32[]{:S(2)}, u32[]{:S(2)}) collective-permute-start(bf16[352,128]{1,0:T(8,128)(2,1)S(1)} %prior_share.1), channel_id=1, source_target_pairs={{0,16},{2,18},{4,20},{6,22},{8,24},{10,26},{12,28},{14,30},{16,0},... | collective-permute-start | bytes 270344 | tf_op jit(solution)/shard_map/prior_planes/ppermute | solution.py:396
  20.9 8.1 %collective-permute-start.5 = (bf16[352,128]{1,0:T(8,128)(2,1)S(1)}, bf16[352,128]{1,0:T(8,128)(2,1)S(1)}, u32[]{:S(2)}, u32[]{:S(2)}) collective-permute-start(bf16[352,128]{1,0:T(8,128)(2,1)S(1)} %prior_share.1), channel_id=1, source_target_pairs={{0,8},{2,10},{4,12},{6,14},{8,0},{10,2},{12,4},{14,6},{16,24},{18,... | collective-permute-start | bytes 270344 | tf_op jit(solution)/shard_map/prior_planes/ppermute | solution.py:396
  30.8 4.8 %collective-permute-start.10 = (bf16[320,128]{1,0:T(8,128)(2,1)S(1)}, bf16[320,128]{1,0:T(8,128)(2,1)S(1)}, u32[]{:S(2)}, u32[]{:S(2)}) collective-permute-start(bf16[320,128]{1,0:T(8,128)(2,1)S(1)} %get-tuple-element.77), channel_id=1, source_target_pairs={{0,6},{2,4},{4,2},{6,0},{8,14},{10,12},{12,10},{14,8},{16,22},{18,... | collective-permute-start | bytes 245768 | tf_op jit(solution)/shard_map/later_share/ppermute | solution.py:396
  30.9 6.0 %collective-permute-start.9 = (bf16[320,128]{1,0:T(8,128)(2,1)S(1)}, bf16[320,128]{1,0:T(8,128)(2,1)S(1)}, u32[]{:S(2)}, u32[]{:S(2)}) collective-permute-start(bf16[320,128]{1,0:T(8,128)(2,1)S(1)} %get-tuple-element.78), channel_id=1, source_target_pairs={{0,4},{2,6},{4,0},{6,2},{8,12},{10,14},{12,8},{14,10},{16,20},{18,... | collective-permute-start | bytes 245768 | tf_op jit(solution)/shard_map/later_share/ppermute | solution.py:396
  32.1 4.8 %collective-permute-start.8 = (bf16[320,128]{1,0:T(8,128)(2,1)S(1)}, bf16[320,128]{1,0:T(8,128)(2,1)S(1)}, u32[]{:S(2)}, u32[]{:S(2)}) collective-permute-start(bf16[320,128]{1,0:T(8,128)(2,1)S(1)} %get-tuple-element.79), channel_id=1, source_target_pairs={{0,2},{2,0},{4,6},{6,4},{8,10},{10,8},{12,14},{14,12},{16,18},{18,... | collective-permute-start | bytes 245768 | tf_op jit(solution)/shard_map/later_share/ppermute | solution.py:396
  32.8 7.2 %collective-permute-start.14 = (bf16[320,128]{1,0:T(8,128)(2,1)S(1)}, bf16[320,128]{1,0:T(8,128)(2,1)S(1)}, u32[]{:S(2)}, u32[]{:S(2)}) collective-permute-start(bf16[320,128]{1,0:T(8,128)(2,1)S(1)} %get-tuple-element.74), channel_id=1, source_target_pairs={{0,6},{2,4},{4,2},{6,0},{8,14},{10,12},{12,10},{14,8},{16,22},{18,... | collective-permute-start | bytes 245768 | tf_op jit(solution)/shard_map/scaled_grad/ppermute | solution.py:396
  33.2 8.7 %collective-permute-start.13 = (bf16[320,128]{1,0:T(8,128)(2,1)S(1)}, bf16[320,128]{1,0:T(8,128)(2,1)S(1)}, u32[]{:S(2)}, u32[]{:S(2)}) collective-permute-start(bf16[320,128]{1,0:T(8,128)(2,1)S(1)} %get-tuple-element.75), channel_id=1, source_target_pairs={{0,4},{2,6},{4,0},{6,2},{8,12},{10,14},{12,8},{14,10},{16,20},{18,... | collective-permute-start | bytes 245768 | tf_op jit(solution)/shard_map/scaled_grad/ppermute | solution.py:396
  35.6 6.3 %collective-permute-start.12 = (bf16[320,128]{1,0:T(8,128)(2,1)S(1)}, bf16[320,128]{1,0:T(8,128)(2,1)S(1)}, u32[]{:S(2)}, u32[]{:S(2)}) collective-permute-start(bf16[320,128]{1,0:T(8,128)(2,1)S(1)} %get-tuple-element.76), channel_id=1, source_target_pairs={{0,2},{2,0},{4,6},{6,4},{8,10},{10,8},{12,14},{14,12},{16,18},{18,... | collective-permute-start | bytes 245768 | tf_op jit(solution)/shard_map/scaled_grad/ppermute | solution.py:396
  37.5 9.9 %collective-permute-start.16 = (bf16[320,128]{1,0:T(8,128)(2,1)S(1)}, bf16[320,128]{1,0:T(8,128)(2,1)S(1)}, u32[]{:S(2)}, u32[]{:S(2)}) collective-permute-start(bf16[320,128]{1,0:T(8,128)(2,1)S(1)} %later_planes.1), channel_id=1, source_target_pairs={{0,24},{2,26},{4,28},{6,30},{8,16},{10,18},{12,20},{14,22},{16,8},... | collective-permute-start | bytes 245768 | tf_op jit(solution)/shard_map/later_planes/ppermute | solution.py:396
  40.0 7.7 %collective-permute-start.15 = (bf16[320,128]{1,0:T(8,128)(2,1)S(1)}, bf16[320,128]{1,0:T(8,128)(2,1)S(1)}, u32[]{:S(2)}, u32[]{:S(2)}) collective-permute-start(bf16[320,128]{1,0:T(8,128)(2,1)S(1)} %later_planes.1), channel_id=1, source_target_pairs={{0,16},{2,18},{4,20},{6,22},{8,24},{10,26},{12,28},{14,30},{16,0},... | collective-permute-start | bytes 245768 | tf_op jit(solution)/shard_map/later_planes/ppermute | solution.py:396
  40.0 7.4 %collective-permute-start.11 = (bf16[320,128]{1,0:T(8,128)(2,1)S(1)}, bf16[320,128]{1,0:T(8,128)(2,1)S(1)}, u32[]{:S(2)}, u32[]{:S(2)}) collective-permute-start(bf16[320,128]{1,0:T(8,128)(2,1)S(1)} %later_planes.1), channel_id=1, source_target_pairs={{0,8},{2,10},{4,12},{6,14},{8,0},{10,2},{12,4},{14,6},{16,24},{18,... | collective-permute-start | bytes 245768 | tf_op jit(solution)/shard_map/later_planes/ppermute | solution.py:396
  43.5 13.4 %collective-permute-start.20 = (bf16[256,1024]{1,0:T(8,128)(2,1)S(1)}, bf16[256,1024]{1,0:T(8,128)(2,1)S(1)}, u32[]{:S(2)}, u32[]{:S(2)}) collective-permute-start(bf16[256,1024]{1,0:T(8,128)(2,1)S(1)} %get-tuple-element.63), channel_id=1, source_target_pairs={{0,1},{1,0},{2,3},{3,2},{4,5},{5,4},{6,7},{7,6},{8,9},{9,8},{10,11... | collective-permute-start | bytes 1572872 | tf_op jit(solution)/shard_map/attended/ppermute | solution.py:396
  48.4 4.5 %collective-permute-start.19 = (bf16[320,128]{1,0:T(8,128)(2,1)S(1)}, bf16[320,128]{1,0:T(8,128)(2,1)S(1)}, u32[]{:S(2)}, u32[]{:S(2)}) collective-permute-start(bf16[320,128]{1,0:T(8,128)(2,1)S(1)} %get-tuple-element.70), channel_id=1, source_target_pairs={{0,6},{2,4},{4,2},{6,0},{8,14},{10,12},{12,10},{14,8},{16,22},{18,... | collective-permute-start | bytes 245768 | tf_op jit(solution)/shard_map/later_back/ppermute | solution.py:396
  49.0 6.0 %collective-permute-start.18 = (bf16[320,128]{1,0:T(8,128)(2,1)S(1)}, bf16[320,128]{1,0:T(8,128)(2,1)S(1)}, u32[]{:S(2)}, u32[]{:S(2)}) collective-permute-start(bf16[320,128]{1,0:T(8,128)(2,1)S(1)} %get-tuple-element.71), channel_id=1, source_target_pairs={{0,4},{2,6},{4,0},{6,2},{8,12},{10,14},{12,8},{14,10},{16,20},{18,... | collective-permute-start | bytes 245768 | tf_op jit(solution)/shard_map/later_back/ppermute | solution.py:396
  50.3 4.8 %collective-permute-start.17 = (bf16[320,128]{1,0:T(8,128)(2,1)S(1)}, bf16[320,128]{1,0:T(8,128)(2,1)S(1)}, u32[]{:S(2)}, u32[]{:S(2)}) collective-permute-start(bf16[320,128]{1,0:T(8,128)(2,1)S(1)} %get-tuple-element.72), channel_id=1, source_target_pairs={{0,2},{2,0},{4,6},{6,4},{8,10},{10,8},{12,14},{14,12},{16,18},{18,... | collective-permute-start | bytes 245768 | tf_op jit(solution)/shard_map/later_back/ppermute | solution.py:396

commit v5 on v4

--- a/solution.py
+++ b/solution.py
@@ -25,7 +25,7 @@
     return lax.dot_general(a, b, dims, preferred_element_type=F32)
 
 
-def call(body, scalars, operands, out_shape, flops, far=(), scratch=()):
+def call(body, operands, out_shape, flops, far=(), scratch=()):
     moved = sum(x.size * x.dtype.itemsize for x in operands)
     moved += sum(x.size * x.dtype.itemsize for x in out_shape)
     vmem = pl.BlockSpec(memory_space=pltpu.VMEM)
@@ -33,13 +33,12 @@
     return pl.pallas_call(
         body,
         out_shape=out_shape,
-        in_specs=[pl.BlockSpec(memory_space=pltpu.SMEM)]
-        + [hbm if i in far else vmem for i in range(len(operands))],
+        in_specs=[hbm if i in far else vmem for i in range(len(operands))],
         out_specs=[vmem for _ in out_shape],
         scratch_shapes=list(scratch),
         compiler_params=pltpu.CompilerParams(vmem_limit_bytes=VMEM_LIMIT),
         cost_estimate=pl.CostEstimate(flops=flops, bytes_accessed=moved, transcendentals=0),
-    )(scalars, *[in_hbm(x) if i in far else x for i, x in enumerate(operands)])
+    )(*[in_hbm(x) if i in far else x for i, x in enumerate(operands)])
 
 
 def in_hbm(x):
@@ -104,7 +103,6 @@
 
 
 def query_kernel(
-    s_ref,
     q_far,
     k_far,
     v_far,
@@ -127,22 +125,22 @@
         copy.wait()
 
 
-def columns_of(s_ref, w_ref, distance):
+def columns_of(w_ref, distance):
     columns = w_ref.shape[1] // lax.axis_size("head")
-    return pl.ds(pl.multiple_of((s_ref[1] ^ distance) * columns, columns), columns)
-
-
-def turn_kernel(s_ref, qd_ref, kf_ref, qt_ref, kt_ref):
+    return pl.ds(pl.multiple_of((lax.axis_index("head") ^ distance) * columns, columns), columns)
+
+
+def turn_kernel(qd_ref, kf_ref, qt_ref, kt_ref):
     for head in range(qd_ref.shape[0]):
         qt_ref[head] = qd_ref[head].T
         kt_ref[head] = kf_ref[head].T
 
 
-def grad_kernel(s_ref, *refs):
+def grad_kernel(*refs):
     *cots, w_ref, og_ref = refs
     total = None
     for j, cot_ref in enumerate(cots):
-        term = mm(cot_ref[...], w_ref[:, columns_of(s_ref, w_ref, j)], NT)
+        term = mm(cot_ref[...], w_ref[:, columns_of(w_ref, j)], NT)
         total = term if total is None else total + term
     og_ref[...] = total
 
@@ -181,7 +179,6 @@
 
 
 def key_kernel(
-    s_ref,
     k_ref,
     v_ref,
     before_ref,
@@ -193,7 +190,7 @@
     send_ref,
     slots,
 ):
-    rank = s_ref[0]
+    rank = lax.rem(lax.axis_index("ctx"), PLANE)
     heads = kf_ref.shape[0]
     per_piece = heads // PLANE
     width = k_ref.shape[1]
@@ -222,7 +219,7 @@
         send_ref[slot, at:, :] = lines.astype(BF16)
 
 
-def share_kernel(norm_at, s_ref, own_ref, *refs):
+def share_kernel(norm_at, own_ref, *refs):
     sent_at = -1 if refs[-1].dtype == BF16 else -2
     got_refs, sent_ref = refs[:sent_at], refs[sent_at]
     total = own_ref[...]
@@ -236,7 +233,7 @@
         refs[-1][...] = total
 
 
-def store_pieces(sign, strides, s_ref, got_refs, moved_refs, pieces_ref):
+def store_pieces(sign, strides, got_refs, moved_refs, pieces_ref):
     rows = pieces_ref.shape[1]
 
     def masked(ahead, ref):
@@ -248,11 +245,11 @@
     before = jnp.zeros(got_refs[0].shape, F32)
     for ref, (stride, distance) in zip(moved_refs, strides):
         if distance:
-            group = lax.div(s_ref[2], stride)
+            group = lax.div(lax.axis_index("ctx"), PLANE * stride)
             before = before + masked(is_ahead(group ^ distance, group), ref)
         else:
             before = before + ref[...].astype(F32)
-    rank = s_ref[0]
+    rank = lax.rem(lax.axis_index("ctx"), PLANE)
     extra = None
     for slot in range(PLANE):
         total = before
@@ -264,11 +261,11 @@
     return extra
 
 
-def piece_kernel(sign, strides, s_ref, *refs):
-    store_pieces(sign, strides, s_ref, refs[:PLANE], refs[PLANE:-1], refs[-1])
-
-
-def score_kernel(s_ref, qd_ref, kf_ref, vc_ref, low_ref, den_ref, num_ref):
+def piece_kernel(sign, strides, *refs):
+    store_pieces(sign, strides, refs[:PLANE], refs[PLANE:-1], refs[-1])
+
+
+def score_kernel(qd_ref, kf_ref, vc_ref, low_ref, den_ref, num_ref):
     heads = kf_ref.shape[0]
     tokens = kf_ref.shape[2]
     key_at = lax.broadcasted_iota(jnp.int32, (tokens, tokens), 0)
@@ -283,12 +280,12 @@
         num_ref[:, at : at + VDIM] = mm(low, vc_ref[:, at : at + VDIM], TN)
 
 
-def scale_kernel(strides, s_ref, den_ref, qd_ref, og_ref, *refs):
+def scale_kernel(strides, den_ref, qd_ref, og_ref, *refs):
     *refs, pieces_ref, inv_ref, sg_ref, own_ref, send_ref, slots = refs
-    rank = s_ref[0]
+    rank = lax.rem(lax.axis_index("ctx"), PLANE)
     heads = qd_ref.shape[0]
     per_piece = heads // PLANE
-    lines = store_pieces(1, strides, s_ref, refs[:PLANE], refs[PLANE:], pieces_ref)
+    lines = store_pieces(1, strides, refs[:PLANE], refs[PLANE:], pieces_ref)
     norm = norm_values(lines)
     high = norm.astype(BF16).astype(F32)
     middle = (norm - high).astype(BF16).astype(F32)
@@ -310,14 +307,14 @@
     own_ref[...] = slots[0]
 
 
-def near_kernel(s_ref, low_ref, sg_ref, vg_ref):
+def near_kernel(low_ref, sg_ref, vg_ref):
     for head in range(low_ref.shape[0]):
         at = head * VDIM
         vg_ref[:, at : at + VDIM] = mm(low_ref[head], sg_ref[:, at : at + VDIM], NN)
 
 
-def attend_kernel(s_ref, qt_ref, prior_ref, num_ref, inv_ref, w_ref, att_ref, part_ref):
-    rank = s_ref[0]
+def attend_kernel(qt_ref, prior_ref, num_ref, inv_ref, w_ref, att_ref, part_ref):
+    rank = lax.rem(lax.axis_index("ctx"), PLANE)
     heads = qt_ref.shape[0]
     per_piece = heads // PLANE
     for head in range(heads):
@@ -325,17 +322,17 @@
         prior = load_piece(rank, head, per_piece, prior_ref)
         total = num_ref[:, at : at + VDIM] + mm(qt_ref[head], prior, NN)
         att_ref[:, at : at + VDIM] = (total * inv_ref[:, head : head + 1]).astype(BF16)
-    part_ref[...] = mm(att_ref[...], w_ref[:, columns_of(s_ref, w_ref, 1)], NN).astype(BF16)
-
-
-def mix_kernel(distance, s_ref, att_ref, w_ref, part_ref):
-    weight = w_ref[:, columns_of(s_ref, w_ref, distance)]
+    part_ref[...] = mm(att_ref[...], w_ref[:, columns_of(w_ref, 1)], NN).astype(BF16)
+
+
+def mix_kernel(distance, att_ref, w_ref, part_ref):
+    weight = w_ref[:, columns_of(w_ref, distance)]
     part_ref[...] = mm(att_ref[...], weight, NN).astype(part_ref.dtype)
 
 
-def last_kernel(s_ref, kt_ref, later_ref, near_ref, part_ref, *refs):
+def last_kernel(kt_ref, later_ref, near_ref, part_ref, *refs):
     *other_refs, vg_far, mixed_far, vg_ref, mixed_ref, sems = refs
-    rank = s_ref[0]
+    rank = lax.rem(lax.axis_index("ctx"), PLANE)
     heads = kt_ref.shape[0]
     per_piece = heads // PLANE
     copies = []
@@ -407,9 +404,6 @@
     width = heads * VDIM
     columns = cotangent.shape[1]
     groups = lax.axis_size("head")
-    rank = lax.axis_index("ctx") % PLANE
-    places = [rank, lax.axis_index("head"), lax.axis_index("ctx") // PLANE]
-    scalars = jnp.stack(places).astype(jnp.int32)
     piece_rows = heads // PLANE * ROWS
     message = (piece_rows + 4 * heads, VDIM)
     S = jax.ShapeDtypeStruct
@@ -433,7 +427,6 @@
         arrays = (keys, values, conv_keys, conv_values)
         qd, *near_by = call(
             query_kernel,
-            scalars,
             (after(queries, last_rows), *arrays),
             [S((heads, ROWS, tokens), BF16)] + [S(x.shape, x.dtype) for x in arrays],
             1 << 20,
@@ -448,7 +441,7 @@
             S((PLANE, *message), BF16),
         ]
         ops = (*near_by[:2], before, *near_by[2:])
-        kf, vc, own, send = call(key_kernel, scalars, ops, outs, step, scratch=[slots])
+        kf, vc, own, send = call(key_kernel, ops, outs, step, scratch=[slots])
     with jax.named_scope("cotangent"):
         cots = [swapped(after(cotangent, send), "head", j) for j in range(1, groups)]
     with jax.named_scope("prior_share"):
@@ -457,7 +450,7 @@
         def join(norm_at, total, received, more):
             outs = [S(total.shape, BF16), S(total.shape, F32)]
             body = functools.partial(share_kernel, norm_at)
-            made = call(body, scalars, (total, *received), outs[: 2 if more else 1], 1 << 20)
+            made = call(body, (total, *received), outs[: 2 if more else 1], 1 << 20)
             return made if more else (made[0], None)
 
         more = lax.axis_size("ctx") > 4 * PLANE
@@ -468,18 +461,18 @@
             S((heads, tokens), F32),
             S((tokens, width), F32),
         ]
-        low, den, num = call(score_kernel, scalars, (qd, kf, vc), outs, 400 * step)
+        low, den, num = call(score_kernel, (qd, kf, vc), outs, 400 * step)
     with jax.named_scope("prior_planes"):
         sent = after(sent, den)
         norm_join = functools.partial(join, piece_rows)
         moved, strides = planes_ahead(total, sent, 1, norm_join)
     with jax.named_scope("turned"):
         outs = [S((heads, tokens, ROWS), BF16)] * 2
-        qt, kt = call(turn_kernel, scalars, (after(qd, sent), kf), outs, 1 << 22)
+        qt, kt = call(turn_kernel, (after(qd, sent), kf), outs, 1 << 22)
     with jax.named_scope("out_grad"):
         ops = (after(cotangent, qt), *cots, out_weight)
         (out_grad,) = call(
-            grad_kernel, scalars, ops, [S((tokens, width), F32)], groups * project_flops
+            grad_kernel, ops, [S((tokens, width), F32)], groups * project_flops
         )
     with jax.named_scope("scaled_grad"):
         outs = [
@@ -492,7 +485,7 @@
         ops = (den, qd, out_grad, own, *got, *moved)
         body = functools.partial(scale_kernel, strides)
         pieces, inverse, scaled, own_later, send_later = call(
-            body, scalars, ops, outs, step, scratch=[slots]
+            body, ops, outs, step, scratch=[slots]
         )
         prior = handed_back(pieces)
     with jax.named_scope("later_share"):
@@ -504,32 +497,31 @@
     with jax.named_scope("attended"):
         outs = [S((tokens, width), BF16), S((tokens, columns), BF16)]
         ops = (qt, prior, after(num, sent_later), inverse, out_weight)
-        attended, part = call(attend_kernel, scalars, ops, outs, step + project_flops)
+        attended, part = call(attend_kernel, ops, outs, step + project_flops)
         parts = [swapped(part, "head", 1)]
     with jax.named_scope("near"):
         ops = (low, after(scaled, sent_later))
-        (near,) = call(near_kernel, scalars, ops, [S((tokens, width), F32)], 2 * step)
+        (near,) = call(near_kernel, ops, [S((tokens, width), F32)], 2 * step)
     with jax.named_scope("mixed"):
         for j in list(range(2, groups)) + [0]:
             outs = [S((tokens, columns), BF16 if j else F32)]
             body = functools.partial(mix_kernel, j)
             ops = (after(attended, sent_later), out_weight)
-            (part,) = call(body, scalars, ops, outs, 2 * project_flops)
+            (part,) = call(body, ops, outs, 2 * project_flops)
             if j:
                 parts.append(swapped(part, "head", j))
     with jax.named_scope("later_back"):
         outs = [S((PLANE, piece_rows, VDIM), BF16)]
         body = functools.partial(piece_kernel, -1, strides)
         ops = (own_later, *got_later, after(moved_later[0], part, near), *moved_later[1:])
-        (pieces,) = call(body, scalars, ops, outs, 1 << 20)
+        (pieces,) = call(body, ops, outs, 1 << 20)
         later = handed_back(pieces)
     with jax.named_scope("last"):
         whole = (tokens, columns)
         value_grad, mixed_out = pl.pallas_call(
             last_kernel,
             out_shape=[S((tokens, width), BF16), S(whole, BF16)],
-            in_specs=[pl.BlockSpec(memory_space=pltpu.SMEM)]
-            + [pl.BlockSpec(memory_space=vmem)] * (4 + len(parts)),
+            in_specs=[pl.BlockSpec(memory_space=vmem)] * (4 + len(parts)),
             out_specs=[pl.BlockSpec(memory_space=pltpu.HBM)] * 2,
             scratch_shapes=[
                 vmem((tokens, width), BF16),
@@ -537,7 +529,7 @@
                 dma((2 * PLANE,)),
             ],
             compiler_params=pltpu.CompilerParams(vmem_limit_bytes=VMEM_LIMIT),
-        )(scalars, kt, later, near, part, *parts)
+        )(kt, later, near, part, *parts)
     return mixed_out, value_grad
 
 

time: 59 us -> 55.5 us (0.941)
  Pallas kernels: 18.1 us -> 11.1 us
  waiting for transfers between devices: 15 us -> 18.4 us
    pallas_call x12, Pallas kernels: 15.5 us -> 8.98 us  [call(): pl.pallas_call(body, out_shape=out_shape, in_specs=[hbm if i in far else...]
    ppermute x20, waiting for transfers between devices: 15 us -> 18.4 us  [swapped(): return lax.ppermute(x, axis, pairs)]
  transfers between devices with their start and end apart: 21 -> 21, of which waited for: 9 -> 10; matrix products, arithmetic and copies ran while one was open for 0% -> 0% of each run, Pallas kernels for 21% -> 12%
where the time goes in v5:
time: 55.5 us; the launch traced here: 55.3 us
  starting transfers between devices  24.8 us (45%)
  waiting for transfers between devices  18.4 us (33%)
  Pallas kernels  11.1 us (20%)
  between operations  0.8 us (1%)
    ppermute x20, starting transfers between devices, swapped(): return lax.ppermute(x, axis, pairs)  22.4 us
    ppermute x20, waiting for transfers between devices, swapped(): return lax.ppermute(x, axis, pairs)  18.4 us
    pallas_call x12, Pallas kernels, call(): pl.pallas_call(body, out_shape=out_shape, in_specs=[hbm if i in far else...  8.98 us
    ppermute x1, starting transfers between devices, shifted(): return lax.ppermute(x, axis, pairs)  2.36 us
    pallas_call x1, Pallas kernels, per_device(): pl.pallas_call(last_kernel, out_shape=[S((tokens, width), BF16), S(whole,...  1.34 us
  transfers between devices with their start and end apart: 21, of which 10 were waited for; matrix products, arithmetic and copies ran while one was open for 0% of the time, Pallas kernels for 12%

profile of v5, /device:TPU:0, one launch (start us, length us, event | category | flops | bytes accessed | tf_op | source)
XLA Modules:
  0.0 55.3 jit_solution(14455020109688602556)
XLA Ops:
  0.6 0.8 %edge.1 = bf16[2,1152]{1,0:T(2,128)(2,1)S(1)} custom-call(bf16[256,128]{1,0:T(8,128)(2,1)} %k_far.3, bf16[256,1024]{1,0:T(8,128)(2,1)} %v_far.3), custom_call_target="tpu_custom_call" | custom-call | tf_op jit(solution)/shard_map/edge/pallas_call | solution.py:417
  1.4 2.4 %collective-permute-start = (bf16[2,1152]{1,0:T(2,128)(2,1)S(1)}, bf16[2,1152]{1,0:T(2,128)(2,1)S(1)}, u32[]{:S(2)}, u32[]{:S(2)}) collective-permute-start(bf16[2,1152]{1,0:T(2,128)(2,1)S(1)} %edge.1), channel_id=1, source_target_pairs={{0,2},{2,4},{4,6},{6,8},{8,10},{10,12},{12,14},{14,16},{16,18},{18... | collective-permute-start | bytes 13832 | tf_op jit(solution)/shard_map/edge/ppermute | solution.py:364
  3.8 1.2 %query_features.1 = (bf16[8,160,256]{2,1,0:T(8,128)(2,1)S(1)}, bf16[256,128]{1,0:T(8,128)(2,1)S(1)}, bf16[256,1024]{1,0:T(8,128)(2,1)S(1)}, f32[3,128]{1,0:T(4,128)S(1)}, f32[3,1024]{1,0:T(4,128)S(1)}) custom-call(bf16[256,128]{1,0:T(8,128)(2,1)} %q_far, bf16[256,128]{1,0:T(8,128)(2,1)} %k_far.3, bf16[256,1024]{1,0:T(8,128)(2,1)} %v_far.3, f32[3,128]{1,0:T(4,128)} %ck_far.1, ...), custom_call_target="tpu_custom_call" | custom-call | flops 1048576 | bytes 1928192 | tf_op jit(solution)/shard_map/query_features/pallas_call | solution.py:33
  5.0 0.0 collective-permute-done.before_ref
  5.0 0.9 %key_features.1 = (bf16[8,160,256]{2,1,0:T(8,128)(2,1)S(1)}, bf16[256,1024]{1,0:T(8,128)(2,1)S(1)}, f32[352,128]{1,0:T(8,128)S(1)}, bf16[4,352,128]{2,1,0:T(8,128)(2,1)S(1)}) custom-call(bf16[256,128]{1,0:T(8,128)(2,1)S(1)} %get-tuple-element.36.k_ref, bf16[256,1024]{1,0:T(8,128)(2,1)S(1)} %get-tuple-element.37.v_ref, ...), custom_call_target="tpu_custom_call" | custom-call | flops 83886080 | bytes 2328576 | tf_op jit(solution)/shard_map/key_features/pallas_call | solution.py:33
  5.9 3.8 %collective-permute-start.3 = (bf16[352,128]{1,0:T(8,128)(2,1)S(1)}, bf16[352,128]{1,0:T(8,128)(2,1)S(1)}, u32[]{:S(2)}, u32[]{:S(2)}) collective-permute-start(bf16[352,128]{1,0:T(8,128)(2,1)S(1)} %get-tuple-element.66), channel_id=1, source_target_pairs={{0,6},{2,4},{4,2},{6,0},{8,14},{10,12},{12,10},{14,8},{16,22},{18,... | collective-permute-start | bytes 270344 | tf_op jit(solution)/shard_map/prior_share/ppermute | solution.py:393
  9.8 0.7 %collective-permute-start.2 = (bf16[352,128]{1,0:T(8,128)(2,1)S(1)}, bf16[352,128]{1,0:T(8,128)(2,1)S(1)}, u32[]{:S(2)}, u32[]{:S(2)}) collective-permute-start(bf16[352,128]{1,0:T(8,128)(2,1)S(1)} %get-tuple-element.67), channel_id=1, source_target_pairs={{0,4},{2,6},{4,0},{6,2},{8,12},{10,14},{12,8},{14,10},{16,20},{18,... | collective-permute-start | bytes 270344 | tf_op jit(solution)/shard_map/prior_share/ppermute | solution.py:393
  10.4 0.0 collective-permute-start.1
  10.5 1.5 %collective-permute-start.4 = (bf16[256,1024]{1,0:T(8,128)(2,1)}, bf16[256,1024]{1,0:T(8,128)(2,1)S(1)}, u32[]{:S(2)}, u32[]{:S(2)}) collective-permute-start(bf16[256,1024]{1,0:T(8,128)(2,1)} %refs_0_), channel_id=1, source_target_pairs={{0,1},{1,0},{2,3},{3,2},{4,5},{5,4},{6,7},{7,6},{8,9},{9,8},{10,11... | collective-permute-start | bytes 1572872 | tf_op jit(solution)/shard_map/cotangent/ppermute | solution.py:393
  12.0 0.0 copy-start
  12.0 0.0 copy-start.1
  12.0 1.2 %scores.1 = (bf16[8,256,256]{2,1,0:T(8,128)(2,1)S(1)}, f32[8,256]{1,0:T(8,128)S(1)}, f32[256,1024]{1,0:T(8,128)S(1)}) custom-call(bf16[8,160,256]{2,1,0:T(8,128)(2,1)S(1)} %get-tuple-element.46.qd_ref, bf16[8,160,256]{2,1,0:T(8,128)(2,1)S(1)} %get-tuple-element.42.kf_ref, bf16[256,1024]{1,0:T(8,128)(2,1)S(1)} %get-tuple-element.43.vc_ref), custom_call_target="tpu_custom_call" | custom-call | flops 33554432000 | bytes 3940352 | tf_op jit(solution)/shard_map/scores/pallas_call | solution.py:33
  13.2 0.0 collective-permute-done.3.refs_2_.refs_3_
  13.2 1.8 %collective-permute-done.2.refs_1_.refs_2_ = bf16[352,128]{1,0:T(8,128)(2,1)S(1)} collective-permute-done((bf16[352,128]{1,0:T(8,128)(2,1)S(1)}, bf16[352,128]{1,0:T(8,128)(2,1)S(1)}, u32[]{:S(2)}, u32[]{:S(2)}) %collective-permute-start.2) | collective-permute-done | bytes 90144 | tf_op jit(solution)/shard_map/prior_share/ppermute | solution.py:393
  15.0 0.0 collective-permute-done.1.refs_0_.refs_1_
  15.0 0.2 prior_share.1
  15.1 3.9 %collective-permute-start.7 = (bf16[352,128]{1,0:T(8,128)(2,1)S(1)}, bf16[352,128]{1,0:T(8,128)(2,1)S(1)}, u32[]{:S(2)}, u32[]{:S(2)}) collective-permute-start(bf16[352,128]{1,0:T(8,128)(2,1)S(1)} %prior_share.1), channel_id=1, source_target_pairs={{0,24},{2,26},{4,28},{6,30},{8,16},{10,18},{12,20},{14,22},{16,8},... | collective-permute-start | bytes 270344 | tf_op jit(solution)/shard_map/prior_planes/ppermute | solution.py:393
  19.0 0.0 collective-permute-start.6
  19.0 0.6 %collective-permute-start.5 = (bf16[352,128]{1,0:T(8,128)(2,1)S(1)}, bf16[352,128]{1,0:T(8,128)(2,1)S(1)}, u32[]{:S(2)}, u32[]{:S(2)}) collective-permute-start(bf16[352,128]{1,0:T(8,128)(2,1)S(1)} %prior_share.1), channel_id=1, source_target_pairs={{0,8},{2,10},{4,12},{6,14},{8,0},{10,2},{12,4},{14,6},{16,24},{18,... | collective-permute-start | bytes 270344 | tf_op jit(solution)/shard_map/prior_planes/ppermute | solution.py:393
  19.7 0.6 %turned.1 = (bf16[8,256,160]{2,1,0:T(8,128)(2,1)S(1)}, bf16[8,256,160]{2,1,0:T(8,128)(2,1)S(1)}) custom-call(bf16[8,160,256]{2,1,0:T(8,128)(2,1)S(1)} %get-tuple-element.46.qd_ref, bf16[8,160,256]{2,1,0:T(8,128)(2,1)S(1)} %get-tuple-element.42.kf_ref), custom_call_target="tpu_custom_call" | custom-call | flops 4194304 | bytes 2621440 | tf_op jit(solution)/shard_map/turned/pallas_call | solution.py:33
  20.3 4.7 %collective-permute-done.4.refs_1_ = bf16[256,1024]{1,0:T(8,128)(2,1)S(1)} collective-permute-done((bf16[256,1024]{1,0:T(8,128)(2,1)}, bf16[256,1024]{1,0:T(8,128)(2,1)S(1)}, u32[]{:S(2)}, u32[]{:S(2)}) %collective-permute-start.4) | collective-permute-done | bytes 524320 | tf_op jit(solution)/shard_map/cotangent/ppermute | solution.py:393
  25.0 0.0 copy-done
  25.0 0.0 copy-done.1
  25.0 1.3 %out_grad.1.og_ref = f32[256,1024]{1,0:T(8,128)S(1)} custom-call(bf16[256,1024]{1,0:T(8,128)(2,1)S(1)} %copy-done.1, bf16[256,1024]{1,0:T(8,128)(2,1)S(1)} %collective-permute-done.4.refs_1_, bf16[1024,2048]{1,0:T(8,128)(2,1)S(1)} %copy-done), custom_call_target="tpu_custom_call" | custom-call | flops 1073741824 | bytes 6291456 | tf_op jit(solution)/shard_map/out_grad/pallas_call | solution.py:33
  26.3 0.0 collective-permute-done.7.refs_6_
  26.3 1.1 %collective-permute-done.6.refs_5_ = bf16[352,128]{1,0:T(8,128)(2,1)S(1)} collective-permute-done((bf16[352,128]{1,0:T(8,128)(2,1)S(1)}, bf16[352,128]{1,0:T(8,128)(2,1)S(1)}, u32[]{:S(2)}, u32[]{:S(2)}) %collective-permute-start.6) | collective-permute-done | bytes 90144 | tf_op jit(solution)/shard_map/prior_planes/ppermute | solution.py:393
  27.4 0.0 collective-permute-done.5.refs_4_
  27.4 1.2 %scaled_grad.1 = (bf16[4,320,128]{2,1,0:T(8,128)(2,1)S(1)}, f32[256,8]{1,0:T(8,128)S(1)}, bf16[256,1024]{1,0:T(8,128)(2,1)S(1)}, f32[320,128]{1,0:T(8,128)S(1)}, bf16[4,320,128]{2,1,0:T(8,128)(2,1)S(1)}) custom-call(f32[8,256]{1,0:T(8,128)S(1)} %get-tuple-element.44.den_ref, bf16[8,160,256]{2,1,0:T(8,128)(2,1)S(1)} %get-tuple-element.46.qd_ref, ...), custom_call_target="tpu_custom_call" | custom-call | flops 83886080 | bytes 3784704 | tf_op jit(solution)/shard_map/scaled_grad/pallas_call | solution.py:33
  28.7 0.4 collective-permute-start.10
  29.1 1.2 %collective-permute-start.9 = (bf16[320,128]{1,0:T(8,128)(2,1)S(1)}, bf16[320,128]{1,0:T(8,128)(2,1)S(1)}, u32[]{:S(2)}, u32[]{:S(2)}) collective-permute-start(bf16[320,128]{1,0:T(8,128)(2,1)S(1)} %get-tuple-element.78), channel_id=1, source_target_pairs={{0,4},{2,6},{4,0},{6,2},{8,12},{10,14},{12,8},{14,10},{16,20},{18,... | collective-permute-start | bytes 245768 | tf_op jit(solution)/shard_map/later_share/ppermute | solution.py:393
  30.2 0.3 collective-permute-start.8
  30.6 1.1 %collective-permute-start.14 = (bf16[320,128]{1,0:T(8,128)(2,1)S(1)}, bf16[320,128]{1,0:T(8,128)(2,1)S(1)}, u32[]{:S(2)}, u32[]{:S(2)}) collective-permute-start(bf16[320,128]{1,0:T(8,128)(2,1)S(1)} %get-tuple-element.74), channel_id=1, source_target_pairs={{0,6},{2,4},{4,2},{6,0},{8,14},{10,12},{12,10},{14,8},{16,22},{18,... | collective-permute-start | bytes 245768 | tf_op jit(solution)/shard_map/scaled_grad/ppermute | solution.py:393
  31.7 0.8 %collective-permute-start.13 = (bf16[320,128]{1,0:T(8,128)(2,1)S(1)}, bf16[320,128]{1,0:T(8,128)(2,1)S(1)}, u32[]{:S(2)}, u32[]{:S(2)}) collective-permute-start(bf16[320,128]{1,0:T(8,128)(2,1)S(1)} %get-tuple-element.75), channel_id=1, source_target_pairs={{0,4},{2,6},{4,0},{6,2},{8,12},{10,14},{12,8},{14,10},{16,20},{18,... | collective-permute-start | bytes 245768 | tf_op jit(solution)/shard_map/scaled_grad/ppermute | solution.py:393
  32.5 1.0 %collective-permute-done.10.refs_2_.refs_3_ = bf16[320,128]{1,0:T(8,128)(2,1)S(1)} collective-permute-done((bf16[320,128]{1,0:T(8,128)(2,1)S(1)}, bf16[320,128]{1,0:T(8,128)(2,1)S(1)}, u32[]{:S(2)}, u32[]{:S(2)}) %collective-permute-start.10) | collective-permute-done | bytes 81952 | tf_op jit(solution)/shard_map/later_share/ppermute | solution.py:393
  33.4 0.1 collective-permute-start.12
  33.6 1.7 %collective-permute-done.9.refs_1_.refs_2_ = bf16[320,128]{1,0:T(8,128)(2,1)S(1)} collective-permute-done((bf16[320,128]{1,0:T(8,128)(2,1)S(1)}, bf16[320,128]{1,0:T(8,128)(2,1)S(1)}, u32[]{:S(2)}, u32[]{:S(2)}) %collective-permute-start.9) | collective-permute-done | bytes 81952 | tf_op jit(solution)/shard_map/later_share/ppermute | solution.py:393
  35.3 0.0 collective-permute-done.8.refs_0_.refs_1_
  35.3 2.0 %collective-permute-start.16 = (bf16[320,128]{1,0:T(8,128)(2,1)S(1)}, bf16[320,128]{1,0:T(8,128)(2,1)S(1)}, u32[]{:S(2)}, u32[]{:S(2)}) collective-permute-start(bf16[320,128]{1,0:T(8,128)(2,1)S(1)} %later_planes.1), channel_id=1, source_target_pairs={{0,24},{2,26},{4,28},{6,30},{8,16},{10,18},{12,20},{14,22},{16,8},... | collective-permute-start | bytes 245768 | tf_op jit(solution)/shard_map/later_planes/ppermute | solution.py:393
  37.4 0.0 collective-permute-start.15
  37.4 0.0 collective-permute-done.14
  37.4 2.4 %collective-permute-start.11 = (bf16[320,128]{1,0:T(8,128)(2,1)S(1)}, bf16[320,128]{1,0:T(8,128)(2,1)S(1)}, u32[]{:S(2)}, u32[]{:S(2)}) collective-permute-start(bf16[320,128]{1,0:T(8,128)(2,1)S(1)} %later_planes.1), channel_id=1, source_target_pairs={{0,8},{2,10},{4,12},{6,14},{8,0},{10,2},{12,4},{14,6},{16,24},{18,... | collective-permute-start | bytes 245768 | tf_op jit(solution)/shard_map/later_planes/ppermute | solution.py:393
  39.8 0.0 collective-permute-done.13
  39.8 0.0 collective-permute-done.12
  39.8 1.0 %attended.1 = (bf16[256,1024]{1,0:T(8,128)(2,1)S(1)}, bf16[256,1024]{1,0:T(8,128)(2,1)S(1)}) custom-call(bf16[8,256,160]{2,1,0:T(8,128)(2,1)S(1)} %get-tuple-element.48.qt_ref, bf16[4,320,128]{2,1,0:T(8,128)(2,1)S(1)} %pad_maximum_fusion.prior_ref, f32[256,1024]{1,0:T(8,128)S(1)} %get-tuple-element.55.num_ref, f32[256,8]{1,0:T(8,128)S(1)} %get-tuple-element.56.inv_ref, ...), custom_call_target="tpu_custom_call" | custom-call | flops 620756992 | bytes 7282688 | tf_op jit(solution)/shard_map/attended/pallas_call | solution.py:33
  40.8 1.6 %collective-permute-start.20 = (bf16[256,1024]{1,0:T(8,128)(2,1)S(1)}, bf16[256,1024]{1,0:T(8,128)(2,1)S(1)}, u32[]{:S(2)}, u32[]{:S(2)}) collective-permute-start(bf16[256,1024]{1,0:T(8,128)(2,1)S(1)} %get-tuple-element.63), channel_id=1, source_target_pairs={{0,1},{1,0},{2,3},{3,2},{4,5},{5,4},{6,7},{7,6},{8,9},{9,8},{10,11... | collective-permute-start | bytes 1572872 | tf_op jit(solution)/shard_map/attended/ppermute | solution.py:393
  42.4 0.4 near.1.near_ref
  42.8 0.7 %mixed.1.part_ref = f32[256,1024]{1,0:T(8,128)S(1)} custom-call(bf16[256,1024]{1,0:T(8,128)(2,1)S(1)} %get-tuple-element.58.att_ref, bf16[1024,2048]{1,0:T(8,128)(2,1)S(1)} %copy-done), custom_call_target="tpu_custom_call" | custom-call | flops 1073741824 | bytes 5767168 | tf_op jit(solution)/shard_map/mixed/pallas_call | solution.py:33
  43.5 0.4 collective-permute-done.11.refs_4_
  44.0 0.0 collective-permute-done.16.refs_6_
  44.0 1.3 %collective-permute-done.15.refs_5_ = bf16[320,128]{1,0:T(8,128)(2,1)S(1)} collective-permute-done((bf16[320,128]{1,0:T(8,128)(2,1)S(1)}, bf16[320,128]{1,0:T(8,128)(2,1)S(1)}, u32[]{:S(2)}, u32[]{:S(2)}) %collective-permute-start.15) | collective-permute-done | bytes 81952 | tf_op jit(solution)/shard_map/later_planes/ppermute | solution.py:393
  45.3 0.2 later_back.1
  45.5 0.7 %collective-permute-start.19 = (bf16[320,128]{1,0:T(8,128)(2,1)S(1)}, bf16[320,128]{1,0:T(8,128)(2,1)S(1)}, u32[]{:S(2)}, u32[]{:S(2)}) collective-permute-start(bf16[320,128]{1,0:T(8,128)(2,1)S(1)} %get-tuple-element.70), channel_id=1, source_target_pairs={{0,6},{2,4},{4,2},{6,0},{8,14},{10,12},{12,10},{14,8},{16,22},{18,... | collective-permute-start | bytes 245768 | tf_op jit(solution)/shard_map/later_back/ppermute | solution.py:393
  46.3 1.1 %collective-permute-start.18 = (bf16[320,128]{1,0:T(8,128)(2,1)S(1)}, bf16[320,128]{1,0:T(8,128)(2,1)S(1)}, u32[]{:S(2)}, u32[]{:S(2)}) collective-permute-start(bf16[320,128]{1,0:T(8,128)(2,1)S(1)} %get-tuple-element.71), channel_id=1, source_target_pairs={{0,4},{2,6},{4,0},{6,2},{8,12},{10,14},{12,8},{14,10},{16,20},{18,... | collective-permute-start | bytes 245768 | tf_op jit(solution)/shard_map/later_back/ppermute | solution.py:393
  47.3 0.1 collective-permute-start.17
  47.5 2.6 %collective-permute-done.19 = bf16[320,128]{1,0:T(8,128)(2,1)S(1)} collective-permute-done((bf16[320,128]{1,0:T(8,128)(2,1)S(1)}, bf16[320,128]{1,0:T(8,128)(2,1)S(1)}, u32[]{:S(2)}, u32[]{:S(2)}) %collective-permute-start.19) | collective-permute-done | bytes 81952 | tf_op jit(solution)/shard_map/later_back/ppermute | solution.py:393
  50.1 2.0 %collective-permute-done.18 = bf16[320,128]{1,0:T(8,128)(2,1)S(1)} collective-permute-done((bf16[320,128]{1,0:T(8,128)(2,1)S(1)}, bf16[320,128]{1,0:T(8,128)(2,1)S(1)}, u32[]{:S(2)}, u32[]{:S(2)}) %collective-permute-start.18) | collective-permute-done | bytes 81952 | tf_op jit(solution)/shard_map/later_back/ppermute | solution.py:393
  52.1 0.0 collective-permute-done.17
  52.2 1.8 %collective-permute-done.20.refs_0_ = bf16[256,1024]{1,0:T(8,128)(2,1)S(1)} collective-permute-done((bf16[256,1024]{1,0:T(8,128)(2,1)S(1)}, bf16[256,1024]{1,0:T(8,128)(2,1)S(1)}, u32[]{:S(2)}, u32[]{:S(2)}) %collective-permute-start.20) | collective-permute-done | bytes 524320 | tf_op jit(solution)/shard_map/attended/ppermute | solution.py:393
  53.9 1.3 %last.1 = (bf16[256,1024]{1,0:T(8,128)(2,1)}, bf16[256,1024]{1,0:T(8,128)(2,1)}) custom-call(bf16[8,256,160]{2,1,0:T(8,128)(2,1)S(1)} %get-tuple-element.47.kt_ref, bf16[4,320,128]{2,1,0:T(8,128)(2,1)S(1)} %pad_maximum_fusion.1.later_ref, f32[256,1024]{1,0:T(8,128)S(1)} %near.1.near_ref, f32[256,1024]{1,0:T(8,128)S(1)} %mixed.1.part_ref, ...), custom_call_target="tpu_custom_call" | custom-call | tf_op jit(solution)/shard_map/last/pallas_call | solution.py:521
  (7 shorter events, 0.2 us)
Async XLA Ops:
  1.4 3.5 %collective-permute-start = (bf16[2,1152]{1,0:T(2,128)(2,1)S(1)}, bf16[2,1152]{1,0:T(2,128)(2,1)S(1)}, u32[]{:S(2)}, u32[]{:S(2)}) collective-permute-start(bf16[2,1152]{1,0:T(2,128)(2,1)S(1)} %edge.1), channel_id=1, source_target_pairs={{0,2},{2,4},{4,6},{6,8},{8,10},{10,12},{12,14},{14,16},{16,18},{18... | collective-permute-start | bytes 13832 | tf_op jit(solution)/shard_map/edge/ppermute | solution.py:364
  5.9 7.2 %collective-permute-start.3 = (bf16[352,128]{1,0:T(8,128)(2,1)S(1)}, bf16[352,128]{1,0:T(8,128)(2,1)S(1)}, u32[]{:S(2)}, u32[]{:S(2)}) collective-permute-start(bf16[352,128]{1,0:T(8,128)(2,1)S(1)} %get-tuple-element.66), channel_id=1, source_target_pairs={{0,6},{2,4},{4,2},{6,0},{8,14},{10,12},{12,10},{14,8},{16,22},{18,... | collective-permute-start | bytes 270344 | tf_op jit(solution)/shard_map/prior_share/ppermute | solution.py:393
  9.8 5.2 %collective-permute-start.2 = (bf16[352,128]{1,0:T(8,128)(2,1)S(1)}, bf16[352,128]{1,0:T(8,128)(2,1)S(1)}, u32[]{:S(2)}, u32[]{:S(2)}) collective-permute-start(bf16[352,128]{1,0:T(8,128)(2,1)S(1)} %get-tuple-element.67), channel_id=1, source_target_pairs={{0,4},{2,6},{4,0},{6,2},{8,12},{10,14},{12,8},{14,10},{16,20},{18,... | collective-permute-start | bytes 270344 | tf_op jit(solution)/shard_map/prior_share/ppermute | solution.py:393
  10.4 4.6 %collective-permute-start.1 = (bf16[352,128]{1,0:T(8,128)(2,1)S(1)}, bf16[352,128]{1,0:T(8,128)(2,1)S(1)}, u32[]{:S(2)}, u32[]{:S(2)}) collective-permute-start(bf16[352,128]{1,0:T(8,128)(2,1)S(1)} %get-tuple-element.68), channel_id=1, source_target_pairs={{0,2},{2,0},{4,6},{6,4},{8,10},{10,8},{12,14},{14,12},{16,18},{18,... | collective-permute-start | bytes 270344 | tf_op jit(solution)/shard_map/prior_share/ppermute | solution.py:393
  10.5 14.5 %collective-permute-start.4 = (bf16[256,1024]{1,0:T(8,128)(2,1)}, bf16[256,1024]{1,0:T(8,128)(2,1)S(1)}, u32[]{:S(2)}, u32[]{:S(2)}) collective-permute-start(bf16[256,1024]{1,0:T(8,128)(2,1)} %refs_0_), channel_id=1, source_target_pairs={{0,1},{1,0},{2,3},{3,2},{4,5},{5,4},{6,7},{7,6},{8,9},{9,8},{10,11... | collective-permute-start | bytes 1572872 | tf_op jit(solution)/shard_map/cotangent/ppermute | solution.py:393
  12.0 13.0 %copy-start = (bf16[1024,2048]{1,0:T(8,128)(2,1)S(1)}, bf16[1024,2048]{1,0:T(8,128)(2,1)}, u32[]{:S(2)}) copy-start(bf16[1024,2048]{1,0:T(8,128)(2,1)} %w_ref.3) | copy-start | bytes 12582916
  12.0 13.0 %copy-start.1 = (bf16[256,1024]{1,0:T(8,128)(2,1)S(1)}, bf16[256,1024]{1,0:T(8,128)(2,1)}, u32[]{:S(2)}) copy-start(bf16[256,1024]{1,0:T(8,128)(2,1)} %refs_0_) | copy-start | bytes 1572868
  15.1 11.1 %collective-permute-start.7 = (bf16[352,128]{1,0:T(8,128)(2,1)S(1)}, bf16[352,128]{1,0:T(8,128)(2,1)S(1)}, u32[]{:S(2)}, u32[]{:S(2)}) collective-permute-start(bf16[352,128]{1,0:T(8,128)(2,1)S(1)} %prior_share.1), channel_id=1, source_target_pairs={{0,24},{2,26},{4,28},{6,30},{8,16},{10,18},{12,20},{14,22},{16,8},... | collective-permute-start | bytes 270344 | tf_op jit(solution)/shard_map/prior_planes/ppermute | solution.py:393
  19.0 8.3 %collective-permute-start.6 = (bf16[352,128]{1,0:T(8,128)(2,1)S(1)}, bf16[352,128]{1,0:T(8,128)(2,1)S(1)}, u32[]{:S(2)}, u32[]{:S(2)}) collective-permute-start(bf16[352,128]{1,0:T(8,128)(2,1)S(1)} %prior_share.1), channel_id=1, source_target_pairs={{0,16},{2,18},{4,20},{6,22},{8,24},{10,26},{12,28},{14,30},{16,0},... | collective-permute-start | bytes 270344 | tf_op jit(solution)/shard_map/prior_planes/ppermute | solution.py:393
  19.0 8.3 %collective-permute-start.5 = (bf16[352,128]{1,0:T(8,128)(2,1)S(1)}, bf16[352,128]{1,0:T(8,128)(2,1)S(1)}, u32[]{:S(2)}, u32[]{:S(2)}) collective-permute-start(bf16[352,128]{1,0:T(8,128)(2,1)S(1)} %prior_share.1), channel_id=1, source_target_pairs={{0,8},{2,10},{4,12},{6,14},{8,0},{10,2},{12,4},{14,6},{16,24},{18,... | collective-permute-start | bytes 270344 | tf_op jit(solution)/shard_map/prior_planes/ppermute | solution.py:393
  28.7 4.8 %collective-permute-start.10 = (bf16[320,128]{1,0:T(8,128)(2,1)S(1)}, bf16[320,128]{1,0:T(8,128)(2,1)S(1)}, u32[]{:S(2)}, u32[]{:S(2)}) collective-permute-start(bf16[320,128]{1,0:T(8,128)(2,1)S(1)} %get-tuple-element.77), channel_id=1, source_target_pairs={{0,6},{2,4},{4,2},{6,0},{8,14},{10,12},{12,10},{14,8},{16,22},{18,... | collective-permute-start | bytes 245768 | tf_op jit(solution)/shard_map/later_share/ppermute | solution.py:393
  29.1 6.2 %collective-permute-start.9 = (bf16[320,128]{1,0:T(8,128)(2,1)S(1)}, bf16[320,128]{1,0:T(8,128)(2,1)S(1)}, u32[]{:S(2)}, u32[]{:S(2)}) collective-permute-start(bf16[320,128]{1,0:T(8,128)(2,1)S(1)} %get-tuple-element.78), channel_id=1, source_target_pairs={{0,4},{2,6},{4,0},{6,2},{8,12},{10,14},{12,8},{14,10},{16,20},{18,... | collective-permute-start | bytes 245768 | tf_op jit(solution)/shard_map/later_share/ppermute | solution.py:393
  30.2 5.0 %collective-permute-start.8 = (bf16[320,128]{1,0:T(8,128)(2,1)S(1)}, bf16[320,128]{1,0:T(8,128)(2,1)S(1)}, u32[]{:S(2)}, u32[]{:S(2)}) collective-permute-start(bf16[320,128]{1,0:T(8,128)(2,1)S(1)} %get-tuple-element.79), channel_id=1, source_target_pairs={{0,2},{2,0},{4,6},{6,4},{8,10},{10,8},{12,14},{14,12},{16,18},{18,... | collective-permute-start | bytes 245768 | tf_op jit(solution)/shard_map/later_share/ppermute | solution.py:393
  30.6 6.7 %collective-permute-start.14 = (bf16[320,128]{1,0:T(8,128)(2,1)S(1)}, bf16[320,128]{1,0:T(8,128)(2,1)S(1)}, u32[]{:S(2)}, u32[]{:S(2)}) collective-permute-start(bf16[320,128]{1,0:T(8,128)(2,1)S(1)} %get-tuple-element.74), channel_id=1, source_target_pairs={{0,6},{2,4},{4,2},{6,0},{8,14},{10,12},{12,10},{14,8},{16,22},{18,... | collective-permute-start | bytes 245768 | tf_op jit(solution)/shard_map/scaled_grad/ppermute | solution.py:393
  31.7 8.0 %collective-permute-start.13 = (bf16[320,128]{1,0:T(8,128)(2,1)S(1)}, bf16[320,128]{1,0:T(8,128)(2,1)S(1)}, u32[]{:S(2)}, u32[]{:S(2)}) collective-permute-start(bf16[320,128]{1,0:T(8,128)(2,1)S(1)} %get-tuple-element.75), channel_id=1, source_target_pairs={{0,4},{2,6},{4,0},{6,2},{8,12},{10,14},{12,8},{14,10},{16,20},{18,... | collective-permute-start | bytes 245768 | tf_op jit(solution)/shard_map/scaled_grad/ppermute | solution.py:393
  33.4 6.3 %collective-permute-start.12 = (bf16[320,128]{1,0:T(8,128)(2,1)S(1)}, bf16[320,128]{1,0:T(8,128)(2,1)S(1)}, u32[]{:S(2)}, u32[]{:S(2)}) collective-permute-start(bf16[320,128]{1,0:T(8,128)(2,1)S(1)} %get-tuple-element.76), channel_id=1, source_target_pairs={{0,2},{2,0},{4,6},{6,4},{8,10},{10,8},{12,14},{14,12},{16,18},{18,... | collective-permute-start | bytes 245768 | tf_op jit(solution)/shard_map/scaled_grad/ppermute | solution.py:393
  35.3 8.7 %collective-permute-start.16 = (bf16[320,128]{1,0:T(8,128)(2,1)S(1)}, bf16[320,128]{1,0:T(8,128)(2,1)S(1)}, u32[]{:S(2)}, u32[]{:S(2)}) collective-permute-start(bf16[320,128]{1,0:T(8,128)(2,1)S(1)} %later_planes.1), channel_id=1, source_target_pairs={{0,24},{2,26},{4,28},{6,30},{8,16},{10,18},{12,20},{14,22},{16,8},... | collective-permute-start | bytes 245768 | tf_op jit(solution)/shard_map/later_planes/ppermute | solution.py:393
  37.4 7.9 %collective-permute-start.15 = (bf16[320,128]{1,0:T(8,128)(2,1)S(1)}, bf16[320,128]{1,0:T(8,128)(2,1)S(1)}, u32[]{:S(2)}, u32[]{:S(2)}) collective-permute-start(bf16[320,128]{1,0:T(8,128)(2,1)S(1)} %later_planes.1), channel_id=1, source_target_pairs={{0,16},{2,18},{4,20},{6,22},{8,24},{10,26},{12,28},{14,30},{16,0},... | collective-permute-start | bytes 245768 | tf_op jit(solution)/shard_map/later_planes/ppermute | solution.py:393
  37.4 6.6 %collective-permute-start.11 = (bf16[320,128]{1,0:T(8,128)(2,1)S(1)}, bf16[320,128]{1,0:T(8,128)(2,1)S(1)}, u32[]{:S(2)}, u32[]{:S(2)}) collective-permute-start(bf16[320,128]{1,0:T(8,128)(2,1)S(1)} %later_planes.1), channel_id=1, source_target_pairs={{0,8},{2,10},{4,12},{6,14},{8,0},{10,2},{12,4},{14,6},{16,24},{18,... | collective-permute-start | bytes 245768 | tf_op jit(solution)/shard_map/later_planes/ppermute | solution.py:393
  40.8 13.1 %collective-permute-start.20 = (bf16[256,1024]{1,0:T(8,128)(2,1)S(1)}, bf16[256,1024]{1,0:T(8,128)(2,1)S(1)}, u32[]{:S(2)}, u32[]{:S(2)}) collective-permute-start(bf16[256,1024]{1,0:T(8,128)(2,1)S(1)} %get-tuple-element.63), channel_id=1, source_target_pairs={{0,1},{1,0},{2,3},{3,2},{4,5},{5,4},{6,7},{7,6},{8,9},{9,8},{10,11... | collective-permute-start | bytes 1572872 | tf_op jit(solution)/shard_map/attended/ppermute | solution.py:393
  45.5 4.5 %collective-permute-start.19 = (bf16[320,128]{1,0:T(8,128)(2,1)S(1)}, bf16[320,128]{1,0:T(8,128)(2,1)S(1)}, u32[]{:S(2)}, u32[]{:S(2)}) collective-permute-start(bf16[320,128]{1,0:T(8,128)(2,1)S(1)} %get-tuple-element.70), channel_id=1, source_target_pairs={{0,6},{2,4},{4,2},{6,0},{8,14},{10,12},{12,10},{14,8},{16,22},{18,... | collective-permute-start | bytes 245768 | tf_op jit(solution)/shard_map/later_back/ppermute | solution.py:393
  46.3 5.8 %collective-permute-start.18 = (bf16[320,128]{1,0:T(8,128)(2,1)S(1)}, bf16[320,128]{1,0:T(8,128)(2,1)S(1)}, u32[]{:S(2)}, u32[]{:S(2)}) collective-permute-start(bf16[320,128]{1,0:T(8,128)(2,1)S(1)} %get-tuple-element.71), channel_id=1, source_target_pairs={{0,4},{2,6},{4,0},{6,2},{8,12},{10,14},{12,8},{14,10},{16,20},{18,... | collective-permute-start | bytes 245768 | tf_op jit(solution)/shard_map/later_back/ppermute | solution.py:393
  47.3 4.8 %collective-permute-start.17 = (bf16[320,128]{1,0:T(8,128)(2,1)S(1)}, bf16[320,128]{1,0:T(8,128)(2,1)S(1)}, u32[]{:S(2)}, u32[]{:S(2)}) collective-permute-start(bf16[320,128]{1,0:T(8,128)(2,1)S(1)} %get-tuple-element.72), channel_id=1, source_target_pairs={{0,2},{2,0},{4,6},{6,4},{8,10},{10,8},{12,14},{14,12},{16,18},{18,... | collective-permute-start | bytes 245768 | tf_op jit(solution)/shard_map/later_back/ppermute | solution.py:393

commit v6 on v5

--- a/solution.py
+++ b/solution.py
@@ -25,7 +25,7 @@
     return lax.dot_general(a, b, dims, preferred_element_type=F32)
 
 
-def call(body, operands, out_shape, flops, far=(), scratch=()):
+def call(body, operands, out_shape, flops, far=(), scratch=(), out_far=False):
     moved = sum(x.size * x.dtype.itemsize for x in operands)
     moved += sum(x.size * x.dtype.itemsize for x in out_shape)
     vmem = pl.BlockSpec(memory_space=pltpu.VMEM)
@@ -34,7 +34,7 @@
         body,
         out_shape=out_shape,
         in_specs=[hbm if i in far else vmem for i in range(len(operands))],
-        out_specs=[vmem for _ in out_shape],
+        out_specs=[hbm if out_far else vmem for _ in out_shape],
         scratch_shapes=list(scratch),
         compiler_params=pltpu.CompilerParams(vmem_limit_bytes=VMEM_LIMIT),
         cost_estimate=pl.CostEstimate(flops=flops, bytes_accessed=moved, transcendentals=0),
@@ -145,6 +145,10 @@
     og_ref[...] = total
 
 
+def masked(wanted, value):
+    return jnp.where(wanted, value.astype(F32), 0.0)
+
+
 def conv_rows(x, before, taps):
     x = x.astype(F32)
     row = lax.broadcasted_iota(jnp.int32, x.shape, 0)
@@ -194,7 +198,7 @@
     heads = kf_ref.shape[0]
     per_piece = heads // PLANE
     width = k_ref.shape[1]
-    before = before_ref[...].astype(F32)
+    before = masked(lax.axis_index("ctx") > 0, before_ref[...])
     key_conv = conv_rows(k_ref[...], before[:, :width], ck_ref[...])
     store_features(kf_ref, key_conv.T, False)
     ones = jnp.ones((heads, k_ref.shape[0]), BF16)
@@ -236,9 +240,6 @@
 def store_pieces(sign, strides, got_refs, moved_refs, pieces_ref):
     rows = pieces_ref.shape[1]
 
-    def masked(ahead, ref):
-        return jnp.where(ahead, ref[...].astype(F32), 0.0)
-
     def is_ahead(other, here):
         return other < here if sign > 0 else other > here
 
@@ -246,7 +247,7 @@
     for ref, (stride, distance) in zip(moved_refs, strides):
         if distance:
             group = lax.div(lax.axis_index("ctx"), PLANE * stride)
-            before = before + masked(is_ahead(group ^ distance, group), ref)
+            before = before + masked(is_ahead(group ^ distance, group), ref[...])
         else:
             before = before + ref[...].astype(F32)
     rank = lax.rem(lax.axis_index("ctx"), PLANE)
@@ -255,7 +256,7 @@
         total = before
         for i in range(PLANE):
             if i != slot:
-                total = total + masked(is_ahead(rank ^ i, rank ^ slot), got_refs[i])
+                total = total + masked(is_ahead(rank ^ i, rank ^ slot), got_refs[i][...])
         pieces_ref[slot] = total[:rows].astype(BF16)
         extra = total[rows:] if slot == 0 else extra
     return extra
@@ -330,30 +331,52 @@
     part_ref[...] = mm(att_ref[...], weight, NN).astype(part_ref.dtype)
 
 
-def last_kernel(kt_ref, later_ref, near_ref, part_ref, *refs):
-    *other_refs, vg_far, mixed_far, vg_ref, mixed_ref, sems = refs
+def far_block(distance, kt_ref, near_ref, later_ref):
+    per_piece = kt_ref.shape[0] // PLANE
+    first = (lax.rem(lax.axis_index("ctx"), PLANE) ^ distance) * per_piece
+    blocks = []
+    for i in range(per_piece):
+        columns = pl.ds(pl.multiple_of((first + i) * VDIM, VDIM), VDIM)
+        later = later_ref[i * ROWS : (i + 1) * ROWS, :]
+        total = near_ref[:, columns] + mm(kt_ref[first + i], later, NN)
+        blocks.append(total.astype(BF16))
+    return jnp.concatenate(blocks, 1)
+
+
+def early_kernel(kt_ref, near_ref, *refs):
+    *later_refs, block_ref = refs
+    for distance, later_ref in enumerate(later_refs):
+        block_ref[distance] = far_block(distance, kt_ref, near_ref, later_ref)
+
+
+def late_kernel(kt_ref, near_ref, early_ref, *refs):
+    *later_refs, vg_far, block_ref, sems = refs
+    early, columns = early_ref.shape[0], early_ref.shape[2]
     rank = lax.rem(lax.axis_index("ctx"), PLANE)
-    heads = kt_ref.shape[0]
-    per_piece = heads // PLANE
+
+    def send(distance, ref):
+        start = pl.multiple_of((rank ^ distance) * columns, columns)
+        return fetch(ref, vg_far.at[:, pl.ds(start, columns)], sems.at[distance])
+
+    copies = [send(distance, early_ref.at[distance]) for distance in range(early)]
+    for i, later_ref in enumerate(later_refs):
+        block_ref[i] = far_block(early + i, kt_ref, near_ref, later_ref)
+        copies.append(send(early + i, block_ref.at[i]))
+    for copy in copies:
+        copy.wait()
+
+
+def sum_kernel(part_ref, *refs):
+    *other_refs, mixed_far, mixed_ref, sems = refs
     copies = []
-    for head in range(heads):
-        at = head * VDIM
-        later = load_piece(rank, head, per_piece, later_ref)
-        total = near_ref[:, at : at + VDIM] + mm(kt_ref[head], later, NN)
-        vg_ref[:, at : at + VDIM] = total.astype(BF16)
-        if head % per_piece == per_piece - 1:
-            columns = pl.ds((head + 1 - per_piece) * VDIM, per_piece * VDIM)
-            sem = sems.at[head // per_piece]
-            copies.append(fetch(vg_ref.at[:, columns], vg_far.at[:, columns], sem))
     deep = part_ref.shape[0] // PLANE
     for step in range(PLANE):
-        total = part_ref[step * deep : (step + 1) * deep, :]
+        rows = pl.ds(step * deep, deep)
+        total = part_ref[rows, :]
         for other_ref in other_refs:
-            total = total + other_ref[step * deep : (step + 1) * deep, :].astype(F32)
-        mixed_ref[step * deep : (step + 1) * deep, :] = total.astype(BF16)
-        rows = pl.ds(step * deep, deep)
-        sem = sems.at[PLANE + step]
-        copies.append(fetch(mixed_ref.at[rows], mixed_far.at[rows], sem))
+            total = total + other_ref[rows, :].astype(F32)
+        mixed_ref[rows, :] = total.astype(BF16)
+        copies.append(fetch(mixed_ref.at[rows], mixed_far.at[rows], sems.at[step]))
     for copy in copies:
         copy.wait()
 
@@ -422,7 +445,8 @@
             scratch_shapes=[vmem((16, keys.shape[1]), BF16), vmem((16, width), BF16), dma((2,))],
             compiler_params=pltpu.CompilerParams(vmem_limit_bytes=VMEM_LIMIT),
         )(in_hbm(keys), in_hbm(values))
-        before = shifted(last_rows, "ctx", 1)
+        slabs = lax.axis_size("ctx")
+        before = lax.ppermute(last_rows, "ctx", [(i, (i + 1) % slabs) for i in range(slabs)])
     with jax.named_scope("query_features"):
         arrays = (keys, values, conv_keys, conv_values)
         qd, *near_by = call(
@@ -513,23 +537,47 @@
     with jax.named_scope("later_back"):
         outs = [S((PLANE, piece_rows, VDIM), BF16)]
         body = functools.partial(piece_kernel, -1, strides)
+        ops = (own_later, *got_later, after(moved_later[0], part), *moved_later[1:])
+        (pieces,) = call(body, ops, outs, 1 << 20)
+        later = [pieces[0]] + [swapped(pieces[j], "ctx", j) for j in range(1, PLANE)]
+    with jax.named_scope("near"):
+        ops = (low, after(scaled, sent_later))
+        (near,) = call(near_kernel, ops, [S((tokens, width), F32)], 2 * step)
+    with jax.named_scope("mixed"):
+        for j in list(range(2, groups)) + [0]:
+            outs = [S((tokens, columns), BF16 if j else F32)]
+            body = functools.partial(mix_kernel, j)
+            ops = (after(attended, sent_later), out_weight)
+            (part,) = call(body, ops, outs, 2 * project_flops)
+            if j:
+                parts.append(swapped(part, "head", j))
+    with jax.named_scope("later_back"):
+        outs = [S((PLANE, piece_rows, VDIM), BF16)]
+        body = functools.partial(piece_kernel, -1, strides)
         ops = (own_later, *got_later, after(moved_later[0], part, near), *moved_later[1:])
         (pieces,) = call(body, ops, outs, 1 << 20)
         later = handed_back(pieces)
-    with jax.named_scope("last"):
-        whole = (tokens, columns)
-        value_grad, mixed_out = pl.pallas_call(
-            last_kernel,
-            out_shape=[S((tokens, width), BF16), S(whole, BF16)],
-            in_specs=[pl.BlockSpec(memory_space=vmem)] * (4 + len(parts)),
-            out_specs=[pl.BlockSpec(memory_space=pltpu.HBM)] * 2,
-            scratch_shapes=[
-                vmem((tokens, width), BF16),
-                vmem(whole, BF16),
-                dma((2 * PLANE,)),
-            ],
-            compiler_params=pltpu.CompilerParams(vmem_limit_bytes=VMEM_LIMIT),
-        )(kt, later, near, part, *parts)
+    with jax.named_scope("far_grad"):
+        block = (tokens, width // PLANE)
+        outs = [S((2, *block), BF16)]
+        (early,) = call(early_kernel, (kt, near, *later[:2]), outs, 16 * step)
+        (value_grad,) = call(
+            late_kernel,
+            (kt, near, early, *later[2:]),
+            [S((tokens, width), BF16)],
+            16 * step,
+            scratch=[vmem((PLANE - 2, *block), BF16), dma((PLANE,))],
+            out_far=True,
+        )
+    with jax.named_scope("mixed_out"):
+        (mixed_out,) = call(
+            sum_kernel,
+            (part, *[after(x, value_grad) for x in parts]),
+            [S((tokens, columns), BF16)],
+            1 << 20,
+            scratch=[vmem((tokens, columns), BF16), dma((PLANE,))],
+            out_far=True,
+        )
     return mixed_out, value_grad
 
 

time: 55.5 us -> 53.9 us (0.971)
  starting transfers between devices: 24.8 us -> 20.2 us
  waiting for transfers between devices: 18.4 us -> 20.7 us
  Pallas kernels: 11.1 us -> 11.9 us
    ppermute x1, waiting for transfers between devices: 0.01 us -> 5.12 us  [per_device(): lax.ppermute(last_rows, 'ctx', [(i, (i + 1) % slabs) for i in range(slabs)])]
    ppermute x20, waiting for transfers between devices: 18.4 us -> 15.6 us  [swapped(): return lax.ppermute(x, axis, pairs)]
    ppermute x20, starting transfers between devices: 22.4 us -> 19.7 us  [swapped(): return lax.ppermute(x, axis, pairs)]
    pallas_call x12 -> x15, Pallas kernels: 8.98 us -> 11.1 us  [call(): pl.pallas_call(body, out_shape=out_shape, in_specs=[hbm if i in far else...]
    ppermute x1, starting transfers between devices: 2.36 us -> 0.5 us  [per_device(): lax.ppermute(last_rows, 'ctx', [(i, (i + 1) % slabs) for i in range(slabs)])]
    pallas_call x1 -> x0, Pallas kernels: 1.34 us -> none  [per_device(): pl.pallas_call(last_kernel, out_shape=[S((tokens, width), BF16), S(whole,...]
  transfers between devices with their start and end apart: 21 -> 21, of which waited for: 10 -> 11; matrix products, arithmetic and copies ran while one was open for 0% -> 0% of each run, Pallas kernels for 12% -> 15%
where the time goes in v6:
time: 53.9 us; the launch traced here: 53.7 us
  waiting for transfers between devices  20.7 us (38%)
  starting transfers between devices  20.2 us (37%)
  Pallas kernels  11.9 us (22%)
  between operations  0.83 us (2%)
    ppermute x20, starting transfers between devices, swapped(): return lax.ppermute(x, axis, pairs)  19.7 us
    ppermute x20, waiting for transfers between devices, swapped(): return lax.ppermute(x, axis, pairs)  15.6 us
    pallas_call x15, Pallas kernels, call(): pl.pallas_call(body, out_shape=out_shape, in_specs=[hbm if i in far else...  11.1 us
    ppermute x1, waiting for transfers between devices, per_device(): lax.ppermute(last_rows, 'ctx', [(i, (i + 1) % slabs) for i in range(slabs)])  5.12 us
  transfers between devices with their start and end apart: 21, of which 11 were waited for; matrix products, arithmetic and copies ran while one was open for 0% of the time, Pallas kernels for 15%

profile of v6, /device:TPU:0, one launch (start us, length us, event | category | flops | bytes accessed | tf_op | source)
XLA Modules:
  0.0 53.7 jit_solution(2928944959842565401)
XLA Ops:
  0.6 0.8 %edge.1 = bf16[2,1152]{1,0:T(2,128)(2,1)S(1)} custom-call(bf16[256,128]{1,0:T(8,128)(2,1)} %k_far.3, bf16[256,1024]{1,0:T(8,128)(2,1)} %v_far.3), custom_call_target="tpu_custom_call" | custom-call | tf_op jit(solution)/shard_map/edge/pallas_call | solution.py:440
  1.4 0.5 collective-permute-start
  1.9 1.2 %query_features.1 = (bf16[8,160,256]{2,1,0:T(8,128)(2,1)S(1)}, bf16[256,128]{1,0:T(8,128)(2,1)S(1)}, bf16[256,1024]{1,0:T(8,128)(2,1)S(1)}, f32[3,128]{1,0:T(4,128)S(1)}, f32[3,1024]{1,0:T(4,128)S(1)}) custom-call(bf16[256,128]{1,0:T(8,128)(2,1)} %q_far, bf16[256,128]{1,0:T(8,128)(2,1)} %k_far.3, bf16[256,1024]{1,0:T(8,128)(2,1)} %v_far.3, f32[3,128]{1,0:T(4,128)} %ck_far.1, ...), custom_call_target="tpu_custom_call" | custom-call | flops 1048576 | bytes 1928192 | tf_op jit(solution)/shard_map/query_features/pallas_call | solution.py:33
  3.1 5.1 %collective-permute-done.before_ref = bf16[2,1152]{1,0:T(2,128)(2,1)S(1)} collective-permute-done((bf16[2,1152]{1,0:T(2,128)(2,1)S(1)}, bf16[2,1152]{1,0:T(2,128)(2,1)S(1)}, u32[]{:S(2)}, u32[]{:S(2)}) %collective-permute-start) | collective-permute-done | bytes 4640 | tf_op jit(solution)/shard_map/edge/ppermute | solution.py:449
  8.2 0.9 %key_features.1 = (bf16[8,160,256]{2,1,0:T(8,128)(2,1)S(1)}, bf16[256,1024]{1,0:T(8,128)(2,1)S(1)}, f32[352,128]{1,0:T(8,128)S(1)}, bf16[4,352,128]{2,1,0:T(8,128)(2,1)S(1)}) custom-call(bf16[256,128]{1,0:T(8,128)(2,1)S(1)} %get-tuple-element.35.k_ref, bf16[256,1024]{1,0:T(8,128)(2,1)S(1)} %get-tuple-element.36.v_ref, ...), custom_call_target="tpu_custom_call" | custom-call | flops 83886080 | bytes 2328576 | tf_op jit(solution)/shard_map/key_features/pallas_call | solution.py:33
  9.2 0.1 collective-permute-start.3
  9.3 0.1 collective-permute-start.2
  9.3 1.8 %collective-permute-start.1 = (bf16[352,128]{1,0:T(8,128)(2,1)S(1)}, bf16[352,128]{1,0:T(8,128)(2,1)S(1)}, u32[]{:S(2)}, u32[]{:S(2)}) collective-permute-start(bf16[352,128]{1,0:T(8,128)(2,1)S(1)} %get-tuple-element.66), channel_id=1, source_target_pairs={{0,2},{2,0},{4,6},{6,4},{8,10},{10,8},{12,14},{14,12},{16,18},{18,... | collective-permute-start | bytes 270344 | tf_op jit(solution)/shard_map/prior_share/ppermute | solution.py:416
  11.1 1.9 %collective-permute-start.4 = (bf16[256,1024]{1,0:T(8,128)(2,1)}, bf16[256,1024]{1,0:T(8,128)(2,1)S(1)}, u32[]{:S(2)}, u32[]{:S(2)}) collective-permute-start(bf16[256,1024]{1,0:T(8,128)(2,1)} %refs_0_), channel_id=1, source_target_pairs={{0,1},{1,0},{2,3},{3,2},{4,5},{5,4},{6,7},{7,6},{8,9},{9,8},{10,11... | collective-permute-start | bytes 1572872 | tf_op jit(solution)/shard_map/cotangent/ppermute | solution.py:416
  13.0 0.0 copy-start
  13.0 0.0 copy-start.1
  13.0 1.2 %scores.1 = (bf16[8,256,256]{2,1,0:T(8,128)(2,1)S(1)}, f32[8,256]{1,0:T(8,128)S(1)}, f32[256,1024]{1,0:T(8,128)S(1)}) custom-call(bf16[8,160,256]{2,1,0:T(8,128)(2,1)S(1)} %get-tuple-element.45.qd_ref, bf16[8,160,256]{2,1,0:T(8,128)(2,1)S(1)} %get-tuple-element.41.kf_ref, bf16[256,1024]{1,0:T(8,128)(2,1)S(1)} %get-tuple-element.42.vc_ref), custom_call_target="tpu_custom_call" | custom-call | flops 33554432000 | bytes 3940352 | tf_op jit(solution)/shard_map/scores/pallas_call | solution.py:33
  14.2 0.0 collective-permute-done.3.refs_2_.refs_3_
  14.3 0.5 collective-permute-done.2.refs_1_.refs_2_
  14.8 0.0 collective-permute-done.1.refs_0_.refs_1_
  14.8 0.2 prior_share.1
  14.9 2.3 %collective-permute-start.7 = (bf16[352,128]{1,0:T(8,128)(2,1)S(1)}, bf16[352,128]{1,0:T(8,128)(2,1)S(1)}, u32[]{:S(2)}, u32[]{:S(2)}) collective-permute-start(bf16[352,128]{1,0:T(8,128)(2,1)S(1)} %prior_share.1), channel_id=1, source_target_pairs={{0,24},{2,26},{4,28},{6,30},{8,16},{10,18},{12,20},{14,22},{16,8},... | collective-permute-start | bytes 270344 | tf_op jit(solution)/shard_map/prior_planes/ppermute | solution.py:416
  17.2 0.0 collective-permute-start.6
  17.2 2.1 %collective-permute-start.5 = (bf16[352,128]{1,0:T(8,128)(2,1)S(1)}, bf16[352,128]{1,0:T(8,128)(2,1)S(1)}, u32[]{:S(2)}, u32[]{:S(2)}) collective-permute-start(bf16[352,128]{1,0:T(8,128)(2,1)S(1)} %prior_share.1), channel_id=1, source_target_pairs={{0,8},{2,10},{4,12},{6,14},{8,0},{10,2},{12,4},{14,6},{16,24},{18,... | collective-permute-start | bytes 270344 | tf_op jit(solution)/shard_map/prior_planes/ppermute | solution.py:416
  19.4 0.6 %turned.1 = (bf16[8,256,160]{2,1,0:T(8,128)(2,1)S(1)}, bf16[8,256,160]{2,1,0:T(8,128)(2,1)S(1)}) custom-call(bf16[8,160,256]{2,1,0:T(8,128)(2,1)S(1)} %get-tuple-element.45.qd_ref, bf16[8,160,256]{2,1,0:T(8,128)(2,1)S(1)} %get-tuple-element.41.kf_ref), custom_call_target="tpu_custom_call" | custom-call | flops 4194304 | bytes 2621440 | tf_op jit(solution)/shard_map/turned/pallas_call | solution.py:33
  20.0 5.4 %collective-permute-done.4.refs_1_ = bf16[256,1024]{1,0:T(8,128)(2,1)S(1)} collective-permute-done((bf16[256,1024]{1,0:T(8,128)(2,1)}, bf16[256,1024]{1,0:T(8,128)(2,1)S(1)}, u32[]{:S(2)}, u32[]{:S(2)}) %collective-permute-start.4) | collective-permute-done | bytes 524320 | tf_op jit(solution)/shard_map/cotangent/ppermute | solution.py:416
  25.3 0.0 copy-done
  25.3 0.0 copy-done.1
  25.3 1.3 %out_grad.1.og_ref = f32[256,1024]{1,0:T(8,128)S(1)} custom-call(bf16[256,1024]{1,0:T(8,128)(2,1)S(1)} %copy-done.1, bf16[256,1024]{1,0:T(8,128)(2,1)S(1)} %collective-permute-done.4.refs_1_, bf16[1024,2048]{1,0:T(8,128)(2,1)S(1)} %copy-done), custom_call_target="tpu_custom_call" | custom-call | flops 1073741824 | bytes 6291456 | tf_op jit(solution)/shard_map/out_grad/pallas_call | solution.py:33
  26.6 0.0 collective-permute-done.7.refs_6_
  26.6 0.0 collective-permute-done.6.refs_5_
  26.7 0.0 collective-permute-done.5.refs_4_
  26.7 1.2 %scaled_grad.1 = (bf16[4,320,128]{2,1,0:T(8,128)(2,1)S(1)}, f32[256,8]{1,0:T(8,128)S(1)}, bf16[256,1024]{1,0:T(8,128)(2,1)S(1)}, f32[320,128]{1,0:T(8,128)S(1)}, bf16[4,320,128]{2,1,0:T(8,128)(2,1)S(1)}) custom-call(f32[8,256]{1,0:T(8,128)S(1)} %get-tuple-element.43.den_ref, bf16[8,160,256]{2,1,0:T(8,128)(2,1)S(1)} %get-tuple-element.45.qd_ref, ...), custom_call_target="tpu_custom_call" | custom-call | flops 83886080 | bytes 3784704 | tf_op jit(solution)/shard_map/scaled_grad/pallas_call | solution.py:33
  27.9 0.2 collective-permute-start.13
  28.2 0.8 %collective-permute-start.12 = (bf16[320,128]{1,0:T(8,128)(2,1)S(1)}, bf16[320,128]{1,0:T(8,128)(2,1)S(1)}, u32[]{:S(2)}, u32[]{:S(2)}) collective-permute-start(bf16[320,128]{1,0:T(8,128)(2,1)S(1)} %get-tuple-element.72), channel_id=1, source_target_pairs={{0,4},{2,6},{4,0},{6,2},{8,12},{10,14},{12,8},{14,10},{16,20},{18,... | collective-permute-start | bytes 245768 | tf_op jit(solution)/shard_map/later_share/ppermute | solution.py:416
  29.0 0.9 %collective-permute-start.11 = (bf16[320,128]{1,0:T(8,128)(2,1)S(1)}, bf16[320,128]{1,0:T(8,128)(2,1)S(1)}, u32[]{:S(2)}, u32[]{:S(2)}) collective-permute-start(bf16[320,128]{1,0:T(8,128)(2,1)S(1)} %get-tuple-element.73), channel_id=1, source_target_pairs={{0,2},{2,0},{4,6},{6,4},{8,10},{10,8},{12,14},{14,12},{16,18},{18,... | collective-permute-start | bytes 245768 | tf_op jit(solution)/shard_map/later_share/ppermute | solution.py:416
  29.9 0.5 collective-permute-start.10
  30.4 1.2 %collective-permute-start.9 = (bf16[320,128]{1,0:T(8,128)(2,1)S(1)}, bf16[320,128]{1,0:T(8,128)(2,1)S(1)}, u32[]{:S(2)}, u32[]{:S(2)}) collective-permute-start(bf16[320,128]{1,0:T(8,128)(2,1)S(1)} %get-tuple-element.76), channel_id=1, source_target_pairs={{0,4},{2,6},{4,0},{6,2},{8,12},{10,14},{12,8},{14,10},{16,20},{18,... | collective-permute-start | bytes 245768 | tf_op jit(solution)/shard_map/scaled_grad/ppermute | solution.py:416
  31.6 1.1 %collective-permute-done.13.refs_2_.refs_3_ = bf16[320,128]{1,0:T(8,128)(2,1)S(1)} collective-permute-done((bf16[320,128]{1,0:T(8,128)(2,1)S(1)}, bf16[320,128]{1,0:T(8,128)(2,1)S(1)}, u32[]{:S(2)}, u32[]{:S(2)}) %collective-permute-start.13) | collective-permute-done | bytes 81952 | tf_op jit(solution)/shard_map/later_share/ppermute | solution.py:416
  32.7 0.0 collective-permute-start.8
  32.7 1.0 %collective-permute-done.12.refs_1_.refs_2_ = bf16[320,128]{1,0:T(8,128)(2,1)S(1)} collective-permute-done((bf16[320,128]{1,0:T(8,128)(2,1)S(1)}, bf16[320,128]{1,0:T(8,128)(2,1)S(1)}, u32[]{:S(2)}, u32[]{:S(2)}) %collective-permute-start.12) | collective-permute-done | bytes 81952 | tf_op jit(solution)/shard_map/later_share/ppermute | solution.py:416
  33.7 0.0 collective-permute-done.11.refs_0_.refs_1_
  33.7 2.1 %collective-permute-start.17 = (bf16[320,128]{1,0:T(8,128)(2,1)S(1)}, bf16[320,128]{1,0:T(8,128)(2,1)S(1)}, u32[]{:S(2)}, u32[]{:S(2)}) collective-permute-start(bf16[320,128]{1,0:T(8,128)(2,1)S(1)} %later_planes.1), channel_id=1, source_target_pairs={{0,24},{2,26},{4,28},{6,30},{8,16},{10,18},{12,20},{14,22},{16,8},... | collective-permute-start | bytes 245768 | tf_op jit(solution)/shard_map/later_planes/ppermute | solution.py:416
  35.8 0.0 collective-permute-start.16
  35.8 0.4 collective-permute-done.10
  36.2 2.0 %collective-permute-start.15 = (bf16[320,128]{1,0:T(8,128)(2,1)S(1)}, bf16[320,128]{1,0:T(8,128)(2,1)S(1)}, u32[]{:S(2)}, u32[]{:S(2)}) collective-permute-start(bf16[320,128]{1,0:T(8,128)(2,1)S(1)} %later_planes.1), channel_id=1, source_target_pairs={{0,8},{2,10},{4,12},{6,14},{8,0},{10,2},{12,4},{14,6},{16,24},{18,... | collective-permute-start | bytes 245768 | tf_op jit(solution)/shard_map/later_planes/ppermute | solution.py:416
  38.2 0.0 collective-permute-done.9
  38.2 0.0 collective-permute-done.8
  38.2 1.0 %attended.1 = (bf16[256,1024]{1,0:T(8,128)(2,1)S(1)}, bf16[256,1024]{1,0:T(8,128)(2,1)S(1)}) custom-call(bf16[8,256,160]{2,1,0:T(8,128)(2,1)S(1)} %get-tuple-element.46.qt_ref, bf16[4,320,128]{2,1,0:T(8,128)(2,1)S(1)} %pad_maximum_fusion.prior_ref, f32[256,1024]{1,0:T(8,128)S(1)} %get-tuple-element.53.num_ref, f32[256,8]{1,0:T(8,128)S(1)} %get-tuple-element.54.inv_ref, ...), custom_call_target="tpu_custom_call" | custom-call | flops 620756992 | bytes 7282688 | tf_op jit(solution)/shard_map/attended/pallas_call | solution.py:33
  39.2 1.5 %collective-permute-start.14 = (bf16[256,1024]{1,0:T(8,128)(2,1)S(1)}, bf16[256,1024]{1,0:T(8,128)(2,1)S(1)}, u32[]{:S(2)}, u32[]{:S(2)}) collective-permute-start(bf16[256,1024]{1,0:T(8,128)(2,1)S(1)} %get-tuple-element.57), channel_id=1, source_target_pairs={{0,1},{1,0},{2,3},{3,2},{4,5},{5,4},{6,7},{7,6},{8,9},{9,8},{10,11... | collective-permute-start | bytes 1572872 | tf_op jit(solution)/shard_map/attended/ppermute | solution.py:416
  40.7 0.4 near.1.near_ref
  41.2 0.7 %mixed.1.part_ref = f32[256,1024]{1,0:T(8,128)S(1)} custom-call(bf16[256,1024]{1,0:T(8,128)(2,1)S(1)} %get-tuple-element.56.att_ref, bf16[1024,2048]{1,0:T(8,128)(2,1)S(1)} %copy-done), custom_call_target="tpu_custom_call" | custom-call | flops 1073741824 | bytes 5767168 | tf_op jit(solution)/shard_map/mixed/pallas_call | solution.py:33
  41.9 0.7 %collective-permute-done.15.refs_4_ = bf16[320,128]{1,0:T(8,128)(2,1)S(1)} collective-permute-done((bf16[320,128]{1,0:T(8,128)(2,1)S(1)}, bf16[320,128]{1,0:T(8,128)(2,1)S(1)}, u32[]{:S(2)}, u32[]{:S(2)}) %collective-permute-start.15) | collective-permute-done | bytes 81952 | tf_op jit(solution)/shard_map/later_planes/ppermute | solution.py:416
  42.6 0.0 collective-permute-done.17.refs_6_
  42.6 1.4 %collective-permute-done.16.refs_5_ = bf16[320,128]{1,0:T(8,128)(2,1)S(1)} collective-permute-done((bf16[320,128]{1,0:T(8,128)(2,1)S(1)}, bf16[320,128]{1,0:T(8,128)(2,1)S(1)}, u32[]{:S(2)}, u32[]{:S(2)}) %collective-permute-start.16) | collective-permute-done | bytes 81952 | tf_op jit(solution)/shard_map/later_planes/ppermute | solution.py:416
  44.0 0.2 later_back.1
  44.3 0.1 collective-permute-start.18
  44.4 1.2 %collective-permute-start.20 = (bf16[320,128]{1,0:T(8,128)(2,1)S(1)}, bf16[320,128]{1,0:T(8,128)(2,1)S(1)}, u32[]{:S(2)}, u32[]{:S(2)}) collective-permute-start(bf16[320,128]{1,0:T(8,128)(2,1)S(1)} %get-tuple-element.67), channel_id=1, source_target_pairs={{0,6},{2,4},{4,2},{6,0},{8,14},{10,12},{12,10},{14,8},{16,22},{18,... | collective-permute-start | bytes 245768 | tf_op jit(solution)/shard_map/later_back/ppermute | solution.py:416
  45.6 0.9 %collective-permute-start.19 = (bf16[320,128]{1,0:T(8,128)(2,1)S(1)}, bf16[320,128]{1,0:T(8,128)(2,1)S(1)}, u32[]{:S(2)}, u32[]{:S(2)}) collective-permute-start(bf16[320,128]{1,0:T(8,128)(2,1)S(1)} %get-tuple-element.68), channel_id=1, source_target_pairs={{0,4},{2,6},{4,0},{6,2},{8,12},{10,14},{12,8},{14,10},{16,20},{18,... | collective-permute-start | bytes 245768 | tf_op jit(solution)/shard_map/later_back/ppermute | solution.py:416
  46.5 0.0 collective-permute-done.18.refs_1_
  46.5 0.3 far_grad.2.early_ref
  46.8 1.8 %collective-permute-done.20.refs_1_ = bf16[320,128]{1,0:T(8,128)(2,1)S(1)} collective-permute-done((bf16[320,128]{1,0:T(8,128)(2,1)S(1)}, bf16[320,128]{1,0:T(8,128)(2,1)S(1)}, u32[]{:S(2)}, u32[]{:S(2)}) %collective-permute-start.20) | collective-permute-done | bytes 81952 | tf_op jit(solution)/shard_map/later_back/ppermute | solution.py:416
  48.6 2.3 %collective-permute-done.19.refs_0_ = bf16[320,128]{1,0:T(8,128)(2,1)S(1)} collective-permute-done((bf16[320,128]{1,0:T(8,128)(2,1)S(1)}, bf16[320,128]{1,0:T(8,128)(2,1)S(1)}, u32[]{:S(2)}, u32[]{:S(2)}) %collective-permute-start.19) | collective-permute-done | bytes 81952 | tf_op jit(solution)/shard_map/later_back/ppermute | solution.py:416
  50.9 1.0 %far_grad.3 = bf16[256,1024]{1,0:T(8,128)(2,1)} custom-call(bf16[8,256,160]{2,1,0:T(8,128)(2,1)S(1)} %get-tuple-element.58.kt_ref, f32[256,1024]{1,0:T(8,128)S(1)} %near.1.near_ref, bf16[2,256,256]{2,1,0:T(8,128)(2,1)S(1)} %far_grad.2.early_ref, bf16[320,128]{1,0:T(8,128)(2,1)S(1)} %collective-permute-done.19.refs_0_, ...), custom_call_target="tpu_custom_call" | custom-call | flops 1342177280 | bytes 2654208 | tf_op jit(solution)/shard_map/far_grad/pallas_call | solution.py:33
  51.9 1.0 %collective-permute-done.14.refs_0_ = bf16[256,1024]{1,0:T(8,128)(2,1)S(1)} collective-permute-done((bf16[256,1024]{1,0:T(8,128)(2,1)S(1)}, bf16[256,1024]{1,0:T(8,128)(2,1)S(1)}, u32[]{:S(2)}, u32[]{:S(2)}) %collective-permute-start.14) | collective-permute-done | bytes 524320 | tf_op jit(solution)/shard_map/attended/ppermute | solution.py:416
  52.9 0.8 %mixed_out.1 = bf16[256,1024]{1,0:T(8,128)(2,1)} custom-call(f32[256,1024]{1,0:T(8,128)S(1)} %mixed.1.part_ref, bf16[256,1024]{1,0:T(8,128)(2,1)S(1)} %collective-permute-done.14.refs_0_), custom_call_target="tpu_custom_call" | custom-call | flops 1048576 | bytes 2097152 | tf_op jit(solution)/shard_map/mixed_out/pallas_call | solution.py:33
  (6 shorter events, 0.2 us)
Async XLA Ops:
  1.4 6.8 %collective-permute-start = (bf16[2,1152]{1,0:T(2,128)(2,1)S(1)}, bf16[2,1152]{1,0:T(2,128)(2,1)S(1)}, u32[]{:S(2)}, u32[]{:S(2)}) collective-permute-start(bf16[2,1152]{1,0:T(2,128)(2,1)S(1)} %edge.1), channel_id=1, source_target_pairs={{0,2},{2,4},{4,6},{6,8},{8,10},{10,12},{12,14},{14,16},{16,18},{18... | collective-permute-start | bytes 13832 | tf_op jit(solution)/shard_map/edge/ppermute | solution.py:449
  9.2 5.1 %collective-permute-start.3 = (bf16[352,128]{1,0:T(8,128)(2,1)S(1)}, bf16[352,128]{1,0:T(8,128)(2,1)S(1)}, u32[]{:S(2)}, u32[]{:S(2)}) collective-permute-start(bf16[352,128]{1,0:T(8,128)(2,1)S(1)} %get-tuple-element.64), channel_id=1, source_target_pairs={{0,6},{2,4},{4,2},{6,0},{8,14},{10,12},{12,10},{14,8},{16,22},{18,... | collective-permute-start | bytes 270344 | tf_op jit(solution)/shard_map/prior_share/ppermute | solution.py:416
  9.3 5.5 %collective-permute-start.2 = (bf16[352,128]{1,0:T(8,128)(2,1)S(1)}, bf16[352,128]{1,0:T(8,128)(2,1)S(1)}, u32[]{:S(2)}, u32[]{:S(2)}) collective-permute-start(bf16[352,128]{1,0:T(8,128)(2,1)S(1)} %get-tuple-element.65), channel_id=1, source_target_pairs={{0,4},{2,6},{4,0},{6,2},{8,12},{10,14},{12,8},{14,10},{16,20},{18,... | collective-permute-start | bytes 270344 | tf_op jit(solution)/shard_map/prior_share/ppermute | solution.py:416
  9.3 5.4 %collective-permute-start.1 = (bf16[352,128]{1,0:T(8,128)(2,1)S(1)}, bf16[352,128]{1,0:T(8,128)(2,1)S(1)}, u32[]{:S(2)}, u32[]{:S(2)}) collective-permute-start(bf16[352,128]{1,0:T(8,128)(2,1)S(1)} %get-tuple-element.66), channel_id=1, source_target_pairs={{0,2},{2,0},{4,6},{6,4},{8,10},{10,8},{12,14},{14,12},{16,18},{18,... | collective-permute-start | bytes 270344 | tf_op jit(solution)/shard_map/prior_share/ppermute | solution.py:416
  11.1 14.2 %collective-permute-start.4 = (bf16[256,1024]{1,0:T(8,128)(2,1)}, bf16[256,1024]{1,0:T(8,128)(2,1)S(1)}, u32[]{:S(2)}, u32[]{:S(2)}) collective-permute-start(bf16[256,1024]{1,0:T(8,128)(2,1)} %refs_0_), channel_id=1, source_target_pairs={{0,1},{1,0},{2,3},{3,2},{4,5},{5,4},{6,7},{7,6},{8,9},{9,8},{10,11... | collective-permute-start | bytes 1572872 | tf_op jit(solution)/shard_map/cotangent/ppermute | solution.py:416
  13.0 12.3 %copy-start = (bf16[1024,2048]{1,0:T(8,128)(2,1)S(1)}, bf16[1024,2048]{1,0:T(8,128)(2,1)}, u32[]{:S(2)}) copy-start(bf16[1024,2048]{1,0:T(8,128)(2,1)} %w_ref.3) | copy-start | bytes 12582916
  13.0 12.3 %copy-start.1 = (bf16[256,1024]{1,0:T(8,128)(2,1)S(1)}, bf16[256,1024]{1,0:T(8,128)(2,1)}, u32[]{:S(2)}) copy-start(bf16[256,1024]{1,0:T(8,128)(2,1)} %refs_0_) | copy-start | bytes 1572868
  14.9 11.7 %collective-permute-start.7 = (bf16[352,128]{1,0:T(8,128)(2,1)S(1)}, bf16[352,128]{1,0:T(8,128)(2,1)S(1)}, u32[]{:S(2)}, u32[]{:S(2)}) collective-permute-start(bf16[352,128]{1,0:T(8,128)(2,1)S(1)} %prior_share.1), channel_id=1, source_target_pairs={{0,24},{2,26},{4,28},{6,30},{8,16},{10,18},{12,20},{14,22},{16,8},... | collective-permute-start | bytes 270344 | tf_op jit(solution)/shard_map/prior_planes/ppermute | solution.py:416
  17.2 9.4 %collective-permute-start.6 = (bf16[352,128]{1,0:T(8,128)(2,1)S(1)}, bf16[352,128]{1,0:T(8,128)(2,1)S(1)}, u32[]{:S(2)}, u32[]{:S(2)}) collective-permute-start(bf16[352,128]{1,0:T(8,128)(2,1)S(1)} %prior_share.1), channel_id=1, source_target_pairs={{0,16},{2,18},{4,20},{6,22},{8,24},{10,26},{12,28},{14,30},{16,0},... | collective-permute-start | bytes 270344 | tf_op jit(solution)/shard_map/prior_planes/ppermute | solution.py:416
  17.2 9.4 %collective-permute-start.5 = (bf16[352,128]{1,0:T(8,128)(2,1)S(1)}, bf16[352,128]{1,0:T(8,128)(2,1)S(1)}, u32[]{:S(2)}, u32[]{:S(2)}) collective-permute-start(bf16[352,128]{1,0:T(8,128)(2,1)S(1)} %prior_share.1), channel_id=1, source_target_pairs={{0,8},{2,10},{4,12},{6,14},{8,0},{10,2},{12,4},{14,6},{16,24},{18,... | collective-permute-start | bytes 270344 | tf_op jit(solution)/shard_map/prior_planes/ppermute | solution.py:416
  27.9 4.7 %collective-permute-start.13 = (bf16[320,128]{1,0:T(8,128)(2,1)S(1)}, bf16[320,128]{1,0:T(8,128)(2,1)S(1)}, u32[]{:S(2)}, u32[]{:S(2)}) collective-permute-start(bf16[320,128]{1,0:T(8,128)(2,1)S(1)} %get-tuple-element.71), channel_id=1, source_target_pairs={{0,6},{2,4},{4,2},{6,0},{8,14},{10,12},{12,10},{14,8},{16,22},{18,... | collective-permute-start | bytes 245768 | tf_op jit(solution)/shard_map/later_share/ppermute | solution.py:416
  28.2 5.5 %collective-permute-start.12 = (bf16[320,128]{1,0:T(8,128)(2,1)S(1)}, bf16[320,128]{1,0:T(8,128)(2,1)S(1)}, u32[]{:S(2)}, u32[]{:S(2)}) collective-permute-start(bf16[320,128]{1,0:T(8,128)(2,1)S(1)} %get-tuple-element.72), channel_id=1, source_target_pairs={{0,4},{2,6},{4,0},{6,2},{8,12},{10,14},{12,8},{14,10},{16,20},{18,... | collective-permute-start | bytes 245768 | tf_op jit(solution)/shard_map/later_share/ppermute | solution.py:416
  29.0 4.7 %collective-permute-start.11 = (bf16[320,128]{1,0:T(8,128)(2,1)S(1)}, bf16[320,128]{1,0:T(8,128)(2,1)S(1)}, u32[]{:S(2)}, u32[]{:S(2)}) collective-permute-start(bf16[320,128]{1,0:T(8,128)(2,1)S(1)} %get-tuple-element.73), channel_id=1, source_target_pairs={{0,2},{2,0},{4,6},{6,4},{8,10},{10,8},{12,14},{14,12},{16,18},{18,... | collective-permute-start | bytes 245768 | tf_op jit(solution)/shard_map/later_share/ppermute | solution.py:416
  29.9 6.3 %collective-permute-start.10 = (bf16[320,128]{1,0:T(8,128)(2,1)S(1)}, bf16[320,128]{1,0:T(8,128)(2,1)S(1)}, u32[]{:S(2)}, u32[]{:S(2)}) collective-permute-start(bf16[320,128]{1,0:T(8,128)(2,1)S(1)} %get-tuple-element.75), channel_id=1, source_target_pairs={{0,6},{2,4},{4,2},{6,0},{8,14},{10,12},{12,10},{14,8},{16,22},{18,... | collective-permute-start | bytes 245768 | tf_op jit(solution)/shard_map/scaled_grad/ppermute | solution.py:416
  30.4 7.8 %collective-permute-start.9 = (bf16[320,128]{1,0:T(8,128)(2,1)S(1)}, bf16[320,128]{1,0:T(8,128)(2,1)S(1)}, u32[]{:S(2)}, u32[]{:S(2)}) collective-permute-start(bf16[320,128]{1,0:T(8,128)(2,1)S(1)} %get-tuple-element.76), channel_id=1, source_target_pairs={{0,4},{2,6},{4,0},{6,2},{8,12},{10,14},{12,8},{14,10},{16,20},{18,... | collective-permute-start | bytes 245768 | tf_op jit(solution)/shard_map/scaled_grad/ppermute | solution.py:416
  32.7 5.5 %collective-permute-start.8 = (bf16[320,128]{1,0:T(8,128)(2,1)S(1)}, bf16[320,128]{1,0:T(8,128)(2,1)S(1)}, u32[]{:S(2)}, u32[]{:S(2)}) collective-permute-start(bf16[320,128]{1,0:T(8,128)(2,1)S(1)} %get-tuple-element.77), channel_id=1, source_target_pairs={{0,2},{2,0},{4,6},{6,4},{8,10},{10,8},{12,14},{14,12},{16,18},{18,... | collective-permute-start | bytes 245768 | tf_op jit(solution)/shard_map/scaled_grad/ppermute | solution.py:416
  33.7 8.9 %collective-permute-start.17 = (bf16[320,128]{1,0:T(8,128)(2,1)S(1)}, bf16[320,128]{1,0:T(8,128)(2,1)S(1)}, u32[]{:S(2)}, u32[]{:S(2)}) collective-permute-start(bf16[320,128]{1,0:T(8,128)(2,1)S(1)} %later_planes.1), channel_id=1, source_target_pairs={{0,24},{2,26},{4,28},{6,30},{8,16},{10,18},{12,20},{14,22},{16,8},... | collective-permute-start | bytes 245768 | tf_op jit(solution)/shard_map/later_planes/ppermute | solution.py:416
  35.8 8.2 %collective-permute-start.16 = (bf16[320,128]{1,0:T(8,128)(2,1)S(1)}, bf16[320,128]{1,0:T(8,128)(2,1)S(1)}, u32[]{:S(2)}, u32[]{:S(2)}) collective-permute-start(bf16[320,128]{1,0:T(8,128)(2,1)S(1)} %later_planes.1), channel_id=1, source_target_pairs={{0,16},{2,18},{4,20},{6,22},{8,24},{10,26},{12,28},{14,30},{16,0},... | collective-permute-start | bytes 245768 | tf_op jit(solution)/shard_map/later_planes/ppermute | solution.py:416
  36.2 6.4 %collective-permute-start.15 = (bf16[320,128]{1,0:T(8,128)(2,1)S(1)}, bf16[320,128]{1,0:T(8,128)(2,1)S(1)}, u32[]{:S(2)}, u32[]{:S(2)}) collective-permute-start(bf16[320,128]{1,0:T(8,128)(2,1)S(1)} %later_planes.1), channel_id=1, source_target_pairs={{0,8},{2,10},{4,12},{6,14},{8,0},{10,2},{12,4},{14,6},{16,24},{18,... | collective-permute-start | bytes 245768 | tf_op jit(solution)/shard_map/later_planes/ppermute | solution.py:416
  39.2 13.6 %collective-permute-start.14 = (bf16[256,1024]{1,0:T(8,128)(2,1)S(1)}, bf16[256,1024]{1,0:T(8,128)(2,1)S(1)}, u32[]{:S(2)}, u32[]{:S(2)}) collective-permute-start(bf16[256,1024]{1,0:T(8,128)(2,1)S(1)} %get-tuple-element.57), channel_id=1, source_target_pairs={{0,1},{1,0},{2,3},{3,2},{4,5},{5,4},{6,7},{7,6},{8,9},{9,8},{10,11... | collective-permute-start | bytes 1572872 | tf_op jit(solution)/shard_map/attended/ppermute | solution.py:416
  44.3 2.2 %collective-permute-start.18 = (bf16[320,128]{1,0:T(8,128)(2,1)S(1)}, bf16[320,128]{1,0:T(8,128)(2,1)S(1)}, u32[]{:S(2)}, u32[]{:S(2)}) collective-permute-start(bf16[320,128]{1,0:T(8,128)(2,1)S(1)} %get-tuple-element.69), channel_id=1, source_target_pairs={{0,2},{2,0},{4,6},{6,4},{8,10},{10,8},{12,14},{14,12},{16,18},{18,... | collective-permute-start | bytes 245768 | tf_op jit(solution)/shard_map/later_back/ppermute | solution.py:416
  44.4 4.2 %collective-permute-start.20 = (bf16[320,128]{1,0:T(8,128)(2,1)S(1)}, bf16[320,128]{1,0:T(8,128)(2,1)S(1)}, u32[]{:S(2)}, u32[]{:S(2)}) collective-permute-start(bf16[320,128]{1,0:T(8,128)(2,1)S(1)} %get-tuple-element.67), channel_id=1, source_target_pairs={{0,6},{2,4},{4,2},{6,0},{8,14},{10,12},{12,10},{14,8},{16,22},{18,... | collective-permute-start | bytes 245768 | tf_op jit(solution)/shard_map/later_back/ppermute | solution.py:416
  45.6 5.4 %collective-permute-start.19 = (bf16[320,128]{1,0:T(8,128)(2,1)S(1)}, bf16[320,128]{1,0:T(8,128)(2,1)S(1)}, u32[]{:S(2)}, u32[]{:S(2)}) collective-permute-start(bf16[320,128]{1,0:T(8,128)(2,1)S(1)} %get-tuple-element.68), channel_id=1, source_target_pairs={{0,4},{2,6},{4,0},{6,2},{8,12},{10,14},{12,8},{14,10},{16,20},{18,... | collective-permute-start | bytes 245768 | tf_op jit(solution)/shard_map/later_back/ppermute | solution.py:416

commit v7 on v6

--- a/solution.py
+++ b/solution.py
@@ -12,6 +12,7 @@
 CONV = 3
 ROWS = 160
 VMEM_LIMIT = 14 * 1024 * 1024
+SPARE = 7
 PLANE = 4
 
 F32 = jnp.float32
@@ -165,21 +166,51 @@
 def norm_rows(norm):
     high = norm.astype(BF16).astype(F32)
     middle = (norm - high).astype(BF16).astype(F32)
-    rest = norm - high - middle
-    parts = (high, middle, rest)
-    tail = [x[:, VDIM:] for x in parts]
-    filler = jnp.zeros((norm.shape[0], VDIM - 3 * (ROWS - VDIM)), F32)
-    tail = jnp.concatenate(tail + [filler], 1)
-    return jnp.concatenate([x[:, :VDIM] for x in parts] + [tail], 0)
-
-
-def norm_values(rows):
-    heads = rows.shape[0] // 4
-    extra = ROWS - VDIM
-    tail = rows[3 * heads :]
-    tail = tail[:, :extra] + tail[:, extra : 2 * extra] + tail[:, 2 * extra : 3 * extra]
-    main = rows[:heads] + rows[heads : 2 * heads] + rows[2 * heads : 3 * heads]
-    return jnp.concatenate([main, tail], 1)
+    parts = jnp.concatenate([high, middle, norm - high - middle], 0)
+    deep = parts.shape[0] // 4
+    tail = [parts[i * deep : (i + 1) * deep, VDIM:] for i in range(4)]
+    return jnp.concatenate([parts[:, :VDIM], jnp.concatenate(tail, 1)], 0)
+
+
+def norm_values(lines):
+    heads = lines.shape[0] * 4 // 15
+    wide = ROWS - VDIM
+    tail = [lines[3 * heads :, i * wide : (i + 1) * wide] for i in range(4)]
+    parts = jnp.concatenate([lines[: 3 * heads], jnp.concatenate(tail, 0)], 1)
+    return parts[:heads] + parts[heads : 2 * heads] + parts[2 * heads :]
+
+
+def with_lines(state, lines, rows):
+    pieces, used = [], 0
+    for first in range(0, state.shape[0], ROWS):
+        free = min(SPARE, lines.shape[0] - used)
+        last = jnp.concatenate(
+            [
+                state[first + ROWS - SPARE - 1 : first + ROWS - SPARE],
+                lines[used : used + free],
+                jnp.zeros((SPARE - free, VDIM), F32),
+            ][: 3 if free < SPARE else 2],
+            0,
+        )
+        pieces += [state[first : first + ROWS - SPARE - 1], last]
+        used += free
+    left = rows - state.shape[0]
+    blank = left - (lines.shape[0] - used)
+    if left > 0:
+        pieces.append(lines[used:])
+        if blank > 0:
+            pieces.append(jnp.zeros((blank, VDIM), F32))
+    return jnp.concatenate(pieces, 0)
+
+
+def lines_in(state, piece_rows):
+    count = 15 * (piece_rows // ROWS * PLANE) // 4
+    found, used = [], 0
+    for first in range(0, piece_rows, ROWS):
+        free = min(SPARE, count - used)
+        found.append(state[first + ROWS - SPARE : first + ROWS - SPARE + free])
+        used += free
+    return jnp.concatenate(found + [state[piece_rows : piece_rows + count - used]], 0)
 
 
 def key_kernel(
@@ -214,13 +245,15 @@
         vc_ref[:, at : at + VDIM] = value
         feat = kf_ref[head]
         norm = jnp.where(row == head, mm(ones, feat, NT), norm)
-        store_piece(rank, head, per_piece, mm(feat, value, NN), slots, send_ref)
+        first = (head % per_piece) * ROWS
+        slots[rank ^ (head // per_piece), first : first + ROWS, :] = mm(feat, value, NN)
     lines = norm_rows(norm)
-    at = per_piece * ROWS
-    own_ref[:at, :] = slots[0]
-    own_ref[at:, :] = lines
     for slot in range(PLANE):
-        send_ref[slot, at:, :] = lines.astype(BF16)
+        piece = with_lines(slots[slot], lines, own_ref.shape[0])
+        if slot == 0:
+            own_ref[...] = piece
+        else:
+            send_ref[slot] = piece.astype(BF16)
 
 
 def share_kernel(norm_at, own_ref, *refs):
@@ -230,8 +263,8 @@
     for got_ref in got_refs:
         total = total + got_ref[...].astype(F32)
     if norm_at is not None:
-        lines = norm_rows(norm_values(total[norm_at:]))
-        total = jnp.concatenate([total[:norm_at], lines], 0)
+        lines = norm_rows(norm_values(lines_in(total, norm_at)))
+        total = with_lines(total[:norm_at], lines, total.shape[0])
     sent_ref[...] = total.astype(BF16)
     if sent_at == -2:
         refs[-1][...] = total
@@ -258,7 +291,7 @@
             if i != slot:
                 total = total + masked(is_ahead(rank ^ i, rank ^ slot), got_refs[i][...])
         pieces_ref[slot] = total[:rows].astype(BF16)
-        extra = total[rows:] if slot == 0 else extra
+        extra = total if slot == 0 else extra
     return extra
 
 
@@ -287,7 +320,7 @@
     heads = qd_ref.shape[0]
     per_piece = heads // PLANE
     lines = store_pieces(1, strides, refs[:PLANE], refs[PLANE:], pieces_ref)
-    norm = norm_values(lines)
+    norm = norm_values(lines_in(lines, pieces_ref.shape[1]))
     high = norm.astype(BF16).astype(F32)
     middle = (norm - high).astype(BF16).astype(F32)
     rest = norm - high - middle
@@ -428,7 +461,8 @@
     columns = cotangent.shape[1]
     groups = lax.axis_size("head")
     piece_rows = heads // PLANE * ROWS
-    message = (piece_rows + 4 * heads, VDIM)
+    extra = max(0, 15 * heads // 4 - SPARE * heads // PLANE)
+    message = (piece_rows + -(-extra // 16) * 16, VDIM)
     S = jax.ShapeDtypeStruct
     step = 2 * tokens * ROWS * VDIM * heads
     project_flops = 2 * tokens * width * columns
@@ -467,7 +501,7 @@
         ops = (*near_by[:2], before, *near_by[2:])
         kf, vc, own, send = call(key_kernel, ops, outs, step, scratch=[slots])
     with jax.named_scope("cotangent"):
-        cots = [swapped(after(cotangent, send), "head", j) for j in range(1, groups)]
+        cots = [swapped(after(cotangent, last_rows), "head", j) for j in range(1, groups)]
     with jax.named_scope("prior_share"):
         got = [swapped(send[j], "ctx", j) for j in range(1, PLANE)]
 

time: 53.9 us -> 53.3 us (0.989)
  waiting for transfers between devices: 20.7 us -> 18.6 us
  starting transfers between devices: 20.2 us -> 21.5 us
    ppermute x1, waiting for transfers between devices: 5.12 us -> 2.55 us  [per_device(): lax.ppermute(last_rows, 'ctx', [(i, (i + 1) % slabs) for i in range(slabs)])]
    ppermute x20, starting transfers between devices: 19.7 us -> 21 us  [swapped(): return lax.ppermute(x, axis, pairs)]
  transfers between devices with their start and end apart: 21 -> 21, of which waited for: 11 -> 12; matrix products, arithmetic and copies ran while one was open for 0% -> 0% of each run, Pallas kernels for 15% -> 17%
where the time goes in v7:
time: 53.3 us; the launch traced here: 53.1 us
  starting transfers between devices  21.5 us (40%)
  waiting for transfers between devices  18.6 us (35%)
  Pallas kernels  11.9 us (22%)
  between operations  0.82 us (2%)
    ppermute x20, starting transfers between devices, swapped(): return lax.ppermute(x, axis, pairs)  21 us
    ppermute x20, waiting for transfers between devices, swapped(): return lax.ppermute(x, axis, pairs)  16.1 us
    pallas_call x15, Pallas kernels, call(): pl.pallas_call(body, out_shape=out_shape, in_specs=[hbm if i in far else...  11.1 us
    ppermute x1, waiting for transfers between devices, per_device(): lax.ppermute(last_rows, 'ctx', [(i, (i + 1) % slabs) for i in range(slabs)])  2.55 us
  transfers between devices with their start and end apart: 21, of which 12 were waited for; matrix products, arithmetic and copies ran while one was open for 0% of the time, Pallas kernels for 17%

profile of v7, /device:TPU:0, one launch (start us, length us, event | category | flops | bytes accessed | tf_op | source)
XLA Modules:
  0.0 53.1 jit_solution(964758761065945969)
XLA Ops:
  0.6 0.8 %edge.1 = bf16[2,1152]{1,0:T(2,128)(2,1)S(1)} custom-call(bf16[256,128]{1,0:T(8,128)(2,1)} %k_far.3, bf16[256,1024]{1,0:T(8,128)(2,1)} %v_far.3), custom_call_target="tpu_custom_call" | custom-call | tf_op jit(solution)/shard_map/edge/pallas_call | solution.py:474
  1.4 0.5 collective-permute-start
  1.9 2.6 %collective-permute-start.4 = (bf16[256,1024]{1,0:T(8,128)(2,1)}, bf16[256,1024]{1,0:T(8,128)(2,1)S(1)}, u32[]{:S(2)}, u32[]{:S(2)}) collective-permute-start(bf16[256,1024]{1,0:T(8,128)(2,1)} %refs_0_), channel_id=1, source_target_pairs={{0,1},{1,0},{2,3},{3,2},{4,5},{5,4},{6,7},{7,6},{8,9},{9,8},{10,11... | collective-permute-start | bytes 1572872 | tf_op jit(solution)/shard_map/cotangent/ppermute | solution.py:449
  4.5 1.2 %query_features.1 = (bf16[8,160,256]{2,1,0:T(8,128)(2,1)S(1)}, bf16[256,128]{1,0:T(8,128)(2,1)S(1)}, bf16[256,1024]{1,0:T(8,128)(2,1)S(1)}, f32[3,128]{1,0:T(4,128)S(1)}, f32[3,1024]{1,0:T(4,128)S(1)}) custom-call(bf16[256,128]{1,0:T(8,128)(2,1)} %q_far, bf16[256,128]{1,0:T(8,128)(2,1)} %k_far.3, bf16[256,1024]{1,0:T(8,128)(2,1)} %v_far.3, f32[3,128]{1,0:T(4,128)} %ck_far.1, ...), custom_call_target="tpu_custom_call" | custom-call | flops 1048576 | bytes 1928192 | tf_op jit(solution)/shard_map/query_features/pallas_call | solution.py:34
  5.7 2.6 %collective-permute-done.before_ref = bf16[2,1152]{1,0:T(2,128)(2,1)S(1)} collective-permute-done((bf16[2,1152]{1,0:T(2,128)(2,1)S(1)}, bf16[2,1152]{1,0:T(2,128)(2,1)S(1)}, u32[]{:S(2)}, u32[]{:S(2)}) %collective-permute-start) | collective-permute-done | bytes 4640 | tf_op jit(solution)/shard_map/edge/ppermute | solution.py:483
  8.2 0.9 %key_features.1 = (bf16[8,160,256]{2,1,0:T(8,128)(2,1)S(1)}, bf16[256,1024]{1,0:T(8,128)(2,1)S(1)}, f32[336,128]{1,0:T(8,128)S(1)}, bf16[4,336,128]{2,1,0:T(8,128)(2,1)S(1)}) custom-call(bf16[256,128]{1,0:T(8,128)(2,1)S(1)} %get-tuple-element.35.k_ref, bf16[256,1024]{1,0:T(8,128)(2,1)S(1)} %get-tuple-element.36.v_ref, ...), custom_call_target="tpu_custom_call" | custom-call | flops 83886080 | bytes 2304000 | tf_op jit(solution)/shard_map/key_features/pallas_call | solution.py:34
  9.2 0.1 collective-permute-start.3
  9.3 0.4 collective-permute-start.2
  9.6 1.5 %collective-permute-start.1 = (bf16[336,128]{1,0:T(8,128)(2,1)S(1)}, bf16[336,128]{1,0:T(8,128)(2,1)S(1)}, u32[]{:S(2)}, u32[]{:S(2)}) collective-permute-start(bf16[336,128]{1,0:T(8,128)(2,1)S(1)} %get-tuple-element.66), channel_id=1, source_target_pairs={{0,2},{2,0},{4,6},{6,4},{8,10},{10,8},{12,14},{14,12},{16,18},{18,... | collective-permute-start | bytes 258056 | tf_op jit(solution)/shard_map/prior_share/ppermute | solution.py:449
  11.1 0.0 copy-start
  11.1 0.0 copy-start.1
  11.1 1.2 %scores.1 = (bf16[8,256,256]{2,1,0:T(8,128)(2,1)S(1)}, f32[8,256]{1,0:T(8,128)S(1)}, f32[256,1024]{1,0:T(8,128)S(1)}) custom-call(bf16[8,160,256]{2,1,0:T(8,128)(2,1)S(1)} %get-tuple-element.45.qd_ref, bf16[8,160,256]{2,1,0:T(8,128)(2,1)S(1)} %get-tuple-element.41.kf_ref, bf16[256,1024]{1,0:T(8,128)(2,1)S(1)} %get-tuple-element.42.vc_ref), custom_call_target="tpu_custom_call" | custom-call | flops 33554432000 | bytes 3940352 | tf_op jit(solution)/shard_map/scores/pallas_call | solution.py:34
  12.3 1.2 %collective-permute-done.3.refs_2_.refs_3_ = bf16[336,128]{1,0:T(8,128)(2,1)S(1)} collective-permute-done((bf16[336,128]{1,0:T(8,128)(2,1)S(1)}, bf16[336,128]{1,0:T(8,128)(2,1)S(1)}, u32[]{:S(2)}, u32[]{:S(2)}) %collective-permute-start.3) | collective-permute-done | bytes 86048 | tf_op jit(solution)/shard_map/prior_share/ppermute | solution.py:449
  13.5 1.2 %collective-permute-done.2.refs_1_.refs_2_ = bf16[336,128]{1,0:T(8,128)(2,1)S(1)} collective-permute-done((bf16[336,128]{1,0:T(8,128)(2,1)S(1)}, bf16[336,128]{1,0:T(8,128)(2,1)S(1)}, u32[]{:S(2)}, u32[]{:S(2)}) %collective-permute-start.2) | collective-permute-done | bytes 86048 | tf_op jit(solution)/shard_map/prior_share/ppermute | solution.py:449
  14.7 0.0 collective-permute-done.1.refs_0_.refs_1_
  14.7 0.2 prior_share.1
  14.9 3.5 %collective-permute-start.7 = (bf16[336,128]{1,0:T(8,128)(2,1)S(1)}, bf16[336,128]{1,0:T(8,128)(2,1)S(1)}, u32[]{:S(2)}, u32[]{:S(2)}) collective-permute-start(bf16[336,128]{1,0:T(8,128)(2,1)S(1)} %prior_share.1), channel_id=1, source_target_pairs={{0,24},{2,26},{4,28},{6,30},{8,16},{10,18},{12,20},{14,22},{16,8},... | collective-permute-start | bytes 258056 | tf_op jit(solution)/shard_map/prior_planes/ppermute | solution.py:449
  18.4 0.0 collective-permute-start.6
  18.4 0.9 %collective-permute-start.5 = (bf16[336,128]{1,0:T(8,128)(2,1)S(1)}, bf16[336,128]{1,0:T(8,128)(2,1)S(1)}, u32[]{:S(2)}, u32[]{:S(2)}) collective-permute-start(bf16[336,128]{1,0:T(8,128)(2,1)S(1)} %prior_share.1), channel_id=1, source_target_pairs={{0,8},{2,10},{4,12},{6,14},{8,0},{10,2},{12,4},{14,6},{16,24},{18,... | collective-permute-start | bytes 258056 | tf_op jit(solution)/shard_map/prior_planes/ppermute | solution.py:449
  19.3 0.6 %turned.1 = (bf16[8,256,160]{2,1,0:T(8,128)(2,1)S(1)}, bf16[8,256,160]{2,1,0:T(8,128)(2,1)S(1)}) custom-call(bf16[8,160,256]{2,1,0:T(8,128)(2,1)S(1)} %get-tuple-element.45.qd_ref, bf16[8,160,256]{2,1,0:T(8,128)(2,1)S(1)} %get-tuple-element.41.kf_ref), custom_call_target="tpu_custom_call" | custom-call | flops 4194304 | bytes 2621440 | tf_op jit(solution)/shard_map/turned/pallas_call | solution.py:34
  19.9 0.0 collective-permute-done.4.refs_1_
  19.9 0.0 copy-done
  19.9 0.0 copy-done.1
  19.9 1.3 %out_grad.1.og_ref = f32[256,1024]{1,0:T(8,128)S(1)} custom-call(bf16[256,1024]{1,0:T(8,128)(2,1)S(1)} %copy-done.1, bf16[256,1024]{1,0:T(8,128)(2,1)S(1)} %collective-permute-done.4.refs_1_, bf16[1024,2048]{1,0:T(8,128)(2,1)S(1)} %copy-done), custom_call_target="tpu_custom_call" | custom-call | flops 1073741824 | bytes 6291456 | tf_op jit(solution)/shard_map/out_grad/pallas_call | solution.py:34
  21.2 0.9 %collective-permute-done.7.refs_6_ = bf16[336,128]{1,0:T(8,128)(2,1)S(1)} collective-permute-done((bf16[336,128]{1,0:T(8,128)(2,1)S(1)}, bf16[336,128]{1,0:T(8,128)(2,1)S(1)}, u32[]{:S(2)}, u32[]{:S(2)}) %collective-permute-start.7) | collective-permute-done | bytes 86048 | tf_op jit(solution)/shard_map/prior_planes/ppermute | solution.py:449
  22.1 3.7 %collective-permute-done.6.refs_5_ = bf16[336,128]{1,0:T(8,128)(2,1)S(1)} collective-permute-done((bf16[336,128]{1,0:T(8,128)(2,1)S(1)}, bf16[336,128]{1,0:T(8,128)(2,1)S(1)}, u32[]{:S(2)}, u32[]{:S(2)}) %collective-permute-start.6) | collective-permute-done | bytes 86048 | tf_op jit(solution)/shard_map/prior_planes/ppermute | solution.py:449
  25.8 0.0 collective-permute-done.5.refs_4_
  25.8 1.3 %scaled_grad.1 = (bf16[4,320,128]{2,1,0:T(8,128)(2,1)S(1)}, f32[256,8]{1,0:T(8,128)S(1)}, bf16[256,1024]{1,0:T(8,128)(2,1)S(1)}, f32[320,128]{1,0:T(8,128)S(1)}, bf16[4,320,128]{2,1,0:T(8,128)(2,1)S(1)}) custom-call(f32[8,256]{1,0:T(8,128)S(1)} %get-tuple-element.43.den_ref, bf16[8,160,256]{2,1,0:T(8,128)(2,1)S(1)} %get-tuple-element.45.qd_ref, ...), custom_call_target="tpu_custom_call" | custom-call | flops 83886080 | bytes 3751936 | tf_op jit(solution)/shard_map/scaled_grad/pallas_call | solution.py:34
  27.1 0.1 collective-permute-start.13
  27.2 1.4 %collective-permute-start.12 = (bf16[320,128]{1,0:T(8,128)(2,1)S(1)}, bf16[320,128]{1,0:T(8,128)(2,1)S(1)}, u32[]{:S(2)}, u32[]{:S(2)}) collective-permute-start(bf16[320,128]{1,0:T(8,128)(2,1)S(1)} %get-tuple-element.72), channel_id=1, source_target_pairs={{0,4},{2,6},{4,0},{6,2},{8,12},{10,14},{12,8},{14,10},{16,20},{18,... | collective-permute-start | bytes 245768 | tf_op jit(solution)/shard_map/later_share/ppermute | solution.py:449
  28.5 0.5 collective-permute-start.11
  29.1 0.5 collective-permute-start.10
  29.6 1.2 %collective-permute-start.9 = (bf16[320,128]{1,0:T(8,128)(2,1)S(1)}, bf16[320,128]{1,0:T(8,128)(2,1)S(1)}, u32[]{:S(2)}, u32[]{:S(2)}) collective-permute-start(bf16[320,128]{1,0:T(8,128)(2,1)S(1)} %get-tuple-element.76), channel_id=1, source_target_pairs={{0,4},{2,6},{4,0},{6,2},{8,12},{10,14},{12,8},{14,10},{16,20},{18,... | collective-permute-start | bytes 245768 | tf_op jit(solution)/shard_map/scaled_grad/ppermute | solution.py:449
  30.8 1.1 %collective-permute-done.13.refs_2_.refs_3_ = bf16[320,128]{1,0:T(8,128)(2,1)S(1)} collective-permute-done((bf16[320,128]{1,0:T(8,128)(2,1)S(1)}, bf16[320,128]{1,0:T(8,128)(2,1)S(1)}, u32[]{:S(2)}, u32[]{:S(2)}) %collective-permute-start.13) | collective-permute-done | bytes 81952 | tf_op jit(solution)/shard_map/later_share/ppermute | solution.py:449
  31.9 0.0 collective-permute-start.8
  31.9 1.6 %collective-permute-done.12.refs_1_.refs_2_ = bf16[320,128]{1,0:T(8,128)(2,1)S(1)} collective-permute-done((bf16[320,128]{1,0:T(8,128)(2,1)S(1)}, bf16[320,128]{1,0:T(8,128)(2,1)S(1)}, u32[]{:S(2)}, u32[]{:S(2)}) %collective-permute-start.12) | collective-permute-done | bytes 81952 | tf_op jit(solution)/shard_map/later_share/ppermute | solution.py:449
  33.5 0.0 collective-permute-done.11.refs_0_.refs_1_
  33.5 2.4 %collective-permute-start.17 = (bf16[320,128]{1,0:T(8,128)(2,1)S(1)}, bf16[320,128]{1,0:T(8,128)(2,1)S(1)}, u32[]{:S(2)}, u32[]{:S(2)}) collective-permute-start(bf16[320,128]{1,0:T(8,128)(2,1)S(1)} %later_planes.1), channel_id=1, source_target_pairs={{0,24},{2,26},{4,28},{6,30},{8,16},{10,18},{12,20},{14,22},{16,8},... | collective-permute-start | bytes 245768 | tf_op jit(solution)/shard_map/later_planes/ppermute | solution.py:449
  36.0 0.0 collective-permute-start.16
  36.0 0.0 collective-permute-done.10
  36.0 2.0 %collective-permute-start.15 = (bf16[320,128]{1,0:T(8,128)(2,1)S(1)}, bf16[320,128]{1,0:T(8,128)(2,1)S(1)}, u32[]{:S(2)}, u32[]{:S(2)}) collective-permute-start(bf16[320,128]{1,0:T(8,128)(2,1)S(1)} %later_planes.1), channel_id=1, source_target_pairs={{0,8},{2,10},{4,12},{6,14},{8,0},{10,2},{12,4},{14,6},{16,24},{18,... | collective-permute-start | bytes 245768 | tf_op jit(solution)/shard_map/later_planes/ppermute | solution.py:449
  38.0 0.0 collective-permute-done.9
  38.0 0.0 collective-permute-done.8
  38.1 1.0 %attended.1 = (bf16[256,1024]{1,0:T(8,128)(2,1)S(1)}, bf16[256,1024]{1,0:T(8,128)(2,1)S(1)}) custom-call(bf16[8,256,160]{2,1,0:T(8,128)(2,1)S(1)} %get-tuple-element.46.qt_ref, bf16[4,320,128]{2,1,0:T(8,128)(2,1)S(1)} %pad_maximum_fusion.prior_ref, f32[256,1024]{1,0:T(8,128)S(1)} %get-tuple-element.53.num_ref, f32[256,8]{1,0:T(8,128)S(1)} %get-tuple-element.54.inv_ref, ...), custom_call_target="tpu_custom_call" | custom-call | flops 620756992 | bytes 7282688 | tf_op jit(solution)/shard_map/attended/pallas_call | solution.py:34
  39.0 1.9 %collective-permute-start.14 = (bf16[256,1024]{1,0:T(8,128)(2,1)S(1)}, bf16[256,1024]{1,0:T(8,128)(2,1)S(1)}, u32[]{:S(2)}, u32[]{:S(2)}) collective-permute-start(bf16[256,1024]{1,0:T(8,128)(2,1)S(1)} %get-tuple-element.57), channel_id=1, source_target_pairs={{0,1},{1,0},{2,3},{3,2},{4,5},{5,4},{6,7},{7,6},{8,9},{9,8},{10,11... | collective-permute-start | bytes 1572872 | tf_op jit(solution)/shard_map/attended/ppermute | solution.py:449
  40.9 0.4 near.1.near_ref
  41.3 0.7 %mixed.1.part_ref = f32[256,1024]{1,0:T(8,128)S(1)} custom-call(bf16[256,1024]{1,0:T(8,128)(2,1)S(1)} %get-tuple-element.56.att_ref, bf16[1024,2048]{1,0:T(8,128)(2,1)S(1)} %copy-done), custom_call_target="tpu_custom_call" | custom-call | flops 1073741824 | bytes 5767168 | tf_op jit(solution)/shard_map/mixed/pallas_call | solution.py:34
  42.0 0.4 collective-permute-done.15.refs_4_
  42.5 0.0 collective-permute-done.17.refs_6_
  42.5 0.9 %collective-permute-done.16.refs_5_ = bf16[320,128]{1,0:T(8,128)(2,1)S(1)} collective-permute-done((bf16[320,128]{1,0:T(8,128)(2,1)S(1)}, bf16[320,128]{1,0:T(8,128)(2,1)S(1)}, u32[]{:S(2)}, u32[]{:S(2)}) %collective-permute-start.16) | collective-permute-done | bytes 81952 | tf_op jit(solution)/shard_map/later_planes/ppermute | solution.py:449
  43.4 0.2 later_back.1
  43.7 0.1 collective-permute-start.18
  43.7 0.8 %collective-permute-start.20 = (bf16[320,128]{1,0:T(8,128)(2,1)S(1)}, bf16[320,128]{1,0:T(8,128)(2,1)S(1)}, u32[]{:S(2)}, u32[]{:S(2)}) collective-permute-start(bf16[320,128]{1,0:T(8,128)(2,1)S(1)} %get-tuple-element.67), channel_id=1, source_target_pairs={{0,6},{2,4},{4,2},{6,0},{8,14},{10,12},{12,10},{14,8},{16,22},{18,... | collective-permute-start | bytes 245768 | tf_op jit(solution)/shard_map/later_back/ppermute | solution.py:449
  44.6 1.3 %collective-permute-start.19 = (bf16[320,128]{1,0:T(8,128)(2,1)S(1)}, bf16[320,128]{1,0:T(8,128)(2,1)S(1)}, u32[]{:S(2)}, u32[]{:S(2)}) collective-permute-start(bf16[320,128]{1,0:T(8,128)(2,1)S(1)} %get-tuple-element.68), channel_id=1, source_target_pairs={{0,4},{2,6},{4,0},{6,2},{8,12},{10,14},{12,8},{14,10},{16,20},{18,... | collective-permute-start | bytes 245768 | tf_op jit(solution)/shard_map/later_back/ppermute | solution.py:449
  45.9 0.0 collective-permute-done.18.refs_1_
  45.9 0.3 far_grad.2.early_ref
  46.2 1.8 %collective-permute-done.20.refs_1_ = bf16[320,128]{1,0:T(8,128)(2,1)S(1)} collective-permute-done((bf16[320,128]{1,0:T(8,128)(2,1)S(1)}, bf16[320,128]{1,0:T(8,128)(2,1)S(1)}, u32[]{:S(2)}, u32[]{:S(2)}) %collective-permute-start.20) | collective-permute-done | bytes 81952 | tf_op jit(solution)/shard_map/later_back/ppermute | solution.py:449
  48.0 2.3 %collective-permute-done.19.refs_0_ = bf16[320,128]{1,0:T(8,128)(2,1)S(1)} collective-permute-done((bf16[320,128]{1,0:T(8,128)(2,1)S(1)}, bf16[320,128]{1,0:T(8,128)(2,1)S(1)}, u32[]{:S(2)}, u32[]{:S(2)}) %collective-permute-start.19) | collective-permute-done | bytes 81952 | tf_op jit(solution)/shard_map/later_back/ppermute | solution.py:449
  50.3 1.0 %far_grad.3 = bf16[256,1024]{1,0:T(8,128)(2,1)} custom-call(bf16[8,256,160]{2,1,0:T(8,128)(2,1)S(1)} %get-tuple-element.58.kt_ref, f32[256,1024]{1,0:T(8,128)S(1)} %near.1.near_ref, bf16[2,256,256]{2,1,0:T(8,128)(2,1)S(1)} %far_grad.2.early_ref, bf16[320,128]{1,0:T(8,128)(2,1)S(1)} %collective-permute-done.19.refs_0_, ...), custom_call_target="tpu_custom_call" | custom-call | flops 1342177280 | bytes 2654208 | tf_op jit(solution)/shard_map/far_grad/pallas_call | solution.py:34
  51.3 0.9 %collective-permute-done.14.refs_0_ = bf16[256,1024]{1,0:T(8,128)(2,1)S(1)} collective-permute-done((bf16[256,1024]{1,0:T(8,128)(2,1)S(1)}, bf16[256,1024]{1,0:T(8,128)(2,1)S(1)}, u32[]{:S(2)}, u32[]{:S(2)}) %collective-permute-start.14) | collective-permute-done | bytes 524320 | tf_op jit(solution)/shard_map/attended/ppermute | solution.py:449
  52.2 0.8 %mixed_out.1 = bf16[256,1024]{1,0:T(8,128)(2,1)} custom-call(f32[256,1024]{1,0:T(8,128)S(1)} %mixed.1.part_ref, bf16[256,1024]{1,0:T(8,128)(2,1)S(1)} %collective-permute-done.14.refs_0_), custom_call_target="tpu_custom_call" | custom-call | flops 1048576 | bytes 2097152 | tf_op jit(solution)/shard_map/mixed_out/pallas_call | solution.py:34
  (6 shorter events, 0.2 us)
Async XLA Ops:
  1.4 6.8 %collective-permute-start = (bf16[2,1152]{1,0:T(2,128)(2,1)S(1)}, bf16[2,1152]{1,0:T(2,128)(2,1)S(1)}, u32[]{:S(2)}, u32[]{:S(2)}) collective-permute-start(bf16[2,1152]{1,0:T(2,128)(2,1)S(1)} %edge.1), channel_id=1, source_target_pairs={{0,2},{2,4},{4,6},{6,8},{8,10},{10,12},{12,14},{14,16},{16,18},{18... | collective-permute-start | bytes 13832 | tf_op jit(solution)/shard_map/edge/ppermute | solution.py:483
  1.9 18.0 %collective-permute-start.4 = (bf16[256,1024]{1,0:T(8,128)(2,1)}, bf16[256,1024]{1,0:T(8,128)(2,1)S(1)}, u32[]{:S(2)}, u32[]{:S(2)}) collective-permute-start(bf16[256,1024]{1,0:T(8,128)(2,1)} %refs_0_), channel_id=1, source_target_pairs={{0,1},{1,0},{2,3},{3,2},{4,5},{5,4},{6,7},{7,6},{8,9},{9,8},{10,11... | collective-permute-start | bytes 1572872 | tf_op jit(solution)/shard_map/cotangent/ppermute | solution.py:449
  9.2 4.3 %collective-permute-start.3 = (bf16[336,128]{1,0:T(8,128)(2,1)S(1)}, bf16[336,128]{1,0:T(8,128)(2,1)S(1)}, u32[]{:S(2)}, u32[]{:S(2)}) collective-permute-start(bf16[336,128]{1,0:T(8,128)(2,1)S(1)} %get-tuple-element.64), channel_id=1, source_target_pairs={{0,6},{2,4},{4,2},{6,0},{8,14},{10,12},{12,10},{14,8},{16,22},{18,... | collective-permute-start | bytes 258056 | tf_op jit(solution)/shard_map/prior_share/ppermute | solution.py:449
  9.3 5.4 %collective-permute-start.2 = (bf16[336,128]{1,0:T(8,128)(2,1)S(1)}, bf16[336,128]{1,0:T(8,128)(2,1)S(1)}, u32[]{:S(2)}, u32[]{:S(2)}) collective-permute-start(bf16[336,128]{1,0:T(8,128)(2,1)S(1)} %get-tuple-element.65), channel_id=1, source_target_pairs={{0,4},{2,6},{4,0},{6,2},{8,12},{10,14},{12,8},{14,10},{16,20},{18,... | collective-permute-start | bytes 258056 | tf_op jit(solution)/shard_map/prior_share/ppermute | solution.py:449
  9.6 5.1 %collective-permute-start.1 = (bf16[336,128]{1,0:T(8,128)(2,1)S(1)}, bf16[336,128]{1,0:T(8,128)(2,1)S(1)}, u32[]{:S(2)}, u32[]{:S(2)}) collective-permute-start(bf16[336,128]{1,0:T(8,128)(2,1)S(1)} %get-tuple-element.66), channel_id=1, source_target_pairs={{0,2},{2,0},{4,6},{6,4},{8,10},{10,8},{12,14},{14,12},{16,18},{18,... | collective-permute-start | bytes 258056 | tf_op jit(solution)/shard_map/prior_share/ppermute | solution.py:449
  11.1 8.8 %copy-start = (bf16[1024,2048]{1,0:T(8,128)(2,1)S(1)}, bf16[1024,2048]{1,0:T(8,128)(2,1)}, u32[]{:S(2)}) copy-start(bf16[1024,2048]{1,0:T(8,128)(2,1)} %w_ref.3) | copy-start | bytes 12582916
  11.1 8.8 %copy-start.1 = (bf16[256,1024]{1,0:T(8,128)(2,1)S(1)}, bf16[256,1024]{1,0:T(8,128)(2,1)}, u32[]{:S(2)}) copy-start(bf16[256,1024]{1,0:T(8,128)(2,1)} %refs_0_) | copy-start | bytes 1572868
  14.9 7.2 %collective-permute-start.7 = (bf16[336,128]{1,0:T(8,128)(2,1)S(1)}, bf16[336,128]{1,0:T(8,128)(2,1)S(1)}, u32[]{:S(2)}, u32[]{:S(2)}) collective-permute-start(bf16[336,128]{1,0:T(8,128)(2,1)S(1)} %prior_share.1), channel_id=1, source_target_pairs={{0,24},{2,26},{4,28},{6,30},{8,16},{10,18},{12,20},{14,22},{16,8},... | collective-permute-start | bytes 258056 | tf_op jit(solution)/shard_map/prior_planes/ppermute | solution.py:449
  18.4 7.4 %collective-permute-start.6 = (bf16[336,128]{1,0:T(8,128)(2,1)S(1)}, bf16[336,128]{1,0:T(8,128)(2,1)S(1)}, u32[]{:S(2)}, u32[]{:S(2)}) collective-permute-start(bf16[336,128]{1,0:T(8,128)(2,1)S(1)} %prior_share.1), channel_id=1, source_target_pairs={{0,16},{2,18},{4,20},{6,22},{8,24},{10,26},{12,28},{14,30},{16,0},... | collective-permute-start | bytes 258056 | tf_op jit(solution)/shard_map/prior_planes/ppermute | solution.py:449
  18.4 7.4 %collective-permute-start.5 = (bf16[336,128]{1,0:T(8,128)(2,1)S(1)}, bf16[336,128]{1,0:T(8,128)(2,1)S(1)}, u32[]{:S(2)}, u32[]{:S(2)}) collective-permute-start(bf16[336,128]{1,0:T(8,128)(2,1)S(1)} %prior_share.1), channel_id=1, source_target_pairs={{0,8},{2,10},{4,12},{6,14},{8,0},{10,2},{12,4},{14,6},{16,24},{18,... | collective-permute-start | bytes 258056 | tf_op jit(solution)/shard_map/prior_planes/ppermute | solution.py:449
  27.1 4.8 %collective-permute-start.13 = (bf16[320,128]{1,0:T(8,128)(2,1)S(1)}, bf16[320,128]{1,0:T(8,128)(2,1)S(1)}, u32[]{:S(2)}, u32[]{:S(2)}) collective-permute-start(bf16[320,128]{1,0:T(8,128)(2,1)S(1)} %get-tuple-element.71), channel_id=1, source_target_pairs={{0,6},{2,4},{4,2},{6,0},{8,14},{10,12},{12,10},{14,8},{16,22},{18,... | collective-permute-start | bytes 245768 | tf_op jit(solution)/shard_map/later_share/ppermute | solution.py:449
  27.2 6.3 %collective-permute-start.12 = (bf16[320,128]{1,0:T(8,128)(2,1)S(1)}, bf16[320,128]{1,0:T(8,128)(2,1)S(1)}, u32[]{:S(2)}, u32[]{:S(2)}) collective-permute-start(bf16[320,128]{1,0:T(8,128)(2,1)S(1)} %get-tuple-element.72), channel_id=1, source_target_pairs={{0,4},{2,6},{4,0},{6,2},{8,12},{10,14},{12,8},{14,10},{16,20},{18,... | collective-permute-start | bytes 245768 | tf_op jit(solution)/shard_map/later_share/ppermute | solution.py:449
  28.5 5.0 %collective-permute-start.11 = (bf16[320,128]{1,0:T(8,128)(2,1)S(1)}, bf16[320,128]{1,0:T(8,128)(2,1)S(1)}, u32[]{:S(2)}, u32[]{:S(2)}) collective-permute-start(bf16[320,128]{1,0:T(8,128)(2,1)S(1)} %get-tuple-element.73), channel_id=1, source_target_pairs={{0,2},{2,0},{4,6},{6,4},{8,10},{10,8},{12,14},{14,12},{16,18},{18,... | collective-permute-start | bytes 245768 | tf_op jit(solution)/shard_map/later_share/ppermute | solution.py:449
  29.1 6.9 %collective-permute-start.10 = (bf16[320,128]{1,0:T(8,128)(2,1)S(1)}, bf16[320,128]{1,0:T(8,128)(2,1)S(1)}, u32[]{:S(2)}, u32[]{:S(2)}) collective-permute-start(bf16[320,128]{1,0:T(8,128)(2,1)S(1)} %get-tuple-element.75), channel_id=1, source_target_pairs={{0,6},{2,4},{4,2},{6,0},{8,14},{10,12},{12,10},{14,8},{16,22},{18,... | collective-permute-start | bytes 245768 | tf_op jit(solution)/shard_map/scaled_grad/ppermute | solution.py:449
  29.6 8.4 %collective-permute-start.9 = (bf16[320,128]{1,0:T(8,128)(2,1)S(1)}, bf16[320,128]{1,0:T(8,128)(2,1)S(1)}, u32[]{:S(2)}, u32[]{:S(2)}) collective-permute-start(bf16[320,128]{1,0:T(8,128)(2,1)S(1)} %get-tuple-element.76), channel_id=1, source_target_pairs={{0,4},{2,6},{4,0},{6,2},{8,12},{10,14},{12,8},{14,10},{16,20},{18,... | collective-permute-start | bytes 245768 | tf_op jit(solution)/shard_map/scaled_grad/ppermute | solution.py:449
  31.9 6.1 %collective-permute-start.8 = (bf16[320,128]{1,0:T(8,128)(2,1)S(1)}, bf16[320,128]{1,0:T(8,128)(2,1)S(1)}, u32[]{:S(2)}, u32[]{:S(2)}) collective-permute-start(bf16[320,128]{1,0:T(8,128)(2,1)S(1)} %get-tuple-element.77), channel_id=1, source_target_pairs={{0,2},{2,0},{4,6},{6,4},{8,10},{10,8},{12,14},{14,12},{16,18},{18,... | collective-permute-start | bytes 245768 | tf_op jit(solution)/shard_map/scaled_grad/ppermute | solution.py:449
  33.5 8.9 %collective-permute-start.17 = (bf16[320,128]{1,0:T(8,128)(2,1)S(1)}, bf16[320,128]{1,0:T(8,128)(2,1)S(1)}, u32[]{:S(2)}, u32[]{:S(2)}) collective-permute-start(bf16[320,128]{1,0:T(8,128)(2,1)S(1)} %later_planes.1), channel_id=1, source_target_pairs={{0,24},{2,26},{4,28},{6,30},{8,16},{10,18},{12,20},{14,22},{16,8},... | collective-permute-start | bytes 245768 | tf_op jit(solution)/shard_map/later_planes/ppermute | solution.py:449
  36.0 7.4 %collective-permute-start.16 = (bf16[320,128]{1,0:T(8,128)(2,1)S(1)}, bf16[320,128]{1,0:T(8,128)(2,1)S(1)}, u32[]{:S(2)}, u32[]{:S(2)}) collective-permute-start(bf16[320,128]{1,0:T(8,128)(2,1)S(1)} %later_planes.1), channel_id=1, source_target_pairs={{0,16},{2,18},{4,20},{6,22},{8,24},{10,26},{12,28},{14,30},{16,0},... | collective-permute-start | bytes 245768 | tf_op jit(solution)/shard_map/later_planes/ppermute | solution.py:449
  36.0 6.5 %collective-permute-start.15 = (bf16[320,128]{1,0:T(8,128)(2,1)S(1)}, bf16[320,128]{1,0:T(8,128)(2,1)S(1)}, u32[]{:S(2)}, u32[]{:S(2)}) collective-permute-start(bf16[320,128]{1,0:T(8,128)(2,1)S(1)} %later_planes.1), channel_id=1, source_target_pairs={{0,8},{2,10},{4,12},{6,14},{8,0},{10,2},{12,4},{14,6},{16,24},{18,... | collective-permute-start | bytes 245768 | tf_op jit(solution)/shard_map/later_planes/ppermute | solution.py:449
  39.0 13.2 %collective-permute-start.14 = (bf16[256,1024]{1,0:T(8,128)(2,1)S(1)}, bf16[256,1024]{1,0:T(8,128)(2,1)S(1)}, u32[]{:S(2)}, u32[]{:S(2)}) collective-permute-start(bf16[256,1024]{1,0:T(8,128)(2,1)S(1)} %get-tuple-element.57), channel_id=1, source_target_pairs={{0,1},{1,0},{2,3},{3,2},{4,5},{5,4},{6,7},{7,6},{8,9},{9,8},{10,11... | collective-permute-start | bytes 1572872 | tf_op jit(solution)/shard_map/attended/ppermute | solution.py:449
  43.7 2.2 %collective-permute-start.18 = (bf16[320,128]{1,0:T(8,128)(2,1)S(1)}, bf16[320,128]{1,0:T(8,128)(2,1)S(1)}, u32[]{:S(2)}, u32[]{:S(2)}) collective-permute-start(bf16[320,128]{1,0:T(8,128)(2,1)S(1)} %get-tuple-element.69), channel_id=1, source_target_pairs={{0,2},{2,0},{4,6},{6,4},{8,10},{10,8},{12,14},{14,12},{16,18},{18,... | collective-permute-start | bytes 245768 | tf_op jit(solution)/shard_map/later_back/ppermute | solution.py:449
  43.7 4.2 %collective-permute-start.20 = (bf16[320,128]{1,0:T(8,128)(2,1)S(1)}, bf16[320,128]{1,0:T(8,128)(2,1)S(1)}, u32[]{:S(2)}, u32[]{:S(2)}) collective-permute-start(bf16[320,128]{1,0:T(8,128)(2,1)S(1)} %get-tuple-element.67), channel_id=1, source_target_pairs={{0,6},{2,4},{4,2},{6,0},{8,14},{10,12},{12,10},{14,8},{16,22},{18,... | collective-permute-start | bytes 245768 | tf_op jit(solution)/shard_map/later_back/ppermute | solution.py:449
  44.6 5.7 %collective-permute-start.19 = (bf16[320,128]{1,0:T(8,128)(2,1)S(1)}, bf16[320,128]{1,0:T(8,128)(2,1)S(1)}, u32[]{:S(2)}, u32[]{:S(2)}) collective-permute-start(bf16[320,128]{1,0:T(8,128)(2,1)S(1)} %get-tuple-element.68), channel_id=1, source_target_pairs={{0,4},{2,6},{4,0},{6,2},{8,12},{10,14},{12,8},{14,10},{16,20},{18,... | collective-permute-start | bytes 245768 | tf_op jit(solution)/shard_map/later_back/ppermute | solution.py:449

commit v8 on v7

--- a/solution.py
+++ b/solution.py
@@ -208,9 +208,10 @@
     found, used = [], 0
     for first in range(0, piece_rows, ROWS):
         free = min(SPARE, count - used)
-        found.append(state[first + ROWS - SPARE : first + ROWS - SPARE + free])
+        found.append(state[first + ROWS - SPARE - 1 : first + ROWS, :][1 : 1 + free].astype(F32))
         used += free
-    return jnp.concatenate(found + [state[piece_rows : piece_rows + count - used]], 0)
+    rest = state[piece_rows:, :][: count - used].astype(F32)
+    return jnp.concatenate(found + [rest], 0)
 
 
 def key_kernel(
@@ -256,47 +257,70 @@
             send_ref[slot] = piece.astype(BF16)
 
 
-def share_kernel(norm_at, own_ref, *refs):
-    sent_at = -1 if refs[-1].dtype == BF16 else -2
-    got_refs, sent_ref = refs[:sent_at], refs[sent_at]
+def share_kernel(piece_rows, own_ref, *refs):
+    got_refs, out_refs = refs[: PLANE - 1], refs[PLANE - 1 :]
     total = own_ref[...]
     for got_ref in got_refs:
         total = total + got_ref[...].astype(F32)
-    if norm_at is not None:
-        lines = norm_rows(norm_values(lines_in(total, norm_at)))
-        total = with_lines(total[:norm_at], lines, total.shape[0])
-    sent_ref[...] = total.astype(BF16)
-    if sent_at == -2:
+    half = piece_rows // 2
+    lines = norm_rows(norm_values(lines_in(total, piece_rows)))
+    parts = (with_tail(total[:half], lines, out_refs[0].shape[0]), total[half:piece_rows])
+    for ref, part in zip(out_refs, parts):
+        ref[...] = part.astype(BF16)
+    for ref, part in zip(out_refs[2:], parts):
+        ref[...] = part
+
+
+def with_tail(state, lines, rows):
+    blank = jnp.zeros((rows - state.shape[0] - lines.shape[0], VDIM), F32)
+    return jnp.concatenate([state, lines, blank], 0)
+
+
+def join_kernel(tail, total_ref, *refs):
+    out_at = -1 if refs[-1].dtype == BF16 else -2
+    total = total_ref[...]
+    for got_ref in refs[:out_at]:
+        total = total + got_ref[...].astype(F32)
+    if tail is not None:
+        lines = norm_rows(norm_values(total[tail[0] : tail[1]]))
+        total = with_tail(total[: tail[0]], lines, total.shape[0])
+    refs[out_at][...] = total.astype(BF16)
+    if out_at == -2:
         refs[-1][...] = total
 
 
-def store_pieces(sign, strides, got_refs, moved_refs, pieces_ref):
-    rows = pieces_ref.shape[1]
-
-    def is_ahead(other, here):
-        return other < here if sign > 0 else other > here
-
-    before = jnp.zeros(got_refs[0].shape, F32)
-    for ref, (stride, distance) in zip(moved_refs, strides):
+def is_ahead(sign, other, here):
+    return other < here if sign > 0 else other > here
+
+
+def before_plane(sign, strides, refs, rows):
+    total = 0.0
+    for ref, (stride, distance) in zip(refs, strides):
         if distance:
             group = lax.div(lax.axis_index("ctx"), PLANE * stride)
-            before = before + masked(is_ahead(group ^ distance, group), ref[...])
+            total = total + masked(is_ahead(sign, group ^ distance, group), ref[rows, :])
         else:
-            before = before + ref[...].astype(F32)
+            total = total + ref[rows, :].astype(F32)
+    return total
+
+
+def piece_kernel(sign, strides, *refs):
+    got_refs, moved_refs, pieces_ref = refs[:PLANE], refs[PLANE:-1], refs[-1]
     rank = lax.rem(lax.axis_index("ctx"), PLANE)
-    extra = None
-    for slot in range(PLANE):
-        total = before
-        for i in range(PLANE):
-            if i != slot:
-                total = total + masked(is_ahead(rank ^ i, rank ^ slot), got_refs[i][...])
-        pieces_ref[slot] = total[:rows].astype(BF16)
-        extra = total if slot == 0 else extra
-    return extra
-
-
-def piece_kernel(sign, strides, *refs):
-    store_pieces(sign, strides, refs[:PLANE], refs[PLANE:-1], refs[-1])
+    count = len(strides)
+    parts = len(moved_refs) // count
+    deep = pieces_ref.shape[1] // parts
+    for part in range(parts):
+        refs = moved_refs[part * count : (part + 1) * count]
+        before = before_plane(sign, strides, refs, pl.ds(0, deep))
+        rows = pl.ds(part * deep, deep)
+        for slot in range(PLANE):
+            total = before
+            for i in range(PLANE):
+                if i != slot:
+                    ahead = is_ahead(sign, rank ^ i, rank ^ slot)
+                    total = total + masked(ahead, got_refs[i][rows, :])
+            pieces_ref[slot, rows, :] = total.astype(BF16)
 
 
 def score_kernel(qd_ref, kf_ref, vc_ref, low_ref, den_ref, num_ref):
@@ -315,12 +339,17 @@
 
 
 def scale_kernel(strides, den_ref, qd_ref, og_ref, *refs):
-    *refs, pieces_ref, inv_ref, sg_ref, own_ref, send_ref, slots = refs
+    *refs, inv_ref, sg_ref, own_ref, send_ref, slots = refs
+    got_refs, moved_refs = refs[:PLANE], refs[PLANE:]
     rank = lax.rem(lax.axis_index("ctx"), PLANE)
     heads = qd_ref.shape[0]
     per_piece = heads // PLANE
-    lines = store_pieces(1, strides, refs[:PLANE], refs[PLANE:], pieces_ref)
-    norm = norm_values(lines_in(lines, pieces_ref.shape[1]))
+    piece_rows = per_piece * ROWS
+    lines = before_plane(1, strides, moved_refs, pl.ds(piece_rows // 2, 15 * heads // 4))
+    for i in range(1, PLANE):
+        here = lines_in(got_refs[i], piece_rows)
+        lines = lines + masked(is_ahead(1, rank ^ i, rank), here)
+    norm = norm_values(lines)
     high = norm.astype(BF16).astype(F32)
     middle = (norm - high).astype(BF16).astype(F32)
     rest = norm - high - middle
@@ -505,14 +534,22 @@
     with jax.named_scope("prior_share"):
         got = [swapped(send[j], "ctx", j) for j in range(1, PLANE)]
 
-        def join(norm_at, total, received, more):
+        more = lax.axis_size("ctx") > 4 * PLANE
+        half = piece_rows // 2
+        count = 15 * heads // 4
+        shapes = [(half + -(-count // 16) * 16, VDIM), (half, VDIM)]
+        outs = [S(x, BF16) for x in shapes] + [S(x, F32) for x in shapes]
+        body = functools.partial(share_kernel, piece_rows)
+        sent = call(body, (own, *got), outs[: 4 if more else 2], 1 << 20)
+        total = sent[2:] if more else (None, None)
+        got = [own] + got
+
+        def join(tail, total, received, more):
             outs = [S(total.shape, BF16), S(total.shape, F32)]
-            body = functools.partial(share_kernel, norm_at)
-            made = call(body, (total, *received), outs[: 2 if more else 1], 1 << 20)
+            body = functools.partial(join_kernel, tail)
+            made = call(body, (total, *received[::-1]), outs[: 2 if more else 1], 1 << 20)
             return made if more else (made[0], None)
 
-        more = lax.axis_size("ctx") > 4 * PLANE
-        sent, total = join(piece_rows, own, got, more)
     with jax.named_scope("scores"):
         outs = [
             S((heads, tokens, tokens), BF16),
@@ -520,34 +557,36 @@
             S((tokens, width), F32),
         ]
         low, den, num = call(score_kernel, (qd, kf, vc), outs, 400 * step)
-    with jax.named_scope("prior_planes"):
-        sent = after(sent, den)
-        norm_join = functools.partial(join, piece_rows)
-        moved, strides = planes_ahead(total, sent, 1, norm_join)
     with jax.named_scope("turned"):
         outs = [S((heads, tokens, ROWS), BF16)] * 2
-        qt, kt = call(turn_kernel, (after(qd, sent), kf), outs, 1 << 22)
+        qt, kt = call(turn_kernel, (after(qd, den), kf), outs, 1 << 22)
+    with jax.named_scope("prior_planes"):
+        sent = lax.optimization_barrier((*sent[:2], qt))[:2]
+        norm_join = functools.partial(join, (half, half + count))
+        rest, strides = planes_ahead(total[1], sent[1], 1, functools.partial(join, None))
+        moved, _ = planes_ahead(total[0], sent[0], 1, norm_join)
     with jax.named_scope("out_grad"):
-        ops = (after(cotangent, qt), *cots, out_weight)
+        ops = (after(cotangent, *sent), *cots, out_weight)
         (out_grad,) = call(
             grad_kernel, ops, [S((tokens, width), F32)], groups * project_flops
         )
     with jax.named_scope("scaled_grad"):
         outs = [
-            S((PLANE, piece_rows, VDIM), BF16),
             S((tokens, heads), F32),
             S((tokens, width), BF16),
             S((piece_rows, VDIM), F32),
             S((PLANE, piece_rows, VDIM), BF16),
         ]
-        ops = (den, qd, out_grad, own, *got, *moved)
+        ops = (den, qd, out_grad, *got, *moved)
         body = functools.partial(scale_kernel, strides)
-        pieces, inverse, scaled, own_later, send_later = call(
-            body, ops, outs, step, scratch=[slots]
-        )
-        prior = handed_back(pieces)
+        inverse, scaled, own_later, send_later = call(body, ops, outs, step, scratch=[slots])
     with jax.named_scope("later_share"):
         got_later = [swapped(send_later[j], "ctx", j) for j in range(1, PLANE)]
+    with jax.named_scope("prior_back"):
+        body = functools.partial(piece_kernel, 1, strides)
+        ops = (*got, *moved, after(rest[0], scaled), *rest[1:])
+        (pieces,) = call(body, ops, [S((PLANE, piece_rows, VDIM), BF16)], 1 << 20)
+        prior = handed_back(pieces)
     with jax.named_scope("later_planes"):
         plain_join = functools.partial(join, None)
         sent_later, total_later = plain_join(own_later, got_later, more)

time: 53.3 us -> 51.8 us (0.972)
  waiting for transfers between devices: 18.6 us -> 13.8 us
  starting transfers between devices: 21.5 us -> 24.9 us
    ppermute x20 -> x23, waiting for transfers between devices: 16.1 us -> 11.2 us  [swapped(): return lax.ppermute(x, axis, pairs)]
    ppermute x20 -> x23, starting transfers between devices: 21 us -> 24.3 us  [swapped(): return lax.ppermute(x, axis, pairs)]
    pallas_call x15 -> x16, Pallas kernels: 11.1 us -> 11.2 us  [call(): pl.pallas_call(body, out_shape=out_shape, in_specs=[hbm if i in far else...]
  transfers between devices with their start and end apart: 21 -> 24, of which waited for: 12 -> 10; matrix products, arithmetic and copies ran while one was open for 0% -> 0% of each run, Pallas kernels for 17% -> 20%
where the time goes in v8:
time: 51.8 us; the launch traced here: 51.5 us
  starting transfers between devices  24.9 us (48%)
  waiting for transfers between devices  13.8 us (27%)
  Pallas kernels  12 us (23%)
  between operations  0.84 us (2%)
    ppermute x23, starting transfers between devices, swapped(): return lax.ppermute(x, axis, pairs)  24.3 us
    ppermute x23, waiting for transfers between devices, swapped(): return lax.ppermute(x, axis, pairs)  11.2 us
    pallas_call x16, Pallas kernels, call(): pl.pallas_call(body, out_shape=out_shape, in_specs=[hbm if i in far else...  11.2 us
    ppermute x1, waiting for transfers between devices, per_device(): lax.ppermute(last_rows, 'ctx', [(i, (i + 1) % slabs) for i in range(slabs)])  2.55 us
  transfers between devices with their start and end apart: 24, of which 10 were waited for; matrix products, arithmetic and copies ran while one was open for 0% of the time, Pallas kernels for 20%

profile of v8, /device:TPU:0, one launch (start us, length us, event | category | flops | bytes accessed | tf_op | source)
XLA Modules:
  0.0 51.5 jit_solution(15396057236072431965)
XLA Ops:
  0.6 0.8 %edge.1 = bf16[2,1152]{1,0:T(2,128)(2,1)S(1)} custom-call(bf16[256,128]{1,0:T(8,128)(2,1)} %k_far.3, bf16[256,1024]{1,0:T(8,128)(2,1)} %v_far.3), custom_call_target="tpu_custom_call" | custom-call | tf_op jit(solution)/shard_map/edge/pallas_call | solution.py:503
  1.4 0.5 collective-permute-start
  1.9 2.6 %collective-permute-start.8 = (bf16[256,1024]{1,0:T(8,128)(2,1)}, bf16[256,1024]{1,0:T(8,128)(2,1)S(1)}, u32[]{:S(2)}, u32[]{:S(2)}) collective-permute-start(bf16[256,1024]{1,0:T(8,128)(2,1)} %refs_0_), channel_id=1, source_target_pairs={{0,1},{1,0},{2,3},{3,2},{4,5},{5,4},{6,7},{7,6},{8,9},{9,8},{10,11... | collective-permute-start | bytes 1572872 | tf_op jit(solution)/shard_map/cotangent/ppermute | solution.py:478
  4.5 1.2 %query_features.1 = (bf16[8,160,256]{2,1,0:T(8,128)(2,1)S(1)}, bf16[256,128]{1,0:T(8,128)(2,1)S(1)}, bf16[256,1024]{1,0:T(8,128)(2,1)S(1)}, f32[3,128]{1,0:T(4,128)S(1)}, f32[3,1024]{1,0:T(4,128)S(1)}) custom-call(bf16[256,128]{1,0:T(8,128)(2,1)} %q_far, bf16[256,128]{1,0:T(8,128)(2,1)} %k_far.3, bf16[256,1024]{1,0:T(8,128)(2,1)} %v_far.3, f32[3,128]{1,0:T(4,128)} %ck_far.1, ...), custom_call_target="tpu_custom_call" | custom-call | flops 1048576 | bytes 1928192 | tf_op jit(solution)/shard_map/query_features/pallas_call | solution.py:34
  5.7 2.6 %collective-permute-done.before_ref = bf16[2,1152]{1,0:T(2,128)(2,1)S(1)} collective-permute-done((bf16[2,1152]{1,0:T(2,128)(2,1)S(1)}, bf16[2,1152]{1,0:T(2,128)(2,1)S(1)}, u32[]{:S(2)}, u32[]{:S(2)}) %collective-permute-start) | collective-permute-done | bytes 4640 | tf_op jit(solution)/shard_map/edge/ppermute | solution.py:512
  8.2 0.9 %key_features.1 = (bf16[8,160,256]{2,1,0:T(8,128)(2,1)S(1)}, bf16[256,1024]{1,0:T(8,128)(2,1)S(1)}, f32[336,128]{1,0:T(8,128)S(1)}, bf16[4,336,128]{2,1,0:T(8,128)(2,1)S(1)}) custom-call(bf16[256,128]{1,0:T(8,128)(2,1)S(1)} %get-tuple-element.38.k_ref, bf16[256,1024]{1,0:T(8,128)(2,1)S(1)} %get-tuple-element.39.v_ref, ...), custom_call_target="tpu_custom_call" | custom-call | flops 83886080 | bytes 2304000 | tf_op jit(solution)/shard_map/key_features/pallas_call | solution.py:34
  9.2 0.1 collective-permute-start.1
  9.3 0.2 collective-permute-start.2
  9.5 1.6 %collective-permute-start.3 = (bf16[336,128]{1,0:T(8,128)(2,1)S(1)}, bf16[336,128]{1,0:T(8,128)(2,1)S(1)}, u32[]{:S(2)}, u32[]{:S(2)}) collective-permute-start(bf16[336,128]{1,0:T(8,128)(2,1)S(1)} %get-tuple-element.70), channel_id=1, source_target_pairs={{0,6},{2,4},{4,2},{6,0},{8,14},{10,12},{12,10},{14,8},{16,22},{18,... | collective-permute-start | bytes 258056 | tf_op jit(solution)/shard_map/prior_share/ppermute | solution.py:478
  11.1 1.2 %scores.1 = (bf16[8,256,256]{2,1,0:T(8,128)(2,1)S(1)}, f32[8,256]{1,0:T(8,128)S(1)}, f32[256,1024]{1,0:T(8,128)S(1)}) custom-call(bf16[8,160,256]{2,1,0:T(8,128)(2,1)S(1)} %get-tuple-element.45.qd_ref, bf16[8,160,256]{2,1,0:T(8,128)(2,1)S(1)} %get-tuple-element.42.kf_ref, bf16[256,1024]{1,0:T(8,128)(2,1)S(1)} %get-tuple-element.43.vc_ref), custom_call_target="tpu_custom_call" | custom-call | flops 33554432000 | bytes 3940352 | tf_op jit(solution)/shard_map/scores/pallas_call | solution.py:34
  12.3 0.6 %turned.1 = (bf16[8,256,160]{2,1,0:T(8,128)(2,1)S(1)}, bf16[8,256,160]{2,1,0:T(8,128)(2,1)S(1)}) custom-call(bf16[8,160,256]{2,1,0:T(8,128)(2,1)S(1)} %get-tuple-element.45.qd_ref, bf16[8,160,256]{2,1,0:T(8,128)(2,1)S(1)} %get-tuple-element.42.kf_ref), custom_call_target="tpu_custom_call" | custom-call | flops 4194304 | bytes 2621440 | tf_op jit(solution)/shard_map/turned/pallas_call | solution.py:34
  13.0 0.0 collective-permute-done.1.refs_0_.refs_1_
  13.0 1.7 %collective-permute-done.2.refs_1_.refs_2_ = bf16[336,128]{1,0:T(8,128)(2,1)S(1)} collective-permute-done((bf16[336,128]{1,0:T(8,128)(2,1)S(1)}, bf16[336,128]{1,0:T(8,128)(2,1)S(1)}, u32[]{:S(2)}, u32[]{:S(2)}) %collective-permute-start.2) | collective-permute-done | bytes 86048 | tf_op jit(solution)/shard_map/prior_share/ppermute | solution.py:478
  14.7 0.9 %collective-permute-done.3.refs_2_.refs_3_ = bf16[336,128]{1,0:T(8,128)(2,1)S(1)} collective-permute-done((bf16[336,128]{1,0:T(8,128)(2,1)S(1)}, bf16[336,128]{1,0:T(8,128)(2,1)S(1)}, u32[]{:S(2)}, u32[]{:S(2)}) %collective-permute-start.3) | collective-permute-done | bytes 86048 | tf_op jit(solution)/shard_map/prior_share/ppermute | solution.py:478
  15.6 0.2 prior_share.1
  15.8 0.3 collective-permute-start.4
  16.1 2.5 %collective-permute-start.5 = (bf16[192,128]{1,0:T(8,128)(2,1)S(1)}, bf16[192,128]{1,0:T(8,128)(2,1)S(1)}, u32[]{:S(2)}, u32[]{:S(2)}) collective-permute-start(bf16[192,128]{1,0:T(8,128)(2,1)S(1)} %get-tuple-element.51), channel_id=1, source_target_pairs={{0,16},{2,18},{4,20},{6,22},{8,24},{10,26},{12,28},{14,30},{16,0},... | collective-permute-start | bytes 147464 | tf_op jit(solution)/shard_map/prior_planes/ppermute | solution.py:478
  18.6 1.6 %collective-permute-start.6 = (bf16[192,128]{1,0:T(8,128)(2,1)S(1)}, bf16[192,128]{1,0:T(8,128)(2,1)S(1)}, u32[]{:S(2)}, u32[]{:S(2)}) collective-permute-start(bf16[192,128]{1,0:T(8,128)(2,1)S(1)} %get-tuple-element.51), channel_id=1, source_target_pairs={{0,24},{2,26},{4,28},{6,30},{8,16},{10,18},{12,20},{14,22},{16,8},... | collective-permute-start | bytes 147464 | tf_op jit(solution)/shard_map/prior_planes/ppermute | solution.py:478
  20.2 0.0 collective-permute-start.7
  20.2 0.0 collective-permute-done.8.refs_1_
  20.2 2.2 %collective-permute-start.10 = (bf16[160,128]{1,0:T(8,128)(2,1)S(1)}, bf16[160,128]{1,0:T(8,128)(2,1)S(1)}, u32[]{:S(2)}, u32[]{:S(2)}) collective-permute-start(bf16[160,128]{1,0:T(8,128)(2,1)S(1)} %get-tuple-element.52), channel_id=1, source_target_pairs={{0,24},{2,26},{4,28},{6,30},{8,16},{10,18},{12,20},{14,22},{16,8},... | collective-permute-start | bytes 122888 | tf_op jit(solution)/shard_map/prior_planes/ppermute | solution.py:478
  22.4 1.3 %out_grad.1.og_ref = f32[256,1024]{1,0:T(8,128)S(1)} custom-call(bf16[256,1024]{1,0:T(8,128)(2,1)S(1)} %copy-done.1, bf16[256,1024]{1,0:T(8,128)(2,1)S(1)} %collective-permute-done.8.refs_1_, bf16[1024,2048]{1,0:T(8,128)(2,1)S(1)} %copy-done), custom_call_target="tpu_custom_call" | custom-call | flops 1073741824 | bytes 6291456 | tf_op jit(solution)/shard_map/out_grad/pallas_call | solution.py:34
  23.7 0.0 collective-permute-done.4.refs_4_
  23.7 1.3 %collective-permute-start.9 = (bf16[160,128]{1,0:T(8,128)(2,1)S(1)}, bf16[160,128]{1,0:T(8,128)(2,1)S(1)}, u32[]{:S(2)}, u32[]{:S(2)}) collective-permute-start(bf16[160,128]{1,0:T(8,128)(2,1)S(1)} %get-tuple-element.52), channel_id=1, source_target_pairs={{0,16},{2,18},{4,20},{6,22},{8,24},{10,26},{12,28},{14,30},{16,0},... | collective-permute-start | bytes 122888 | tf_op jit(solution)/shard_map/prior_planes/ppermute | solution.py:478
  25.0 0.0 collective-permute-done.5.refs_5_
  25.0 0.0 collective-permute-done.6.refs_6_
  25.0 1.0 %scaled_grad.1 = (f32[256,8]{1,0:T(8,128)S(1)}, bf16[256,1024]{1,0:T(8,128)(2,1)S(1)}, f32[320,128]{1,0:T(8,128)S(1)}, bf16[4,320,128]{2,1,0:T(8,128)(2,1)S(1)}) custom-call(f32[8,256]{1,0:T(8,128)S(1)} %get-tuple-element.44.den_ref, bf16[8,160,256]{2,1,0:T(8,128)(2,1)S(1)} %get-tuple-element.45.qd_ref, f32[256,1024]{1,0:T(8,128)S(1)} %out_grad.1.og_ref, ...), custom_call_target="tpu_custom_call" | custom-call | flops 83886080 | bytes 3313664 | tf_op jit(solution)/shard_map/scaled_grad/pallas_call | solution.py:34
  26.1 0.1 collective-permute-start.14
  26.2 0.7 %collective-permute-start.15 = (bf16[320,128]{1,0:T(8,128)(2,1)S(1)}, bf16[320,128]{1,0:T(8,128)(2,1)S(1)}, u32[]{:S(2)}, u32[]{:S(2)}) collective-permute-start(bf16[320,128]{1,0:T(8,128)(2,1)S(1)} %get-tuple-element.78), channel_id=1, source_target_pairs={{0,4},{2,6},{4,0},{6,2},{8,12},{10,14},{12,8},{14,10},{16,20},{18,... | collective-permute-start | bytes 245768 | tf_op jit(solution)/shard_map/later_share/ppermute | solution.py:478
  26.9 0.0 collective-permute-done.7.refs_7_
  26.9 1.2 %collective-permute-start.16 = (bf16[320,128]{1,0:T(8,128)(2,1)S(1)}, bf16[320,128]{1,0:T(8,128)(2,1)S(1)}, u32[]{:S(2)}, u32[]{:S(2)}) collective-permute-start(bf16[320,128]{1,0:T(8,128)(2,1)S(1)} %get-tuple-element.77), channel_id=1, source_target_pairs={{0,2},{2,0},{4,6},{6,4},{8,10},{10,8},{12,14},{14,12},{16,18},{18,... | collective-permute-start | bytes 245768 | tf_op jit(solution)/shard_map/later_share/ppermute | solution.py:478
  28.0 0.0 collective-permute-done.10.refs_9_
  28.0 0.6 %collective-permute-done.9.refs_8_ = bf16[160,128]{1,0:T(8,128)(2,1)S(1)} collective-permute-done((bf16[160,128]{1,0:T(8,128)(2,1)S(1)}, bf16[160,128]{1,0:T(8,128)(2,1)S(1)}, u32[]{:S(2)}, u32[]{:S(2)}) %collective-permute-start.9) | collective-permute-done | bytes 40992 | tf_op jit(solution)/shard_map/prior_planes/ppermute | solution.py:478
  28.7 0.3 prior_back.1
  28.9 0.1 collective-permute-start.11
  29.0 0.7 %collective-permute-start.12 = (bf16[320,128]{1,0:T(8,128)(2,1)S(1)}, bf16[320,128]{1,0:T(8,128)(2,1)S(1)}, u32[]{:S(2)}, u32[]{:S(2)}) collective-permute-start(bf16[320,128]{1,0:T(8,128)(2,1)S(1)} %get-tuple-element.82), channel_id=1, source_target_pairs={{0,4},{2,6},{4,0},{6,2},{8,12},{10,14},{12,8},{14,10},{16,20},{18,... | collective-permute-start | bytes 245768 | tf_op jit(solution)/shard_map/prior_back/ppermute | solution.py:478
  29.7 0.7 %collective-permute-done.14.refs_0_.refs_3_ = bf16[320,128]{1,0:T(8,128)(2,1)S(1)} collective-permute-done((bf16[320,128]{1,0:T(8,128)(2,1)S(1)}, bf16[320,128]{1,0:T(8,128)(2,1)S(1)}, u32[]{:S(2)}, u32[]{:S(2)}) %collective-permute-start.14) | collective-permute-done | bytes 81952 | tf_op jit(solution)/shard_map/later_share/ppermute | solution.py:478
  30.4 0.8 %collective-permute-start.13 = (bf16[320,128]{1,0:T(8,128)(2,1)S(1)}, bf16[320,128]{1,0:T(8,128)(2,1)S(1)}, u32[]{:S(2)}, u32[]{:S(2)}) collective-permute-start(bf16[320,128]{1,0:T(8,128)(2,1)S(1)} %get-tuple-element.81), channel_id=1, source_target_pairs={{0,6},{2,4},{4,2},{6,0},{8,14},{10,12},{12,10},{14,8},{16,22},{18,... | collective-permute-start | bytes 245768 | tf_op jit(solution)/shard_map/prior_back/ppermute | solution.py:478
  31.2 0.3 collective-permute-done.15.refs_1_.refs_2_
  31.5 0.0 collective-permute-done.16.refs_2_.refs_1_
  31.6 1.0 %collective-permute-start.18 = (bf16[320,128]{1,0:T(8,128)(2,1)S(1)}, bf16[320,128]{1,0:T(8,128)(2,1)S(1)}, u32[]{:S(2)}, u32[]{:S(2)}) collective-permute-start(bf16[320,128]{1,0:T(8,128)(2,1)S(1)} %later_planes.1), channel_id=1, source_target_pairs={{0,8},{2,10},{4,12},{6,14},{8,0},{10,2},{12,4},{14,6},{16,24},{18,... | collective-permute-start | bytes 245768 | tf_op jit(solution)/shard_map/later_planes/ppermute | solution.py:478
  32.5 1.9 %collective-permute-start.19 = (bf16[320,128]{1,0:T(8,128)(2,1)S(1)}, bf16[320,128]{1,0:T(8,128)(2,1)S(1)}, u32[]{:S(2)}, u32[]{:S(2)}) collective-permute-start(bf16[320,128]{1,0:T(8,128)(2,1)S(1)} %later_planes.1), channel_id=1, source_target_pairs={{0,16},{2,18},{4,20},{6,22},{8,24},{10,26},{12,28},{14,30},{16,0},... | collective-permute-start | bytes 245768 | tf_op jit(solution)/shard_map/later_planes/ppermute | solution.py:478
  34.4 0.0 collective-permute-done.11
  34.4 1.6 %collective-permute-start.20 = (bf16[320,128]{1,0:T(8,128)(2,1)S(1)}, bf16[320,128]{1,0:T(8,128)(2,1)S(1)}, u32[]{:S(2)}, u32[]{:S(2)}) collective-permute-start(bf16[320,128]{1,0:T(8,128)(2,1)S(1)} %later_planes.1), channel_id=1, source_target_pairs={{0,24},{2,26},{4,28},{6,30},{8,16},{10,18},{12,20},{14,22},{16,8},... | collective-permute-start | bytes 245768 | tf_op jit(solution)/shard_map/later_planes/ppermute | solution.py:478
  36.0 0.0 collective-permute-done.12
  36.0 0.0 collective-permute-done.13
  36.1 1.0 %attended.1 = (bf16[256,1024]{1,0:T(8,128)(2,1)S(1)}, bf16[256,1024]{1,0:T(8,128)(2,1)S(1)}) custom-call(bf16[8,256,160]{2,1,0:T(8,128)(2,1)S(1)} %get-tuple-element.46.qt_ref, bf16[4,320,128]{2,1,0:T(8,128)(2,1)S(1)} %pad_maximum_fusion.prior_ref, f32[256,1024]{1,0:T(8,128)S(1)} %get-tuple-element.60.num_ref, f32[256,8]{1,0:T(8,128)S(1)} %get-tuple-element.61.inv_ref, ...), custom_call_target="tpu_custom_call" | custom-call | flops 620756992 | bytes 7282688 | tf_op jit(solution)/shard_map/attended/pallas_call | solution.py:34
  37.1 2.0 %collective-permute-start.17 = (bf16[256,1024]{1,0:T(8,128)(2,1)S(1)}, bf16[256,1024]{1,0:T(8,128)(2,1)S(1)}, u32[]{:S(2)}, u32[]{:S(2)}) collective-permute-start(bf16[256,1024]{1,0:T(8,128)(2,1)S(1)} %get-tuple-element.64), channel_id=1, source_target_pairs={{0,1},{1,0},{2,3},{3,2},{4,5},{5,4},{6,7},{7,6},{8,9},{9,8},{10,11... | collective-permute-start | bytes 1572872 | tf_op jit(solution)/shard_map/attended/ppermute | solution.py:478
  39.1 0.4 near.1.near_ref
  39.5 0.7 %mixed.1.part_ref = f32[256,1024]{1,0:T(8,128)S(1)} custom-call(bf16[256,1024]{1,0:T(8,128)(2,1)S(1)} %get-tuple-element.63.att_ref, bf16[1024,2048]{1,0:T(8,128)(2,1)S(1)} %copy-done), custom_call_target="tpu_custom_call" | custom-call | flops 1073741824 | bytes 5767168 | tf_op jit(solution)/shard_map/mixed/pallas_call | solution.py:34
  40.2 0.0 collective-permute-done.18.refs_4_
  40.2 1.9 %collective-permute-done.19.refs_5_ = bf16[320,128]{1,0:T(8,128)(2,1)S(1)} collective-permute-done((bf16[320,128]{1,0:T(8,128)(2,1)S(1)}, bf16[320,128]{1,0:T(8,128)(2,1)S(1)}, u32[]{:S(2)}, u32[]{:S(2)}) %collective-permute-start.19) | collective-permute-done | bytes 81952 | tf_op jit(solution)/shard_map/later_planes/ppermute | solution.py:478
  42.1 0.0 collective-permute-done.20.refs_6_
  42.1 0.2 later_back.1
  42.4 0.1 collective-permute-start.21
  42.5 1.8 %collective-permute-start.22 = (bf16[320,128]{1,0:T(8,128)(2,1)S(1)}, bf16[320,128]{1,0:T(8,128)(2,1)S(1)}, u32[]{:S(2)}, u32[]{:S(2)}) collective-permute-start(bf16[320,128]{1,0:T(8,128)(2,1)S(1)} %get-tuple-element.74), channel_id=1, source_target_pairs={{0,4},{2,6},{4,0},{6,2},{8,12},{10,14},{12,8},{14,10},{16,20},{18,... | collective-permute-start | bytes 245768 | tf_op jit(solution)/shard_map/later_back/ppermute | solution.py:478
  44.3 0.1 collective-permute-start.23
  44.4 0.0 collective-permute-done.21.refs_1_
  44.4 0.3 far_grad.2.early_ref
  44.7 2.7 %collective-permute-done.22.refs_0_ = bf16[320,128]{1,0:T(8,128)(2,1)S(1)} collective-permute-done((bf16[320,128]{1,0:T(8,128)(2,1)S(1)}, bf16[320,128]{1,0:T(8,128)(2,1)S(1)}, u32[]{:S(2)}, u32[]{:S(2)}) %collective-permute-start.22) | collective-permute-done | bytes 81952 | tf_op jit(solution)/shard_map/later_back/ppermute | solution.py:478
  47.4 1.4 %collective-permute-done.23.refs_1_ = bf16[320,128]{1,0:T(8,128)(2,1)S(1)} collective-permute-done((bf16[320,128]{1,0:T(8,128)(2,1)S(1)}, bf16[320,128]{1,0:T(8,128)(2,1)S(1)}, u32[]{:S(2)}, u32[]{:S(2)}) %collective-permute-start.23) | collective-permute-done | bytes 81952 | tf_op jit(solution)/shard_map/later_back/ppermute | solution.py:478
  48.8 1.0 %far_grad.3 = bf16[256,1024]{1,0:T(8,128)(2,1)} custom-call(bf16[8,256,160]{2,1,0:T(8,128)(2,1)S(1)} %get-tuple-element.65.kt_ref, f32[256,1024]{1,0:T(8,128)S(1)} %near.1.near_ref, bf16[2,256,256]{2,1,0:T(8,128)(2,1)S(1)} %far_grad.2.early_ref, bf16[320,128]{1,0:T(8,128)(2,1)S(1)} %collective-permute-done.22.refs_0_, ...), custom_call_target="tpu_custom_call" | custom-call | flops 1342177280 | bytes 2654208 | tf_op jit(solution)/shard_map/far_grad/pallas_call | solution.py:34
  49.8 0.9 %collective-permute-done.17.refs_0_ = bf16[256,1024]{1,0:T(8,128)(2,1)S(1)} collective-permute-done((bf16[256,1024]{1,0:T(8,128)(2,1)S(1)}, bf16[256,1024]{1,0:T(8,128)(2,1)S(1)}, u32[]{:S(2)}, u32[]{:S(2)}) %collective-permute-start.17) | collective-permute-done | bytes 524320 | tf_op jit(solution)/shard_map/attended/ppermute | solution.py:478
  50.7 0.8 %mixed_out.1 = bf16[256,1024]{1,0:T(8,128)(2,1)} custom-call(f32[256,1024]{1,0:T(8,128)S(1)} %mixed.1.part_ref, bf16[256,1024]{1,0:T(8,128)(2,1)S(1)} %collective-permute-done.17.refs_0_), custom_call_target="tpu_custom_call" | custom-call | flops 1048576 | bytes 2097152 | tf_op jit(solution)/shard_map/mixed_out/pallas_call | solution.py:34
  (10 shorter events, 0.2 us)
Async XLA Ops:
  1.4 6.8 %collective-permute-start = (bf16[2,1152]{1,0:T(2,128)(2,1)S(1)}, bf16[2,1152]{1,0:T(2,128)(2,1)S(1)}, u32[]{:S(2)}, u32[]{:S(2)}) collective-permute-start(bf16[2,1152]{1,0:T(2,128)(2,1)S(1)} %edge.1), channel_id=1, source_target_pairs={{0,2},{2,4},{4,6},{6,8},{8,10},{10,12},{12,14},{14,16},{16,18},{18... | collective-permute-start | bytes 13832 | tf_op jit(solution)/shard_map/edge/ppermute | solution.py:512
  1.9 18.2 %collective-permute-start.8 = (bf16[256,1024]{1,0:T(8,128)(2,1)}, bf16[256,1024]{1,0:T(8,128)(2,1)S(1)}, u32[]{:S(2)}, u32[]{:S(2)}) collective-permute-start(bf16[256,1024]{1,0:T(8,128)(2,1)} %refs_0_), channel_id=1, source_target_pairs={{0,1},{1,0},{2,3},{3,2},{4,5},{5,4},{6,7},{7,6},{8,9},{9,8},{10,11... | collective-permute-start | bytes 1572872 | tf_op jit(solution)/shard_map/cotangent/ppermute | solution.py:478
  9.2 3.8 %collective-permute-start.1 = (bf16[336,128]{1,0:T(8,128)(2,1)S(1)}, bf16[336,128]{1,0:T(8,128)(2,1)S(1)}, u32[]{:S(2)}, u32[]{:S(2)}) collective-permute-start(bf16[336,128]{1,0:T(8,128)(2,1)S(1)} %get-tuple-element.72), channel_id=1, source_target_pairs={{0,2},{2,0},{4,6},{6,4},{8,10},{10,8},{12,14},{14,12},{16,18},{18,... | collective-permute-start | bytes 258056 | tf_op jit(solution)/shard_map/prior_share/ppermute | solution.py:478
  9.3 5.4 %collective-permute-start.2 = (bf16[336,128]{1,0:T(8,128)(2,1)S(1)}, bf16[336,128]{1,0:T(8,128)(2,1)S(1)}, u32[]{:S(2)}, u32[]{:S(2)}) collective-permute-start(bf16[336,128]{1,0:T(8,128)(2,1)S(1)} %get-tuple-element.71), channel_id=1, source_target_pairs={{0,4},{2,6},{4,0},{6,2},{8,12},{10,14},{12,8},{14,10},{16,20},{18,... | collective-permute-start | bytes 258056 | tf_op jit(solution)/shard_map/prior_share/ppermute | solution.py:478
  9.5 6.1 %collective-permute-start.3 = (bf16[336,128]{1,0:T(8,128)(2,1)S(1)}, bf16[336,128]{1,0:T(8,128)(2,1)S(1)}, u32[]{:S(2)}, u32[]{:S(2)}) collective-permute-start(bf16[336,128]{1,0:T(8,128)(2,1)S(1)} %get-tuple-element.70), channel_id=1, source_target_pairs={{0,6},{2,4},{4,2},{6,0},{8,14},{10,12},{12,10},{14,8},{16,22},{18,... | collective-permute-start | bytes 258056 | tf_op jit(solution)/shard_map/prior_share/ppermute | solution.py:478
  11.1 11.3 %copy-start = (bf16[1024,2048]{1,0:T(8,128)(2,1)S(1)}, bf16[1024,2048]{1,0:T(8,128)(2,1)}, u32[]{:S(2)}) copy-start(bf16[1024,2048]{1,0:T(8,128)(2,1)} %w_ref.3) | copy-start | bytes 12582916
  11.1 11.3 %copy-start.1 = (bf16[256,1024]{1,0:T(8,128)(2,1)S(1)}, bf16[256,1024]{1,0:T(8,128)(2,1)}, u32[]{:S(2)}) copy-start(bf16[256,1024]{1,0:T(8,128)(2,1)} %refs_0_) | copy-start | bytes 1572868
  15.8 7.9 %collective-permute-start.4 = (bf16[192,128]{1,0:T(8,128)(2,1)S(1)}, bf16[192,128]{1,0:T(8,128)(2,1)S(1)}, u32[]{:S(2)}, u32[]{:S(2)}) collective-permute-start(bf16[192,128]{1,0:T(8,128)(2,1)S(1)} %get-tuple-element.51), channel_id=1, source_target_pairs={{0,8},{2,10},{4,12},{6,14},{8,0},{10,2},{12,4},{14,6},{16,24},{18,... | collective-permute-start | bytes 147464 | tf_op jit(solution)/shard_map/prior_planes/ppermute | solution.py:478
  16.1 8.9 %collective-permute-start.5 = (bf16[192,128]{1,0:T(8,128)(2,1)S(1)}, bf16[192,128]{1,0:T(8,128)(2,1)S(1)}, u32[]{:S(2)}, u32[]{:S(2)}) collective-permute-start(bf16[192,128]{1,0:T(8,128)(2,1)S(1)} %get-tuple-element.51), channel_id=1, source_target_pairs={{0,16},{2,18},{4,20},{6,22},{8,24},{10,26},{12,28},{14,30},{16,0},... | collective-permute-start | bytes 147464 | tf_op jit(solution)/shard_map/prior_planes/ppermute | solution.py:478
  18.6 6.5 %collective-permute-start.6 = (bf16[192,128]{1,0:T(8,128)(2,1)S(1)}, bf16[192,128]{1,0:T(8,128)(2,1)S(1)}, u32[]{:S(2)}, u32[]{:S(2)}) collective-permute-start(bf16[192,128]{1,0:T(8,128)(2,1)S(1)} %get-tuple-element.51), channel_id=1, source_target_pairs={{0,24},{2,26},{4,28},{6,30},{8,16},{10,18},{12,20},{14,22},{16,8},... | collective-permute-start | bytes 147464 | tf_op jit(solution)/shard_map/prior_planes/ppermute | solution.py:478
  20.2 6.7 %collective-permute-start.7 = (bf16[160,128]{1,0:T(8,128)(2,1)S(1)}, bf16[160,128]{1,0:T(8,128)(2,1)S(1)}, u32[]{:S(2)}, u32[]{:S(2)}) collective-permute-start(bf16[160,128]{1,0:T(8,128)(2,1)S(1)} %get-tuple-element.52), channel_id=1, source_target_pairs={{0,8},{2,10},{4,12},{6,14},{8,0},{10,2},{12,4},{14,6},{16,24},{18,... | collective-permute-start | bytes 122888 | tf_op jit(solution)/shard_map/prior_planes/ppermute | solution.py:478
  20.2 7.9 %collective-permute-start.10 = (bf16[160,128]{1,0:T(8,128)(2,1)S(1)}, bf16[160,128]{1,0:T(8,128)(2,1)S(1)}, u32[]{:S(2)}, u32[]{:S(2)}) collective-permute-start(bf16[160,128]{1,0:T(8,128)(2,1)S(1)} %get-tuple-element.52), channel_id=1, source_target_pairs={{0,24},{2,26},{4,28},{6,30},{8,16},{10,18},{12,20},{14,22},{16,8},... | collective-permute-start | bytes 122888 | tf_op jit(solution)/shard_map/prior_planes/ppermute | solution.py:478
  23.7 5.0 %collective-permute-start.9 = (bf16[160,128]{1,0:T(8,128)(2,1)S(1)}, bf16[160,128]{1,0:T(8,128)(2,1)S(1)}, u32[]{:S(2)}, u32[]{:S(2)}) collective-permute-start(bf16[160,128]{1,0:T(8,128)(2,1)S(1)} %get-tuple-element.52), channel_id=1, source_target_pairs={{0,16},{2,18},{4,20},{6,22},{8,24},{10,26},{12,28},{14,30},{16,0},... | collective-permute-start | bytes 122888 | tf_op jit(solution)/shard_map/prior_planes/ppermute | solution.py:478
  26.1 4.3 %collective-permute-start.14 = (bf16[320,128]{1,0:T(8,128)(2,1)S(1)}, bf16[320,128]{1,0:T(8,128)(2,1)S(1)}, u32[]{:S(2)}, u32[]{:S(2)}) collective-permute-start(bf16[320,128]{1,0:T(8,128)(2,1)S(1)} %get-tuple-element.79), channel_id=1, source_target_pairs={{0,6},{2,4},{4,2},{6,0},{8,14},{10,12},{12,10},{14,8},{16,22},{18,... | collective-permute-start | bytes 245768 | tf_op jit(solution)/shard_map/later_share/ppermute | solution.py:478
  26.2 5.3 %collective-permute-start.15 = (bf16[320,128]{1,0:T(8,128)(2,1)S(1)}, bf16[320,128]{1,0:T(8,128)(2,1)S(1)}, u32[]{:S(2)}, u32[]{:S(2)}) collective-permute-start(bf16[320,128]{1,0:T(8,128)(2,1)S(1)} %get-tuple-element.78), channel_id=1, source_target_pairs={{0,4},{2,6},{4,0},{6,2},{8,12},{10,14},{12,8},{14,10},{16,20},{18,... | collective-permute-start | bytes 245768 | tf_op jit(solution)/shard_map/later_share/ppermute | solution.py:478
  26.9 4.7 %collective-permute-start.16 = (bf16[320,128]{1,0:T(8,128)(2,1)S(1)}, bf16[320,128]{1,0:T(8,128)(2,1)S(1)}, u32[]{:S(2)}, u32[]{:S(2)}) collective-permute-start(bf16[320,128]{1,0:T(8,128)(2,1)S(1)} %get-tuple-element.77), channel_id=1, source_target_pairs={{0,2},{2,0},{4,6},{6,4},{8,10},{10,8},{12,14},{14,12},{16,18},{18,... | collective-permute-start | bytes 245768 | tf_op jit(solution)/shard_map/later_share/ppermute | solution.py:478
  28.9 5.5 %collective-permute-start.11 = (bf16[320,128]{1,0:T(8,128)(2,1)S(1)}, bf16[320,128]{1,0:T(8,128)(2,1)S(1)}, u32[]{:S(2)}, u32[]{:S(2)}) collective-permute-start(bf16[320,128]{1,0:T(8,128)(2,1)S(1)} %get-tuple-element.83), channel_id=1, source_target_pairs={{0,2},{2,0},{4,6},{6,4},{8,10},{10,8},{12,14},{14,12},{16,18},{18,... | collective-permute-start | bytes 245768 | tf_op jit(solution)/shard_map/prior_back/ppermute | solution.py:478
  29.0 7.0 %collective-permute-start.12 = (bf16[320,128]{1,0:T(8,128)(2,1)S(1)}, bf16[320,128]{1,0:T(8,128)(2,1)S(1)}, u32[]{:S(2)}, u32[]{:S(2)}) collective-permute-start(bf16[320,128]{1,0:T(8,128)(2,1)S(1)} %get-tuple-element.82), channel_id=1, source_target_pairs={{0,4},{2,6},{4,0},{6,2},{8,12},{10,14},{12,8},{14,10},{16,20},{18,... | collective-permute-start | bytes 245768 | tf_op jit(solution)/shard_map/prior_back/ppermute | solution.py:478
  30.4 5.6 %collective-permute-start.13 = (bf16[320,128]{1,0:T(8,128)(2,1)S(1)}, bf16[320,128]{1,0:T(8,128)(2,1)S(1)}, u32[]{:S(2)}, u32[]{:S(2)}) collective-permute-start(bf16[320,128]{1,0:T(8,128)(2,1)S(1)} %get-tuple-element.81), channel_id=1, source_target_pairs={{0,6},{2,4},{4,2},{6,0},{8,14},{10,12},{12,10},{14,8},{16,22},{18,... | collective-permute-start | bytes 245768 | tf_op jit(solution)/shard_map/prior_back/ppermute | solution.py:478
  31.6 8.7 %collective-permute-start.18 = (bf16[320,128]{1,0:T(8,128)(2,1)S(1)}, bf16[320,128]{1,0:T(8,128)(2,1)S(1)}, u32[]{:S(2)}, u32[]{:S(2)}) collective-permute-start(bf16[320,128]{1,0:T(8,128)(2,1)S(1)} %later_planes.1), channel_id=1, source_target_pairs={{0,8},{2,10},{4,12},{6,14},{8,0},{10,2},{12,4},{14,6},{16,24},{18,... | collective-permute-start | bytes 245768 | tf_op jit(solution)/shard_map/later_planes/ppermute | solution.py:478
  32.5 9.6 %collective-permute-start.19 = (bf16[320,128]{1,0:T(8,128)(2,1)S(1)}, bf16[320,128]{1,0:T(8,128)(2,1)S(1)}, u32[]{:S(2)}, u32[]{:S(2)}) collective-permute-start(bf16[320,128]{1,0:T(8,128)(2,1)S(1)} %later_planes.1), channel_id=1, source_target_pairs={{0,16},{2,18},{4,20},{6,22},{8,24},{10,26},{12,28},{14,30},{16,0},... | collective-permute-start | bytes 245768 | tf_op jit(solution)/shard_map/later_planes/ppermute | solution.py:478
  34.4 7.7 %collective-permute-start.20 = (bf16[320,128]{1,0:T(8,128)(2,1)S(1)}, bf16[320,128]{1,0:T(8,128)(2,1)S(1)}, u32[]{:S(2)}, u32[]{:S(2)}) collective-permute-start(bf16[320,128]{1,0:T(8,128)(2,1)S(1)} %later_planes.1), channel_id=1, source_target_pairs={{0,24},{2,26},{4,28},{6,30},{8,16},{10,18},{12,20},{14,22},{16,8},... | collective-permute-start | bytes 245768 | tf_op jit(solution)/shard_map/later_planes/ppermute | solution.py:478
  37.1 13.6 %collective-permute-start.17 = (bf16[256,1024]{1,0:T(8,128)(2,1)S(1)}, bf16[256,1024]{1,0:T(8,128)(2,1)S(1)}, u32[]{:S(2)}, u32[]{:S(2)}) collective-permute-start(bf16[256,1024]{1,0:T(8,128)(2,1)S(1)} %get-tuple-element.64), channel_id=1, source_target_pairs={{0,1},{1,0},{2,3},{3,2},{4,5},{5,4},{6,7},{7,6},{8,9},{9,8},{10,11... | collective-permute-start | bytes 1572872 | tf_op jit(solution)/shard_map/attended/ppermute | solution.py:478
  42.4 2.0 %collective-permute-start.21 = (bf16[320,128]{1,0:T(8,128)(2,1)S(1)}, bf16[320,128]{1,0:T(8,128)(2,1)S(1)}, u32[]{:S(2)}, u32[]{:S(2)}) collective-permute-start(bf16[320,128]{1,0:T(8,128)(2,1)S(1)} %get-tuple-element.75), channel_id=1, source_target_pairs={{0,2},{2,0},{4,6},{6,4},{8,10},{10,8},{12,14},{14,12},{16,18},{18,... | collective-permute-start | bytes 245768 | tf_op jit(solution)/shard_map/later_back/ppermute | solution.py:478
  42.5 4.9 %collective-permute-start.22 = (bf16[320,128]{1,0:T(8,128)(2,1)S(1)}, bf16[320,128]{1,0:T(8,128)(2,1)S(1)}, u32[]{:S(2)}, u32[]{:S(2)}) collective-permute-start(bf16[320,128]{1,0:T(8,128)(2,1)S(1)} %get-tuple-element.74), channel_id=1, source_target_pairs={{0,4},{2,6},{4,0},{6,2},{8,12},{10,14},{12,8},{14,10},{16,20},{18,... | collective-permute-start | bytes 245768 | tf_op jit(solution)/shard_map/later_back/ppermute | solution.py:478
  44.3 4.5 %collective-permute-start.23 = (bf16[320,128]{1,0:T(8,128)(2,1)S(1)}, bf16[320,128]{1,0:T(8,128)(2,1)S(1)}, u32[]{:S(2)}, u32[]{:S(2)}) collective-permute-start(bf16[320,128]{1,0:T(8,128)(2,1)S(1)} %get-tuple-element.73), channel_id=1, source_target_pairs={{0,6},{2,4},{4,2},{6,0},{8,14},{10,12},{12,10},{14,8},{16,22},{18,... | collective-permute-start | bytes 245768 | tf_op jit(solution)/shard_map/later_back/ppermute | solution.py:478

commit v9 on v8

--- a/solution.py
+++ b/solution.py
@@ -81,7 +81,7 @@
 
 def load_piece(rank, head, per_piece, ref):
     at = (head % per_piece) * ROWS
-    return ref[rank ^ (head // per_piece), at : at + ROWS, :]
+    return ref[lax.rem(PLANE - (rank ^ (head // per_piece)), PLANE), at : at + ROWS, :]
 
 
 def edge_kernel(k_far, v_far, edge_ref, k_ref, v_ref, sems):
@@ -305,7 +305,7 @@
 
 
 def piece_kernel(sign, strides, *refs):
-    got_refs, moved_refs, pieces_ref = refs[:PLANE], refs[PLANE:-1], refs[-1]
+    got_refs, moved_refs, pieces_ref = refs[:PLANE][::-1], refs[PLANE:-1], refs[-1]
     rank = lax.rem(lax.axis_index("ctx"), PLANE)
     count = len(strides)
     parts = len(moved_refs) // count
@@ -340,7 +340,7 @@
 
 def scale_kernel(strides, den_ref, qd_ref, og_ref, *refs):
     *refs, inv_ref, sg_ref, own_ref, send_ref, slots = refs
-    got_refs, moved_refs = refs[:PLANE], refs[PLANE:]
+    got_refs, moved_refs = refs[:PLANE][::-1], refs[PLANE:]
     rank = lax.rem(lax.axis_index("ctx"), PLANE)
     heads = qd_ref.shape[0]
     per_piece = heads // PLANE
@@ -453,13 +453,14 @@
     return lax.optimization_barrier((x, *others))[0]
 
 
-def planes_ahead(total, sent, sign, join):
+def planes_ahead(total, sent, sign, join, last=None):
     planes = lax.axis_size("ctx") // PLANE
     received, strides = [], []
     stride = 1
     while stride < planes:
         if (planes // stride) % 4 == 0:
-            moved = [swapped(sent, "ctx", j, stride * PLANE) for j in range(1, 4)]
+            near = sent if last is None else after(sent, last)
+            moved = [swapped(near if j == 1 else sent, "ctx", j, stride * PLANE) for j in range(1, 4)]
             strides += [(stride, j) for j in range(1, 4)]
             stride = stride * 4
         else:
@@ -479,8 +480,7 @@
 
 
 def handed_back(pieces):
-    back = [swapped(pieces[j], "ctx", j) for j in range(1, PLANE)]
-    return jnp.stack([pieces[0]] + back, 0)
+    return [pieces[0]] + [swapped(pieces[j], "ctx", j) for j in range(1, PLANE)]
 
 
 def per_device(queries, keys, values, conv_keys, conv_values, out_weight, cotangent):
@@ -540,7 +540,7 @@
         shapes = [(half + -(-count // 16) * 16, VDIM), (half, VDIM)]
         outs = [S(x, BF16) for x in shapes] + [S(x, F32) for x in shapes]
         body = functools.partial(share_kernel, piece_rows)
-        sent = call(body, (own, *got), outs[: 4 if more else 2], 1 << 20)
+        sent = call(body, (own, *got[::-1]), outs[: 4 if more else 2], 1 << 20)
         total = sent[2:] if more else (None, None)
         got = [own] + got
 
@@ -566,7 +566,7 @@
         rest, strides = planes_ahead(total[1], sent[1], 1, functools.partial(join, None))
         moved, _ = planes_ahead(total[0], sent[0], 1, norm_join)
     with jax.named_scope("out_grad"):
-        ops = (after(cotangent, *sent), *cots, out_weight)
+        ops = (after(cotangent, moved[0]), *cots, out_weight)
         (out_grad,) = call(
             grad_kernel, ops, [S((tokens, width), F32)], groups * project_flops
         )
@@ -577,25 +577,27 @@
             S((piece_rows, VDIM), F32),
             S((PLANE, piece_rows, VDIM), BF16),
         ]
-        ops = (den, qd, out_grad, *got, *moved)
+        ops = (den, qd, out_grad, *got[::-1], *moved)
         body = functools.partial(scale_kernel, strides)
         inverse, scaled, own_later, send_later = call(body, ops, outs, step, scratch=[slots])
     with jax.named_scope("later_share"):
         got_later = [swapped(send_later[j], "ctx", j) for j in range(1, PLANE)]
     with jax.named_scope("prior_back"):
         body = functools.partial(piece_kernel, 1, strides)
-        ops = (*got, *moved, after(rest[0], scaled), *rest[1:])
+        ops = (*got[::-1], *moved, after(rest[0], scaled), *rest[1:])
         (pieces,) = call(body, ops, [S((PLANE, piece_rows, VDIM), BF16)], 1 << 20)
         prior = handed_back(pieces)
+        prior = jnp.stack([prior[0]] + prior[:0:-1], 0)
     with jax.named_scope("later_planes"):
         plain_join = functools.partial(join, None)
         sent_later, total_later = plain_join(own_later, got_later, more)
-        moved_later, strides = planes_ahead(total_later, sent_later, -1, plain_join)
     with jax.named_scope("attended"):
         outs = [S((tokens, width), BF16), S((tokens, columns), BF16)]
         ops = (qt, prior, after(num, sent_later), inverse, out_weight)
         attended, part = call(attend_kernel, ops, outs, step + project_flops)
         parts = [swapped(part, "head", 1)]
+    with jax.named_scope("later_planes"):
+        moved_later, strides = planes_ahead(total_later, sent_later, -1, plain_join, part)
     with jax.named_scope("near"):
         ops = (low, after(scaled, sent_later))
         (near,) = call(near_kernel, ops, [S((tokens, width), F32)], 2 * step)
@@ -610,24 +612,7 @@
     with jax.named_scope("later_back"):
         outs = [S((PLANE, piece_rows, VDIM), BF16)]
         body = functools.partial(piece_kernel, -1, strides)
-        ops = (own_later, *got_later, after(moved_later[0], part), *moved_later[1:])
-        (pieces,) = call(body, ops, outs, 1 << 20)
-        later = [pieces[0]] + [swapped(pieces[j], "ctx", j) for j in range(1, PLANE)]
-    with jax.named_scope("near"):
-        ops = (low, after(scaled, sent_later))
-        (near,) = call(near_kernel, ops, [S((tokens, width), F32)], 2 * step)
-    with jax.named_scope("mixed"):
-        for j in list(range(2, groups)) + [0]:
-            outs = [S((tokens, columns), BF16 if j else F32)]
-            body = functools.partial(mix_kernel, j)
-            ops = (after(attended, sent_later), out_weight)
-            (part,) = call(body, ops, outs, 2 * project_flops)
-            if j:
-                parts.append(swapped(part, "head", j))
-    with jax.named_scope("later_back"):
-        outs = [S((PLANE, piece_rows, VDIM), BF16)]
-        body = functools.partial(piece_kernel, -1, strides)
-        ops = (own_later, *got_later, after(moved_later[0], part, near), *moved_later[1:])
+        ops = (*got_later[::-1], own_later, after(moved_later[0], part, near), *moved_later[1:])
         (pieces,) = call(body, ops, outs, 1 << 20)
         later = handed_back(pieces)
     with jax.named_scope("far_grad"):

time: 51.8 us -> 51.1 us (0.986)
  starting transfers between devices: 24.9 us -> 24.3 us
    ppermute x23, starting transfers between devices: 24.3 us -> 23.8 us  [swapped(): return lax.ppermute(x, axis, pairs)]
  transfers between devices with their start and end apart: 24 -> 24, of which waited for: 10 -> 11; matrix products, arithmetic and copies ran while one was open for 0% -> 0% of each run, Pallas kernels for 20% -> 20%
where the time goes in v9:
time: 51.1 us; the launch traced here: 50.9 us
  starting transfers between devices  24.3 us (48%)
  waiting for transfers between devices  13.6 us (27%)
  Pallas kernels  12 us (23%)
  between operations  0.82 us (2%)
    ppermute x23, starting transfers between devices, swapped(): return lax.ppermute(x, axis, pairs)  23.8 us
    pallas_call x16, Pallas kernels, call(): pl.pallas_call(body, out_shape=out_shape, in_specs=[hbm if i in far else...  11.2 us
    ppermute x23, waiting for transfers between devices, swapped(): return lax.ppermute(x, axis, pairs)  11.1 us
    ppermute x1, waiting for transfers between devices, per_device(): lax.ppermute(last_rows, 'ctx', [(i, (i + 1) % slabs) for i in range(slabs)])  2.55 us
  transfers between devices with their start and end apart: 24, of which 11 were waited for; matrix products, arithmetic and copies ran while one was open for 0% of the time, Pallas kernels for 20%

profile of v9, /device:TPU:0, one launch (start us, length us, event | category | flops | bytes accessed | tf_op | source)
XLA Modules:
  0.0 50.9 jit_solution(7091934463352840907)
XLA Ops:
  0.6 0.8 %edge.1 = bf16[2,1152]{1,0:T(2,128)(2,1)S(1)} custom-call(bf16[256,128]{1,0:T(8,128)(2,1)} %k_far.3, bf16[256,1024]{1,0:T(8,128)(2,1)} %v_far.3), custom_call_target="tpu_custom_call" | custom-call | tf_op jit(solution)/shard_map/edge/pallas_call | solution.py:503
  1.4 0.5 collective-permute-start
  1.9 2.6 %collective-permute-start.8 = (bf16[256,1024]{1,0:T(8,128)(2,1)}, bf16[256,1024]{1,0:T(8,128)(2,1)S(1)}, u32[]{:S(2)}, u32[]{:S(2)}) collective-permute-start(bf16[256,1024]{1,0:T(8,128)(2,1)} %refs_0_), channel_id=1, source_target_pairs={{0,1},{1,0},{2,3},{3,2},{4,5},{5,4},{6,7},{7,6},{8,9},{9,8},{10,11... | collective-permute-start | bytes 1572872 | tf_op jit(solution)/shard_map/cotangent/ppermute | solution.py:479
  4.5 1.2 %query_features.1 = (bf16[8,160,256]{2,1,0:T(8,128)(2,1)S(1)}, bf16[256,128]{1,0:T(8,128)(2,1)S(1)}, bf16[256,1024]{1,0:T(8,128)(2,1)S(1)}, f32[3,128]{1,0:T(4,128)S(1)}, f32[3,1024]{1,0:T(4,128)S(1)}) custom-call(bf16[256,128]{1,0:T(8,128)(2,1)} %q_far, bf16[256,128]{1,0:T(8,128)(2,1)} %k_far.3, bf16[256,1024]{1,0:T(8,128)(2,1)} %v_far.3, f32[3,128]{1,0:T(4,128)} %ck_far.1, ...), custom_call_target="tpu_custom_call" | custom-call | flops 1048576 | bytes 1928192 | tf_op jit(solution)/shard_map/query_features/pallas_call | solution.py:34
  5.7 2.6 %collective-permute-done.before_ref = bf16[2,1152]{1,0:T(2,128)(2,1)S(1)} collective-permute-done((bf16[2,1152]{1,0:T(2,128)(2,1)S(1)}, bf16[2,1152]{1,0:T(2,128)(2,1)S(1)}, u32[]{:S(2)}, u32[]{:S(2)}) %collective-permute-start) | collective-permute-done | bytes 4640 | tf_op jit(solution)/shard_map/edge/ppermute | solution.py:512
  8.2 0.9 %key_features.1 = (bf16[8,160,256]{2,1,0:T(8,128)(2,1)S(1)}, bf16[256,1024]{1,0:T(8,128)(2,1)S(1)}, f32[336,128]{1,0:T(8,128)S(1)}, bf16[4,336,128]{2,1,0:T(8,128)(2,1)S(1)}) custom-call(bf16[256,128]{1,0:T(8,128)(2,1)S(1)} %get-tuple-element.39.k_ref, bf16[256,1024]{1,0:T(8,128)(2,1)S(1)} %get-tuple-element.40.v_ref, ...), custom_call_target="tpu_custom_call" | custom-call | flops 83886080 | bytes 2304000 | tf_op jit(solution)/shard_map/key_features/pallas_call | solution.py:34
  9.2 0.1 collective-permute-start.1
  9.3 0.4 collective-permute-start.2
  9.6 1.5 %collective-permute-start.3 = (bf16[336,128]{1,0:T(8,128)(2,1)S(1)}, bf16[336,128]{1,0:T(8,128)(2,1)S(1)}, u32[]{:S(2)}, u32[]{:S(2)}) collective-permute-start(bf16[336,128]{1,0:T(8,128)(2,1)S(1)} %get-tuple-element.72), channel_id=1, source_target_pairs={{0,2},{2,0},{4,6},{6,4},{8,10},{10,8},{12,14},{14,12},{16,18},{18,... | collective-permute-start | bytes 258056 | tf_op jit(solution)/shard_map/prior_share/ppermute | solution.py:479
  11.1 1.2 %scores.1 = (bf16[8,256,256]{2,1,0:T(8,128)(2,1)S(1)}, f32[8,256]{1,0:T(8,128)S(1)}, f32[256,1024]{1,0:T(8,128)S(1)}) custom-call(bf16[8,160,256]{2,1,0:T(8,128)(2,1)S(1)} %get-tuple-element.46.qd_ref, bf16[8,160,256]{2,1,0:T(8,128)(2,1)S(1)} %get-tuple-element.43.kf_ref, bf16[256,1024]{1,0:T(8,128)(2,1)S(1)} %get-tuple-element.44.vc_ref), custom_call_target="tpu_custom_call" | custom-call | flops 33554432000 | bytes 3940352 | tf_op jit(solution)/shard_map/scores/pallas_call | solution.py:34
  12.3 0.6 %turned.1 = (bf16[8,256,160]{2,1,0:T(8,128)(2,1)S(1)}, bf16[8,256,160]{2,1,0:T(8,128)(2,1)S(1)}) custom-call(bf16[8,160,256]{2,1,0:T(8,128)(2,1)S(1)} %get-tuple-element.46.qd_ref, bf16[8,160,256]{2,1,0:T(8,128)(2,1)S(1)} %get-tuple-element.43.kf_ref), custom_call_target="tpu_custom_call" | custom-call | flops 4194304 | bytes 2621440 | tf_op jit(solution)/shard_map/turned/pallas_call | solution.py:34
  12.9 0.5 %collective-permute-done.1.refs_0_ = bf16[336,128]{1,0:T(8,128)(2,1)S(1)} collective-permute-done((bf16[336,128]{1,0:T(8,128)(2,1)S(1)}, bf16[336,128]{1,0:T(8,128)(2,1)S(1)}, u32[]{:S(2)}, u32[]{:S(2)}) %collective-permute-start.1) | collective-permute-done | bytes 86048 | tf_op jit(solution)/shard_map/prior_share/ppermute | solution.py:479
  13.5 1.2 %collective-permute-done.2.refs_1_ = bf16[336,128]{1,0:T(8,128)(2,1)S(1)} collective-permute-done((bf16[336,128]{1,0:T(8,128)(2,1)S(1)}, bf16[336,128]{1,0:T(8,128)(2,1)S(1)}, u32[]{:S(2)}, u32[]{:S(2)}) %collective-permute-start.2) | collective-permute-done | bytes 86048 | tf_op jit(solution)/shard_map/prior_share/ppermute | solution.py:479
  14.7 0.0 collective-permute-done.3.refs_2_
  14.7 0.2 prior_share.1
  14.9 1.5 %collective-permute-start.4 = (bf16[192,128]{1,0:T(8,128)(2,1)S(1)}, bf16[192,128]{1,0:T(8,128)(2,1)S(1)}, u32[]{:S(2)}, u32[]{:S(2)}) collective-permute-start(bf16[192,128]{1,0:T(8,128)(2,1)S(1)} %get-tuple-element.52), channel_id=1, source_target_pairs={{0,8},{2,10},{4,12},{6,14},{8,0},{10,2},{12,4},{14,6},{16,24},{18,... | collective-permute-start | bytes 147464 | tf_op jit(solution)/shard_map/prior_planes/ppermute | solution.py:479
  16.3 2.6 %collective-permute-start.5 = (bf16[192,128]{1,0:T(8,128)(2,1)S(1)}, bf16[192,128]{1,0:T(8,128)(2,1)S(1)}, u32[]{:S(2)}, u32[]{:S(2)}) collective-permute-start(bf16[192,128]{1,0:T(8,128)(2,1)S(1)} %get-tuple-element.52), channel_id=1, source_target_pairs={{0,16},{2,18},{4,20},{6,22},{8,24},{10,26},{12,28},{14,30},{16,0},... | collective-permute-start | bytes 147464 | tf_op jit(solution)/shard_map/prior_planes/ppermute | solution.py:479
  18.9 0.3 collective-permute-start.6
  19.2 0.6 %collective-permute-start.7 = (bf16[160,128]{1,0:T(8,128)(2,1)S(1)}, bf16[160,128]{1,0:T(8,128)(2,1)S(1)}, u32[]{:S(2)}, u32[]{:S(2)}) collective-permute-start(bf16[160,128]{1,0:T(8,128)(2,1)S(1)} %get-tuple-element.53), channel_id=1, source_target_pairs={{0,8},{2,10},{4,12},{6,14},{8,0},{10,2},{12,4},{14,6},{16,24},{18,... | collective-permute-start | bytes 122888 | tf_op jit(solution)/shard_map/prior_planes/ppermute | solution.py:479
  19.8 0.0 collective-permute-done.4.refs_4_
  19.8 3.1 %collective-permute-start.10 = (bf16[160,128]{1,0:T(8,128)(2,1)S(1)}, bf16[160,128]{1,0:T(8,128)(2,1)S(1)}, u32[]{:S(2)}, u32[]{:S(2)}) collective-permute-start(bf16[160,128]{1,0:T(8,128)(2,1)S(1)} %get-tuple-element.53), channel_id=1, source_target_pairs={{0,24},{2,26},{4,28},{6,30},{8,16},{10,18},{12,20},{14,22},{16,8},... | collective-permute-start | bytes 122888 | tf_op jit(solution)/shard_map/prior_planes/ppermute | solution.py:479
  22.9 0.0 collective-permute-done.8.refs_1_
  22.9 0.5 collective-permute-start.9
  23.4 1.3 %out_grad.1.og_ref = f32[256,1024]{1,0:T(8,128)S(1)} custom-call(bf16[256,1024]{1,0:T(8,128)(2,1)S(1)} %copy-done.1, bf16[256,1024]{1,0:T(8,128)(2,1)S(1)} %collective-permute-done.8.refs_1_, bf16[1024,2048]{1,0:T(8,128)(2,1)S(1)} %copy-done), custom_call_target="tpu_custom_call" | custom-call | flops 1073741824 | bytes 6291456 | tf_op jit(solution)/shard_map/out_grad/pallas_call | solution.py:34
  24.7 0.0 collective-permute-done.5.refs_5_
  24.7 0.1 collective-permute-done.6.refs_6_
  24.8 1.0 %scaled_grad.1 = (f32[256,8]{1,0:T(8,128)S(1)}, bf16[256,1024]{1,0:T(8,128)(2,1)S(1)}, f32[320,128]{1,0:T(8,128)S(1)}, bf16[4,320,128]{2,1,0:T(8,128)(2,1)S(1)}) custom-call(f32[8,256]{1,0:T(8,128)S(1)} %get-tuple-element.45.den_ref, bf16[8,160,256]{2,1,0:T(8,128)(2,1)S(1)} %get-tuple-element.46.qd_ref, f32[256,1024]{1,0:T(8,128)S(1)} %out_grad.1.og_ref, ...), custom_call_target="tpu_custom_call" | custom-call | flops 83886080 | bytes 3313664 | tf_op jit(solution)/shard_map/scaled_grad/pallas_call | solution.py:34
  25.9 0.1 collective-permute-start.14
  26.0 0.7 %collective-permute-start.15 = (bf16[320,128]{1,0:T(8,128)(2,1)S(1)}, bf16[320,128]{1,0:T(8,128)(2,1)S(1)}, u32[]{:S(2)}, u32[]{:S(2)}) collective-permute-start(bf16[320,128]{1,0:T(8,128)(2,1)S(1)} %get-tuple-element.80), channel_id=1, source_target_pairs={{0,4},{2,6},{4,0},{6,2},{8,12},{10,14},{12,8},{14,10},{16,20},{18,... | collective-permute-start | bytes 245768 | tf_op jit(solution)/shard_map/later_share/ppermute | solution.py:479
  26.6 0.0 collective-permute-done.7.refs_7_
  26.6 1.2 %collective-permute-start.16 = (bf16[320,128]{1,0:T(8,128)(2,1)S(1)}, bf16[320,128]{1,0:T(8,128)(2,1)S(1)}, u32[]{:S(2)}, u32[]{:S(2)}) collective-permute-start(bf16[320,128]{1,0:T(8,128)(2,1)S(1)} %get-tuple-element.79), channel_id=1, source_target_pairs={{0,2},{2,0},{4,6},{6,4},{8,10},{10,8},{12,14},{14,12},{16,18},{18,... | collective-permute-start | bytes 245768 | tf_op jit(solution)/shard_map/later_share/ppermute | solution.py:479
  27.8 0.0 collective-permute-done.10.refs_9_
  27.8 0.0 collective-permute-done.9.refs_8_
  27.8 0.3 prior_back.1
  28.1 0.4 collective-permute-start.11
  28.5 1.3 %collective-permute-start.12 = (bf16[320,128]{1,0:T(8,128)(2,1)S(1)}, bf16[320,128]{1,0:T(8,128)(2,1)S(1)}, u32[]{:S(2)}, u32[]{:S(2)}) collective-permute-start(bf16[320,128]{1,0:T(8,128)(2,1)S(1)} %get-tuple-element.84), channel_id=1, source_target_pairs={{0,4},{2,6},{4,0},{6,2},{8,12},{10,14},{12,8},{14,10},{16,20},{18,... | collective-permute-start | bytes 245768 | tf_op jit(solution)/shard_map/prior_back/ppermute | solution.py:479
  29.8 0.4 collective-permute-done.14.refs_0_
  30.2 0.0 collective-permute-start.13
  30.2 1.1 %collective-permute-done.15.refs_1_ = bf16[320,128]{1,0:T(8,128)(2,1)S(1)} collective-permute-done((bf16[320,128]{1,0:T(8,128)(2,1)S(1)}, bf16[320,128]{1,0:T(8,128)(2,1)S(1)}, u32[]{:S(2)}, u32[]{:S(2)}) %collective-permute-start.15) | collective-permute-done | bytes 81952 | tf_op jit(solution)/shard_map/later_share/ppermute | solution.py:479
  31.3 0.0 collective-permute-done.16.refs_2_
  31.4 2.4 %collective-permute-start.19 = (bf16[320,128]{1,0:T(8,128)(2,1)S(1)}, bf16[320,128]{1,0:T(8,128)(2,1)S(1)}, u32[]{:S(2)}, u32[]{:S(2)}) collective-permute-start(bf16[320,128]{1,0:T(8,128)(2,1)S(1)} %later_planes.1), channel_id=1, source_target_pairs={{0,16},{2,18},{4,20},{6,22},{8,24},{10,26},{12,28},{14,30},{16,0},... | collective-permute-start | bytes 245768 | tf_op jit(solution)/shard_map/later_planes/ppermute | solution.py:479
  33.7 0.7 %collective-permute-start.20 = (bf16[320,128]{1,0:T(8,128)(2,1)S(1)}, bf16[320,128]{1,0:T(8,128)(2,1)S(1)}, u32[]{:S(2)}, u32[]{:S(2)}) collective-permute-start(bf16[320,128]{1,0:T(8,128)(2,1)S(1)} %later_planes.1), channel_id=1, source_target_pairs={{0,24},{2,26},{4,28},{6,30},{8,16},{10,18},{12,20},{14,22},{16,8},... | collective-permute-start | bytes 245768 | tf_op jit(solution)/shard_map/later_planes/ppermute | solution.py:479
  34.5 0.0 collective-permute-done.11
  34.5 0.4 collective-permute-done.12
  34.9 0.0 collective-permute-done.13
  35.0 1.0 %attended.1 = (bf16[256,1024]{1,0:T(8,128)(2,1)S(1)}, bf16[256,1024]{1,0:T(8,128)(2,1)S(1)}) custom-call(bf16[8,256,160]{2,1,0:T(8,128)(2,1)S(1)} %get-tuple-element.47.qt_ref, bf16[4,320,128]{2,1,0:T(8,128)(2,1)S(1)} %pad_maximum_fusion.prior_ref, f32[256,1024]{1,0:T(8,128)S(1)} %get-tuple-element.61.num_ref, f32[256,8]{1,0:T(8,128)S(1)} %get-tuple-element.62.inv_ref, ...), custom_call_target="tpu_custom_call" | custom-call | flops 620756992 | bytes 7282688 | tf_op jit(solution)/shard_map/attended/pallas_call | solution.py:34
  36.0 1.4 %collective-permute-start.17 = (bf16[256,1024]{1,0:T(8,128)(2,1)S(1)}, bf16[256,1024]{1,0:T(8,128)(2,1)S(1)}, u32[]{:S(2)}, u32[]{:S(2)}) collective-permute-start(bf16[256,1024]{1,0:T(8,128)(2,1)S(1)} %get-tuple-element.65), channel_id=1, source_target_pairs={{0,1},{1,0},{2,3},{3,2},{4,5},{5,4},{6,7},{7,6},{8,9},{9,8},{10,11... | collective-permute-start | bytes 1572872 | tf_op jit(solution)/shard_map/attended/ppermute | solution.py:479
  37.4 0.7 %collective-permute-start.18 = (bf16[320,128]{1,0:T(8,128)(2,1)S(1)}, bf16[320,128]{1,0:T(8,128)(2,1)S(1)}, u32[]{:S(2)}, u32[]{:S(2)}) collective-permute-start(bf16[320,128]{1,0:T(8,128)(2,1)S(1)} %later_planes.1), channel_id=1, source_target_pairs={{0,8},{2,10},{4,12},{6,14},{8,0},{10,2},{12,4},{14,6},{16,24},{18,... | collective-permute-start | bytes 245768 | tf_op jit(solution)/shard_map/later_planes/ppermute | solution.py:479
  38.1 0.4 near.1.near_ref
  38.6 0.7 %mixed.1.part_ref = f32[256,1024]{1,0:T(8,128)S(1)} custom-call(bf16[256,1024]{1,0:T(8,128)(2,1)S(1)} %get-tuple-element.64.att_ref, bf16[1024,2048]{1,0:T(8,128)(2,1)S(1)} %copy-done), custom_call_target="tpu_custom_call" | custom-call | flops 1073741824 | bytes 5767168 | tf_op jit(solution)/shard_map/mixed/pallas_call | solution.py:34
  39.3 3.0 %collective-permute-done.18.refs_4_ = bf16[320,128]{1,0:T(8,128)(2,1)S(1)} collective-permute-done((bf16[320,128]{1,0:T(8,128)(2,1)S(1)}, bf16[320,128]{1,0:T(8,128)(2,1)S(1)}, u32[]{:S(2)}, u32[]{:S(2)}) %collective-permute-start.18) | collective-permute-done | bytes 81952 | tf_op jit(solution)/shard_map/later_planes/ppermute | solution.py:479
  42.3 0.0 collective-permute-done.19.refs_5_
  42.3 0.0 collective-permute-done.20.refs_6_
  42.3 0.2 later_back.1
  42.6 0.1 collective-permute-start.21
  42.7 1.5 %collective-permute-start.22 = (bf16[320,128]{1,0:T(8,128)(2,1)S(1)}, bf16[320,128]{1,0:T(8,128)(2,1)S(1)}, u32[]{:S(2)}, u32[]{:S(2)}) collective-permute-start(bf16[320,128]{1,0:T(8,128)(2,1)S(1)} %get-tuple-element.76), channel_id=1, source_target_pairs={{0,4},{2,6},{4,0},{6,2},{8,12},{10,14},{12,8},{14,10},{16,20},{18,... | collective-permute-start | bytes 245768 | tf_op jit(solution)/shard_map/later_back/ppermute | solution.py:479
  44.2 0.4 collective-permute-start.23
  44.6 0.0 collective-permute-done.21.refs_1_
  44.6 0.3 far_grad.2.early_ref
  44.8 3.1 %collective-permute-done.22.refs_0_ = bf16[320,128]{1,0:T(8,128)(2,1)S(1)} collective-permute-done((bf16[320,128]{1,0:T(8,128)(2,1)S(1)}, bf16[320,128]{1,0:T(8,128)(2,1)S(1)}, u32[]{:S(2)}, u32[]{:S(2)}) %collective-permute-start.22) | collective-permute-done | bytes 81952 | tf_op jit(solution)/shard_map/later_back/ppermute | solution.py:479
  47.9 1.0 %collective-permute-done.23.refs_1_ = bf16[320,128]{1,0:T(8,128)(2,1)S(1)} collective-permute-done((bf16[320,128]{1,0:T(8,128)(2,1)S(1)}, bf16[320,128]{1,0:T(8,128)(2,1)S(1)}, u32[]{:S(2)}, u32[]{:S(2)}) %collective-permute-start.23) | collective-permute-done | bytes 81952 | tf_op jit(solution)/shard_map/later_back/ppermute | solution.py:479
  48.9 1.0 %far_grad.3 = bf16[256,1024]{1,0:T(8,128)(2,1)} custom-call(bf16[8,256,160]{2,1,0:T(8,128)(2,1)S(1)} %get-tuple-element.66.kt_ref, f32[256,1024]{1,0:T(8,128)S(1)} %near.1.near_ref, bf16[2,256,256]{2,1,0:T(8,128)(2,1)S(1)} %far_grad.2.early_ref, bf16[320,128]{1,0:T(8,128)(2,1)S(1)} %collective-permute-done.22.refs_0_, ...), custom_call_target="tpu_custom_call" | custom-call | flops 1342177280 | bytes 2654208 | tf_op jit(solution)/shard_map/far_grad/pallas_call | solution.py:34
  49.9 0.1 collective-permute-done.17.refs_0_
  50.0 0.8 %mixed_out.1 = bf16[256,1024]{1,0:T(8,128)(2,1)} custom-call(f32[256,1024]{1,0:T(8,128)S(1)} %mixed.1.part_ref, bf16[256,1024]{1,0:T(8,128)(2,1)S(1)} %collective-permute-done.17.refs_0_), custom_call_target="tpu_custom_call" | custom-call | flops 1048576 | bytes 2097152 | tf_op jit(solution)/shard_map/mixed_out/pallas_call | solution.py:34
  (10 shorter events, 0.2 us)
Async XLA Ops:
  1.4 6.8 %collective-permute-start = (bf16[2,1152]{1,0:T(2,128)(2,1)S(1)}, bf16[2,1152]{1,0:T(2,128)(2,1)S(1)}, u32[]{:S(2)}, u32[]{:S(2)}) collective-permute-start(bf16[2,1152]{1,0:T(2,128)(2,1)S(1)} %edge.1), channel_id=1, source_target_pairs={{0,2},{2,4},{4,6},{6,8},{8,10},{10,12},{12,14},{14,16},{16,18},{18... | collective-permute-start | bytes 13832 | tf_op jit(solution)/shard_map/edge/ppermute | solution.py:512
  1.9 21.0 %collective-permute-start.8 = (bf16[256,1024]{1,0:T(8,128)(2,1)}, bf16[256,1024]{1,0:T(8,128)(2,1)S(1)}, u32[]{:S(2)}, u32[]{:S(2)}) collective-permute-start(bf16[256,1024]{1,0:T(8,128)(2,1)} %refs_0_), channel_id=1, source_target_pairs={{0,1},{1,0},{2,3},{3,2},{4,5},{5,4},{6,7},{7,6},{8,9},{9,8},{10,11... | collective-permute-start | bytes 1572872 | tf_op jit(solution)/shard_map/cotangent/ppermute | solution.py:479
  9.2 4.3 %collective-permute-start.1 = (bf16[336,128]{1,0:T(8,128)(2,1)S(1)}, bf16[336,128]{1,0:T(8,128)(2,1)S(1)}, u32[]{:S(2)}, u32[]{:S(2)}) collective-permute-start(bf16[336,128]{1,0:T(8,128)(2,1)S(1)} %get-tuple-element.74), channel_id=1, source_target_pairs={{0,6},{2,4},{4,2},{6,0},{8,14},{10,12},{12,10},{14,8},{16,22},{18,... | collective-permute-start | bytes 258056 | tf_op jit(solution)/shard_map/prior_share/ppermute | solution.py:479
  9.3 5.4 %collective-permute-start.2 = (bf16[336,128]{1,0:T(8,128)(2,1)S(1)}, bf16[336,128]{1,0:T(8,128)(2,1)S(1)}, u32[]{:S(2)}, u32[]{:S(2)}) collective-permute-start(bf16[336,128]{1,0:T(8,128)(2,1)S(1)} %get-tuple-element.73), channel_id=1, source_target_pairs={{0,4},{2,6},{4,0},{6,2},{8,12},{10,14},{12,8},{14,10},{16,20},{18,... | collective-permute-start | bytes 258056 | tf_op jit(solution)/shard_map/prior_share/ppermute | solution.py:479
  9.6 5.1 %collective-permute-start.3 = (bf16[336,128]{1,0:T(8,128)(2,1)S(1)}, bf16[336,128]{1,0:T(8,128)(2,1)S(1)}, u32[]{:S(2)}, u32[]{:S(2)}) collective-permute-start(bf16[336,128]{1,0:T(8,128)(2,1)S(1)} %get-tuple-element.72), channel_id=1, source_target_pairs={{0,2},{2,0},{4,6},{6,4},{8,10},{10,8},{12,14},{14,12},{16,18},{18,... | collective-permute-start | bytes 258056 | tf_op jit(solution)/shard_map/prior_share/ppermute | solution.py:479
  11.1 12.3 %copy-start = (bf16[1024,2048]{1,0:T(8,128)(2,1)S(1)}, bf16[1024,2048]{1,0:T(8,128)(2,1)}, u32[]{:S(2)}) copy-start(bf16[1024,2048]{1,0:T(8,128)(2,1)} %w_ref.3) | copy-start | bytes 12582916
  11.1 12.3 %copy-start.1 = (bf16[256,1024]{1,0:T(8,128)(2,1)S(1)}, bf16[256,1024]{1,0:T(8,128)(2,1)}, u32[]{:S(2)}) copy-start(bf16[256,1024]{1,0:T(8,128)(2,1)} %refs_0_) | copy-start | bytes 1572868
  14.9 5.0 %collective-permute-start.4 = (bf16[192,128]{1,0:T(8,128)(2,1)S(1)}, bf16[192,128]{1,0:T(8,128)(2,1)S(1)}, u32[]{:S(2)}, u32[]{:S(2)}) collective-permute-start(bf16[192,128]{1,0:T(8,128)(2,1)S(1)} %get-tuple-element.52), channel_id=1, source_target_pairs={{0,8},{2,10},{4,12},{6,14},{8,0},{10,2},{12,4},{14,6},{16,24},{18,... | collective-permute-start | bytes 147464 | tf_op jit(solution)/shard_map/prior_planes/ppermute | solution.py:479
  16.3 8.4 %collective-permute-start.5 = (bf16[192,128]{1,0:T(8,128)(2,1)S(1)}, bf16[192,128]{1,0:T(8,128)(2,1)S(1)}, u32[]{:S(2)}, u32[]{:S(2)}) collective-permute-start(bf16[192,128]{1,0:T(8,128)(2,1)S(1)} %get-tuple-element.52), channel_id=1, source_target_pairs={{0,16},{2,18},{4,20},{6,22},{8,24},{10,26},{12,28},{14,30},{16,0},... | collective-permute-start | bytes 147464 | tf_op jit(solution)/shard_map/prior_planes/ppermute | solution.py:479
  18.9 5.9 %collective-permute-start.6 = (bf16[192,128]{1,0:T(8,128)(2,1)S(1)}, bf16[192,128]{1,0:T(8,128)(2,1)S(1)}, u32[]{:S(2)}, u32[]{:S(2)}) collective-permute-start(bf16[192,128]{1,0:T(8,128)(2,1)S(1)} %get-tuple-element.52), channel_id=1, source_target_pairs={{0,24},{2,26},{4,28},{6,30},{8,16},{10,18},{12,20},{14,22},{16,8},... | collective-permute-start | bytes 147464 | tf_op jit(solution)/shard_map/prior_planes/ppermute | solution.py:479
  19.2 7.4 %collective-permute-start.7 = (bf16[160,128]{1,0:T(8,128)(2,1)S(1)}, bf16[160,128]{1,0:T(8,128)(2,1)S(1)}, u32[]{:S(2)}, u32[]{:S(2)}) collective-permute-start(bf16[160,128]{1,0:T(8,128)(2,1)S(1)} %get-tuple-element.53), channel_id=1, source_target_pairs={{0,8},{2,10},{4,12},{6,14},{8,0},{10,2},{12,4},{14,6},{16,24},{18,... | collective-permute-start | bytes 122888 | tf_op jit(solution)/shard_map/prior_planes/ppermute | solution.py:479
  19.8 8.0 %collective-permute-start.10 = (bf16[160,128]{1,0:T(8,128)(2,1)S(1)}, bf16[160,128]{1,0:T(8,128)(2,1)S(1)}, u32[]{:S(2)}, u32[]{:S(2)}) collective-permute-start(bf16[160,128]{1,0:T(8,128)(2,1)S(1)} %get-tuple-element.53), channel_id=1, source_target_pairs={{0,24},{2,26},{4,28},{6,30},{8,16},{10,18},{12,20},{14,22},{16,8},... | collective-permute-start | bytes 122888 | tf_op jit(solution)/shard_map/prior_planes/ppermute | solution.py:479
  22.9 4.9 %collective-permute-start.9 = (bf16[160,128]{1,0:T(8,128)(2,1)S(1)}, bf16[160,128]{1,0:T(8,128)(2,1)S(1)}, u32[]{:S(2)}, u32[]{:S(2)}) collective-permute-start(bf16[160,128]{1,0:T(8,128)(2,1)S(1)} %get-tuple-element.53), channel_id=1, source_target_pairs={{0,16},{2,18},{4,20},{6,22},{8,24},{10,26},{12,28},{14,30},{16,0},... | collective-permute-start | bytes 122888 | tf_op jit(solution)/shard_map/prior_planes/ppermute | solution.py:479
  25.9 4.3 %collective-permute-start.14 = (bf16[320,128]{1,0:T(8,128)(2,1)S(1)}, bf16[320,128]{1,0:T(8,128)(2,1)S(1)}, u32[]{:S(2)}, u32[]{:S(2)}) collective-permute-start(bf16[320,128]{1,0:T(8,128)(2,1)S(1)} %get-tuple-element.81), channel_id=1, source_target_pairs={{0,6},{2,4},{4,2},{6,0},{8,14},{10,12},{12,10},{14,8},{16,22},{18,... | collective-permute-start | bytes 245768 | tf_op jit(solution)/shard_map/later_share/ppermute | solution.py:479
  26.0 5.3 %collective-permute-start.15 = (bf16[320,128]{1,0:T(8,128)(2,1)S(1)}, bf16[320,128]{1,0:T(8,128)(2,1)S(1)}, u32[]{:S(2)}, u32[]{:S(2)}) collective-permute-start(bf16[320,128]{1,0:T(8,128)(2,1)S(1)} %get-tuple-element.80), channel_id=1, source_target_pairs={{0,4},{2,6},{4,0},{6,2},{8,12},{10,14},{12,8},{14,10},{16,20},{18,... | collective-permute-start | bytes 245768 | tf_op jit(solution)/shard_map/later_share/ppermute | solution.py:479
  26.6 4.7 %collective-permute-start.16 = (bf16[320,128]{1,0:T(8,128)(2,1)S(1)}, bf16[320,128]{1,0:T(8,128)(2,1)S(1)}, u32[]{:S(2)}, u32[]{:S(2)}) collective-permute-start(bf16[320,128]{1,0:T(8,128)(2,1)S(1)} %get-tuple-element.79), channel_id=1, source_target_pairs={{0,2},{2,0},{4,6},{6,4},{8,10},{10,8},{12,14},{14,12},{16,18},{18,... | collective-permute-start | bytes 245768 | tf_op jit(solution)/shard_map/later_share/ppermute | solution.py:479
  28.1 6.4 %collective-permute-start.11 = (bf16[320,128]{1,0:T(8,128)(2,1)S(1)}, bf16[320,128]{1,0:T(8,128)(2,1)S(1)}, u32[]{:S(2)}, u32[]{:S(2)}) collective-permute-start(bf16[320,128]{1,0:T(8,128)(2,1)S(1)} %get-tuple-element.85), channel_id=1, source_target_pairs={{0,6},{2,4},{4,2},{6,0},{8,14},{10,12},{12,10},{14,8},{16,22},{18,... | collective-permute-start | bytes 245768 | tf_op jit(solution)/shard_map/prior_back/ppermute | solution.py:479
  28.5 6.4 %collective-permute-start.12 = (bf16[320,128]{1,0:T(8,128)(2,1)S(1)}, bf16[320,128]{1,0:T(8,128)(2,1)S(1)}, u32[]{:S(2)}, u32[]{:S(2)}) collective-permute-start(bf16[320,128]{1,0:T(8,128)(2,1)S(1)} %get-tuple-element.84), channel_id=1, source_target_pairs={{0,4},{2,6},{4,0},{6,2},{8,12},{10,14},{12,8},{14,10},{16,20},{18,... | collective-permute-start | bytes 245768 | tf_op jit(solution)/shard_map/prior_back/ppermute | solution.py:479
  30.2 4.8 %collective-permute-start.13 = (bf16[320,128]{1,0:T(8,128)(2,1)S(1)}, bf16[320,128]{1,0:T(8,128)(2,1)S(1)}, u32[]{:S(2)}, u32[]{:S(2)}) collective-permute-start(bf16[320,128]{1,0:T(8,128)(2,1)S(1)} %get-tuple-element.83), channel_id=1, source_target_pairs={{0,2},{2,0},{4,6},{6,4},{8,10},{10,8},{12,14},{14,12},{16,18},{18,... | collective-permute-start | bytes 245768 | tf_op jit(solution)/shard_map/prior_back/ppermute | solution.py:479
  31.4 11.0 %collective-permute-start.19 = (bf16[320,128]{1,0:T(8,128)(2,1)S(1)}, bf16[320,128]{1,0:T(8,128)(2,1)S(1)}, u32[]{:S(2)}, u32[]{:S(2)}) collective-permute-start(bf16[320,128]{1,0:T(8,128)(2,1)S(1)} %later_planes.1), channel_id=1, source_target_pairs={{0,16},{2,18},{4,20},{6,22},{8,24},{10,26},{12,28},{14,30},{16,0},... | collective-permute-start | bytes 245768 | tf_op jit(solution)/shard_map/later_planes/ppermute | solution.py:479
  33.7 8.6 %collective-permute-start.20 = (bf16[320,128]{1,0:T(8,128)(2,1)S(1)}, bf16[320,128]{1,0:T(8,128)(2,1)S(1)}, u32[]{:S(2)}, u32[]{:S(2)}) collective-permute-start(bf16[320,128]{1,0:T(8,128)(2,1)S(1)} %later_planes.1), channel_id=1, source_target_pairs={{0,24},{2,26},{4,28},{6,30},{8,16},{10,18},{12,20},{14,22},{16,8},... | collective-permute-start | bytes 245768 | tf_op jit(solution)/shard_map/later_planes/ppermute | solution.py:479
  36.0 14.0 %collective-permute-start.17 = (bf16[256,1024]{1,0:T(8,128)(2,1)S(1)}, bf16[256,1024]{1,0:T(8,128)(2,1)S(1)}, u32[]{:S(2)}, u32[]{:S(2)}) collective-permute-start(bf16[256,1024]{1,0:T(8,128)(2,1)S(1)} %get-tuple-element.65), channel_id=1, source_target_pairs={{0,1},{1,0},{2,3},{3,2},{4,5},{5,4},{6,7},{7,6},{8,9},{9,8},{10,11... | collective-permute-start | bytes 1572872 | tf_op jit(solution)/shard_map/attended/ppermute | solution.py:479
  37.4 4.9 %collective-permute-start.18 = (bf16[320,128]{1,0:T(8,128)(2,1)S(1)}, bf16[320,128]{1,0:T(8,128)(2,1)S(1)}, u32[]{:S(2)}, u32[]{:S(2)}) collective-permute-start(bf16[320,128]{1,0:T(8,128)(2,1)S(1)} %later_planes.1), channel_id=1, source_target_pairs={{0,8},{2,10},{4,12},{6,14},{8,0},{10,2},{12,4},{14,6},{16,24},{18,... | collective-permute-start | bytes 245768 | tf_op jit(solution)/shard_map/later_planes/ppermute | solution.py:479
  42.6 1.9 %collective-permute-start.21 = (bf16[320,128]{1,0:T(8,128)(2,1)S(1)}, bf16[320,128]{1,0:T(8,128)(2,1)S(1)}, u32[]{:S(2)}, u32[]{:S(2)}) collective-permute-start(bf16[320,128]{1,0:T(8,128)(2,1)S(1)} %get-tuple-element.77), channel_id=1, source_target_pairs={{0,2},{2,0},{4,6},{6,4},{8,10},{10,8},{12,14},{14,12},{16,18},{18,... | collective-permute-start | bytes 245768 | tf_op jit(solution)/shard_map/later_back/ppermute | solution.py:479
  42.7 5.3 %collective-permute-start.22 = (bf16[320,128]{1,0:T(8,128)(2,1)S(1)}, bf16[320,128]{1,0:T(8,128)(2,1)S(1)}, u32[]{:S(2)}, u32[]{:S(2)}) collective-permute-start(bf16[320,128]{1,0:T(8,128)(2,1)S(1)} %get-tuple-element.76), channel_id=1, source_target_pairs={{0,4},{2,6},{4,0},{6,2},{8,12},{10,14},{12,8},{14,10},{16,20},{18,... | collective-permute-start | bytes 245768 | tf_op jit(solution)/shard_map/later_back/ppermute | solution.py:479
  44.2 4.7 %collective-permute-start.23 = (bf16[320,128]{1,0:T(8,128)(2,1)S(1)}, bf16[320,128]{1,0:T(8,128)(2,1)S(1)}, u32[]{:S(2)}, u32[]{:S(2)}) collective-permute-start(bf16[320,128]{1,0:T(8,128)(2,1)S(1)} %get-tuple-element.75), channel_id=1, source_target_pairs={{0,6},{2,4},{4,2},{6,0},{8,14},{10,12},{12,10},{14,8},{16,22},{18,... | collective-permute-start | bytes 245768 | tf_op jit(solution)/shard_map/later_back/ppermute | solution.py:479

commit v10 on v9

--- a/solution.py
+++ b/solution.py
@@ -137,12 +137,15 @@
         kt_ref[head] = kf_ref[head].T
 
 
-def grad_kernel(*refs):
+def own_grad_kernel(cot_ref, w_ref, og_ref):
+    og_ref[...] = mm(cot_ref[...], w_ref[:, columns_of(w_ref, 0)], NT)
+
+
+def grad_kernel(before_ref, *refs):
     *cots, w_ref, og_ref = refs
-    total = None
+    total = before_ref[...]
     for j, cot_ref in enumerate(cots):
-        term = mm(cot_ref[...], w_ref[:, columns_of(w_ref, j)], NT)
-        total = term if total is None else total + term
+        total = total + mm(cot_ref[...], w_ref[:, columns_of(w_ref, j + 1)], NT)
     og_ref[...] = total
 
 
@@ -208,10 +211,11 @@
     found, used = [], 0
     for first in range(0, piece_rows, ROWS):
         free = min(SPARE, count - used)
-        found.append(state[first + ROWS - SPARE - 1 : first + ROWS, :][1 : 1 + free].astype(F32))
+        tile = state[first + ROWS - 16 : first + ROWS, :].astype(F32)
+        found.append(tile[16 - SPARE : 16 - SPARE + free])
         used += free
-    rest = state[piece_rows:, :][: count - used].astype(F32)
-    return jnp.concatenate(found + [rest], 0)
+    rest = state[piece_rows:, :].astype(F32)
+    return jnp.concatenate(found + [rest[: count - used]], 0)
 
 
 def key_kernel(
@@ -345,7 +349,9 @@
     heads = qd_ref.shape[0]
     per_piece = heads // PLANE
     piece_rows = per_piece * ROWS
-    lines = before_plane(1, strides, moved_refs, pl.ds(piece_rows // 2, 15 * heads // 4))
+    half = piece_rows // 2
+    lines = before_plane(1, strides, moved_refs, pl.ds(half, moved_refs[0].shape[0] - half))
+    lines = lines[: 15 * heads // 4]
     for i in range(1, PLANE):
         here = lines_in(got_refs[i], piece_rows)
         lines = lines + masked(is_ahead(1, rank ^ i, rank), here)
@@ -560,15 +566,19 @@
     with jax.named_scope("turned"):
         outs = [S((heads, tokens, ROWS), BF16)] * 2
         qt, kt = call(turn_kernel, (after(qd, den), kf), outs, 1 << 22)
+    with jax.named_scope("own_grad"):
+        ops = (after(cotangent, den), out_weight)
+        outs = [S((tokens, width), F32)]
+        (own_grad,) = call(own_grad_kernel, ops, outs, project_flops)
     with jax.named_scope("prior_planes"):
-        sent = lax.optimization_barrier((*sent[:2], qt))[:2]
+        sent = lax.optimization_barrier((*sent[:2], qt, own_grad))[:2]
         norm_join = functools.partial(join, (half, half + count))
         rest, strides = planes_ahead(total[1], sent[1], 1, functools.partial(join, None))
         moved, _ = planes_ahead(total[0], sent[0], 1, norm_join)
     with jax.named_scope("out_grad"):
-        ops = (after(cotangent, moved[0]), *cots, out_weight)
+        ops = (after(own_grad, moved[0]), *cots, out_weight)
         (out_grad,) = call(
-            grad_kernel, ops, [S((tokens, width), F32)], groups * project_flops
+            grad_kernel, ops, [S((tokens, width), F32)], (groups - 1) * project_flops
         )
     with jax.named_scope("scaled_grad"):
         outs = [

time: 51.1 us -> 51.1 us (level)
    pallas_call x16 -> x17, Pallas kernels: 11.2 us -> 11.4 us  [call(): pl.pallas_call(body, out_shape=out_shape, in_specs=[hbm if i in far else...]
  transfers between devices with their start and end apart: 24 -> 24, of which waited for: 11 -> 10; matrix products, arithmetic and copies ran while one was open for 0% -> 0% of each run, Pallas kernels for 20% -> 21%
where the time goes in v10:
time: 51.1 us; the launch traced here: 50.9 us
  starting transfers between devices  23.9 us (47%)
  waiting for transfers between devices  13.4 us (26%)
  Pallas kernels  12.2 us (24%)
  between operations  0.84 us (2%)
  local copies, waits for them, and re-layouts  0.56 us (1%)
    ppermute x23, starting transfers between devices, swapped(): return lax.ppermute(x, axis, pairs)  23.4 us
    pallas_call x17, Pallas kernels, call(): pl.pallas_call(body, out_shape=out_shape, in_specs=[hbm if i in far else...  11.4 us
    ppermute x23, waiting for transfers between devices, swapped(): return lax.ppermute(x, axis, pairs)  10.8 us
    ppermute x1, waiting for transfers between devices, per_device(): lax.ppermute(last_rows, 'ctx', [(i, (i + 1) % slabs) for i in range(slabs)])  2.55 us
  transfers between devices with their start and end apart: 24, of which 10 were waited for; matrix products, arithmetic and copies ran while one was open for 0% of the time, Pallas kernels for 21%

profile of v10, /device:TPU:0, one launch (start us, length us, event | category | flops | bytes accessed | tf_op | source)
XLA Modules:
  0.0 50.9 jit_solution(6177509293679658003)
XLA Ops:
  0.6 0.8 %edge.1 = bf16[2,1152]{1,0:T(2,128)(2,1)S(1)} custom-call(bf16[256,128]{1,0:T(8,128)(2,1)} %k_far.3, bf16[256,1024]{1,0:T(8,128)(2,1)} %v_far.3), custom_call_target="tpu_custom_call" | custom-call | tf_op jit(solution)/shard_map/edge/pallas_call | solution.py:509
  1.4 0.5 collective-permute-start
  1.9 2.6 %collective-permute-start.8 = (bf16[256,1024]{1,0:T(8,128)(2,1)}, bf16[256,1024]{1,0:T(8,128)(2,1)S(1)}, u32[]{:S(2)}, u32[]{:S(2)}) collective-permute-start(bf16[256,1024]{1,0:T(8,128)(2,1)} %cot_ref), channel_id=1, source_target_pairs={{0,1},{1,0},{2,3},{3,2},{4,5},{5,4},{6,7},{7,6},{8,9},{9,8},{10,11... | collective-permute-start | bytes 1572872 | tf_op jit(solution)/shard_map/cotangent/ppermute | solution.py:485
  4.5 1.2 %query_features.1 = (bf16[8,160,256]{2,1,0:T(8,128)(2,1)S(1)}, bf16[256,128]{1,0:T(8,128)(2,1)S(1)}, bf16[256,1024]{1,0:T(8,128)(2,1)S(1)}, f32[3,128]{1,0:T(4,128)S(1)}, f32[3,1024]{1,0:T(4,128)S(1)}) custom-call(bf16[256,128]{1,0:T(8,128)(2,1)} %q_far, bf16[256,128]{1,0:T(8,128)(2,1)} %k_far.3, bf16[256,1024]{1,0:T(8,128)(2,1)} %v_far.3, f32[3,128]{1,0:T(4,128)} %ck_far.1, ...), custom_call_target="tpu_custom_call" | custom-call | flops 1048576 | bytes 1928192 | tf_op jit(solution)/shard_map/query_features/pallas_call | solution.py:34
  5.7 2.6 %collective-permute-done.before_ref = bf16[2,1152]{1,0:T(2,128)(2,1)S(1)} collective-permute-done((bf16[2,1152]{1,0:T(2,128)(2,1)S(1)}, bf16[2,1152]{1,0:T(2,128)(2,1)S(1)}, u32[]{:S(2)}, u32[]{:S(2)}) %collective-permute-start) | collective-permute-done | bytes 4640 | tf_op jit(solution)/shard_map/edge/ppermute | solution.py:518
  8.2 0.9 %key_features.1 = (bf16[8,160,256]{2,1,0:T(8,128)(2,1)S(1)}, bf16[256,1024]{1,0:T(8,128)(2,1)S(1)}, f32[336,128]{1,0:T(8,128)S(1)}, bf16[4,336,128]{2,1,0:T(8,128)(2,1)S(1)}) custom-call(bf16[256,128]{1,0:T(8,128)(2,1)S(1)} %get-tuple-element.40.k_ref, bf16[256,1024]{1,0:T(8,128)(2,1)S(1)} %get-tuple-element.41.v_ref, ...), custom_call_target="tpu_custom_call" | custom-call | flops 83886080 | bytes 2304000 | tf_op jit(solution)/shard_map/key_features/pallas_call | solution.py:34
  9.2 0.1 collective-permute-start.1
  9.3 0.4 collective-permute-start.2
  9.6 1.5 %collective-permute-start.3 = (bf16[336,128]{1,0:T(8,128)(2,1)S(1)}, bf16[336,128]{1,0:T(8,128)(2,1)S(1)}, u32[]{:S(2)}, u32[]{:S(2)}) collective-permute-start(bf16[336,128]{1,0:T(8,128)(2,1)S(1)} %get-tuple-element.74), channel_id=1, source_target_pairs={{0,2},{2,0},{4,6},{6,4},{8,10},{10,8},{12,14},{14,12},{16,18},{18,... | collective-permute-start | bytes 258056 | tf_op jit(solution)/shard_map/prior_share/ppermute | solution.py:485
  11.1 1.2 %scores.1 = (bf16[8,256,256]{2,1,0:T(8,128)(2,1)S(1)}, f32[8,256]{1,0:T(8,128)S(1)}, f32[256,1024]{1,0:T(8,128)S(1)}) custom-call(bf16[8,160,256]{2,1,0:T(8,128)(2,1)S(1)} %get-tuple-element.47.qd_ref, bf16[8,160,256]{2,1,0:T(8,128)(2,1)S(1)} %get-tuple-element.44.kf_ref, bf16[256,1024]{1,0:T(8,128)(2,1)S(1)} %get-tuple-element.45.vc_ref), custom_call_target="tpu_custom_call" | custom-call | flops 33554432000 | bytes 3940352 | tf_op jit(solution)/shard_map/scores/pallas_call | solution.py:34
  12.3 0.6 %turned.1 = (bf16[8,256,160]{2,1,0:T(8,128)(2,1)S(1)}, bf16[8,256,160]{2,1,0:T(8,128)(2,1)S(1)}) custom-call(bf16[8,160,256]{2,1,0:T(8,128)(2,1)S(1)} %get-tuple-element.47.qd_ref, bf16[8,160,256]{2,1,0:T(8,128)(2,1)S(1)} %get-tuple-element.44.kf_ref), custom_call_target="tpu_custom_call" | custom-call | flops 4194304 | bytes 2621440 | tf_op jit(solution)/shard_map/turned/pallas_call | solution.py:34
  13.0 0.4 copy-done
  13.3 0.1 copy-done.1
  13.4 0.7 %own_grad.1.before_ref = f32[256,1024]{1,0:T(8,128)S(1)} custom-call(bf16[256,1024]{1,0:T(8,128)(2,1)S(1)} %copy-done.1, bf16[1024,2048]{1,0:T(8,128)(2,1)S(1)} %copy-done), custom_call_target="tpu_custom_call" | custom-call | flops 536870912 | bytes 5767168 | tf_op jit(solution)/shard_map/own_grad/pallas_call | solution.py:34
  14.2 0.0 collective-permute-done.1.refs_0_
  14.2 0.5 %collective-permute-done.2.refs_1_ = bf16[336,128]{1,0:T(8,128)(2,1)S(1)} collective-permute-done((bf16[336,128]{1,0:T(8,128)(2,1)S(1)}, bf16[336,128]{1,0:T(8,128)(2,1)S(1)}, u32[]{:S(2)}, u32[]{:S(2)}) %collective-permute-start.2) | collective-permute-done | bytes 86048 | tf_op jit(solution)/shard_map/prior_share/ppermute | solution.py:485
  14.7 0.0 collective-permute-done.3.refs_2_
  14.7 0.2 prior_share.1
  14.9 1.5 %collective-permute-start.4 = (bf16[192,128]{1,0:T(8,128)(2,1)S(1)}, bf16[192,128]{1,0:T(8,128)(2,1)S(1)}, u32[]{:S(2)}, u32[]{:S(2)}) collective-permute-start(bf16[192,128]{1,0:T(8,128)(2,1)S(1)} %get-tuple-element.54), channel_id=1, source_target_pairs={{0,8},{2,10},{4,12},{6,14},{8,0},{10,2},{12,4},{14,6},{16,24},{18,... | collective-permute-start | bytes 147464 | tf_op jit(solution)/shard_map/prior_planes/ppermute | solution.py:485
  16.3 2.6 %collective-permute-start.5 = (bf16[192,128]{1,0:T(8,128)(2,1)S(1)}, bf16[192,128]{1,0:T(8,128)(2,1)S(1)}, u32[]{:S(2)}, u32[]{:S(2)}) collective-permute-start(bf16[192,128]{1,0:T(8,128)(2,1)S(1)} %get-tuple-element.54), channel_id=1, source_target_pairs={{0,16},{2,18},{4,20},{6,22},{8,24},{10,26},{12,28},{14,30},{16,0},... | collective-permute-start | bytes 147464 | tf_op jit(solution)/shard_map/prior_planes/ppermute | solution.py:485
  18.9 0.3 collective-permute-start.6
  19.2 0.6 %collective-permute-start.7 = (bf16[160,128]{1,0:T(8,128)(2,1)S(1)}, bf16[160,128]{1,0:T(8,128)(2,1)S(1)}, u32[]{:S(2)}, u32[]{:S(2)}) collective-permute-start(bf16[160,128]{1,0:T(8,128)(2,1)S(1)} %get-tuple-element.55), channel_id=1, source_target_pairs={{0,8},{2,10},{4,12},{6,14},{8,0},{10,2},{12,4},{14,6},{16,24},{18,... | collective-permute-start | bytes 122888 | tf_op jit(solution)/shard_map/prior_planes/ppermute | solution.py:485
  19.8 0.0 collective-permute-done.4.refs_4_
  19.8 3.1 %collective-permute-start.10 = (bf16[160,128]{1,0:T(8,128)(2,1)S(1)}, bf16[160,128]{1,0:T(8,128)(2,1)S(1)}, u32[]{:S(2)}, u32[]{:S(2)}) collective-permute-start(bf16[160,128]{1,0:T(8,128)(2,1)S(1)} %get-tuple-element.55), channel_id=1, source_target_pairs={{0,24},{2,26},{4,28},{6,30},{8,16},{10,18},{12,20},{14,22},{16,8},... | collective-permute-start | bytes 122888 | tf_op jit(solution)/shard_map/prior_planes/ppermute | solution.py:485
  22.9 0.0 collective-permute-done.8.refs_0_
  22.9 0.5 collective-permute-start.9
  23.4 0.7 %out_grad.1.og_ref = f32[256,1024]{1,0:T(8,128)S(1)} custom-call(f32[256,1024]{1,0:T(8,128)S(1)} %own_grad.1.before_ref, bf16[256,1024]{1,0:T(8,128)(2,1)S(1)} %collective-permute-done.8.refs_0_, bf16[1024,2048]{1,0:T(8,128)(2,1)S(1)} %copy-done), custom_call_target="tpu_custom_call" | custom-call | flops 536870912 | bytes 6815744 | tf_op jit(solution)/shard_map/out_grad/pallas_call | solution.py:34
  24.1 0.0 collective-permute-done.5.refs_5_
  24.1 0.7 %collective-permute-done.6.refs_6_ = bf16[192,128]{1,0:T(8,128)(2,1)S(1)} collective-permute-done((bf16[192,128]{1,0:T(8,128)(2,1)S(1)}, bf16[192,128]{1,0:T(8,128)(2,1)S(1)}, u32[]{:S(2)}, u32[]{:S(2)}) %collective-permute-start.6) | collective-permute-done | bytes 49184 | tf_op jit(solution)/shard_map/prior_planes/ppermute | solution.py:485
  24.8 1.0 %scaled_grad.1 = (f32[256,8]{1,0:T(8,128)S(1)}, bf16[256,1024]{1,0:T(8,128)(2,1)S(1)}, f32[320,128]{1,0:T(8,128)S(1)}, bf16[4,320,128]{2,1,0:T(8,128)(2,1)S(1)}) custom-call(f32[8,256]{1,0:T(8,128)S(1)} %get-tuple-element.46.den_ref, bf16[8,160,256]{2,1,0:T(8,128)(2,1)S(1)} %get-tuple-element.47.qd_ref, f32[256,1024]{1,0:T(8,128)S(1)} %out_grad.1.og_ref, ...), custom_call_target="tpu_custom_call" | custom-call | flops 83886080 | bytes 3313664 | tf_op jit(solution)/shard_map/scaled_grad/pallas_call | solution.py:34
  25.9 0.1 collective-permute-start.14
  26.0 0.7 %collective-permute-start.15 = (bf16[320,128]{1,0:T(8,128)(2,1)S(1)}, bf16[320,128]{1,0:T(8,128)(2,1)S(1)}, u32[]{:S(2)}, u32[]{:S(2)}) collective-permute-start(bf16[320,128]{1,0:T(8,128)(2,1)S(1)} %get-tuple-element.82), channel_id=1, source_target_pairs={{0,4},{2,6},{4,0},{6,2},{8,12},{10,14},{12,8},{14,10},{16,20},{18,... | collective-permute-start | bytes 245768 | tf_op jit(solution)/shard_map/later_share/ppermute | solution.py:485
  26.6 0.0 collective-permute-done.7.refs_7_
  26.6 1.2 %collective-permute-start.16 = (bf16[320,128]{1,0:T(8,128)(2,1)S(1)}, bf16[320,128]{1,0:T(8,128)(2,1)S(1)}, u32[]{:S(2)}, u32[]{:S(2)}) collective-permute-start(bf16[320,128]{1,0:T(8,128)(2,1)S(1)} %get-tuple-element.81), channel_id=1, source_target_pairs={{0,2},{2,0},{4,6},{6,4},{8,10},{10,8},{12,14},{14,12},{16,18},{18,... | collective-permute-start | bytes 245768 | tf_op jit(solution)/shard_map/later_share/ppermute | solution.py:485
  27.8 0.0 collective-permute-done.10.refs_9_
  27.8 0.0 collective-permute-done.9.refs_8_
  27.8 0.3 prior_back.1
  28.1 0.4 collective-permute-start.11
  28.5 1.3 %collective-permute-start.12 = (bf16[320,128]{1,0:T(8,128)(2,1)S(1)}, bf16[320,128]{1,0:T(8,128)(2,1)S(1)}, u32[]{:S(2)}, u32[]{:S(2)}) collective-permute-start(bf16[320,128]{1,0:T(8,128)(2,1)S(1)} %get-tuple-element.86), channel_id=1, source_target_pairs={{0,4},{2,6},{4,0},{6,2},{8,12},{10,14},{12,8},{14,10},{16,20},{18,... | collective-permute-start | bytes 245768 | tf_op jit(solution)/shard_map/prior_back/ppermute | solution.py:485
  29.8 0.3 collective-permute-done.14.refs_0_
  30.2 0.0 collective-permute-start.13
  30.2 1.1 %collective-permute-done.15.refs_1_ = bf16[320,128]{1,0:T(8,128)(2,1)S(1)} collective-permute-done((bf16[320,128]{1,0:T(8,128)(2,1)S(1)}, bf16[320,128]{1,0:T(8,128)(2,1)S(1)}, u32[]{:S(2)}, u32[]{:S(2)}) %collective-permute-start.15) | collective-permute-done | bytes 81952 | tf_op jit(solution)/shard_map/later_share/ppermute | solution.py:485
  31.3 0.0 collective-permute-done.16.refs_2_
  31.4 1.8 %collective-permute-start.19 = (bf16[320,128]{1,0:T(8,128)(2,1)S(1)}, bf16[320,128]{1,0:T(8,128)(2,1)S(1)}, u32[]{:S(2)}, u32[]{:S(2)}) collective-permute-start(bf16[320,128]{1,0:T(8,128)(2,1)S(1)} %later_planes.1), channel_id=1, source_target_pairs={{0,16},{2,18},{4,20},{6,22},{8,24},{10,26},{12,28},{14,30},{16,0},... | collective-permute-start | bytes 245768 | tf_op jit(solution)/shard_map/later_planes/ppermute | solution.py:485
  33.2 0.7 %collective-permute-start.20 = (bf16[320,128]{1,0:T(8,128)(2,1)S(1)}, bf16[320,128]{1,0:T(8,128)(2,1)S(1)}, u32[]{:S(2)}, u32[]{:S(2)}) collective-permute-start(bf16[320,128]{1,0:T(8,128)(2,1)S(1)} %later_planes.1), channel_id=1, source_target_pairs={{0,24},{2,26},{4,28},{6,30},{8,16},{10,18},{12,20},{14,22},{16,8},... | collective-permute-start | bytes 245768 | tf_op jit(solution)/shard_map/later_planes/ppermute | solution.py:485
  33.9 0.0 collective-permute-done.11
  33.9 1.0 %collective-permute-done.12 = bf16[320,128]{1,0:T(8,128)(2,1)S(1)} collective-permute-done((bf16[320,128]{1,0:T(8,128)(2,1)S(1)}, bf16[320,128]{1,0:T(8,128)(2,1)S(1)}, u32[]{:S(2)}, u32[]{:S(2)}) %collective-permute-start.12) | collective-permute-done | bytes 81952 | tf_op jit(solution)/shard_map/prior_back/ppermute | solution.py:485
  35.0 1.0 %attended.1 = (bf16[256,1024]{1,0:T(8,128)(2,1)S(1)}, bf16[256,1024]{1,0:T(8,128)(2,1)S(1)}) custom-call(bf16[8,256,160]{2,1,0:T(8,128)(2,1)S(1)} %get-tuple-element.48.qt_ref, bf16[4,320,128]{2,1,0:T(8,128)(2,1)S(1)} %pad_maximum_fusion.prior_ref, f32[256,1024]{1,0:T(8,128)S(1)} %get-tuple-element.63.num_ref, f32[256,8]{1,0:T(8,128)S(1)} %get-tuple-element.64.inv_ref, ...), custom_call_target="tpu_custom_call" | custom-call | flops 620756992 | bytes 7282688 | tf_op jit(solution)/shard_map/attended/pallas_call | solution.py:34
  36.0 1.7 %collective-permute-start.17 = (bf16[256,1024]{1,0:T(8,128)(2,1)S(1)}, bf16[256,1024]{1,0:T(8,128)(2,1)S(1)}, u32[]{:S(2)}, u32[]{:S(2)}) collective-permute-start(bf16[256,1024]{1,0:T(8,128)(2,1)S(1)} %get-tuple-element.67), channel_id=1, source_target_pairs={{0,1},{1,0},{2,3},{3,2},{4,5},{5,4},{6,7},{7,6},{8,9},{9,8},{10,11... | collective-permute-start | bytes 1572872 | tf_op jit(solution)/shard_map/attended/ppermute | solution.py:485
  37.7 0.5 collective-permute-start.18
  38.3 0.4 near.1.near_ref
  38.7 0.7 %mixed.1.part_ref = f32[256,1024]{1,0:T(8,128)S(1)} custom-call(bf16[256,1024]{1,0:T(8,128)(2,1)S(1)} %get-tuple-element.66.att_ref, bf16[1024,2048]{1,0:T(8,128)(2,1)S(1)} %copy-done), custom_call_target="tpu_custom_call" | custom-call | flops 1073741824 | bytes 5767168 | tf_op jit(solution)/shard_map/mixed/pallas_call | solution.py:34
  39.4 2.8 %collective-permute-done.18.refs_4_ = bf16[320,128]{1,0:T(8,128)(2,1)S(1)} collective-permute-done((bf16[320,128]{1,0:T(8,128)(2,1)S(1)}, bf16[320,128]{1,0:T(8,128)(2,1)S(1)}, u32[]{:S(2)}, u32[]{:S(2)}) %collective-permute-start.18) | collective-permute-done | bytes 81952 | tf_op jit(solution)/shard_map/later_planes/ppermute | solution.py:485
  42.2 0.0 collective-permute-done.19.refs_5_
  42.3 0.2 later_back.1
  42.5 0.1 collective-permute-start.21
  42.6 1.2 %collective-permute-start.22 = (bf16[320,128]{1,0:T(8,128)(2,1)S(1)}, bf16[320,128]{1,0:T(8,128)(2,1)S(1)}, u32[]{:S(2)}, u32[]{:S(2)}) collective-permute-start(bf16[320,128]{1,0:T(8,128)(2,1)S(1)} %get-tuple-element.78), channel_id=1, source_target_pairs={{0,4},{2,6},{4,0},{6,2},{8,12},{10,14},{12,8},{14,10},{16,20},{18,... | collective-permute-start | bytes 245768 | tf_op jit(solution)/shard_map/later_back/ppermute | solution.py:485
  43.8 0.7 %collective-permute-start.23 = (bf16[320,128]{1,0:T(8,128)(2,1)S(1)}, bf16[320,128]{1,0:T(8,128)(2,1)S(1)}, u32[]{:S(2)}, u32[]{:S(2)}) collective-permute-start(bf16[320,128]{1,0:T(8,128)(2,1)S(1)} %get-tuple-element.77), channel_id=1, source_target_pairs={{0,6},{2,4},{4,2},{6,0},{8,14},{10,12},{12,10},{14,8},{16,22},{18,... | collective-permute-start | bytes 245768 | tf_op jit(solution)/shard_map/later_back/ppermute | solution.py:485
  44.5 0.3 far_grad.2.early_ref
  44.8 3.2 %collective-permute-done.22.refs_0_ = bf16[320,128]{1,0:T(8,128)(2,1)S(1)} collective-permute-done((bf16[320,128]{1,0:T(8,128)(2,1)S(1)}, bf16[320,128]{1,0:T(8,128)(2,1)S(1)}, u32[]{:S(2)}, u32[]{:S(2)}) %collective-permute-start.22) | collective-permute-done | bytes 81952 | tf_op jit(solution)/shard_map/later_back/ppermute | solution.py:485
  47.9 0.8 %collective-permute-done.23.refs_1_ = bf16[320,128]{1,0:T(8,128)(2,1)S(1)} collective-permute-done((bf16[320,128]{1,0:T(8,128)(2,1)S(1)}, bf16[320,128]{1,0:T(8,128)(2,1)S(1)}, u32[]{:S(2)}, u32[]{:S(2)}) %collective-permute-start.23) | collective-permute-done | bytes 81952 | tf_op jit(solution)/shard_map/later_back/ppermute | solution.py:485
  48.8 1.0 %far_grad.3 = bf16[256,1024]{1,0:T(8,128)(2,1)} custom-call(bf16[8,256,160]{2,1,0:T(8,128)(2,1)S(1)} %get-tuple-element.68.kt_ref, f32[256,1024]{1,0:T(8,128)S(1)} %near.1.near_ref, bf16[2,256,256]{2,1,0:T(8,128)(2,1)S(1)} %far_grad.2.early_ref, bf16[320,128]{1,0:T(8,128)(2,1)S(1)} %collective-permute-done.22.refs_0_, ...), custom_call_target="tpu_custom_call" | custom-call | flops 1342177280 | bytes 2654208 | tf_op jit(solution)/shard_map/far_grad/pallas_call | solution.py:34
  49.8 0.3 collective-permute-done.17.refs_0_
  50.0 0.8 %mixed_out.1 = bf16[256,1024]{1,0:T(8,128)(2,1)} custom-call(f32[256,1024]{1,0:T(8,128)S(1)} %mixed.1.part_ref, bf16[256,1024]{1,0:T(8,128)(2,1)S(1)} %collective-permute-done.17.refs_0_), custom_call_target="tpu_custom_call" | custom-call | flops 1048576 | bytes 2097152 | tf_op jit(solution)/shard_map/mixed_out/pallas_call | solution.py:34
  (11 shorter events, 0.2 us)
Async XLA Ops:
  1.4 6.8 %collective-permute-start = (bf16[2,1152]{1,0:T(2,128)(2,1)S(1)}, bf16[2,1152]{1,0:T(2,128)(2,1)S(1)}, u32[]{:S(2)}, u32[]{:S(2)}) collective-permute-start(bf16[2,1152]{1,0:T(2,128)(2,1)S(1)} %edge.1), channel_id=1, source_target_pairs={{0,2},{2,4},{4,6},{6,8},{8,10},{10,12},{12,14},{14,16},{16,18},{18... | collective-permute-start | bytes 13832 | tf_op jit(solution)/shard_map/edge/ppermute | solution.py:518
  1.9 21.0 %collective-permute-start.8 = (bf16[256,1024]{1,0:T(8,128)(2,1)}, bf16[256,1024]{1,0:T(8,128)(2,1)S(1)}, u32[]{:S(2)}, u32[]{:S(2)}) collective-permute-start(bf16[256,1024]{1,0:T(8,128)(2,1)} %cot_ref), channel_id=1, source_target_pairs={{0,1},{1,0},{2,3},{3,2},{4,5},{5,4},{6,7},{7,6},{8,9},{9,8},{10,11... | collective-permute-start | bytes 1572872 | tf_op jit(solution)/shard_map/cotangent/ppermute | solution.py:485
  9.2 5.0 %collective-permute-start.1 = (bf16[336,128]{1,0:T(8,128)(2,1)S(1)}, bf16[336,128]{1,0:T(8,128)(2,1)S(1)}, u32[]{:S(2)}, u32[]{:S(2)}) collective-permute-start(bf16[336,128]{1,0:T(8,128)(2,1)S(1)} %get-tuple-element.76), channel_id=1, source_target_pairs={{0,6},{2,4},{4,2},{6,0},{8,14},{10,12},{12,10},{14,8},{16,22},{18,... | collective-permute-start | bytes 258056 | tf_op jit(solution)/shard_map/prior_share/ppermute | solution.py:485
  9.3 5.4 %collective-permute-start.2 = (bf16[336,128]{1,0:T(8,128)(2,1)S(1)}, bf16[336,128]{1,0:T(8,128)(2,1)S(1)}, u32[]{:S(2)}, u32[]{:S(2)}) collective-permute-start(bf16[336,128]{1,0:T(8,128)(2,1)S(1)} %get-tuple-element.75), channel_id=1, source_target_pairs={{0,4},{2,6},{4,0},{6,2},{8,12},{10,14},{12,8},{14,10},{16,20},{18,... | collective-permute-start | bytes 258056 | tf_op jit(solution)/shard_map/prior_share/ppermute | solution.py:485
  9.6 5.1 %collective-permute-start.3 = (bf16[336,128]{1,0:T(8,128)(2,1)S(1)}, bf16[336,128]{1,0:T(8,128)(2,1)S(1)}, u32[]{:S(2)}, u32[]{:S(2)}) collective-permute-start(bf16[336,128]{1,0:T(8,128)(2,1)S(1)} %get-tuple-element.74), channel_id=1, source_target_pairs={{0,2},{2,0},{4,6},{6,4},{8,10},{10,8},{12,14},{14,12},{16,18},{18,... | collective-permute-start | bytes 258056 | tf_op jit(solution)/shard_map/prior_share/ppermute | solution.py:485
  11.1 2.2 %copy-start = (bf16[1024,2048]{1,0:T(8,128)(2,1)S(1)}, bf16[1024,2048]{1,0:T(8,128)(2,1)}, u32[]{:S(2)}) copy-start(bf16[1024,2048]{1,0:T(8,128)(2,1)} %w_ref.5) | copy-start | bytes 12582916
  11.1 2.3 %copy-start.1 = (bf16[256,1024]{1,0:T(8,128)(2,1)S(1)}, bf16[256,1024]{1,0:T(8,128)(2,1)}, u32[]{:S(2)}) copy-start(bf16[256,1024]{1,0:T(8,128)(2,1)} %cot_ref) | copy-start | bytes 1572868
  14.9 5.0 %collective-permute-start.4 = (bf16[192,128]{1,0:T(8,128)(2,1)S(1)}, bf16[192,128]{1,0:T(8,128)(2,1)S(1)}, u32[]{:S(2)}, u32[]{:S(2)}) collective-permute-start(bf16[192,128]{1,0:T(8,128)(2,1)S(1)} %get-tuple-element.54), channel_id=1, source_target_pairs={{0,8},{2,10},{4,12},{6,14},{8,0},{10,2},{12,4},{14,6},{16,24},{18,... | collective-permute-start | bytes 147464 | tf_op jit(solution)/shard_map/prior_planes/ppermute | solution.py:485
  16.3 7.8 %collective-permute-start.5 = (bf16[192,128]{1,0:T(8,128)(2,1)S(1)}, bf16[192,128]{1,0:T(8,128)(2,1)S(1)}, u32[]{:S(2)}, u32[]{:S(2)}) collective-permute-start(bf16[192,128]{1,0:T(8,128)(2,1)S(1)} %get-tuple-element.54), channel_id=1, source_target_pairs={{0,16},{2,18},{4,20},{6,22},{8,24},{10,26},{12,28},{14,30},{16,0},... | collective-permute-start | bytes 147464 | tf_op jit(solution)/shard_map/prior_planes/ppermute | solution.py:485
  18.9 5.9 %collective-permute-start.6 = (bf16[192,128]{1,0:T(8,128)(2,1)S(1)}, bf16[192,128]{1,0:T(8,128)(2,1)S(1)}, u32[]{:S(2)}, u32[]{:S(2)}) collective-permute-start(bf16[192,128]{1,0:T(8,128)(2,1)S(1)} %get-tuple-element.54), channel_id=1, source_target_pairs={{0,24},{2,26},{4,28},{6,30},{8,16},{10,18},{12,20},{14,22},{16,8},... | collective-permute-start | bytes 147464 | tf_op jit(solution)/shard_map/prior_planes/ppermute | solution.py:485
  19.2 7.4 %collective-permute-start.7 = (bf16[160,128]{1,0:T(8,128)(2,1)S(1)}, bf16[160,128]{1,0:T(8,128)(2,1)S(1)}, u32[]{:S(2)}, u32[]{:S(2)}) collective-permute-start(bf16[160,128]{1,0:T(8,128)(2,1)S(1)} %get-tuple-element.55), channel_id=1, source_target_pairs={{0,8},{2,10},{4,12},{6,14},{8,0},{10,2},{12,4},{14,6},{16,24},{18,... | collective-permute-start | bytes 122888 | tf_op jit(solution)/shard_map/prior_planes/ppermute | solution.py:485
  19.8 8.0 %collective-permute-start.10 = (bf16[160,128]{1,0:T(8,128)(2,1)S(1)}, bf16[160,128]{1,0:T(8,128)(2,1)S(1)}, u32[]{:S(2)}, u32[]{:S(2)}) collective-permute-start(bf16[160,128]{1,0:T(8,128)(2,1)S(1)} %get-tuple-element.55), channel_id=1, source_target_pairs={{0,24},{2,26},{4,28},{6,30},{8,16},{10,18},{12,20},{14,22},{16,8},... | collective-permute-start | bytes 122888 | tf_op jit(solution)/shard_map/prior_planes/ppermute | solution.py:485
  22.9 4.9 %collective-permute-start.9 = (bf16[160,128]{1,0:T(8,128)(2,1)S(1)}, bf16[160,128]{1,0:T(8,128)(2,1)S(1)}, u32[]{:S(2)}, u32[]{:S(2)}) collective-permute-start(bf16[160,128]{1,0:T(8,128)(2,1)S(1)} %get-tuple-element.55), channel_id=1, source_target_pairs={{0,16},{2,18},{4,20},{6,22},{8,24},{10,26},{12,28},{14,30},{16,0},... | collective-permute-start | bytes 122888 | tf_op jit(solution)/shard_map/prior_planes/ppermute | solution.py:485
  25.9 4.3 %collective-permute-start.14 = (bf16[320,128]{1,0:T(8,128)(2,1)S(1)}, bf16[320,128]{1,0:T(8,128)(2,1)S(1)}, u32[]{:S(2)}, u32[]{:S(2)}) collective-permute-start(bf16[320,128]{1,0:T(8,128)(2,1)S(1)} %get-tuple-element.83), channel_id=1, source_target_pairs={{0,6},{2,4},{4,2},{6,0},{8,14},{10,12},{12,10},{14,8},{16,22},{18,... | collective-permute-start | bytes 245768 | tf_op jit(solution)/shard_map/later_share/ppermute | solution.py:485
  26.0 5.3 %collective-permute-start.15 = (bf16[320,128]{1,0:T(8,128)(2,1)S(1)}, bf16[320,128]{1,0:T(8,128)(2,1)S(1)}, u32[]{:S(2)}, u32[]{:S(2)}) collective-permute-start(bf16[320,128]{1,0:T(8,128)(2,1)S(1)} %get-tuple-element.82), channel_id=1, source_target_pairs={{0,4},{2,6},{4,0},{6,2},{8,12},{10,14},{12,8},{14,10},{16,20},{18,... | collective-permute-start | bytes 245768 | tf_op jit(solution)/shard_map/later_share/ppermute | solution.py:485
  26.6 4.7 %collective-permute-start.16 = (bf16[320,128]{1,0:T(8,128)(2,1)S(1)}, bf16[320,128]{1,0:T(8,128)(2,1)S(1)}, u32[]{:S(2)}, u32[]{:S(2)}) collective-permute-start(bf16[320,128]{1,0:T(8,128)(2,1)S(1)} %get-tuple-element.81), channel_id=1, source_target_pairs={{0,2},{2,0},{4,6},{6,4},{8,10},{10,8},{12,14},{14,12},{16,18},{18,... | collective-permute-start | bytes 245768 | tf_op jit(solution)/shard_map/later_share/ppermute | solution.py:485
  28.1 5.8 %collective-permute-start.11 = (bf16[320,128]{1,0:T(8,128)(2,1)S(1)}, bf16[320,128]{1,0:T(8,128)(2,1)S(1)}, u32[]{:S(2)}, u32[]{:S(2)}) collective-permute-start(bf16[320,128]{1,0:T(8,128)(2,1)S(1)} %get-tuple-element.87), channel_id=1, source_target_pairs={{0,6},{2,4},{4,2},{6,0},{8,14},{10,12},{12,10},{14,8},{16,22},{18,... | collective-permute-start | bytes 245768 | tf_op jit(solution)/shard_map/prior_back/ppermute | solution.py:485
  28.5 6.4 %collective-permute-start.12 = (bf16[320,128]{1,0:T(8,128)(2,1)S(1)}, bf16[320,128]{1,0:T(8,128)(2,1)S(1)}, u32[]{:S(2)}, u32[]{:S(2)}) collective-permute-start(bf16[320,128]{1,0:T(8,128)(2,1)S(1)} %get-tuple-element.86), channel_id=1, source_target_pairs={{0,4},{2,6},{4,0},{6,2},{8,12},{10,14},{12,8},{14,10},{16,20},{18,... | collective-permute-start | bytes 245768 | tf_op jit(solution)/shard_map/prior_back/ppermute | solution.py:485
  30.2 4.8 %collective-permute-start.13 = (bf16[320,128]{1,0:T(8,128)(2,1)S(1)}, bf16[320,128]{1,0:T(8,128)(2,1)S(1)}, u32[]{:S(2)}, u32[]{:S(2)}) collective-permute-start(bf16[320,128]{1,0:T(8,128)(2,1)S(1)} %get-tuple-element.85), channel_id=1, source_target_pairs={{0,2},{2,0},{4,6},{6,4},{8,10},{10,8},{12,14},{14,12},{16,18},{18,... | collective-permute-start | bytes 245768 | tf_op jit(solution)/shard_map/prior_back/ppermute | solution.py:485
  31.4 10.9 %collective-permute-start.19 = (bf16[320,128]{1,0:T(8,128)(2,1)S(1)}, bf16[320,128]{1,0:T(8,128)(2,1)S(1)}, u32[]{:S(2)}, u32[]{:S(2)}) collective-permute-start(bf16[320,128]{1,0:T(8,128)(2,1)S(1)} %later_planes.1), channel_id=1, source_target_pairs={{0,16},{2,18},{4,20},{6,22},{8,24},{10,26},{12,28},{14,30},{16,0},... | collective-permute-start | bytes 245768 | tf_op jit(solution)/shard_map/later_planes/ppermute | solution.py:485
  33.2 9.1 %collective-permute-start.20 = (bf16[320,128]{1,0:T(8,128)(2,1)S(1)}, bf16[320,128]{1,0:T(8,128)(2,1)S(1)}, u32[]{:S(2)}, u32[]{:S(2)}) collective-permute-start(bf16[320,128]{1,0:T(8,128)(2,1)S(1)} %later_planes.1), channel_id=1, source_target_pairs={{0,24},{2,26},{4,28},{6,30},{8,16},{10,18},{12,20},{14,22},{16,8},... | collective-permute-start | bytes 245768 | tf_op jit(solution)/shard_map/later_planes/ppermute | solution.py:485
  36.0 14.0 %collective-permute-start.17 = (bf16[256,1024]{1,0:T(8,128)(2,1)S(1)}, bf16[256,1024]{1,0:T(8,128)(2,1)S(1)}, u32[]{:S(2)}, u32[]{:S(2)}) collective-permute-start(bf16[256,1024]{1,0:T(8,128)(2,1)S(1)} %get-tuple-element.67), channel_id=1, source_target_pairs={{0,1},{1,0},{2,3},{3,2},{4,5},{5,4},{6,7},{7,6},{8,9},{9,8},{10,11... | collective-permute-start | bytes 1572872 | tf_op jit(solution)/shard_map/attended/ppermute | solution.py:485
  37.7 4.5 %collective-permute-start.18 = (bf16[320,128]{1,0:T(8,128)(2,1)S(1)}, bf16[320,128]{1,0:T(8,128)(2,1)S(1)}, u32[]{:S(2)}, u32[]{:S(2)}) collective-permute-start(bf16[320,128]{1,0:T(8,128)(2,1)S(1)} %later_planes.1), channel_id=1, source_target_pairs={{0,8},{2,10},{4,12},{6,14},{8,0},{10,2},{12,4},{14,6},{16,24},{18,... | collective-permute-start | bytes 245768 | tf_op jit(solution)/shard_map/later_planes/ppermute | solution.py:485
  42.5 1.9 %collective-permute-start.21 = (bf16[320,128]{1,0:T(8,128)(2,1)S(1)}, bf16[320,128]{1,0:T(8,128)(2,1)S(1)}, u32[]{:S(2)}, u32[]{:S(2)}) collective-permute-start(bf16[320,128]{1,0:T(8,128)(2,1)S(1)} %get-tuple-element.79), channel_id=1, source_target_pairs={{0,2},{2,0},{4,6},{6,4},{8,10},{10,8},{12,14},{14,12},{16,18},{18,... | collective-permute-start | bytes 245768 | tf_op jit(solution)/shard_map/later_back/ppermute | solution.py:485
  42.6 5.3 %collective-permute-start.22 = (bf16[320,128]{1,0:T(8,128)(2,1)S(1)}, bf16[320,128]{1,0:T(8,128)(2,1)S(1)}, u32[]{:S(2)}, u32[]{:S(2)}) collective-permute-start(bf16[320,128]{1,0:T(8,128)(2,1)S(1)} %get-tuple-element.78), channel_id=1, source_target_pairs={{0,4},{2,6},{4,0},{6,2},{8,12},{10,14},{12,8},{14,10},{16,20},{18,... | collective-permute-start | bytes 245768 | tf_op jit(solution)/shard_map/later_back/ppermute | solution.py:485
  43.8 5.0 %collective-permute-start.23 = (bf16[320,128]{1,0:T(8,128)(2,1)S(1)}, bf16[320,128]{1,0:T(8,128)(2,1)S(1)}, u32[]{:S(2)}, u32[]{:S(2)}) collective-permute-start(bf16[320,128]{1,0:T(8,128)(2,1)S(1)} %get-tuple-element.77), channel_id=1, source_target_pairs={{0,6},{2,4},{4,2},{6,0},{8,14},{10,12},{12,10},{14,8},{16,22},{18,... | collective-permute-start | bytes 245768 | tf_op jit(solution)/shard_map/later_back/ppermute | solution.py:485

commit v11 on v10

--- a/solution.py
+++ b/solution.py
@@ -13,6 +13,7 @@
 ROWS = 160
 VMEM_LIMIT = 14 * 1024 * 1024
 SPARE = 7
+FIRST = 4
 PLANE = 4
 
 F32 = jnp.float32
@@ -266,7 +267,7 @@
     total = own_ref[...]
     for got_ref in got_refs:
         total = total + got_ref[...].astype(F32)
-    half = piece_rows // 2
+    half = piece_rows * FIRST // 10
     lines = norm_rows(norm_values(lines_in(total, piece_rows)))
     parts = (with_tail(total[:half], lines, out_refs[0].shape[0]), total[half:piece_rows])
     for ref, part in zip(out_refs, parts):
@@ -312,12 +313,13 @@
     got_refs, moved_refs, pieces_ref = refs[:PLANE][::-1], refs[PLANE:-1], refs[-1]
     rank = lax.rem(lax.axis_index("ctx"), PLANE)
     count = len(strides)
-    parts = len(moved_refs) // count
-    deep = pieces_ref.shape[1] // parts
-    for part in range(parts):
+    whole = pieces_ref.shape[1]
+    cuts = [0, whole] if len(moved_refs) == count else [0, whole * FIRST // 10, whole]
+    for part in range(len(cuts) - 1):
+        deep = cuts[part + 1] - cuts[part]
         refs = moved_refs[part * count : (part + 1) * count]
         before = before_plane(sign, strides, refs, pl.ds(0, deep))
-        rows = pl.ds(part * deep, deep)
+        rows = pl.ds(cuts[part], deep)
         for slot in range(PLANE):
             total = before
             for i in range(PLANE):
@@ -349,7 +351,7 @@
     heads = qd_ref.shape[0]
     per_piece = heads // PLANE
     piece_rows = per_piece * ROWS
-    half = piece_rows // 2
+    half = piece_rows * FIRST // 10
     lines = before_plane(1, strides, moved_refs, pl.ds(half, moved_refs[0].shape[0] - half))
     lines = lines[: 15 * heads // 4]
     for i in range(1, PLANE):
@@ -541,9 +543,9 @@
         got = [swapped(send[j], "ctx", j) for j in range(1, PLANE)]
 
         more = lax.axis_size("ctx") > 4 * PLANE
-        half = piece_rows // 2
+        half = piece_rows * FIRST // 10
         count = 15 * heads // 4
-        shapes = [(half + -(-count // 16) * 16, VDIM), (half, VDIM)]
+        shapes = [(half + -(-count // 16) * 16, VDIM), (piece_rows - half, VDIM)]
         outs = [S(x, BF16) for x in shapes] + [S(x, F32) for x in shapes]
         body = functools.partial(share_kernel, piece_rows)
         sent = call(body, (own, *got[::-1]), outs[: 4 if more else 2], 1 << 20)

time: 51.1 us -> 51 us (level)
  no operation moved by 1% of the time
where the time goes in v11:
time: 51 us; the launch traced here: 50.8 us
  starting transfers between devices  23.7 us (46%)
  waiting for transfers between devices  13.5 us (26%)
  Pallas kernels  12.2 us (24%)
  between operations  0.84 us (2%)
  local copies, waits for them, and re-layouts  0.56 us (1%)
    ppermute x23, starting transfers between devices, swapped(): return lax.ppermute(x, axis, pairs)  23.1 us
    pallas_call x17, Pallas kernels, call(): pl.pallas_call(body, out_shape=out_shape, in_specs=[hbm if i in far else...  11.4 us
    ppermute x23, waiting for transfers between devices, swapped(): return lax.ppermute(x, axis, pairs)  11 us
    ppermute x1, waiting for transfers between devices, per_device(): lax.ppermute(last_rows, 'ctx', [(i, (i + 1) % slabs) for i in range(slabs)])  2.55 us
  transfers between devices with their start and end apart: 24, of which 10 were waited for; matrix products, arithmetic and copies ran while one was open for 0% of the time, Pallas kernels for 21%

profile of v11, /device:TPU:0, one launch (start us, length us, event | category | flops | bytes accessed | tf_op | source)
XLA Modules:
  0.0 50.8 jit_solution(16271298761256970649)
XLA Ops:
  0.6 0.8 %edge.1 = bf16[2,1152]{1,0:T(2,128)(2,1)S(1)} custom-call(bf16[256,128]{1,0:T(8,128)(2,1)} %k_far.3, bf16[256,1024]{1,0:T(8,128)(2,1)} %v_far.3), custom_call_target="tpu_custom_call" | custom-call | tf_op jit(solution)/shard_map/edge/pallas_call | solution.py:511
  1.4 0.5 collective-permute-start
  1.9 2.6 %collective-permute-start.8 = (bf16[256,1024]{1,0:T(8,128)(2,1)}, bf16[256,1024]{1,0:T(8,128)(2,1)S(1)}, u32[]{:S(2)}, u32[]{:S(2)}) collective-permute-start(bf16[256,1024]{1,0:T(8,128)(2,1)} %cot_ref), channel_id=1, source_target_pairs={{0,1},{1,0},{2,3},{3,2},{4,5},{5,4},{6,7},{7,6},{8,9},{9,8},{10,11... | collective-permute-start | bytes 1572872 | tf_op jit(solution)/shard_map/cotangent/ppermute | solution.py:487
  4.5 1.2 %query_features.1 = (bf16[8,160,256]{2,1,0:T(8,128)(2,1)S(1)}, bf16[256,128]{1,0:T(8,128)(2,1)S(1)}, bf16[256,1024]{1,0:T(8,128)(2,1)S(1)}, f32[3,128]{1,0:T(4,128)S(1)}, f32[3,1024]{1,0:T(4,128)S(1)}) custom-call(bf16[256,128]{1,0:T(8,128)(2,1)} %q_far, bf16[256,128]{1,0:T(8,128)(2,1)} %k_far.3, bf16[256,1024]{1,0:T(8,128)(2,1)} %v_far.3, f32[3,128]{1,0:T(4,128)} %ck_far.1, ...), custom_call_target="tpu_custom_call" | custom-call | flops 1048576 | bytes 1928192 | tf_op jit(solution)/shard_map/query_features/pallas_call | solution.py:35
  5.7 2.6 %collective-permute-done.before_ref = bf16[2,1152]{1,0:T(2,128)(2,1)S(1)} collective-permute-done((bf16[2,1152]{1,0:T(2,128)(2,1)S(1)}, bf16[2,1152]{1,0:T(2,128)(2,1)S(1)}, u32[]{:S(2)}, u32[]{:S(2)}) %collective-permute-start) | collective-permute-done | bytes 4640 | tf_op jit(solution)/shard_map/edge/ppermute | solution.py:520
  8.2 0.9 %key_features.1 = (bf16[8,160,256]{2,1,0:T(8,128)(2,1)S(1)}, bf16[256,1024]{1,0:T(8,128)(2,1)S(1)}, f32[336,128]{1,0:T(8,128)S(1)}, bf16[4,336,128]{2,1,0:T(8,128)(2,1)S(1)}) custom-call(bf16[256,128]{1,0:T(8,128)(2,1)S(1)} %get-tuple-element.40.k_ref, bf16[256,1024]{1,0:T(8,128)(2,1)S(1)} %get-tuple-element.41.v_ref, ...), custom_call_target="tpu_custom_call" | custom-call | flops 83886080 | bytes 2304000 | tf_op jit(solution)/shard_map/key_features/pallas_call | solution.py:35
  9.2 0.1 collective-permute-start.1
  9.3 0.4 collective-permute-start.2
  9.6 1.5 %collective-permute-start.3 = (bf16[336,128]{1,0:T(8,128)(2,1)S(1)}, bf16[336,128]{1,0:T(8,128)(2,1)S(1)}, u32[]{:S(2)}, u32[]{:S(2)}) collective-permute-start(bf16[336,128]{1,0:T(8,128)(2,1)S(1)} %get-tuple-element.74), channel_id=1, source_target_pairs={{0,2},{2,0},{4,6},{6,4},{8,10},{10,8},{12,14},{14,12},{16,18},{18,... | collective-permute-start | bytes 258056 | tf_op jit(solution)/shard_map/prior_share/ppermute | solution.py:487
  11.1 1.2 %scores.1 = (bf16[8,256,256]{2,1,0:T(8,128)(2,1)S(1)}, f32[8,256]{1,0:T(8,128)S(1)}, f32[256,1024]{1,0:T(8,128)S(1)}) custom-call(bf16[8,160,256]{2,1,0:T(8,128)(2,1)S(1)} %get-tuple-element.47.qd_ref, bf16[8,160,256]{2,1,0:T(8,128)(2,1)S(1)} %get-tuple-element.44.kf_ref, bf16[256,1024]{1,0:T(8,128)(2,1)S(1)} %get-tuple-element.45.vc_ref), custom_call_target="tpu_custom_call" | custom-call | flops 33554432000 | bytes 3940352 | tf_op jit(solution)/shard_map/scores/pallas_call | solution.py:35
  12.3 0.6 %turned.1 = (bf16[8,256,160]{2,1,0:T(8,128)(2,1)S(1)}, bf16[8,256,160]{2,1,0:T(8,128)(2,1)S(1)}) custom-call(bf16[8,160,256]{2,1,0:T(8,128)(2,1)S(1)} %get-tuple-element.47.qd_ref, bf16[8,160,256]{2,1,0:T(8,128)(2,1)S(1)} %get-tuple-element.44.kf_ref), custom_call_target="tpu_custom_call" | custom-call | flops 4194304 | bytes 2621440 | tf_op jit(solution)/shard_map/turned/pallas_call | solution.py:35
  12.9 0.4 copy-done
  13.3 0.1 copy-done.1
  13.4 0.7 %own_grad.1.before_ref = f32[256,1024]{1,0:T(8,128)S(1)} custom-call(bf16[256,1024]{1,0:T(8,128)(2,1)S(1)} %copy-done.1, bf16[1024,2048]{1,0:T(8,128)(2,1)S(1)} %copy-done), custom_call_target="tpu_custom_call" | custom-call | flops 536870912 | bytes 5767168 | tf_op jit(solution)/shard_map/own_grad/pallas_call | solution.py:35
  14.2 0.0 collective-permute-done.1.refs_0_
  14.2 0.5 %collective-permute-done.2.refs_1_ = bf16[336,128]{1,0:T(8,128)(2,1)S(1)} collective-permute-done((bf16[336,128]{1,0:T(8,128)(2,1)S(1)}, bf16[336,128]{1,0:T(8,128)(2,1)S(1)}, u32[]{:S(2)}, u32[]{:S(2)}) %collective-permute-start.2) | collective-permute-done | bytes 86048 | tf_op jit(solution)/shard_map/prior_share/ppermute | solution.py:487
  14.7 0.0 collective-permute-done.3.refs_2_
  14.7 0.2 prior_share.1
  14.9 1.5 %collective-permute-start.4 = (bf16[160,128]{1,0:T(8,128)(2,1)S(1)}, bf16[160,128]{1,0:T(8,128)(2,1)S(1)}, u32[]{:S(2)}, u32[]{:S(2)}) collective-permute-start(bf16[160,128]{1,0:T(8,128)(2,1)S(1)} %get-tuple-element.54), channel_id=1, source_target_pairs={{0,8},{2,10},{4,12},{6,14},{8,0},{10,2},{12,4},{14,6},{16,24},{18,... | collective-permute-start | bytes 122888 | tf_op jit(solution)/shard_map/prior_planes/ppermute | solution.py:487
  16.3 2.6 %collective-permute-start.5 = (bf16[160,128]{1,0:T(8,128)(2,1)S(1)}, bf16[160,128]{1,0:T(8,128)(2,1)S(1)}, u32[]{:S(2)}, u32[]{:S(2)}) collective-permute-start(bf16[160,128]{1,0:T(8,128)(2,1)S(1)} %get-tuple-element.54), channel_id=1, source_target_pairs={{0,16},{2,18},{4,20},{6,22},{8,24},{10,26},{12,28},{14,30},{16,0},... | collective-permute-start | bytes 122888 | tf_op jit(solution)/shard_map/prior_planes/ppermute | solution.py:487
  18.9 0.3 collective-permute-start.6
  19.3 0.6 %collective-permute-start.7 = (bf16[192,128]{1,0:T(8,128)(2,1)S(1)}, bf16[192,128]{1,0:T(8,128)(2,1)S(1)}, u32[]{:S(2)}, u32[]{:S(2)}) collective-permute-start(bf16[192,128]{1,0:T(8,128)(2,1)S(1)} %get-tuple-element.55), channel_id=1, source_target_pairs={{0,8},{2,10},{4,12},{6,14},{8,0},{10,2},{12,4},{14,6},{16,24},{18,... | collective-permute-start | bytes 147464 | tf_op jit(solution)/shard_map/prior_planes/ppermute | solution.py:487
  19.8 0.0 collective-permute-done.4.refs_4_
  19.8 2.9 %collective-permute-start.10 = (bf16[192,128]{1,0:T(8,128)(2,1)S(1)}, bf16[192,128]{1,0:T(8,128)(2,1)S(1)}, u32[]{:S(2)}, u32[]{:S(2)}) collective-permute-start(bf16[192,128]{1,0:T(8,128)(2,1)S(1)} %get-tuple-element.55), channel_id=1, source_target_pairs={{0,24},{2,26},{4,28},{6,30},{8,16},{10,18},{12,20},{14,22},{16,8},... | collective-permute-start | bytes 147464 | tf_op jit(solution)/shard_map/prior_planes/ppermute | solution.py:487
  22.8 0.0 collective-permute-done.8.refs_0_
  22.8 0.6 %collective-permute-start.9 = (bf16[192,128]{1,0:T(8,128)(2,1)S(1)}, bf16[192,128]{1,0:T(8,128)(2,1)S(1)}, u32[]{:S(2)}, u32[]{:S(2)}) collective-permute-start(bf16[192,128]{1,0:T(8,128)(2,1)S(1)} %get-tuple-element.55), channel_id=1, source_target_pairs={{0,16},{2,18},{4,20},{6,22},{8,24},{10,26},{12,28},{14,30},{16,0},... | collective-permute-start | bytes 147464 | tf_op jit(solution)/shard_map/prior_planes/ppermute | solution.py:487
  23.4 0.7 %out_grad.1.og_ref = f32[256,1024]{1,0:T(8,128)S(1)} custom-call(f32[256,1024]{1,0:T(8,128)S(1)} %own_grad.1.before_ref, bf16[256,1024]{1,0:T(8,128)(2,1)S(1)} %collective-permute-done.8.refs_0_, bf16[1024,2048]{1,0:T(8,128)(2,1)S(1)} %copy-done), custom_call_target="tpu_custom_call" | custom-call | flops 536870912 | bytes 6815744 | tf_op jit(solution)/shard_map/out_grad/pallas_call | solution.py:35
  24.1 0.0 collective-permute-done.5.refs_5_
  24.2 0.6 %collective-permute-done.6.refs_6_ = bf16[160,128]{1,0:T(8,128)(2,1)S(1)} collective-permute-done((bf16[160,128]{1,0:T(8,128)(2,1)S(1)}, bf16[160,128]{1,0:T(8,128)(2,1)S(1)}, u32[]{:S(2)}, u32[]{:S(2)}) %collective-permute-start.6) | collective-permute-done | bytes 40992 | tf_op jit(solution)/shard_map/prior_planes/ppermute | solution.py:487
  24.7 1.0 %scaled_grad.1 = (f32[256,8]{1,0:T(8,128)S(1)}, bf16[256,1024]{1,0:T(8,128)(2,1)S(1)}, f32[320,128]{1,0:T(8,128)S(1)}, bf16[4,320,128]{2,1,0:T(8,128)(2,1)S(1)}) custom-call(f32[8,256]{1,0:T(8,128)S(1)} %get-tuple-element.46.den_ref, bf16[8,160,256]{2,1,0:T(8,128)(2,1)S(1)} %get-tuple-element.47.qd_ref, f32[256,1024]{1,0:T(8,128)S(1)} %out_grad.1.og_ref, ...), custom_call_target="tpu_custom_call" | custom-call | flops 83886080 | bytes 3289088 | tf_op jit(solution)/shard_map/scaled_grad/pallas_call | solution.py:35
  25.8 0.1 collective-permute-start.14
  25.9 0.8 %collective-permute-start.15 = (bf16[320,128]{1,0:T(8,128)(2,1)S(1)}, bf16[320,128]{1,0:T(8,128)(2,1)S(1)}, u32[]{:S(2)}, u32[]{:S(2)}) collective-permute-start(bf16[320,128]{1,0:T(8,128)(2,1)S(1)} %get-tuple-element.82), channel_id=1, source_target_pairs={{0,4},{2,6},{4,0},{6,2},{8,12},{10,14},{12,8},{14,10},{16,20},{18,... | collective-permute-start | bytes 245768 | tf_op jit(solution)/shard_map/later_share/ppermute | solution.py:487
  26.6 0.0 collective-permute-done.7.refs_7_
  26.7 1.1 %collective-permute-start.16 = (bf16[320,128]{1,0:T(8,128)(2,1)S(1)}, bf16[320,128]{1,0:T(8,128)(2,1)S(1)}, u32[]{:S(2)}, u32[]{:S(2)}) collective-permute-start(bf16[320,128]{1,0:T(8,128)(2,1)S(1)} %get-tuple-element.81), channel_id=1, source_target_pairs={{0,2},{2,0},{4,6},{6,4},{8,10},{10,8},{12,14},{14,12},{16,18},{18,... | collective-permute-start | bytes 245768 | tf_op jit(solution)/shard_map/later_share/ppermute | solution.py:487
  27.7 0.0 collective-permute-done.10.refs_9_
  27.8 0.2 prior_back.1
  28.0 0.4 collective-permute-start.11
  28.5 1.3 %collective-permute-start.12 = (bf16[320,128]{1,0:T(8,128)(2,1)S(1)}, bf16[320,128]{1,0:T(8,128)(2,1)S(1)}, u32[]{:S(2)}, u32[]{:S(2)}) collective-permute-start(bf16[320,128]{1,0:T(8,128)(2,1)S(1)} %get-tuple-element.86), channel_id=1, source_target_pairs={{0,4},{2,6},{4,0},{6,2},{8,12},{10,14},{12,8},{14,10},{16,20},{18,... | collective-permute-start | bytes 245768 | tf_op jit(solution)/shard_map/prior_back/ppermute | solution.py:487
  29.7 0.5 %collective-permute-done.14.refs_0_ = bf16[320,128]{1,0:T(8,128)(2,1)S(1)} collective-permute-done((bf16[320,128]{1,0:T(8,128)(2,1)S(1)}, bf16[320,128]{1,0:T(8,128)(2,1)S(1)}, u32[]{:S(2)}, u32[]{:S(2)}) %collective-permute-start.14) | collective-permute-done | bytes 81952 | tf_op jit(solution)/shard_map/later_share/ppermute | solution.py:487
  30.3 0.0 collective-permute-start.13
  30.3 1.0 %collective-permute-done.15.refs_1_ = bf16[320,128]{1,0:T(8,128)(2,1)S(1)} collective-permute-done((bf16[320,128]{1,0:T(8,128)(2,1)S(1)}, bf16[320,128]{1,0:T(8,128)(2,1)S(1)}, u32[]{:S(2)}, u32[]{:S(2)}) %collective-permute-start.15) | collective-permute-done | bytes 81952 | tf_op jit(solution)/shard_map/later_share/ppermute | solution.py:487
  31.3 1.8 %collective-permute-start.19 = (bf16[320,128]{1,0:T(8,128)(2,1)S(1)}, bf16[320,128]{1,0:T(8,128)(2,1)S(1)}, u32[]{:S(2)}, u32[]{:S(2)}) collective-permute-start(bf16[320,128]{1,0:T(8,128)(2,1)S(1)} %later_planes.1), channel_id=1, source_target_pairs={{0,16},{2,18},{4,20},{6,22},{8,24},{10,26},{12,28},{14,30},{16,0},... | collective-permute-start | bytes 245768 | tf_op jit(solution)/shard_map/later_planes/ppermute | solution.py:487
  33.1 0.9 %collective-permute-start.20 = (bf16[320,128]{1,0:T(8,128)(2,1)S(1)}, bf16[320,128]{1,0:T(8,128)(2,1)S(1)}, u32[]{:S(2)}, u32[]{:S(2)}) collective-permute-start(bf16[320,128]{1,0:T(8,128)(2,1)S(1)} %later_planes.1), channel_id=1, source_target_pairs={{0,24},{2,26},{4,28},{6,30},{8,16},{10,18},{12,20},{14,22},{16,8},... | collective-permute-start | bytes 245768 | tf_op jit(solution)/shard_map/later_planes/ppermute | solution.py:487
  34.0 0.0 collective-permute-done.11
  34.0 0.9 %collective-permute-done.12 = bf16[320,128]{1,0:T(8,128)(2,1)S(1)} collective-permute-done((bf16[320,128]{1,0:T(8,128)(2,1)S(1)}, bf16[320,128]{1,0:T(8,128)(2,1)S(1)}, u32[]{:S(2)}, u32[]{:S(2)}) %collective-permute-start.12) | collective-permute-done | bytes 81952 | tf_op jit(solution)/shard_map/prior_back/ppermute | solution.py:487
  34.9 1.0 %attended.1 = (bf16[256,1024]{1,0:T(8,128)(2,1)S(1)}, bf16[256,1024]{1,0:T(8,128)(2,1)S(1)}) custom-call(bf16[8,256,160]{2,1,0:T(8,128)(2,1)S(1)} %get-tuple-element.48.qt_ref, bf16[4,320,128]{2,1,0:T(8,128)(2,1)S(1)} %pad_maximum_fusion.prior_ref, f32[256,1024]{1,0:T(8,128)S(1)} %get-tuple-element.63.num_ref, f32[256,8]{1,0:T(8,128)S(1)} %get-tuple-element.64.inv_ref, ...), custom_call_target="tpu_custom_call" | custom-call | flops 620756992 | bytes 7282688 | tf_op jit(solution)/shard_map/attended/pallas_call | solution.py:35
  35.9 1.8 %collective-permute-start.17 = (bf16[256,1024]{1,0:T(8,128)(2,1)S(1)}, bf16[256,1024]{1,0:T(8,128)(2,1)S(1)}, u32[]{:S(2)}, u32[]{:S(2)}) collective-permute-start(bf16[256,1024]{1,0:T(8,128)(2,1)S(1)} %get-tuple-element.67), channel_id=1, source_target_pairs={{0,1},{1,0},{2,3},{3,2},{4,5},{5,4},{6,7},{7,6},{8,9},{9,8},{10,11... | collective-permute-start | bytes 1572872 | tf_op jit(solution)/shard_map/attended/ppermute | solution.py:487
  37.7 0.1 collective-permute-start.18
  37.8 0.4 near.1.near_ref
  38.3 0.7 %mixed.1.part_ref = f32[256,1024]{1,0:T(8,128)S(1)} custom-call(bf16[256,1024]{1,0:T(8,128)(2,1)S(1)} %get-tuple-element.66.att_ref, bf16[1024,2048]{1,0:T(8,128)(2,1)S(1)} %copy-done), custom_call_target="tpu_custom_call" | custom-call | flops 1073741824 | bytes 5767168 | tf_op jit(solution)/shard_map/mixed/pallas_call | solution.py:35
  39.0 3.3 %collective-permute-done.18.refs_4_ = bf16[320,128]{1,0:T(8,128)(2,1)S(1)} collective-permute-done((bf16[320,128]{1,0:T(8,128)(2,1)S(1)}, bf16[320,128]{1,0:T(8,128)(2,1)S(1)}, u32[]{:S(2)}, u32[]{:S(2)}) %collective-permute-start.18) | collective-permute-done | bytes 81952 | tf_op jit(solution)/shard_map/later_planes/ppermute | solution.py:487
  42.3 0.0 collective-permute-done.19.refs_5_
  42.3 0.0 collective-permute-done.20.refs_6_
  42.3 0.2 later_back.1
  42.6 0.1 collective-permute-start.21
  42.7 1.1 %collective-permute-start.22 = (bf16[320,128]{1,0:T(8,128)(2,1)S(1)}, bf16[320,128]{1,0:T(8,128)(2,1)S(1)}, u32[]{:S(2)}, u32[]{:S(2)}) collective-permute-start(bf16[320,128]{1,0:T(8,128)(2,1)S(1)} %get-tuple-element.78), channel_id=1, source_target_pairs={{0,4},{2,6},{4,0},{6,2},{8,12},{10,14},{12,8},{14,10},{16,20},{18,... | collective-permute-start | bytes 245768 | tf_op jit(solution)/shard_map/later_back/ppermute | solution.py:487
  43.8 0.8 %collective-permute-start.23 = (bf16[320,128]{1,0:T(8,128)(2,1)S(1)}, bf16[320,128]{1,0:T(8,128)(2,1)S(1)}, u32[]{:S(2)}, u32[]{:S(2)}) collective-permute-start(bf16[320,128]{1,0:T(8,128)(2,1)S(1)} %get-tuple-element.77), channel_id=1, source_target_pairs={{0,6},{2,4},{4,2},{6,0},{8,14},{10,12},{12,10},{14,8},{16,22},{18,... | collective-permute-start | bytes 245768 | tf_op jit(solution)/shard_map/later_back/ppermute | solution.py:487
  44.5 0.0 collective-permute-done.21.refs_1_
  44.6 0.3 far_grad.2.early_ref
  44.8 3.2 %collective-permute-done.22.refs_0_ = bf16[320,128]{1,0:T(8,128)(2,1)S(1)} collective-permute-done((bf16[320,128]{1,0:T(8,128)(2,1)S(1)}, bf16[320,128]{1,0:T(8,128)(2,1)S(1)}, u32[]{:S(2)}, u32[]{:S(2)}) %collective-permute-start.22) | collective-permute-done | bytes 81952 | tf_op jit(solution)/shard_map/later_back/ppermute | solution.py:487
  48.0 0.8 %collective-permute-done.23.refs_1_ = bf16[320,128]{1,0:T(8,128)(2,1)S(1)} collective-permute-done((bf16[320,128]{1,0:T(8,128)(2,1)S(1)}, bf16[320,128]{1,0:T(8,128)(2,1)S(1)}, u32[]{:S(2)}, u32[]{:S(2)}) %collective-permute-start.23) | collective-permute-done | bytes 81952 | tf_op jit(solution)/shard_map/later_back/ppermute | solution.py:487
  48.8 1.0 %far_grad.3 = bf16[256,1024]{1,0:T(8,128)(2,1)} custom-call(bf16[8,256,160]{2,1,0:T(8,128)(2,1)S(1)} %get-tuple-element.68.kt_ref, f32[256,1024]{1,0:T(8,128)S(1)} %near.1.near_ref, bf16[2,256,256]{2,1,0:T(8,128)(2,1)S(1)} %far_grad.2.early_ref, bf16[320,128]{1,0:T(8,128)(2,1)S(1)} %collective-permute-done.22.refs_0_, ...), custom_call_target="tpu_custom_call" | custom-call | flops 1342177280 | bytes 2654208 | tf_op jit(solution)/shard_map/far_grad/pallas_call | solution.py:35
  49.8 0.1 collective-permute-done.17.refs_0_
  50.0 0.8 %mixed_out.1 = bf16[256,1024]{1,0:T(8,128)(2,1)} custom-call(f32[256,1024]{1,0:T(8,128)S(1)} %mixed.1.part_ref, bf16[256,1024]{1,0:T(8,128)(2,1)S(1)} %collective-permute-done.17.refs_0_), custom_call_target="tpu_custom_call" | custom-call | flops 1048576 | bytes 2097152 | tf_op jit(solution)/shard_map/mixed_out/pallas_call | solution.py:35
  (11 shorter events, 0.2 us)
Async XLA Ops:
  1.4 6.8 %collective-permute-start = (bf16[2,1152]{1,0:T(2,128)(2,1)S(1)}, bf16[2,1152]{1,0:T(2,128)(2,1)S(1)}, u32[]{:S(2)}, u32[]{:S(2)}) collective-permute-start(bf16[2,1152]{1,0:T(2,128)(2,1)S(1)} %edge.1), channel_id=1, source_target_pairs={{0,2},{2,4},{4,6},{6,8},{8,10},{10,12},{12,14},{14,16},{16,18},{18... | collective-permute-start | bytes 13832 | tf_op jit(solution)/shard_map/edge/ppermute | solution.py:520
  1.9 20.8 %collective-permute-start.8 = (bf16[256,1024]{1,0:T(8,128)(2,1)}, bf16[256,1024]{1,0:T(8,128)(2,1)S(1)}, u32[]{:S(2)}, u32[]{:S(2)}) collective-permute-start(bf16[256,1024]{1,0:T(8,128)(2,1)} %cot_ref), channel_id=1, source_target_pairs={{0,1},{1,0},{2,3},{3,2},{4,5},{5,4},{6,7},{7,6},{8,9},{9,8},{10,11... | collective-permute-start | bytes 1572872 | tf_op jit(solution)/shard_map/cotangent/ppermute | solution.py:487
  9.2 5.0 %collective-permute-start.1 = (bf16[336,128]{1,0:T(8,128)(2,1)S(1)}, bf16[336,128]{1,0:T(8,128)(2,1)S(1)}, u32[]{:S(2)}, u32[]{:S(2)}) collective-permute-start(bf16[336,128]{1,0:T(8,128)(2,1)S(1)} %get-tuple-element.76), channel_id=1, source_target_pairs={{0,6},{2,4},{4,2},{6,0},{8,14},{10,12},{12,10},{14,8},{16,22},{18,... | collective-permute-start | bytes 258056 | tf_op jit(solution)/shard_map/prior_share/ppermute | solution.py:487
  9.3 5.4 %collective-permute-start.2 = (bf16[336,128]{1,0:T(8,128)(2,1)S(1)}, bf16[336,128]{1,0:T(8,128)(2,1)S(1)}, u32[]{:S(2)}, u32[]{:S(2)}) collective-permute-start(bf16[336,128]{1,0:T(8,128)(2,1)S(1)} %get-tuple-element.75), channel_id=1, source_target_pairs={{0,4},{2,6},{4,0},{6,2},{8,12},{10,14},{12,8},{14,10},{16,20},{18,... | collective-permute-start | bytes 258056 | tf_op jit(solution)/shard_map/prior_share/ppermute | solution.py:487
  9.6 5.1 %collective-permute-start.3 = (bf16[336,128]{1,0:T(8,128)(2,1)S(1)}, bf16[336,128]{1,0:T(8,128)(2,1)S(1)}, u32[]{:S(2)}, u32[]{:S(2)}) collective-permute-start(bf16[336,128]{1,0:T(8,128)(2,1)S(1)} %get-tuple-element.74), channel_id=1, source_target_pairs={{0,2},{2,0},{4,6},{6,4},{8,10},{10,8},{12,14},{14,12},{16,18},{18,... | collective-permute-start | bytes 258056 | tf_op jit(solution)/shard_map/prior_share/ppermute | solution.py:487
  11.1 2.2 %copy-start = (bf16[1024,2048]{1,0:T(8,128)(2,1)S(1)}, bf16[1024,2048]{1,0:T(8,128)(2,1)}, u32[]{:S(2)}) copy-start(bf16[1024,2048]{1,0:T(8,128)(2,1)} %w_ref.5) | copy-start | bytes 12582916
  11.1 2.3 %copy-start.1 = (bf16[256,1024]{1,0:T(8,128)(2,1)S(1)}, bf16[256,1024]{1,0:T(8,128)(2,1)}, u32[]{:S(2)}) copy-start(bf16[256,1024]{1,0:T(8,128)(2,1)} %cot_ref) | copy-start | bytes 1572868
  14.9 5.0 %collective-permute-start.4 = (bf16[160,128]{1,0:T(8,128)(2,1)S(1)}, bf16[160,128]{1,0:T(8,128)(2,1)S(1)}, u32[]{:S(2)}, u32[]{:S(2)}) collective-permute-start(bf16[160,128]{1,0:T(8,128)(2,1)S(1)} %get-tuple-element.54), channel_id=1, source_target_pairs={{0,8},{2,10},{4,12},{6,14},{8,0},{10,2},{12,4},{14,6},{16,24},{18,... | collective-permute-start | bytes 122888 | tf_op jit(solution)/shard_map/prior_planes/ppermute | solution.py:487
  16.3 7.8 %collective-permute-start.5 = (bf16[160,128]{1,0:T(8,128)(2,1)S(1)}, bf16[160,128]{1,0:T(8,128)(2,1)S(1)}, u32[]{:S(2)}, u32[]{:S(2)}) collective-permute-start(bf16[160,128]{1,0:T(8,128)(2,1)S(1)} %get-tuple-element.54), channel_id=1, source_target_pairs={{0,16},{2,18},{4,20},{6,22},{8,24},{10,26},{12,28},{14,30},{16,0},... | collective-permute-start | bytes 122888 | tf_op jit(solution)/shard_map/prior_planes/ppermute | solution.py:487
  18.9 5.8 %collective-permute-start.6 = (bf16[160,128]{1,0:T(8,128)(2,1)S(1)}, bf16[160,128]{1,0:T(8,128)(2,1)S(1)}, u32[]{:S(2)}, u32[]{:S(2)}) collective-permute-start(bf16[160,128]{1,0:T(8,128)(2,1)S(1)} %get-tuple-element.54), channel_id=1, source_target_pairs={{0,24},{2,26},{4,28},{6,30},{8,16},{10,18},{12,20},{14,22},{16,8},... | collective-permute-start | bytes 122888 | tf_op jit(solution)/shard_map/prior_planes/ppermute | solution.py:487
  19.3 7.4 %collective-permute-start.7 = (bf16[192,128]{1,0:T(8,128)(2,1)S(1)}, bf16[192,128]{1,0:T(8,128)(2,1)S(1)}, u32[]{:S(2)}, u32[]{:S(2)}) collective-permute-start(bf16[192,128]{1,0:T(8,128)(2,1)S(1)} %get-tuple-element.55), channel_id=1, source_target_pairs={{0,8},{2,10},{4,12},{6,14},{8,0},{10,2},{12,4},{14,6},{16,24},{18,... | collective-permute-start | bytes 147464 | tf_op jit(solution)/shard_map/prior_planes/ppermute | solution.py:487
  19.8 7.9 %collective-permute-start.10 = (bf16[192,128]{1,0:T(8,128)(2,1)S(1)}, bf16[192,128]{1,0:T(8,128)(2,1)S(1)}, u32[]{:S(2)}, u32[]{:S(2)}) collective-permute-start(bf16[192,128]{1,0:T(8,128)(2,1)S(1)} %get-tuple-element.55), channel_id=1, source_target_pairs={{0,24},{2,26},{4,28},{6,30},{8,16},{10,18},{12,20},{14,22},{16,8},... | collective-permute-start | bytes 147464 | tf_op jit(solution)/shard_map/prior_planes/ppermute | solution.py:487
  22.8 5.0 %collective-permute-start.9 = (bf16[192,128]{1,0:T(8,128)(2,1)S(1)}, bf16[192,128]{1,0:T(8,128)(2,1)S(1)}, u32[]{:S(2)}, u32[]{:S(2)}) collective-permute-start(bf16[192,128]{1,0:T(8,128)(2,1)S(1)} %get-tuple-element.55), channel_id=1, source_target_pairs={{0,16},{2,18},{4,20},{6,22},{8,24},{10,26},{12,28},{14,30},{16,0},... | collective-permute-start | bytes 147464 | tf_op jit(solution)/shard_map/prior_planes/ppermute | solution.py:487
  25.8 4.4 %collective-permute-start.14 = (bf16[320,128]{1,0:T(8,128)(2,1)S(1)}, bf16[320,128]{1,0:T(8,128)(2,1)S(1)}, u32[]{:S(2)}, u32[]{:S(2)}) collective-permute-start(bf16[320,128]{1,0:T(8,128)(2,1)S(1)} %get-tuple-element.83), channel_id=1, source_target_pairs={{0,6},{2,4},{4,2},{6,0},{8,14},{10,12},{12,10},{14,8},{16,22},{18,... | collective-permute-start | bytes 245768 | tf_op jit(solution)/shard_map/later_share/ppermute | solution.py:487
  25.9 5.3 %collective-permute-start.15 = (bf16[320,128]{1,0:T(8,128)(2,1)S(1)}, bf16[320,128]{1,0:T(8,128)(2,1)S(1)}, u32[]{:S(2)}, u32[]{:S(2)}) collective-permute-start(bf16[320,128]{1,0:T(8,128)(2,1)S(1)} %get-tuple-element.82), channel_id=1, source_target_pairs={{0,4},{2,6},{4,0},{6,2},{8,12},{10,14},{12,8},{14,10},{16,20},{18,... | collective-permute-start | bytes 245768 | tf_op jit(solution)/shard_map/later_share/ppermute | solution.py:487
  26.7 4.6 %collective-permute-start.16 = (bf16[320,128]{1,0:T(8,128)(2,1)S(1)}, bf16[320,128]{1,0:T(8,128)(2,1)S(1)}, u32[]{:S(2)}, u32[]{:S(2)}) collective-permute-start(bf16[320,128]{1,0:T(8,128)(2,1)S(1)} %get-tuple-element.81), channel_id=1, source_target_pairs={{0,2},{2,0},{4,6},{6,4},{8,10},{10,8},{12,14},{14,12},{16,18},{18,... | collective-permute-start | bytes 245768 | tf_op jit(solution)/shard_map/later_share/ppermute | solution.py:487
  28.0 5.9 %collective-permute-start.11 = (bf16[320,128]{1,0:T(8,128)(2,1)S(1)}, bf16[320,128]{1,0:T(8,128)(2,1)S(1)}, u32[]{:S(2)}, u32[]{:S(2)}) collective-permute-start(bf16[320,128]{1,0:T(8,128)(2,1)S(1)} %get-tuple-element.87), channel_id=1, source_target_pairs={{0,6},{2,4},{4,2},{6,0},{8,14},{10,12},{12,10},{14,8},{16,22},{18,... | collective-permute-start | bytes 245768 | tf_op jit(solution)/shard_map/prior_back/ppermute | solution.py:487
  28.5 6.4 %collective-permute-start.12 = (bf16[320,128]{1,0:T(8,128)(2,1)S(1)}, bf16[320,128]{1,0:T(8,128)(2,1)S(1)}, u32[]{:S(2)}, u32[]{:S(2)}) collective-permute-start(bf16[320,128]{1,0:T(8,128)(2,1)S(1)} %get-tuple-element.86), channel_id=1, source_target_pairs={{0,4},{2,6},{4,0},{6,2},{8,12},{10,14},{12,8},{14,10},{16,20},{18,... | collective-permute-start | bytes 245768 | tf_op jit(solution)/shard_map/prior_back/ppermute | solution.py:487
  30.3 4.6 %collective-permute-start.13 = (bf16[320,128]{1,0:T(8,128)(2,1)S(1)}, bf16[320,128]{1,0:T(8,128)(2,1)S(1)}, u32[]{:S(2)}, u32[]{:S(2)}) collective-permute-start(bf16[320,128]{1,0:T(8,128)(2,1)S(1)} %get-tuple-element.85), channel_id=1, source_target_pairs={{0,2},{2,0},{4,6},{6,4},{8,10},{10,8},{12,14},{14,12},{16,18},{18,... | collective-permute-start | bytes 245768 | tf_op jit(solution)/shard_map/prior_back/ppermute | solution.py:487
  31.3 11.0 %collective-permute-start.19 = (bf16[320,128]{1,0:T(8,128)(2,1)S(1)}, bf16[320,128]{1,0:T(8,128)(2,1)S(1)}, u32[]{:S(2)}, u32[]{:S(2)}) collective-permute-start(bf16[320,128]{1,0:T(8,128)(2,1)S(1)} %later_planes.1), channel_id=1, source_target_pairs={{0,16},{2,18},{4,20},{6,22},{8,24},{10,26},{12,28},{14,30},{16,0},... | collective-permute-start | bytes 245768 | tf_op jit(solution)/shard_map/later_planes/ppermute | solution.py:487
  33.1 9.3 %collective-permute-start.20 = (bf16[320,128]{1,0:T(8,128)(2,1)S(1)}, bf16[320,128]{1,0:T(8,128)(2,1)S(1)}, u32[]{:S(2)}, u32[]{:S(2)}) collective-permute-start(bf16[320,128]{1,0:T(8,128)(2,1)S(1)} %later_planes.1), channel_id=1, source_target_pairs={{0,24},{2,26},{4,28},{6,30},{8,16},{10,18},{12,20},{14,22},{16,8},... | collective-permute-start | bytes 245768 | tf_op jit(solution)/shard_map/later_planes/ppermute | solution.py:487
  35.9 14.0 %collective-permute-start.17 = (bf16[256,1024]{1,0:T(8,128)(2,1)S(1)}, bf16[256,1024]{1,0:T(8,128)(2,1)S(1)}, u32[]{:S(2)}, u32[]{:S(2)}) collective-permute-start(bf16[256,1024]{1,0:T(8,128)(2,1)S(1)} %get-tuple-element.67), channel_id=1, source_target_pairs={{0,1},{1,0},{2,3},{3,2},{4,5},{5,4},{6,7},{7,6},{8,9},{9,8},{10,11... | collective-permute-start | bytes 1572872 | tf_op jit(solution)/shard_map/attended/ppermute | solution.py:487
  37.7 4.6 %collective-permute-start.18 = (bf16[320,128]{1,0:T(8,128)(2,1)S(1)}, bf16[320,128]{1,0:T(8,128)(2,1)S(1)}, u32[]{:S(2)}, u32[]{:S(2)}) collective-permute-start(bf16[320,128]{1,0:T(8,128)(2,1)S(1)} %later_planes.1), channel_id=1, source_target_pairs={{0,8},{2,10},{4,12},{6,14},{8,0},{10,2},{12,4},{14,6},{16,24},{18,... | collective-permute-start | bytes 245768 | tf_op jit(solution)/shard_map/later_planes/ppermute | solution.py:487
  42.6 1.9 %collective-permute-start.21 = (bf16[320,128]{1,0:T(8,128)(2,1)S(1)}, bf16[320,128]{1,0:T(8,128)(2,1)S(1)}, u32[]{:S(2)}, u32[]{:S(2)}) collective-permute-start(bf16[320,128]{1,0:T(8,128)(2,1)S(1)} %get-tuple-element.79), channel_id=1, source_target_pairs={{0,2},{2,0},{4,6},{6,4},{8,10},{10,8},{12,14},{14,12},{16,18},{18,... | collective-permute-start | bytes 245768 | tf_op jit(solution)/shard_map/later_back/ppermute | solution.py:487
  42.7 5.3 %collective-permute-start.22 = (bf16[320,128]{1,0:T(8,128)(2,1)S(1)}, bf16[320,128]{1,0:T(8,128)(2,1)S(1)}, u32[]{:S(2)}, u32[]{:S(2)}) collective-permute-start(bf16[320,128]{1,0:T(8,128)(2,1)S(1)} %get-tuple-element.78), channel_id=1, source_target_pairs={{0,4},{2,6},{4,0},{6,2},{8,12},{10,14},{12,8},{14,10},{16,20},{18,... | collective-permute-start | bytes 245768 | tf_op jit(solution)/shard_map/later_back/ppermute | solution.py:487
  43.8 5.1 %collective-permute-start.23 = (bf16[320,128]{1,0:T(8,128)(2,1)S(1)}, bf16[320,128]{1,0:T(8,128)(2,1)S(1)}, u32[]{:S(2)}, u32[]{:S(2)}) collective-permute-start(bf16[320,128]{1,0:T(8,128)(2,1)S(1)} %get-tuple-element.77), channel_id=1, source_target_pairs={{0,6},{2,4},{4,2},{6,0},{8,14},{10,12},{12,10},{14,8},{16,22},{18,... | collective-permute-start | bytes 245768 | tf_op jit(solution)/shard_map/later_back/ppermute | solution.py:487
